TPU v7x, 32 devices: a whole 2x2x4 slice. The times are simulated.
32 devices in a mesh: batch: 4 (over y, x), lat: 2 (over core), lon: 4 (over z).
Axes of the slice: x: 2, y: 2, z: 4, core: 2. Of those that a mesh axis runs over, the one named last changes fastest.
Arguments:
- patches: bfloat16 [4, 4, 12, 128, 640], P('batch', 'lat', 'lon'), may hold values from -6 to 6
- kept_index: int32 [4, 4, 12, 64], P('batch', 'lat', 'lon'), may hold values from 0 to 127, as said below
- kept_count: int32 [4, 4, 12], P('batch', 'lat', 'lon'), may hold values from 32 to 64, as said below
- embed_weight: bfloat16 [640, 1280], P('batch'), may hold values from -0.25 to 0.25
- local_qkv: bfloat16 [1280, 3840], P('batch'), may hold values from -6 to 6
- local_out: bfloat16 [1280, 1280], P('batch'), may hold values from -0.15625 to 0.15625
- global_qkv: bfloat16 [1280, 3840], P('batch'), may hold values from -6 to 6
Outputs:
- mixed: bfloat16 [4, 4, 12, 64, 1280], P('batch', 'lat', 'lon')
Inputs may be any that keep to these rules, and one draw needn't show every extreme that they name: `kept_index`: in each window all 64 entries are distinct offsets; the first kept_count of them are the kept tokens in rising order. `kept_count`: every device holds, in its sample, a window with exactly 64 kept tokens.
All inputs are finite; a program needn't handle non-finite values.
Results may differ from a plain program's by a relative error of at most 0.023.
Values may be sent and summed in bfloat16 or wider, within the bound.
No kernel may reach another device: no remote copies, remote signals or barrier semaphores. Data moves between devices by JAX's collectives and lax.ppermute only.
A program may use at most 128 MiB of HBM per device.

v0:
```python
import jax
import jax.numpy as jnp
from jax import lax
from jax.sharding import PartitionSpec as P

HEADS = 8
HD = 160


norm_eps = 1e-05
mask_floor = -1e30


def layer_norm(values):
    centre = values - jnp.mean(values, axis=-1, keepdims=True)
    spread = jnp.mean(centre * centre, axis=-1, keepdims=True)
    return centre * lax.rsqrt(spread + norm_eps)


def fold_product(left_rows, shard_rows):
    return jnp.dot(left_rows, shard_rows, preferred_element_type=jnp.float32)


def attend(query_rows, key_rows, value_rows, keep_mask):
    scores = jnp.einsum(
        "bnhd,bmhd->bhnm", query_rows, key_rows, preferred_element_type=jnp.float32
    ) * HD ** (-0.5)
    scores = jnp.where(keep_mask[:, None, None, :], scores, mask_floor)
    scores = scores - jnp.max(scores, axis=-1, keepdims=True)
    weights = jnp.exp(scores)
    probabilities = (weights / jnp.sum(weights, axis=-1, keepdims=True)).astype(jnp.bfloat16)
    blended = jnp.einsum(
        "bhnm,bmhd->bnhd", probabilities, value_rows, preferred_element_type=jnp.float32
    )
    return blended.astype(jnp.bfloat16).reshape(
        query_rows.shape[0], query_rows.shape[1], HEADS * HD
    )


def owner_work(received, flag_rows, whole_global):
    item_count = received.shape[0]
    slot_values = received.reshape(item_count, -1, received.shape[-1])
    projected = jnp.dot(
        slot_values.reshape(-1, slot_values.shape[-1]),
        whole_global,
        preferred_element_type=jnp.float32,
    )
    slot_values = projected.astype(jnp.bfloat16).reshape(item_count, -1, 3 * HEADS * HD)
    heads_split = slot_values.reshape(item_count, slot_values.shape[1], 3, HEADS, HD)
    keep_mask = flag_rows.reshape(item_count, -1) > 0
    return attend(heads_split[:, :, 0], heads_split[:, :, 1], heads_split[:, :, 2], keep_mask)


def body(patches, kept_index, kept_count, embed_weight, local_qkv, local_out, global_qkv):
    lat_windows = patches.shape[1]
    lon_windows = patches.shape[2]
    windows = lat_windows * lon_windows
    window_tokens = patches.shape[3]
    kept_most = kept_index.shape[3]
    row_count = windows * kept_most
    inner_width = HEADS * HD
    patch_rows = patches.reshape(windows, window_tokens, patches.shape[4])
    index_rows = kept_index.reshape(windows, kept_most)
    kept_mask = lax.broadcasted_iota(jnp.int32, (windows, kept_most), 1) < kept_count.reshape(
        windows, 1
    )
    picked = jnp.take_along_axis(patch_rows, index_rows[:, :, None], axis=1).reshape(row_count, -1)
    embedded = fold_product(
        picked, lax.all_gather(embed_weight, "batch", axis=0, tiled=True)
    ).astype(jnp.bfloat16)
    normed = layer_norm(embedded.astype(jnp.float32)).astype(jnp.bfloat16)
    local_proj = fold_product(
        normed, lax.all_gather(local_qkv, "batch", axis=0, tiled=True)
    ).astype(jnp.bfloat16)
    local_split = local_proj.reshape(windows, kept_most, 3, HEADS, HD)
    local_mix = attend(
        local_split[:, :, 0], local_split[:, :, 1], local_split[:, :, 2], kept_mask
    ).reshape(row_count, inner_width)
    back_sum = fold_product(local_mix, lax.all_gather(local_out, "batch", axis=0, tiled=True))
    hidden = (embedded.astype(jnp.float32) + back_sum).astype(jnp.bfloat16)
    normed_global = layer_norm(hidden.astype(jnp.float32)).astype(jnp.bfloat16)
    whole_global = None
    whole_global = lax.all_gather(global_qkv, "batch", axis=0, tiled=True)
    sent_width = normed_global.shape[1]
    window_ids = lax.broadcasted_iota(jnp.int32, (windows, kept_most), 0)
    slot_rows = (
        jnp.zeros((window_tokens, windows, sent_width), jnp.bfloat16)
        .at[index_rows, window_ids]
        .set(normed_global.reshape(windows, kept_most, sent_width))
    )
    flag_slots = (
        jnp.zeros((window_tokens, windows), jnp.bfloat16)
        .at[index_rows, window_ids]
        .set(kept_mask.astype(jnp.bfloat16))
    )
    lat_size = lax.axis_size("lat")
    lon_size = lax.axis_size("lon")
    owners = lat_size * lon_size
    owned_count = window_tokens // owners
    blended = owner_work(
        lax.all_to_all(
            slot_rows.reshape(owned_count, owners, windows, sent_width),
            ("lat", "lon"),
            split_axis=1,
            concat_axis=2,
            tiled=True,
        ),
        lax.all_to_all(
            flag_slots.reshape(owned_count, owners, windows),
            ("lat", "lon"),
            split_axis=1,
            concat_axis=2,
            tiled=True,
        ),
        whole_global,
    )
    shaped = blended.reshape(blended.shape[0], 1, -1, inner_width)
    returned = lax.all_to_all(shaped, ("lat", "lon"), split_axis=2, concat_axis=1, tiled=True)
    out_slots = returned.reshape(window_tokens, windows, inner_width)
    gathered = out_slots[index_rows, window_ids]
    result = jnp.where(kept_mask[:, :, None], gathered, jnp.zeros_like(gathered))
    return result.reshape(1, lat_windows, lon_windows, kept_most, inner_width)


def solution(mesh):
    return jax.shard_map(
        body,
        mesh=mesh,
        in_specs=(
            P("batch", "lat", "lon", None, None),
            P("batch", "lat", "lon", None),
            P("batch", "lat", "lon"),
            P("batch", None),
            P("batch", None),
            P("batch", None),
            P("batch", None),
        ),
        out_specs=P("batch", "lat", "lon", None, None),
        check_vma=False,
    )
```

profile of v0, /device:TPU:0, one launch (start us, length us, event | category | flops | bytes accessed | tf_op | source)
XLA Modules:
  0.0 416.1 jit_solution(9823738636609916735)
XLA Ops:
  6.5 0.7 all-gather.5.cloned.1.call-update
  7.3 0.0 all-gather.7.cloned.1.call-start
  7.3 0.7 all-gather.7.cloned.1.call-update
  8.0 0.0 all-gather.9.cloned.1.call-start
  8.1 0.7 all-gather.9.cloned.1.call-update
  8.8 0.0 all-gather.11.cloned.1.call-start
  8.8 0.5 all-gather.11.cloned.1.call-update
  9.4 0.1 lt.54
  9.5 0.1 reshape.204
  9.6 0.1 fusion.36
  9.6 0.1 reshape.212
  9.7 18.4 %scatter_fusion.1 = bf16[128,6]{0,1:T(8,128)(2,1)S(1)} fusion(bf16[128,6]{0,1:T(8,128)(2,1)S(1)} %broadcast_in_dim.72, s32[384]{0:T(512)S(1)} %reshape.204, bf16[384]{0:T(512)(128)(2,1)S(1)} %reshape.212), kind=kCustom, calls=%fused_computation.3 | custom fusion | bytes 5376 | tf_op jit(solution)/shard_map/scatter | solution.py:94
  28.1 0.1 reshape.190
  28.2 0.7 copy.43
  28.9 6.3 %all-to-all-start.1 = ((bf16[16,8,6]{0,2,1:T(8,128)(2,1)}), bf16[16,8,6]{0,2,1:T(8,128)(2,1)}, u32[]{:S(2)}, u32[]{:S(2)}) async-start(bf16[16,8,6]{0,2,1:T(8,128)(2,1)} %copy.43), calls=%async_computation.1 | async-start | bytes 32768 | tf_op jit(solution)/shard_map/all_to_all | solution.py:108
  35.3 0.1 reshape.198
  35.3 0.1 broadcast_in_dim_reshape.3
  35.4 4.3 %gather_fusion.1 = bf16[384,640]{1,0:T(8,128)(2,1)S(1)} fusion(bf16[6,128,640]{2,1,0:T(8,128)(2,1)S(1)} %bitcast.64, s32[384]{0:T(512)S(1)} %reshape.198), kind=kCustom, calls=%fused_computation.1 | custom fusion | bytes 986112 | tf_op jit(solution)/shard_map/jit(take_along_axis)/gather | solution.py:67
  39.8 3.7 all-gather.5.cloned.1.call-done
  43.5 2.5 convert_reduce_fusion
  46.0 0.4 fusion.9
  46.4 98.6 %all-gather.7.cloned.1.call-done = bf16[1280,3840]{1,0:T(8,128)(2,1)} async-done(((bf16[320,3840]{1,0:T(8,128)(2,1)}), bf16[1280,3840]{1,0:T(8,128)(2,1)}) %all-gather.7.cloned.1.call-update) | async-done | bytes 9830416 | tf_op jit(solution)/shard_map/all_gather | solution.py:73
  144.9 9.4 %convolution_convert_fusion.1 = bf16[384,3840]{1,0:T(8,128)(2,1)} fusion(bf16[1280,3840]{1,0:T(8,128)(2,1)} %all-gather.7.cloned.1.call-done, bf16[384,1280]{1,0:T(8,128)(2,1)S(1)} %get-tuple-element.17, f32[384]{0:T(512)S(1)} %add_rsqrt_fusion.1, f32[384]{0:T(512)S(1)} %broadcast_multiply_fusion.1), kind=kOutput, calls=%fused_computation.7 | convolution fusion | flops 3778314240 | bytes 13765632 | tf_op jit(solution)/shard_map/dot_general | solution.py:21
  154.3 9.2 %reshape.187 = bf16[6,64,3,8,160]{4,3,2,1,0:T(8,128)(2,1)} reshape(bf16[384,3840]{1,0:T(8,128)(2,1)} %convolution_convert_fusion.1) | data formatting | bytes 5898240 | tf_op jit(solution)/shard_map/reshape | solution.py:75
  163.5 2.7 fusion.39
  166.2 0.8 multiply_select_fusion.4
  167.0 1.1 copy-done.4
  168.1 0.4 fusion.40
  168.5 4.0 fusion.17
  172.5 2.3 copy.39
  174.8 2.0 reshape_reshape.12
  176.8 15.1 %all-gather.9.cloned.1.call-done = bf16[1280,1280]{1,0:T(8,128)(2,1)} async-done(((bf16[320,1280]{1,0:T(8,128)(2,1)}), bf16[1280,1280]{1,0:T(8,128)(2,1)}) %all-gather.9.cloned.1.call-update) | async-done | bytes 3276816 | tf_op jit(solution)/shard_map/all_gather | solution.py:79
  191.9 3.5 fusion.41
  195.4 0.3 multiply_reduce_fusion
  195.7 0.3 multiply_convert_fusion
  196.0 0.1 broadcast_in_dim.67
  196.1 27.9 %scatter_fusion = bf16[128,6,1280]{2,0,1:T(8,128)(2,1)S(1)} fusion(bf16[128,6,1280]{2,0,1:T(8,128)(2,1)S(1)} %broadcast_in_dim.67, s32[384]{0:T(512)S(1)} %reshape.204, bf16[384,1280]{1,0:T(8,128)(2,1)S(1)} %multiply_convert_fusion), kind=kCustom, calls=%fused_computation.2 | custom fusion | bytes 2952192 | tf_op jit(solution)/shard_map/scatter | solution.py:89
  224.1 1.6 copy.40
  225.7 0.0 all-to-all-done.1
  225.7 4.6 %all-to-all-start = ((bf16[16,8,6,1280]{3,0,2,1:T(8,128)(2,1)}), bf16[16,8,6,1280]{3,0,2,1:T(8,128)(2,1)S(1)}, u32[]{:S(2)}, u32[]{:S(2)}) async-start(bf16[16,8,6,1280]{3,0,2,1:T(8,128)(2,1)} %copy.40), calls=%async_computation | async-start | bytes 3932160 | tf_op jit(solution)/shard_map/all_to_all | solution.py:101
  230.3 0.7 broadcast_compare_fusion
  231.0 0.1 copy.44
  231.1 45.0 %all-to-all-done = bf16[16,8,6,1280]{3,0,2,1:T(8,128)(2,1)S(1)} async-done(((bf16[16,8,6,1280]{3,0,2,1:T(8,128)(2,1)}), bf16[16,8,6,1280]{3,0,2,1:T(8,128)(2,1)S(1)}, u32[]{:S(2)}, u32[]{:S(2)}) %all-to-all-start) | async-done | bytes 1966112 | tf_op jit(solution)/shard_map/all_to_all | solution.py:101
  276.1 2.1 copy.41
  278.2 2.8 reshape_reshape.13
  281.0 12.3 %all-gather.11.cloned.1.call-done = bf16[1280,3840]{1,0:T(8,128)(2,1)} async-done(((bf16[320,3840]{1,0:T(8,128)(2,1)}), bf16[1280,3840]{1,0:T(8,128)(2,1)}) %all-gather.11.cloned.1.call-update) | async-done | bytes 9830416 | tf_op jit(solution)/shard_map/all_gather | solution.py:83
  293.2 13.2 %convolution_convert_fusion = bf16[768,3840]{1,0:T(8,128)(2,1)} fusion(bf16[768,1280]{1,0:T(8,128)(2,1)S(1)} %reshape_reshape.13, bf16[1280,3840]{1,0:T(8,128)(2,1)} %all-gather.11.cloned.1.call-done), kind=kOutput, calls=%fused_computation.6 | convolution fusion | flops 7552696320 | bytes 17694720 | tf_op jit(solution)/shard_map/dot_general | solution.py:43
  306.4 16.6 %reshape_reshape.14 = bf16[16,48,3,8,160]{4,3,2,1,0:T(8,128)(2,1)} reshape(bf16[768,3840]{1,0:T(8,128)(2,1)} %convolution_convert_fusion) | data formatting | bytes 11796480 | tf_op jit(solution)/shard_map/reshape;reshape | solution.py:49
  323.0 4.3 %fusion.38 = (bf16[16,48,1,8,160]{4,3,2,1,0:T(8,128)(2,1)S(1)}, bf16[16,48,1,8,160]{4,3,2,1,0:T(8,128)(2,1)S(1)}, bf16[16,48,1,8,160]{4,3,2,1,0:T(8,128)(2,1)S(1)}) fusion(bf16[16,48,3,8,160]{4,3,2,1,0:T(8,128)(2,1)} %reshape_reshape.14), kind=kLoop, calls=%fused_computation.75 | loop fusion | bytes 11796480 | tf_op jit(solution)/shard_map/slice | solution.py:51
  327.4 1.1 fusion.2
  328.5 2.7 fusion.42
  331.2 1.1 convert_bitcast_fusion
  332.3 2.8 copy.54
  335.1 6.3 %reshape.219 = bf16[16,1,48,1280]{3,0,1,2:T(8,128)(2,1)} reshape(bf16[16,48,8,160]{3,2,0,1:T(8,128)(2,1)} %copy.54) | data formatting | bytes 3932160 | tf_op jit(solution)/shard_map/reshape;reshape | solution.py:117
  341.3 4.6 %all-to-all-start.2 = ((bf16[16,1,48,1280]{3,0,1,2:T(8,128)(2,1)}), bf16[16,1,48,1280]{3,0,1,2:T(8,128)(2,1)S(1)}, u32[]{:S(2)}, u32[]{:S(2)}) async-start(bf16[16,1,48,1280]{3,0,1,2:T(8,128)(2,1)} %reshape.219), calls=%async_computation.2 | async-start | bytes 3932160 | tf_op jit(solution)/shard_map/all_to_all | solution.py:118
  345.9 0.1 reshape.192
  346.0 0.1 iota_compare_fusion.1
  346.1 45.6 %all-to-all-done.2 = bf16[16,1,48,1280]{3,0,1,2:T(8,128)(2,1)S(1)} async-done(((bf16[16,1,48,1280]{3,0,1,2:T(8,128)(2,1)}), bf16[16,1,48,1280]{3,0,1,2:T(8,128)(2,1)S(1)}, u32[]{:S(2)}, u32[]{:S(2)}) %all-to-all-start.2) | async-done | bytes 1966112 | tf_op jit(solution)/shard_map/all_to_all | solution.py:118
  391.7 1.8 copy.50
  393.5 4.1 reshape.191
  397.6 2.1 copy.51
  399.7 0.0 copy-start.1
  399.7 7.5 %gather_fusion = bf16[384,1280]{1,0:T(8,128)(2,1)} fusion(bf16[128,6,1280]{2,0,1:T(8,128)(2,1)S(1)} %copy.51, s32[384]{0:T(512)S(1)} %reshape.192), kind=kCustom, calls=%fused_computation | custom fusion | bytes 1969152 | tf_op jit(solution)/shard_map/gather | solution.py:120
  407.3 2.3 broadcast_select_fusion
  (19 shorter events, 0.1 us)
Async XLA Ops:
  6.5 28.9 %copy-start = (bf16[1,2,3,128,640]{4,3,2,1,0:T(8,128)(2,1)S(1)}, bf16[1,2,3,128,640]{4,3,2,1,0:T(8,128)(2,1)}, u32[]{:S(2)}) copy-start(bf16[1,2,3,128,640]{4,3,2,1,0:T(8,128)(2,1)} %param.7) | copy-start | bytes 2949124
  6.5 36.9 %all-gather.5.cloned.1.call-start = ((), (), s32[]{:S(2)}) async-start(), calls=%async_computation.3 | async-start | bytes 2048000 | tf_op jit(solution)/shard_map/all_gather | solution.py:69
  7.3 137.7 %all-gather.7.cloned.1.call-start = ((), (), s32[]{:S(2)}) async-start(), calls=%async_computation.4 | async-start | bytes 12288000 | tf_op jit(solution)/shard_map/all_gather | solution.py:73
  8.0 1.3 copy-start.2
  8.0 1.3 copy-start.3
  8.0 183.9 %all-gather.9.cloned.1.call-start = ((), (), s32[]{:S(2)}) async-start(), calls=%async_computation.5 | async-start | bytes 4096000 | tf_op jit(solution)/shard_map/all_gather | solution.py:79
  8.8 284.5 %all-gather.11.cloned.1.call-start = ((), (), s32[]{:S(2)}) async-start(), calls=%async_computation.6 | async-start | bytes 12288000 | tf_op jit(solution)/shard_map/all_gather | solution.py:83
  28.9 196.8 %all-to-all-start.1 = ((bf16[16,8,6]{0,2,1:T(8,128)(2,1)}), bf16[16,8,6]{0,2,1:T(8,128)(2,1)}, u32[]{:S(2)}, u32[]{:S(2)}) async-start(bf16[16,8,6]{0,2,1:T(8,128)(2,1)} %copy.43), calls=%async_computation.1 | async-start | bytes 32768 | tf_op jit(solution)/shard_map/all_to_all | solution.py:108
  166.9 1.1 copy-start.4
  225.7 50.4 %all-to-all-start = ((bf16[16,8,6,1280]{3,0,2,1:T(8,128)(2,1)}), bf16[16,8,6,1280]{3,0,2,1:T(8,128)(2,1)S(1)}, u32[]{:S(2)}, u32[]{:S(2)}) async-start(bf16[16,8,6,1280]{3,0,2,1:T(8,128)(2,1)} %copy.40), calls=%async_computation | async-start | bytes 3932160 | tf_op jit(solution)/shard_map/all_to_all | solution.py:101
  341.3 50.4 %all-to-all-start.2 = ((bf16[16,1,48,1280]{3,0,1,2:T(8,128)(2,1)}), bf16[16,1,48,1280]{3,0,1,2:T(8,128)(2,1)S(1)}, u32[]{:S(2)}, u32[]{:S(2)}) async-start(bf16[16,1,48,1280]{3,0,1,2:T(8,128)(2,1)} %reshape.219), calls=%async_computation.2 | async-start | bytes 3932160 | tf_op jit(solution)/shard_map/all_to_all | solution.py:118
  399.7 9.8 %copy-start.1 = (bf16[1,2,3,128,640]{4,3,2,1,0:T(8,128)(2,1)S(1)}, bf16[1,2,3,128,640]{4,3,2,1,0:T(8,128)(2,1)}, u32[]{:S(2)}) copy-start(bf16[1,2,3,128,640]{4,3,2,1,0:T(8,128)(2,1)} %param.7) | copy-start | bytes 2949124
Sparse Core Ops, SparseCore 0:
  9.2 34.2 all-gather.4
  45.3 99.5 all-gather.6
  146.8 45.0 all-gather.8
  193.6 99.6 all-gather.10
where the time goes:
time: 417 us; the launch traced here: 416 us
  waiting for transfers between devices  223 us (53%)
  local copies, waits for them, and re-layouts  121 us (29%)
  matrix products  35.5 us (9%)
  starting transfers between devices  15.6 us (4%)
  between operations  13.3 us (3%)
  other arithmetic  7.34 us (2%)
    all_gather x1, waiting for transfers between devices, body(): lax.all_gather(local_qkv, 'batch', axis=0, tiled=True)  98.6 us
    all_to_all x1, waiting for transfers between devices, body(): lax.all_to_all(shaped, ('lat', 'lon'), split_axis=2, concat_axis=1, tiled...  45.6 us
    all_to_all x1, waiting for transfers between devices, body(): lax.all_to_all(slot_rows.reshape(owned_count, owners, windows, sent_width...  45 us
    scatter x1, local copies, waits for them, and re-layouts, body(): slot_rows = jnp.zeros((window_tokens, windows, sent_width), jnp.bfloat16)...  27.9 us
    scatter x1, local copies, waits for them, and re-layouts, body(): flag_slots = jnp.zeros((window_tokens, windows), jnp.bfloat16).at[index_r...  18.4 us
    another operation x1, local copies, waits for them, and re-layouts, owner_work(): slot_values.reshape(item_count, slot_values.shape[1], 3, HEADS, HD)  16.6 us
    dot_general x3, matrix products, fold_product(): return jnp.dot(left_rows, shard_rows, preferred_element_type=jnp.float32)  15.3 us
    all_gather x1, waiting for transfers between devices, body(): lax.all_gather(local_out, 'batch', axis=0, tiled=True)  15.1 us
  transfers between devices with their start and end apart: 7, of which 6 were waited for; matrix products, arithmetic and copies ran while one was open for 23% of the time, Pallas kernels for 0%

commit v1 on v0

--- a/solution.py
+++ b/solution.py
@@ -1,6 +1,10 @@
+import functools
+
 import jax
 import jax.numpy as jnp
 from jax import lax
+from jax.experimental import pallas as pl
+from jax.experimental.pallas import tpu as pltpu
 from jax.sharding import PartitionSpec as P
 
 HEADS = 8
@@ -9,6 +13,8 @@
 
 norm_eps = 1e-05
 mask_floor = -1e30
+vmem_limit = 56 * 1024 * 1024
+exp2_scale = HD ** (-0.5) * 1.4426950408889634
 
 
 def layer_norm(values):
@@ -51,7 +57,7 @@
     return attend(heads_split[:, :, 0], heads_split[:, :, 1], heads_split[:, :, 2], keep_mask)
 
 
-def body(patches, kept_index, kept_count, embed_weight, local_qkv, local_out, global_qkv):
+def owner_body(patches, kept_index, kept_count, embed_weight, local_qkv, local_out, global_qkv):
     lat_windows = patches.shape[1]
     lon_windows = patches.shape[2]
     windows = lat_windows * lon_windows
@@ -79,7 +85,6 @@
     back_sum = fold_product(local_mix, lax.all_gather(local_out, "batch", axis=0, tiled=True))
     hidden = (embedded.astype(jnp.float32) + back_sum).astype(jnp.bfloat16)
     normed_global = layer_norm(hidden.astype(jnp.float32)).astype(jnp.bfloat16)
-    whole_global = None
     whole_global = lax.all_gather(global_qkv, "batch", axis=0, tiled=True)
     sent_width = normed_global.shape[1]
     window_ids = lax.broadcasted_iota(jnp.int32, (windows, kept_most), 0)
@@ -93,9 +98,7 @@
         .at[index_rows, window_ids]
         .set(kept_mask.astype(jnp.bfloat16))
     )
-    lat_size = lax.axis_size("lat")
-    lon_size = lax.axis_size("lon")
-    owners = lat_size * lon_size
+    owners = lax.axis_size("lat") * lax.axis_size("lon")
     owned_count = window_tokens // owners
     blended = owner_work(
         lax.all_to_all(
@@ -122,6 +125,392 @@
     return result.reshape(1, lat_windows, lon_windows, kept_most, inner_width)
 
 
+def whole_block(array):
+    zeros = (0,) * array.ndim
+    return pl.BlockSpec(array.shape, lambda *_: zeros)
+
+
+def assemble(offset_ref, piece_refs, weight_ref):
+    for at, piece in enumerate(piece_refs):
+        start = pl.multiple_of(offset_ref[at], 16)
+        weight_ref[pl.ds(start, piece.shape[0]), :] = piece[...]
+
+
+def call(kernel, steps, offsets, row_inputs, whole_inputs, pieces, outs, scratch, flops, name):
+    specs = [pl.BlockSpec((rows, a.shape[1]), lambda i, _: (i, 0)) for a, rows in row_inputs]
+    specs += [whole_block(a) for a in whole_inputs]
+    specs += [whole_block(a) for a in pieces]
+    arrays = [a for a, _ in row_inputs] + list(whole_inputs) + list(pieces)
+    out_shapes = [jax.ShapeDtypeStruct(s, jnp.bfloat16) for s, _ in outs]
+    moved = sum(a.size * a.dtype.itemsize for a in arrays) + sum(2 * s.size for s in out_shapes)
+    return pl.pallas_call(
+        kernel,
+        grid_spec=pltpu.PrefetchScalarGridSpec(
+            num_scalar_prefetch=1,
+            grid=(steps,),
+            in_specs=specs,
+            out_specs=[pl.BlockSpec((rows, s[1]), lambda i, _: (i, 0)) for s, rows in outs],
+            scratch_shapes=scratch,
+        ),
+        out_shape=out_shapes,
+        compiler_params=pltpu.CompilerParams(vmem_limit_bytes=vmem_limit),
+        cost_estimate=pl.CostEstimate(flops=flops, bytes_accessed=moved, transcendentals=0),
+        name=name,
+    )(offsets, *arrays)
+
+
+def embed_kernel(piece_count, offset_ref, picked_ref, *refs):
+    pieces, (embedded_ref, normed_ref, weight_ref) = refs[:piece_count], refs[piece_count:]
+
+    @pl.when(pl.program_id(0) == 0)
+    def _():
+        assemble(offset_ref, pieces, weight_ref)
+
+    embedded = fold_product(picked_ref[...], weight_ref[...]).astype(jnp.bfloat16)
+    embedded_ref[...] = embedded
+    normed_ref[...] = layer_norm(embedded.astype(jnp.float32)).astype(jnp.bfloat16)
+
+
+def masked_mix(query, key, value, mask):
+    scores = lax.dot_general(
+        query, key, (((1,), (1,)), ((), ())), preferred_element_type=jnp.float32
+    )
+    scores = jnp.where(mask, scores, mask_floor)
+    top = jnp.max(scores, axis=-1, keepdims=True)
+    weights = jnp.exp2((scores - top) * exp2_scale)
+    total = jnp.sum(weights, axis=-1, keepdims=True)
+    mixed = fold_product(weights.astype(jnp.bfloat16), value)
+    return mixed / total
+
+
+def window_kernel(piece_count, kept_most, rows_at_once, offset_ref, normed_ref, code_ref, *refs):
+    pieces, (mix_ref, weight_ref, proj_ref) = refs[:piece_count], refs[piece_count:]
+
+    @pl.when(pl.program_id(0) == 0)
+    def _():
+        assemble(offset_ref, pieces, weight_ref)
+
+    proj_ref[...] = fold_product(normed_ref[...], weight_ref[...]).astype(jnp.bfloat16)
+    width = mix_ref.shape[1]
+    rows = normed_ref.shape[0]
+    own_window = lax.broadcasted_iota(jnp.int32, (rows_at_once, 1), 0) // kept_most
+    for start in range(0, rows, rows_at_once):
+        part = pl.ds(start, rows_at_once)
+        mask = own_window == code_ref[0, :, part]
+        for head in range(width // HD):
+            query, key, value = (
+                proj_ref[part, pl.ds(which * width + head * HD, HD)] for which in range(3)
+            )
+            mix_ref[part, pl.ds(head * HD, HD)] = masked_mix(query, key, value, mask).astype(
+                jnp.bfloat16
+            )
+
+
+def out_kernel(piece_count, mix_count, offset_ref, embedded_ref, *refs):
+    mixes, refs = refs[:mix_count], refs[mix_count:]
+    pieces, (normed_ref, weight_ref) = refs[:piece_count], refs[piece_count:]
+
+    @pl.when(pl.program_id(0) == 0)
+    def _():
+        assemble(offset_ref, pieces, weight_ref)
+
+    hidden = embedded_ref[...].astype(jnp.float32)
+    at = 0
+    for mix in mixes:
+        width = mix.shape[1]
+        hidden += fold_product(mix[...], weight_ref[pl.ds(at, width), :])
+        at += width
+    hidden = hidden.astype(jnp.bfloat16).astype(jnp.float32)
+    normed_ref[...] = layer_norm(hidden).astype(jnp.bfloat16)
+
+
+def project_kernel(piece_count, offset_ref, normed_ref, *refs):
+    pieces, (proj_ref, weight_ref) = refs[:piece_count], refs[piece_count:]
+
+    @pl.when(pl.program_id(0) == 0)
+    def _():
+        assemble(offset_ref, pieces, weight_ref)
+
+    proj_ref[...] = fold_product(normed_ref[...], weight_ref[...]).astype(jnp.bfloat16)
+
+
+def group_kernel(
+    query_ref,
+    code_ref,
+    key_code_ref,
+    key_own_ref,
+    key_other_ref,
+    value_own_ref,
+    value_other_ref,
+    mixed_ref,
+):
+    width = mixed_ref.shape[1]
+    half = key_own_ref.shape[0]
+    codes = code_ref[...]
+    masks = [codes == key_code_ref[:, pl.ds(at, half)] for at in (0, half)]
+    for head in range(width // HD):
+        part = pl.ds(head * HD, HD)
+        query = query_ref[:, part]
+        scores = [
+            jnp.where(
+                mask,
+                lax.dot_general(
+                    query, key[:, part], (((1,), (1,)), ((), ())), preferred_element_type=jnp.float32
+                ),
+                mask_floor,
+            )
+            for key, mask in zip((key_own_ref, key_other_ref), masks)
+        ]
+        top = functools.reduce(
+            jnp.maximum, [jnp.max(s, axis=-1, keepdims=True) for s in scores]
+        )
+        total = 0.0
+        mixed = 0.0
+        for s, value in zip(scores, (value_own_ref, value_other_ref)):
+            weights = jnp.exp2((s - top) * exp2_scale)
+            total += jnp.sum(weights, axis=-1, keepdims=True)
+            mixed += fold_product(weights.astype(jnp.bfloat16), value[:, part])
+        mixed_ref[:, part] = jnp.where(codes >= 0, mixed / total, 0.0).astype(jnp.bfloat16)
+
+
+def swap_perm(size, mask):
+    return [(i, i ^ mask) for i in range(size)]
+
+
+def after(value, earlier):
+    return lax.optimization_barrier((value, earlier))[0]
+
+
+def sample_body(patches, kept_index, kept_count, embed_weight, local_qkv, local_out, global_qkv):
+    lat_windows, lon_windows, window_tokens, pin = patches.shape[1:]
+    windows = lat_windows * lon_windows
+    kept_most = kept_index.shape[3]
+    rows = windows * kept_most
+    inner = HEADS * HD
+    half_inner = inner // 2
+    lon_size = lax.axis_size("lon")
+    batch_size = lax.axis_size("batch")
+    core = lax.axis_index("lat")
+    chip = lax.axis_index("batch")
+    z = lax.axis_index("lon")
+
+    index_rows = kept_index.reshape(windows, kept_most)
+    kept_mask = lax.broadcasted_iota(jnp.int32, (windows, kept_most), 1) < kept_count.reshape(
+        windows, 1
+    )
+    codes = jnp.where(kept_mask, index_rows, -1).reshape(rows)
+    picked = jnp.take_along_axis(
+        patches.reshape(windows, window_tokens, pin), index_rows[:, :, None], axis=1
+    ).reshape(rows, pin)
+
+    ring = [(i, (i + 1) % lon_size) for i in range(lon_size)]
+    picked_parts = [picked]
+    for _ in range(lon_size - 1):
+        picked_parts.append(lax.ppermute(picked_parts[-1], "lon", ring))
+    picked_all = jnp.concatenate(picked_parts, axis=0)
+    all_rows = picked_all.shape[0]
+    all_codes = lax.all_gather(codes, ("lat", "lon"), axis=0, tiled=False).reshape(
+        2, lon_size, rows
+    )
+    order = (z - jnp.arange(lon_size, dtype=jnp.int32)) % lon_size
+    all_codes = all_codes[:, order].reshape(2, all_rows)
+    own_codes = all_codes[core]
+    other_codes = all_codes[1 - core]
+
+    diagonal = []
+    for b in range(batch_size):
+        diagonal += [(2 * b, 2 * (b ^ 1)), (2 * b + 1, 2 * (b ^ 2) + 1)]
+
+    def fetch(part):
+        along_x = lax.ppermute(part, "batch", swap_perm(batch_size, 1))
+        along_y = lax.ppermute(part, "batch", swap_perm(batch_size, 2))
+        forwarded = jnp.where(core == 0, along_y, along_x)
+        across = lax.ppermute(forwarded, ("batch", "lat"), diagonal)
+        return along_x, along_y, across
+
+    def other_core(value):
+        return lax.ppermute(value, "lat", swap_perm(2, 1))
+
+    def shared(shard, got):
+        high = shard.shape[0]
+        part = high // 2
+        pieces, offsets = [shard], [chip * high]
+        for which, value in zip((1, 2, 3), got):
+            pieces += [value, other_core(value)]
+            base = (chip ^ which) * high
+            offsets += [base + core * part, base + (1 - core) * part]
+        return pieces, jnp.stack(offsets).astype(jnp.int32)
+
+    def single(shard, got):
+        high = shard.shape[0]
+        offsets = [(chip ^ which) * high for which in range(4)]
+        return [shard, *got], jnp.stack(offsets).astype(jnp.int32)
+
+    def own_rows(shard):
+        part = shard.shape[0] // 2
+        return lax.dynamic_slice_in_dim(shard, core * part, part, axis=0)
+
+    def head_columns(weight, group):
+        return jnp.concatenate(
+            [
+                weight[:, which * inner + group * half_inner : which * inner + (group + 1) * half_inner]
+                for which in range(3)
+            ],
+            axis=1,
+        )
+
+    local_shards = [head_columns(local_qkv, group) for group in range(2)]
+    global_shards = [
+        lax.dynamic_slice_in_dim(
+            global_qkv, which * inner + core * half_inner, half_inner, axis=1
+        )
+        for which in range(3)
+    ]
+    sent = [own_rows(embed_weight)]
+    sent += [own_rows(s) for s in local_shards]
+    sent += [own_rows(local_out)]
+    sent += [global_shards[1], global_shards[0], global_shards[2]]
+    fetched = []
+    for at, part in enumerate(sent):
+        if at >= 2:
+            part = after(part, fetched[at - 2][:2])
+        fetched.append(fetch(part))
+
+    block = all_rows // 3 if all_rows % 3 == 0 else all_rows
+    steps = all_rows // block
+    weight_scratch = lambda high, wide: pltpu.VMEM((high, wide), jnp.bfloat16)
+    full = pin
+
+    pieces, offsets = shared(embed_weight, fetched[0])
+    width = embed_weight.shape[1]
+    embedded, normed = call(
+        functools.partial(embed_kernel, len(pieces)),
+        steps,
+        offsets,
+        [(picked_all, block)],
+        [],
+        pieces,
+        [((all_rows, width), block)] * 2,
+        [weight_scratch(full, width)],
+        2 * all_rows * full * width,
+        "embed",
+    )
+
+    at_once = 4 * kept_most if block % (4 * kept_most) == 0 else kept_most
+    window_codes = jnp.where(
+        own_codes >= 0, (jnp.arange(all_rows, dtype=jnp.int32) // kept_most) % (at_once // kept_most), -1
+    ).reshape(steps, 1, block)
+    code_spec = [window_codes]
+    mixes = []
+    for group in range(2):
+        pieces, offsets = shared(local_shards[group], fetched[1 + group])
+        specs = [pl.BlockSpec((block, width), lambda i, _: (i, 0))]
+        specs += [pl.BlockSpec((1, 1, block), lambda i, _: (i, 0, 0))]
+        specs += [whole_block(a) for a in pieces]
+        flops = 2 * all_rows * width * 3 * half_inner
+        mixes.append(
+            pl.pallas_call(
+                functools.partial(window_kernel, len(pieces), kept_most, at_once),
+                grid_spec=pltpu.PrefetchScalarGridSpec(
+                    num_scalar_prefetch=1,
+                    grid=(steps,),
+                    in_specs=specs,
+                    out_specs=pl.BlockSpec((block, half_inner), lambda i, _: (i, 0)),
+                    scratch_shapes=[
+                        weight_scratch(width, 3 * half_inner),
+                        weight_scratch(block, 3 * half_inner),
+                    ],
+                ),
+                out_shape=jax.ShapeDtypeStruct((all_rows, half_inner), jnp.bfloat16),
+                compiler_params=pltpu.CompilerParams(vmem_limit_bytes=vmem_limit),
+                cost_estimate=pl.CostEstimate(
+                    flops=flops, bytes_accessed=16 * 1024 * 1024, transcendentals=0
+                ),
+                name="windows",
+            )(offsets, normed, window_codes, *pieces)
+        )
+
+    pieces, offsets = shared(local_out, fetched[3])
+    (normed_own,) = call(
+        functools.partial(out_kernel, len(pieces), len(mixes)),
+        steps,
+        offsets,
+        [(embedded, block)] + [(m, block) for m in mixes],
+        [],
+        pieces,
+        [((all_rows, width), block)],
+        [weight_scratch(inner, width)],
+        2 * all_rows * inner * width,
+        "local_out",
+    )
+    normed_other = other_core(normed_own)
+
+    def project(which, got, values, name):
+        pieces, offsets = single(global_shards[which], got)
+        many = values.shape[0]
+        size = block if many % block == 0 else many
+        (result,) = call(
+            functools.partial(project_kernel, len(pieces)),
+            many // size,
+            offsets,
+            [(values, size)],
+            [],
+            pieces,
+            [((many, half_inner), size)],
+            [weight_scratch(width, half_inner)],
+            2 * many * width * half_inner,
+            name,
+        )
+        return result
+
+    keys = [project(1, fetched[4], v, "keys") for v in (normed_own, normed_other)]
+    queries = project(
+        0, fetched[5], jnp.concatenate([normed_own[:rows], normed_other[:rows]], axis=0), "queries"
+    )
+    values = [project(2, fetched[6], v, "values") for v in (normed_own, normed_other)]
+
+    key_codes = jnp.concatenate([own_codes, other_codes]).reshape(1, 2 * all_rows)
+    query_codes = jnp.concatenate([own_codes[:rows], other_codes[:rows]]).reshape(2 * rows, 1)
+    query_codes = jnp.where(query_codes >= 0, query_codes, -2)
+    query_block = 256 if (2 * rows) % 256 == 0 else 2 * rows
+    resident = [key_codes, *keys, *values]
+    mixed = pl.pallas_call(
+        group_kernel,
+        grid=(2 * rows // query_block,),
+        in_specs=[
+            pl.BlockSpec((query_block, half_inner), lambda i: (i, 0)),
+            pl.BlockSpec((query_block, 1), lambda i: (i, 0)),
+            *[whole_block(a) for a in resident],
+        ],
+        out_specs=pl.BlockSpec((query_block, half_inner), lambda i: (i, 0)),
+        out_shape=jax.ShapeDtypeStruct((2 * rows, half_inner), jnp.bfloat16),
+        compiler_params=pltpu.CompilerParams(vmem_limit_bytes=vmem_limit),
+        cost_estimate=pl.CostEstimate(
+            flops=4 * 2 * rows * 2 * all_rows * half_inner,
+            bytes_accessed=16 * 1024 * 1024,
+            transcendentals=0,
+        ),
+        name="groups",
+    )(queries, query_codes, *resident)
+
+    mine, theirs = mixed[:rows], other_core(mixed[rows:])
+    result = jnp.where(
+        core == 0,
+        jnp.concatenate([mine, theirs], axis=1),
+        jnp.concatenate([theirs, mine], axis=1),
+    )
+    return result.reshape(1, lat_windows, lon_windows, kept_most, inner)
+
+
+def body(patches, kept_index, *weights):
+    rows = patches.shape[1] * patches.shape[2] * kept_index.shape[3]
+    sample_rows = rows * lax.axis_size("lat") * lax.axis_size("lon")
+    fits = sample_rows * HEADS * HD * 2 <= vmem_limit // 4
+    if lax.axis_size("batch") == 4 and lax.axis_size("lat") == 2 and fits:
+        return sample_body(patches, kept_index, *weights)
+    return owner_body(patches, kept_index, *weights)
+
+
 def solution(mesh):
     return jax.shard_map(
         body,

time: 417 us -> 280 us (0.67)
  waiting for transfers between devices: 223 us -> 59.1 us
  Pallas kernels: 0 us -> 124 us
  local copies, waits for them, and re-layouts: 121 us -> 24 us
  matrix products: 35.5 us -> 0 us
  blocking collectives: 0 us -> 25.2 us
  starting transfers between devices: 15.6 us -> 35 us
  between operations: 13.3 us -> 0.43 us
  other arithmetic: 7.34 us -> 11.8 us
    all_gather x4 -> x0, waiting for transfers between devices: 130 us -> none  [the longest x1 98.6 us: body(): lax.all_gather(local_qkv, 'batch', axis=0, tiled=True)]
    pallas_call x0 -> x10, Pallas kernels: none -> 124 us  [the longest x7 57.5 us: call(): pl.pallas_call(kernel, grid_spec=pltpu.PrefetchScalarGridSpec(num_scalar_...]
    all_to_all x3 -> x0, waiting for transfers between devices: 90.6 us -> none  [the longest x1 45.6 us: body(): lax.all_to_all(shaped, ('lat', 'lon'), split_axis=2, concat_axis=1, tiled...]
    ppermute x0 -> x38, waiting for transfers between devices: none -> 59.1 us  [the longest x7 29.3 us: fetch(): along_x = lax.ppermute(part, 'batch', swap_perm(batch_size, 1))]
    scatter x2 -> x0, local copies, waits for them, and re-layouts: 46.3 us -> none  [the longest x1 27.9 us: body(): slot_rows = jnp.zeros((window_tokens, windows, sent_width), jnp.bfloat16)...]
    dot_general x8 -> x0, matrix products: 35.5 us -> none  [the longest x3 15.3 us: fold_product(): return jnp.dot(left_rows, shard_rows, preferred_element_type=jnp.float32)]
    ppermute x0 -> x38, starting transfers between devices: none -> 35 us  [the longest x7 9.22 us: fetch(): along_x = lax.ppermute(part, 'batch', swap_perm(batch_size, 1))]
    another operation x6 -> x3, local copies, waits for them, and re-layouts: 30.4 us -> 1.3 us  [the longest x2 1.22 us: shared(): return (pieces, jnp.stack(offsets).astype(jnp.int32))]
  transfers between devices with their start and end apart: 7 -> 38, of which waited for: 6 -> 12; matrix products, arithmetic and copies ran while one was open for 23% -> 9% of each run, Pallas kernels for 0% -> 29%
where the time goes in v1:
time: 280 us
  Pallas kernels  124 us (44%)
  waiting for transfers between devices  59.1 us (21%)
  starting transfers between devices  35 us (12%)
  blocking collectives  25.2 us (9%)
  local copies, waits for them, and re-layouts  24 us (9%)
  other arithmetic  11.8 us (4%)
    pallas_call x7, Pallas kernels, call(): pl.pallas_call(kernel, grid_spec=pltpu.PrefetchScalarGridSpec(num_scalar_...  57.5 us
    pallas_call x2, Pallas kernels, sample_body(): pl.pallas_call(functools.partial(window_kernel, len(pieces), kept_most, a...  43.3 us
    ppermute x7, waiting for transfers between devices, fetch(): along_x = lax.ppermute(part, 'batch', swap_perm(batch_size, 1))  29.3 us
    all_gather x1, blocking collectives, sample_body(): lax.all_gather(codes, ('lat', 'lon'), axis=0, tiled=False)  25.2 us
    pallas_call x1, Pallas kernels, sample_body(): pl.pallas_call(group_kernel, grid=(2 * rows // query_block,), in_specs=[p...  23.3 us
    ppermute x3, waiting for transfers between devices, sample_body(): picked_parts.append(lax.ppermute(picked_parts[-1], 'lon', ring))  13.3 us
    ppermute x7, waiting for transfers between devices, fetch(): across = lax.ppermute(forwarded, ('batch', 'lat'), diagonal)  10.6 us
    ppermute x7, starting transfers between devices, fetch(): along_x = lax.ppermute(part, 'batch', swap_perm(batch_size, 1))  9.22 us
  transfers between devices with their start and end apart: 38, of which 12 were waited for; matrix products, arithmetic and copies ran while one was open for 9% of the time, Pallas kernels for 29%

profile of v1, /device:TPU:0, one launch (start us, length us, event | category | flops | bytes accessed | tf_op | source)
XLA Modules:
  0.0 279.7 jit_solution(11564114721898218631)
XLA Ops:
  0.0 1.7 constant_dynamic-slice_fusion.8
  1.7 2.9 %collective-permute-start.3 = (bf16[80,1280]{1,0:T(8,128)(2,1)}, bf16[80,1280]{1,0:T(8,128)(2,1)}, u32[]{:S(2)}, u32[]{:S(2)}) collective-permute-start(bf16[80,1280]{1,0:T(8,128)(2,1)} %constant_dynamic-slice_fusion.8), channel_id=1, source_target_pairs={{0,8},{8,0},{16,24},{24,16},{1,9},{9,1},{17,25},{25,17},{2,10},{10... | collective-permute-start | bytes 614408 | tf_op jit(solution)/shard_map/ppermute | solution.py:325
  4.7 1.5 collective-permute-start.5
  6.2 2.8 fusion.10
  8.9 1.2 pad_maximum_fusion.2.refs_0_
  10.2 1.0 constant_dynamic-slice_fusion.7
  11.9 4.3 %gather_fusion.1 = bf16[384,640]{1,0:T(8,128)(2,1)S(1)} fusion(bf16[6,128,640]{2,1,0:T(8,128)(2,1)S(1)} %bitcast.37, s32[384]{0:T(512)S(1)} %reshape.393), kind=kCustom, calls=%fused_computation.1 | custom fusion | bytes 986112 | tf_op jit(solution)/shard_map/jit(take_along_axis)/gather | solution.py:302
  16.4 2.1 collective-permute-start
  18.9 25.2 %all-gather = s32[8,1,384]{2,1,0:T(1,128)S(1)} all-gather(s32[1,1,384]{2,1,0:T(1,128)S(1)} %select_bitcast_fusion), channel_id=1, replica_groups=mesh['batch'=4,'lat'=2,'lon'=4] {'lat','lon'}, dimensions={0}, use_global_device_ids=true | all-gather | bytes 13824 | tf_op jit(solution)/shard_map/all_gather | solution.py:312
  44.2 1.1 pad_maximum_fusion.3.refs_0_
  47.2 1.0 constant_dynamic-slice_fusion.5
  48.9 1.3 collective-permute-start.15
  50.2 1.5 collective-permute-start.17
  51.7 1.1 collective-permute-start.4
  52.9 1.1 broadcast_select_fusion.1
  54.8 1.0 broadcast_select_fusion.7
  55.8 1.6 collective-permute-start.7
  57.3 1.5 collective-permute-start.1
  58.8 6.3 %collective-permute-done.15.refs_1_ = bf16[160,1920]{1,0:T(8,128)(2,1)S(1)} collective-permute-done((bf16[160,1920]{1,0:T(8,128)(2,1)S(1)}, bf16[160,1920]{1,0:T(8,128)(2,1)S(1)}, u32[]{:S(2)}, u32[]{:S(2)}) %collective-permute-start.15) | collective-permute-done | bytes 614432 | tf_op jit(solution)/shard_map/ppermute | solution.py:325
  65.1 1.1 collective-permute-start.21
  66.6 1.5 collective-permute-start.23
  68.2 10.6 %collective-permute-done.7.refs_5_ = bf16[80,1280]{1,0:T(8,128)(2,1)S(1)} collective-permute-done((bf16[80,1280]{1,0:T(8,128)(2,1)S(1)}, bf16[80,1280]{1,0:T(8,128)(2,1)S(1)}, u32[]{:S(2)}, u32[]{:S(2)}) %collective-permute-start.7) | collective-permute-done | bytes 204832 | tf_op jit(solution)/shard_map/ppermute | solution.py:328
  78.8 1.4 collective-permute-start.10
  80.3 2.9 %collective-permute-done.21.refs_3_ = bf16[160,1280]{1,0:T(8,128)(2,1)S(1)} collective-permute-done((bf16[160,1280]{1,0:T(8,128)(2,1)S(1)}, bf16[160,1280]{1,0:T(8,128)(2,1)S(1)}, u32[]{:S(2)}, u32[]{:S(2)}) %collective-permute-start.21) | collective-permute-done | bytes 409632 | tf_op jit(solution)/shard_map/ppermute | solution.py:325
  83.1 1.3 collective-permute-start.19
  84.5 1.4 collective-permute-start.2
  86.0 13.3 %collective-permute-done.2 = bf16[384,640]{1,0:T(8,128)(2,1)S(1)} collective-permute-done((bf16[384,640]{1,0:T(8,128)(2,1)S(1)}, bf16[384,640]{1,0:T(8,128)(2,1)S(1)}, u32[]{:S(2)}, u32[]{:S(2)}) %collective-permute-start.2) | collective-permute-done | bytes 491552 | tf_op jit(solution)/shard_map/ppermute | solution.py:309
  99.2 1.5 pad_maximum_fusion.picked_ref
  101.4 8.9 %embed.1 = (bf16[1536,1280]{1,0:T(8,128)(2,1)}, bf16[1536,1280]{1,0:T(8,128)(2,1)}) custom-call(s32[7]{0:T(128)} %stack.116.offset_ref, bf16[1536,640]{1,0:T(8,128)(2,1)} %pad_maximum_fusion.picked_ref, bf16[160,1280]{1,0:T(8,128)(2,1)} %refs_0_.1, bf16[80,1280]{1,0:T(8,128)(2,1)} %collective-permute-done.3.refs_1_, ...), custom_call_target="tpu_custom_call" | custom-call | flops 2516582400 | bytes 11468800 | tf_op jit(solution)/shard_map/embed/pallas_call | solution.py:146
  112.4 21.7 %windows.2.refs_0_ = bf16[1536,640]{1,0:T(8,128)(2,1)} custom-call(s32[7]{0:T(128)} %stack.51.offset_ref, bf16[1536,1280]{1,0:T(8,128)(2,1)} %get-tuple-element.13.normed_ref, s32[3,1,512]{2,1,0:T(1,128)} %fusion.code_ref, bf16[320,1920]{1,0:T(8,128)(2,1)} %copy-done.2, bf16[160,1920]{1,0:T(8,128)(2,1)} %collective-permute-done.9.refs_1_, ...), custom_call_target="tpu_custom_call" | custom-call | flops 7549747200 | bytes 16777216 | tf_op jit(solution)/shard_map/windows/pallas_call | solution.py:412
  135.6 0.8 copy-done.23
  136.4 21.7 %windows.3.refs_1_ = bf16[1536,640]{1,0:T(8,128)(2,1)} custom-call(s32[7]{0:T(128)} %stack.51.offset_ref, bf16[1536,1280]{1,0:T(8,128)(2,1)} %get-tuple-element.13.normed_ref, s32[3,1,512]{2,1,0:T(1,128)} %fusion.code_ref, bf16[320,1920]{1,0:T(8,128)(2,1)} %copy-done.3, bf16[160,1920]{1,0:T(8,128)(2,1)} %copy-done.5, bf16[160,1920]{1,0:T(8,128)(2,1)} %copy-done.21, ...), custom_call_target="tpu_custom_call" | custom-call | flops 7549747200 | bytes 16777216 | tf_op jit(solution)/shard_map/windows/pallas_call | solution.py:412
  158.1 0.7 copy-done.25
  159.6 13.7 %local_out.1.normed_ref = bf16[1536,1280]{1,0:T(8,128)(2,1)} custom-call(s32[7]{0:T(128)} %stack.51.offset_ref, bf16[1536,1280]{1,0:T(8,128)(2,1)} %get-tuple-element.12.embedded_ref, bf16[1536,640]{1,0:T(8,128)(2,1)} %windows.2.refs_0_, bf16[1536,640]{1,0:T(8,128)(2,1)} %windows.3.refs_1_, bf16[320,1280]{1,0:T(8,128)(2,1)} %refs_2_.1, ...), custom_call_target="tpu_custom_call" | custom-call | flops 5033164800 | bytes 15073280 | tf_op jit(solution)/shard_map/local_out/pallas_call | solution.py:146
  173.6 1.0 constant_dynamic-slice_fusion.1
  174.7 0.8 collective-permute-start.31
  175.5 1.5 collective-permute-start.32
  177.5 0.8 broadcast_select_fusion.8.code_ref
  178.3 8.1 %collective-permute-done.31.refs_1_ = bf16[320,640]{1,0:T(8,128)(2,1)S(1)} collective-permute-done((bf16[320,640]{1,0:T(8,128)(2,1)}, bf16[320,640]{1,0:T(8,128)(2,1)S(1)}, u32[]{:S(2)}, u32[]{:S(2)}) %collective-permute-start.31) | collective-permute-done | bytes 409632 | tf_op jit(solution)/shard_map/ppermute | solution.py:325
  186.4 0.8 collective-permute-done.32.refs_2_
  187.2 1.0 collective-permute-start.34
  188.2 1.1 collective-permute-start.35
  190.5 1.5 collective-permute-start.28
  192.6 7.2 %collective-permute-done.34.refs_1_ = bf16[320,640]{1,0:T(8,128)(2,1)S(1)} collective-permute-done((bf16[320,640]{1,0:T(8,128)(2,1)}, bf16[320,640]{1,0:T(8,128)(2,1)S(1)}, u32[]{:S(2)}, u32[]{:S(2)}) %collective-permute-start.34) | collective-permute-done | bytes 409632 | tf_op jit(solution)/shard_map/ppermute | solution.py:325
  199.8 1.0 collective-permute-start.33
  200.8 1.1 collective-permute-start.36
  202.0 4.8 %collective-permute-done.28.refs_1_ = bf16[320,640]{1,0:T(8,128)(2,1)S(1)} collective-permute-done((bf16[320,640]{1,0:T(8,128)(2,1)S(1)}, bf16[320,640]{1,0:T(8,128)(2,1)S(1)}, u32[]{:S(2)}, u32[]{:S(2)}) %collective-permute-start.28) | collective-permute-done | bytes 409632 | tf_op jit(solution)/shard_map/ppermute | solution.py:325
  206.8 2.7 collective-permute-done.29.refs_2_
  209.6 1.1 collective-permute-start.30
  210.7 1.3 slice.54
  212.1 0.8 copy-done.28
  212.8 7.4 %keys.2.key_own_ref = bf16[1536,640]{1,0:T(8,128)(2,1)} custom-call(s32[4]{0:T(128)} %pad_add_fusion.2.offset_ref, bf16[1536,1280]{1,0:T(8,128)(2,1)} %local_out.1.normed_ref, bf16[320,640]{1,0:T(8,128)(2,1)} %get-tuple-element.17.refs_0_, bf16[320,640]{1,0:T(8,128)(2,1)} %copy-done.10, bf16[320,640]{1,0:T(8,128)(2,1)} %copy-done.11, bf16[320,640]{1,0:T(8,128)(2,1)} %copy-done.28), custom_call_target="tpu_custom_call" | custom-call | flops 2516582400 | bytes 7536640 | tf_op jit(solution)/shard_map/keys/pallas_call | solution.py:146
  220.2 0.7 copy-done.30
  221.0 7.4 %values.2.value_own_ref = bf16[1536,640]{1,0:T(8,128)(2,1)} custom-call(s32[4]{0:T(128)} %pad_add_fusion.2.offset_ref, bf16[1536,1280]{1,0:T(8,128)(2,1)} %local_out.1.normed_ref, bf16[320,640]{1,0:T(8,128)(2,1)} %get-tuple-element.18.refs_0_, bf16[320,640]{1,0:T(8,128)(2,1)} %copy-done.12, bf16[320,640]{1,0:T(8,128)(2,1)} %copy-done.13, ...), custom_call_target="tpu_custom_call" | custom-call | flops 2516582400 | bytes 7536640 | tf_op jit(solution)/shard_map/values/pallas_call | solution.py:146
  228.3 7.4 %keys.3.key_other_ref = bf16[1536,640]{1,0:T(8,128)(2,1)} custom-call(s32[4]{0:T(128)} %pad_add_fusion.2.offset_ref, bf16[1536,1280]{1,0:T(8,128)(2,1)} %collective-permute-done.27.normed_ref, bf16[320,640]{1,0:T(8,128)(2,1)} %get-tuple-element.17.refs_0_, bf16[320,640]{1,0:T(8,128)(2,1)} %copy-done.10, bf16[320,640]{1,0:T(8,128)(2,1)} %copy-done.11, ...), custom_call_target="tpu_custom_call" | custom-call | flops 2516582400 | bytes 7536640 | tf_op jit(solution)/shard_map/keys/pallas_call | solution.py:146
  235.7 7.4 %values.3.value_other_ref = bf16[1536,640]{1,0:T(8,128)(2,1)} custom-call(s32[4]{0:T(128)} %pad_add_fusion.2.offset_ref, bf16[1536,1280]{1,0:T(8,128)(2,1)} %collective-permute-done.27.normed_ref, bf16[320,640]{1,0:T(8,128)(2,1)} %get-tuple-element.18.refs_0_, bf16[320,640]{1,0:T(8,128)(2,1)} %copy-done.12, bf16[320,640]{1,0:T(8,128)(2,1)} %copy-done.13, ...), custom_call_target="tpu_custom_call" | custom-call | flops 2516582400 | bytes 7536640 | tf_op jit(solution)/shard_map/values/pallas_call | solution.py:146
  243.1 1.3 slice.55
  244.4 1.4 pad_maximum_fusion.1.normed_ref
  245.8 0.8 copy-done.27
  246.6 5.4 %queries.1.query_ref = bf16[768,640]{1,0:T(8,128)(2,1)} custom-call(s32[4]{0:T(128)} %pad_add_fusion.2.offset_ref, bf16[768,1280]{1,0:T(8,128)(2,1)} %pad_maximum_fusion.1.normed_ref, bf16[320,640]{1,0:T(8,128)(2,1)} %copy-done.7, bf16[320,640]{1,0:T(8,128)(2,1)} %copy-done.14, bf16[320,640]{1,0:T(8,128)(2,1)} %copy-done.15, bf16[320,640]{1,0:T(8,128)(2,1)} %copy-done.27), custom_call_target="tpu_custom_call" | custom-call | flops 1258291200 | bytes 4587520 | tf_op jit(solution)/shard_map/queries/pallas_call | solution.py:146
  252.0 23.3 %groups.1 = bf16[768,640]{1,0:T(8,128)(2,1)} custom-call(bf16[768,640]{1,0:T(8,128)(2,1)} %queries.1.query_ref, s32[768,1]{1,0:T(8,128)} %broadcast_select_fusion.8.code_ref, s32[1,3072]{1,0:T(1,128)} %bitcast.44, bf16[1536,640]{1,0:T(8,128)(2,1)} %keys.2.key_own_ref, bf16[1536,640]{1,0:T(8,128)(2,1)} %keys.3.key_other_ref, ...), custom_call_target="tpu_custom_call" | custom-call | flops 6039797760 | bytes 16777216 | tf_op jit(solution)/shard_map/groups/pallas_call | solution.py:477
  275.3 1.3 fusion.11
  276.7 1.9 collective-permute-done.37
  278.5 1.2 maximum_select_fusion
  (145 shorter events, 13.0 us)
Async XLA Ops:
  0.0 11.9 %copy-start = (bf16[1,2,3,128,640]{4,3,2,1,0:T(8,128)(2,1)S(1)}, bf16[1,2,3,128,640]{4,3,2,1,0:T(8,128)(2,1)}, u32[]{:S(2)}) copy-start(bf16[1,2,3,128,640]{4,3,2,1,0:T(8,128)(2,1)} %param.7) | copy-start | bytes 2949124
  1.7 47.1 %collective-permute-start.3 = (bf16[80,1280]{1,0:T(8,128)(2,1)}, bf16[80,1280]{1,0:T(8,128)(2,1)}, u32[]{:S(2)}, u32[]{:S(2)}) collective-permute-start(bf16[80,1280]{1,0:T(8,128)(2,1)} %constant_dynamic-slice_fusion.8), channel_id=1, source_target_pairs={{0,8},{8,0},{16,24},{24,16},{1,9},{9,1},{17,25},{25,17},{2,10},{10... | collective-permute-start | bytes 614408 | tf_op jit(solution)/shard_map/ppermute | solution.py:325
  4.7 44.2 %collective-permute-start.5 = (bf16[80,1280]{1,0:T(8,128)(2,1)}, bf16[80,1280]{1,0:T(8,128)(2,1)}, u32[]{:S(2)}, u32[]{:S(2)}) collective-permute-start(bf16[80,1280]{1,0:T(8,128)(2,1)} %constant_dynamic-slice_fusion.8), channel_id=1, source_target_pairs={{0,16},{8,24},{16,0},{24,8},{1,17},{9,25},{17,1},{25,9},{2,18},{10... | collective-permute-start | bytes 614408 | tf_op jit(solution)/shard_map/ppermute | solution.py:326
  8.9 2.7 copy-start.16
  10.2 6.1 %copy-start.2 = (bf16[320,1920]{1,0:T(8,128)(2,1)}, bf16[320,1920]{1,0:T(8,128)(2,1)S(1)}, u32[]{:S(2)}) copy-start(bf16[320,1920]{1,0:T(8,128)(2,1)S(1)} %pad_maximum_fusion.2.refs_0_) | copy-start | bytes 3686404
  11.1 40.6 %collective-permute-start.9 = (bf16[160,1920]{1,0:T(8,128)(2,1)}, bf16[160,1920]{1,0:T(8,128)(2,1)}, u32[]{:S(2)}, u32[]{:S(2)}) collective-permute-start(bf16[160,1920]{1,0:T(8,128)(2,1)} %constant_dynamic-slice_fusion.7), channel_id=1, source_target_pairs={{0,8},{8,0},{16,24},{24,16},{1,9},{9,1},{17,25},{25,17},{2,10},{10... | collective-permute-start | bytes 1843208 | tf_op jit(solution)/shard_map/ppermute | solution.py:325
  11.7 41.1 %collective-permute-start.11 = (bf16[160,1920]{1,0:T(8,128)(2,1)}, bf16[160,1920]{1,0:T(8,128)(2,1)}, u32[]{:S(2)}, u32[]{:S(2)}) collective-permute-start(bf16[160,1920]{1,0:T(8,128)(2,1)} %constant_dynamic-slice_fusion.7), channel_id=1, source_target_pairs={{0,16},{8,24},{16,0},{24,8},{1,17},{9,25},{17,1},{25,9},{2,18},{10... | collective-permute-start | bytes 1843208 | tf_op jit(solution)/shard_map/ppermute | solution.py:326
  11.9 6.7 %copy-start.34 = (s32[1,2,3]{2,1,0:T(2,128)S(1)}, s32[1,2,3]{2,1,0:T(2,128)}, u32[]{:S(2)}) copy-start(s32[1,2,3]{2,1,0:T(2,128)} %param.9) | copy-start | bytes 76
  16.4 40.9 %collective-permute-start = (bf16[384,640]{1,0:T(8,128)(2,1)S(1)}, bf16[384,640]{1,0:T(8,128)(2,1)S(1)}, u32[]{:S(2)}, u32[]{:S(2)}) collective-permute-start(bf16[384,640]{1,0:T(8,128)(2,1)S(1)} %broadcast_select_fusion.2), channel_id=1, source_target_pairs={{0,1},{1,2},{2,3},{3,0},{4,5},{5,6},{6,7},{7,4},{8,9},{9,10},{10,1... | collective-permute-start | bytes 1474568 | tf_op jit(solution)/shard_map/ppermute | solution.py:309
  45.3 8.7 %copy-start.3 = (bf16[320,1920]{1,0:T(8,128)(2,1)}, bf16[320,1920]{1,0:T(8,128)(2,1)S(1)}, u32[]{:S(2)}) copy-start(bf16[320,1920]{1,0:T(8,128)(2,1)S(1)} %pad_maximum_fusion.3.refs_0_) | copy-start | bytes 3686404
  48.9 16.3 %collective-permute-start.15 = (bf16[160,1920]{1,0:T(8,128)(2,1)S(1)}, bf16[160,1920]{1,0:T(8,128)(2,1)S(1)}, u32[]{:S(2)}, u32[]{:S(2)}) collective-permute-start(bf16[160,1920]{1,0:T(8,128)(2,1)S(1)} %constant_dynamic-slice_fusion.6), channel_id=1, source_target_pairs={{0,8},{8,0},{16,24},{24,16},{1,9},{9,1},{17,25},{25,17},{2,10},{10... | collective-permute-start | bytes 1843208 | tf_op jit(solution)/shard_map/ppermute | solution.py:325
  50.2 16.4 %collective-permute-start.17 = (bf16[160,1920]{1,0:T(8,128)(2,1)S(1)}, bf16[160,1920]{1,0:T(8,128)(2,1)S(1)}, u32[]{:S(2)}, u32[]{:S(2)}) collective-permute-start(bf16[160,1920]{1,0:T(8,128)(2,1)S(1)} %constant_dynamic-slice_fusion.6), channel_id=1, source_target_pairs={{0,16},{8,24},{16,0},{24,8},{1,17},{9,25},{17,1},{25,9},{2,18},{10... | collective-permute-start | bytes 1843208 | tf_op jit(solution)/shard_map/ppermute | solution.py:326
  51.7 2.5 collective-permute-start.4
  52.8 2.9 %collective-permute-start.6 = (bf16[80,1280]{1,0:T(8,128)(2,1)}, bf16[80,1280]{1,0:T(8,128)(2,1)S(1)}, u32[]{:S(2)}, u32[]{:S(2)}) collective-permute-start(bf16[80,1280]{1,0:T(8,128)(2,1)} %collective-permute-done.5.refs_3_), channel_id=1, source_target_pairs={{0,4},{4,0},{1,5},{5,1},{2,6},{6,2},{3,7},{7,3},{8,12},{12,8},{9,1... | collective-permute-start | bytes 614408 | tf_op jit(solution)/shard_map/ppermute | solution.py:332
  54.2 31.7 %collective-permute-start.13 = (bf16[160,1920]{1,0:T(8,128)(2,1)S(1)}, bf16[160,1920]{1,0:T(8,128)(2,1)S(1)}, u32[]{:S(2)}, u32[]{:S(2)}) collective-permute-start(bf16[160,1920]{1,0:T(8,128)(2,1)S(1)} %broadcast_select_fusion.1), channel_id=1, source_target_pairs={{0,8},{4,20},{8,0},{12,28},{16,24},{20,4},{24,16},{28,12},{1,9},{5... | collective-permute-start | bytes 1843208 | tf_op jit(solution)/shard_map/ppermute | solution.py:328
  55.8 24.5 %copy-start.31 = (bf16[80,1280]{1,0:T(8,128)(2,1)}, bf16[80,1280]{1,0:T(8,128)(2,1)S(1)}, u32[]{:S(2)}) copy-start(bf16[80,1280]{1,0:T(8,128)(2,1)S(1)} %collective-permute-done.6.refs_4_) | copy-start | bytes 614404
  55.8 23.0 %collective-permute-start.7 = (bf16[80,1280]{1,0:T(8,128)(2,1)S(1)}, bf16[80,1280]{1,0:T(8,128)(2,1)S(1)}, u32[]{:S(2)}, u32[]{:S(2)}) collective-permute-start(bf16[80,1280]{1,0:T(8,128)(2,1)S(1)} %broadcast_select_fusion.7), channel_id=1, source_target_pairs={{0,8},{4,20},{8,0},{12,28},{16,24},{20,4},{24,16},{28,12},{1,9},{5... | collective-permute-start | bytes 614408 | tf_op jit(solution)/shard_map/ppermute | solution.py:328
  57.3 22.9 %collective-permute-start.1 = (bf16[384,640]{1,0:T(8,128)(2,1)S(1)}, bf16[384,640]{1,0:T(8,128)(2,1)S(1)}, u32[]{:S(2)}, u32[]{:S(2)}) collective-permute-start(bf16[384,640]{1,0:T(8,128)(2,1)S(1)} %collective-permute-done), channel_id=1, source_target_pairs={{0,1},{1,2},{2,3},{3,0},{4,5},{5,6},{6,7},{7,4},{8,9},{9,10},{10,1... | collective-permute-start | bytes 1474568 | tf_op jit(solution)/shard_map/ppermute | solution.py:309
  65.1 35.6 %copy-start.5 = (bf16[160,1920]{1,0:T(8,128)(2,1)}, bf16[160,1920]{1,0:T(8,128)(2,1)S(1)}, u32[]{:S(2)}) copy-start(bf16[160,1920]{1,0:T(8,128)(2,1)S(1)} %collective-permute-done.15.refs_1_) | copy-start | bytes 1843204
  65.1 18.0 %collective-permute-start.21 = (bf16[160,1280]{1,0:T(8,128)(2,1)S(1)}, bf16[160,1280]{1,0:T(8,128)(2,1)S(1)}, u32[]{:S(2)}, u32[]{:S(2)}) collective-permute-start(bf16[160,1280]{1,0:T(8,128)(2,1)S(1)} %constant_dynamic-slice_fusion.5), channel_id=1, source_target_pairs={{0,8},{8,0},{16,24},{24,16},{1,9},{9,1},{17,25},{25,17},{2,10},{10... | collective-permute-start | bytes 1228808 | tf_op jit(solution)/shard_map/ppermute | solution.py:325
  66.6 43.8 %copy-start.6 = (bf16[160,1920]{1,0:T(8,128)(2,1)}, bf16[160,1920]{1,0:T(8,128)(2,1)S(1)}, u32[]{:S(2)}) copy-start(bf16[160,1920]{1,0:T(8,128)(2,1)S(1)} %collective-permute-done.17.refs_3_) | copy-start | bytes 1843204
  66.6 17.9 %collective-permute-start.23 = (bf16[160,1280]{1,0:T(8,128)(2,1)S(1)}, bf16[160,1280]{1,0:T(8,128)(2,1)S(1)}, u32[]{:S(2)}, u32[]{:S(2)}) collective-permute-start(bf16[160,1280]{1,0:T(8,128)(2,1)S(1)} %constant_dynamic-slice_fusion.5), channel_id=1, source_target_pairs={{0,16},{8,24},{16,0},{24,8},{1,17},{9,25},{17,1},{25,9},{2,18},{10... | collective-permute-start | bytes 1228808 | tf_op jit(solution)/shard_map/ppermute | solution.py:326
  78.8 22.0 %copy-start.32 = (bf16[80,1280]{1,0:T(8,128)(2,1)}, bf16[80,1280]{1,0:T(8,128)(2,1)S(1)}, u32[]{:S(2)}) copy-start(bf16[80,1280]{1,0:T(8,128)(2,1)S(1)} %collective-permute-done.7.refs_5_) | copy-start | bytes 614404
  78.8 31.6 %collective-permute-start.10 = (bf16[160,1920]{1,0:T(8,128)(2,1)}, bf16[160,1920]{1,0:T(8,128)(2,1)S(1)}, u32[]{:S(2)}, u32[]{:S(2)}) collective-permute-start(bf16[160,1920]{1,0:T(8,128)(2,1)} %collective-permute-done.9.refs_1_), channel_id=1, source_target_pairs={{0,4},{4,0},{1,5},{5,1},{2,6},{6,2},{3,7},{7,3},{8,12},{12,8},{9,1... | collective-permute-start | bytes 1843208 | tf_op jit(solution)/shard_map/ppermute | solution.py:332
  80.2 30.7 %collective-permute-start.12 = (bf16[160,1920]{1,0:T(8,128)(2,1)}, bf16[160,1920]{1,0:T(8,128)(2,1)S(1)}, u32[]{:S(2)}, u32[]{:S(2)}) collective-permute-start(bf16[160,1920]{1,0:T(8,128)(2,1)} %collective-permute-done.11.refs_3_), channel_id=1, source_target_pairs={{0,4},{4,0},{1,5},{5,1},{2,6},{6,2},{3,7},{7,3},{8,12},{12,8},{9,1... | collective-permute-start | bytes 1843208 | tf_op jit(solution)/shard_map/ppermute | solution.py:332
  83.1 28.5 %copy-start.8 = (bf16[160,1280]{1,0:T(8,128)(2,1)}, bf16[160,1280]{1,0:T(8,128)(2,1)S(1)}, u32[]{:S(2)}) copy-start(bf16[160,1280]{1,0:T(8,128)(2,1)S(1)} %collective-permute-done.21.refs_3_) | copy-start | bytes 1228804
  83.1 28.5 %collective-permute-start.19 = (bf16[160,1920]{1,0:T(8,128)(2,1)S(1)}, bf16[160,1920]{1,0:T(8,128)(2,1)S(1)}, u32[]{:S(2)}, u32[]{:S(2)}) collective-permute-start(bf16[160,1920]{1,0:T(8,128)(2,1)S(1)} %broadcast_select_fusion), channel_id=1, source_target_pairs={{0,8},{4,20},{8,0},{12,28},{16,24},{20,4},{24,16},{28,12},{1,9},{5... | collective-permute-start | bytes 1843208 | tf_op jit(solution)/shard_map/ppermute | solution.py:328
  84.5 49.6 %copy-start.9 = (bf16[160,1280]{1,0:T(8,128)(2,1)}, bf16[160,1280]{1,0:T(8,128)(2,1)S(1)}, u32[]{:S(2)}) copy-start(bf16[160,1280]{1,0:T(8,128)(2,1)S(1)} %collective-permute-done.23.refs_5_) | copy-start | bytes 1228804
  84.5 14.7 %collective-permute-start.2 = (bf16[384,640]{1,0:T(8,128)(2,1)S(1)}, bf16[384,640]{1,0:T(8,128)(2,1)S(1)}, u32[]{:S(2)}, u32[]{:S(2)}) collective-permute-start(bf16[384,640]{1,0:T(8,128)(2,1)S(1)} %collective-permute-done.1), channel_id=1, source_target_pairs={{0,1},{1,2},{2,3},{3,0},{4,5},{5,6},{6,7},{7,4},{8,9},{9,10},{10,1... | collective-permute-start | bytes 1474568 | tf_op jit(solution)/shard_map/ppermute | solution.py:309
  85.9 14.8 %copy-start.17 = (bf16[160,1920]{1,0:T(8,128)(2,1)}, bf16[160,1920]{1,0:T(8,128)(2,1)S(1)}, u32[]{:S(2)}) copy-start(bf16[160,1920]{1,0:T(8,128)(2,1)S(1)} %collective-permute-done.13.refs_5_) | copy-start | bytes 1843204
  85.9 26.4 %collective-permute-start.14 = (bf16[160,1920]{1,0:T(8,128)(2,1)S(1)}, bf16[160,1920]{1,0:T(8,128)(2,1)}, u32[]{:S(2)}, u32[]{:S(2)}) collective-permute-start(bf16[160,1920]{1,0:T(8,128)(2,1)S(1)} %collective-permute-done.13.refs_5_), channel_id=1, source_target_pairs={{0,4},{4,0},{1,5},{5,1},{2,6},{6,2},{3,7},{7,3},{8,12},{12,8},{9,1... | collective-permute-start | bytes 1843208 | tf_op jit(solution)/shard_map/ppermute | solution.py:332
  99.2 1.5 collective-permute-start.8
  100.7 33.4 %collective-permute-start.16 = (bf16[160,1920]{1,0:T(8,128)(2,1)S(1)}, bf16[160,1920]{1,0:T(8,128)(2,1)S(1)}, u32[]{:S(2)}, u32[]{:S(2)}) collective-permute-start(bf16[160,1920]{1,0:T(8,128)(2,1)S(1)} %collective-permute-done.15.refs_1_), channel_id=1, source_target_pairs={{0,4},{4,0},{1,5},{5,1},{2,6},{6,2},{3,7},{7,3},{8,12},{12,8},{9,1... | collective-permute-start | bytes 1843208 | tf_op jit(solution)/shard_map/ppermute | solution.py:332
  110.3 2.1 copy-start.19
  110.4 24.4 %collective-permute-start.18 = (bf16[160,1920]{1,0:T(8,128)(2,1)S(1)}, bf16[160,1920]{1,0:T(8,128)(2,1)S(1)}, u32[]{:S(2)}, u32[]{:S(2)}) collective-permute-start(bf16[160,1920]{1,0:T(8,128)(2,1)S(1)} %collective-permute-done.17.refs_3_), channel_id=1, source_target_pairs={{0,4},{4,0},{1,5},{5,1},{2,6},{6,2},{3,7},{7,3},{8,12},{12,8},{9,1... | collective-permute-start | bytes 1843208 | tf_op jit(solution)/shard_map/ppermute | solution.py:332
  110.9 1.5 copy-start.20
  110.9 23.7 %collective-permute-start.25 = (bf16[160,1280]{1,0:T(8,128)(2,1)S(1)}, bf16[160,1280]{1,0:T(8,128)(2,1)S(1)}, u32[]{:S(2)}, u32[]{:S(2)}) collective-permute-start(bf16[160,1280]{1,0:T(8,128)(2,1)S(1)} %broadcast_select_fusion.6), channel_id=1, source_target_pairs={{0,8},{4,20},{8,0},{12,28},{16,24},{20,4},{24,16},{28,12},{1,9},{5... | collective-permute-start | bytes 1228808 | tf_op jit(solution)/shard_map/ppermute | solution.py:328
  111.6 22.5 %copy-start.18 = (bf16[160,1920]{1,0:T(8,128)(2,1)}, bf16[160,1920]{1,0:T(8,128)(2,1)S(1)}, u32[]{:S(2)}) copy-start(bf16[160,1920]{1,0:T(8,128)(2,1)S(1)} %collective-permute-done.19.refs_5_) | copy-start | bytes 1843204
  111.6 46.4 %collective-permute-start.22 = (bf16[160,1280]{1,0:T(8,128)(2,1)S(1)}, bf16[160,1280]{1,0:T(8,128)(2,1)S(1)}, u32[]{:S(2)}, u32[]{:S(2)}) collective-permute-start(bf16[160,1280]{1,0:T(8,128)(2,1)S(1)} %collective-permute-done.21.refs_3_), channel_id=1, source_target_pairs={{0,4},{4,0},{1,5},{5,1},{2,6},{6,2},{3,7},{7,3},{8,12},{12,8},{9,1... | collective-permute-start | bytes 1228808 | tf_op jit(solution)/shard_map/ppermute | solution.py:332
  112.3 22.4 %collective-permute-start.20 = (bf16[160,1920]{1,0:T(8,128)(2,1)S(1)}, bf16[160,1920]{1,0:T(8,128)(2,1)S(1)}, u32[]{:S(2)}, u32[]{:S(2)}) collective-permute-start(bf16[160,1920]{1,0:T(8,128)(2,1)S(1)} %collective-permute-done.19.refs_5_), channel_id=1, source_target_pairs={{0,4},{4,0},{1,5},{5,1},{2,6},{6,2},{3,7},{7,3},{8,12},{12,8},{9,1... | collective-permute-start | bytes 1843208 | tf_op jit(solution)/shard_map/ppermute | solution.py:332
  134.1 24.0 %collective-permute-start.24 = (bf16[160,1280]{1,0:T(8,128)(2,1)S(1)}, bf16[160,1280]{1,0:T(8,128)(2,1)S(1)}, u32[]{:S(2)}, u32[]{:S(2)}) collective-permute-start(bf16[160,1280]{1,0:T(8,128)(2,1)S(1)} %collective-permute-done.23.refs_5_), channel_id=1, source_target_pairs={{0,4},{4,0},{1,5},{5,1},{2,6},{6,2},{3,7},{7,3},{8,12},{12,8},{9,1... | collective-permute-start | bytes 1228808 | tf_op jit(solution)/shard_map/ppermute | solution.py:332
  134.6 23.5 %copy-start.24 = (bf16[160,1280]{1,0:T(8,128)(2,1)}, bf16[160,1280]{1,0:T(8,128)(2,1)S(1)}, u32[]{:S(2)}) copy-start(bf16[160,1280]{1,0:T(8,128)(2,1)S(1)} %collective-permute-done.25.refs_7_) | copy-start | bytes 1228804
  134.6 23.5 %collective-permute-start.26 = (bf16[160,1280]{1,0:T(8,128)(2,1)S(1)}, bf16[160,1280]{1,0:T(8,128)(2,1)S(1)}, u32[]{:S(2)}, u32[]{:S(2)}) collective-permute-start(bf16[160,1280]{1,0:T(8,128)(2,1)S(1)} %collective-permute-done.25.refs_7_), channel_id=1, source_target_pairs={{0,4},{4,0},{1,5},{5,1},{2,6},{6,2},{3,7},{7,3},{8,12},{12,8},{9,1... | collective-permute-start | bytes 1228808 | tf_op jit(solution)/shard_map/ppermute | solution.py:332
  158.1 0.9 copy-start.26
  159.6 14.1 %copy-start.4 = (bf16[320,3840]{1,0:T(8,128)(2,1)S(1)}, bf16[320,3840]{1,0:T(8,128)(2,1)}, u32[]{:S(2)}) copy-start(bf16[320,3840]{1,0:T(8,128)(2,1)} %param.13) | copy-start | bytes 7372804
  173.3 55.1 %collective-permute-start.27 = (bf16[1536,1280]{1,0:T(8,128)(2,1)}, bf16[1536,1280]{1,0:T(8,128)(2,1)}, u32[]{:S(2)}, u32[]{:S(2)}) collective-permute-start(bf16[1536,1280]{1,0:T(8,128)(2,1)} %local_out.1.normed_ref), channel_id=1, source_target_pairs={{0,4},{4,0},{1,5},{5,1},{2,6},{6,2},{3,7},{7,3},{8,12},{12,8},{9,1... | collective-permute-start | bytes 11796488 | tf_op jit(solution)/shard_map/ppermute | solution.py:332
  174.7 26.1 %copy-start.7 = (bf16[320,640]{1,0:T(8,128)(2,1)}, bf16[320,640]{1,0:T(8,128)(2,1)S(1)}, u32[]{:S(2)}) copy-start(bf16[320,640]{1,0:T(8,128)(2,1)S(1)} %get-tuple-element.16.refs_0_) | copy-start | bytes 1228804
  174.7 11.7 %collective-permute-start.31 = (bf16[320,640]{1,0:T(8,128)(2,1)}, bf16[320,640]{1,0:T(8,128)(2,1)S(1)}, u32[]{:S(2)}, u32[]{:S(2)}) collective-permute-start(bf16[320,640]{1,0:T(8,128)(2,1)} %get-tuple-element.17.refs_0_), channel_id=1, source_target_pairs={{0,8},{8,0},{16,24},{24,16},{1,9},{9,1},{17,25},{25,17},{2,10},{10... | collective-permute-start | bytes 1228808 | tf_op jit(solution)/shard_map/ppermute | solution.py:325
  175.5 11.7 %collective-permute-start.32 = (bf16[320,640]{1,0:T(8,128)(2,1)}, bf16[320,640]{1,0:T(8,128)(2,1)S(1)}, u32[]{:S(2)}, u32[]{:S(2)}) collective-permute-start(bf16[320,640]{1,0:T(8,128)(2,1)} %get-tuple-element.17.refs_0_), channel_id=1, source_target_pairs={{0,16},{8,24},{16,0},{24,8},{1,17},{9,25},{17,1},{25,9},{2,18},{10... | collective-permute-start | bytes 1228808 | tf_op jit(solution)/shard_map/ppermute | solution.py:326
  186.4 25.6 %copy-start.10 = (bf16[320,640]{1,0:T(8,128)(2,1)}, bf16[320,640]{1,0:T(8,128)(2,1)S(1)}, u32[]{:S(2)}) copy-start(bf16[320,640]{1,0:T(8,128)(2,1)S(1)} %collective-permute-done.31.refs_1_) | copy-start | bytes 1228804
  187.2 24.8 %copy-start.11 = (bf16[320,640]{1,0:T(8,128)(2,1)}, bf16[320,640]{1,0:T(8,128)(2,1)S(1)}, u32[]{:S(2)}) copy-start(bf16[320,640]{1,0:T(8,128)(2,1)S(1)} %collective-permute-done.32.refs_2_) | copy-start | bytes 1228804
  187.2 12.6 %collective-permute-start.34 = (bf16[320,640]{1,0:T(8,128)(2,1)}, bf16[320,640]{1,0:T(8,128)(2,1)S(1)}, u32[]{:S(2)}, u32[]{:S(2)}) collective-permute-start(bf16[320,640]{1,0:T(8,128)(2,1)} %get-tuple-element.18.refs_0_), channel_id=1, source_target_pairs={{0,8},{8,0},{16,24},{24,16},{1,9},{9,1},{17,25},{25,17},{2,10},{10... | collective-permute-start | bytes 1228808 | tf_op jit(solution)/shard_map/ppermute | solution.py:325
  188.2 12.6 %collective-permute-start.35 = (bf16[320,640]{1,0:T(8,128)(2,1)}, bf16[320,640]{1,0:T(8,128)(2,1)S(1)}, u32[]{:S(2)}, u32[]{:S(2)}) collective-permute-start(bf16[320,640]{1,0:T(8,128)(2,1)} %get-tuple-element.18.refs_0_), channel_id=1, source_target_pairs={{0,16},{8,24},{16,0},{24,8},{1,17},{9,25},{17,1},{25,9},{2,18},{10... | collective-permute-start | bytes 1228808 | tf_op jit(solution)/shard_map/ppermute | solution.py:326
  190.5 16.3 %collective-permute-start.28 = (bf16[320,640]{1,0:T(8,128)(2,1)S(1)}, bf16[320,640]{1,0:T(8,128)(2,1)S(1)}, u32[]{:S(2)}, u32[]{:S(2)}) collective-permute-start(bf16[320,640]{1,0:T(8,128)(2,1)S(1)} %get-tuple-element.16.refs_0_), channel_id=1, source_target_pairs={{0,8},{8,0},{16,24},{24,16},{1,9},{9,1},{17,25},{25,17},{2,10},{10... | collective-permute-start | bytes 1228808 | tf_op jit(solution)/shard_map/ppermute | solution.py:325
  192.0 17.5 %collective-permute-start.29 = (bf16[320,640]{1,0:T(8,128)(2,1)S(1)}, bf16[320,640]{1,0:T(8,128)(2,1)S(1)}, u32[]{:S(2)}, u32[]{:S(2)}) collective-permute-start(bf16[320,640]{1,0:T(8,128)(2,1)S(1)} %get-tuple-element.16.refs_0_), channel_id=1, source_target_pairs={{0,16},{8,24},{16,0},{24,8},{1,17},{9,25},{17,1},{25,9},{2,18},{10... | collective-permute-start | bytes 1228808 | tf_op jit(solution)/shard_map/ppermute | solution.py:326
  199.8 12.2 %copy-start.12 = (bf16[320,640]{1,0:T(8,128)(2,1)}, bf16[320,640]{1,0:T(8,128)(2,1)S(1)}, u32[]{:S(2)}) copy-start(bf16[320,640]{1,0:T(8,128)(2,1)S(1)} %collective-permute-done.34.refs_1_) | copy-start | bytes 1228804
  199.8 12.2 %collective-permute-start.33 = (bf16[320,640]{1,0:T(8,128)(2,1)S(1)}, bf16[320,640]{1,0:T(8,128)(2,1)S(1)}, u32[]{:S(2)}, u32[]{:S(2)}) collective-permute-start(bf16[320,640]{1,0:T(8,128)(2,1)S(1)} %broadcast_select_fusion.4), channel_id=1, source_target_pairs={{0,8},{4,20},{8,0},{12,28},{16,24},{20,4},{24,16},{28,12},{1,9},{5... | collective-permute-start | bytes 1228808 | tf_op jit(solution)/shard_map/ppermute | solution.py:328
  200.8 11.3 %copy-start.13 = (bf16[320,640]{1,0:T(8,128)(2,1)}, bf16[320,640]{1,0:T(8,128)(2,1)S(1)}, u32[]{:S(2)}) copy-start(bf16[320,640]{1,0:T(8,128)(2,1)S(1)} %collective-permute-done.35.refs_2_) | copy-start | bytes 1228804
  200.8 19.4 %collective-permute-start.36 = (bf16[320,640]{1,0:T(8,128)(2,1)S(1)}, bf16[320,640]{1,0:T(8,128)(2,1)S(1)}, u32[]{:S(2)}, u32[]{:S(2)}) collective-permute-start(bf16[320,640]{1,0:T(8,128)(2,1)S(1)} %broadcast_select_fusion.3), channel_id=1, source_target_pairs={{0,8},{4,20},{8,0},{12,28},{16,24},{20,4},{24,16},{28,12},{1,9},{5... | collective-permute-start | bytes 1228808 | tf_op jit(solution)/shard_map/ppermute | solution.py:328
  206.8 13.4 %copy-start.14 = (bf16[320,640]{1,0:T(8,128)(2,1)}, bf16[320,640]{1,0:T(8,128)(2,1)S(1)}, u32[]{:S(2)}) copy-start(bf16[320,640]{1,0:T(8,128)(2,1)S(1)} %collective-permute-done.28.refs_1_) | copy-start | bytes 1228804
  209.5 10.7 %copy-start.15 = (bf16[320,640]{1,0:T(8,128)(2,1)}, bf16[320,640]{1,0:T(8,128)(2,1)S(1)}, u32[]{:S(2)}) copy-start(bf16[320,640]{1,0:T(8,128)(2,1)S(1)} %collective-permute-done.29.refs_2_) | copy-start | bytes 1228804
  209.6 36.2 %collective-permute-start.30 = (bf16[320,640]{1,0:T(8,128)(2,1)S(1)}, bf16[320,640]{1,0:T(8,128)(2,1)S(1)}, u32[]{:S(2)}, u32[]{:S(2)}) collective-permute-start(bf16[320,640]{1,0:T(8,128)(2,1)S(1)} %broadcast_select_fusion.5), channel_id=1, source_target_pairs={{0,8},{4,20},{8,0},{12,28},{16,24},{20,4},{24,16},{28,12},{1,9},{5... | collective-permute-start | bytes 1228808 | tf_op jit(solution)/shard_map/ppermute | solution.py:328
  252.0 27.7 %copy-start.1 = (bf16[1,2,3,128,640]{4,3,2,1,0:T(8,128)(2,1)S(1)}, bf16[1,2,3,128,640]{4,3,2,1,0:T(8,128)(2,1)}, u32[]{:S(2)}) copy-start(bf16[1,2,3,128,640]{4,3,2,1,0:T(8,128)(2,1)} %param.7) | copy-start | bytes 2949124
  276.6 1.9 collective-permute-start.37
  (9 other events, 7.0 us)

commit v2 on v1

--- a/solution.py
+++ b/solution.py
@@ -292,7 +292,6 @@
     batch_size = lax.axis_size("batch")
     core = lax.axis_index("lat")
     chip = lax.axis_index("batch")
-    z = lax.axis_index("lon")
 
     index_rows = kept_index.reshape(windows, kept_most)
     kept_mask = lax.broadcasted_iota(jnp.int32, (windows, kept_most), 1) < kept_count.reshape(
@@ -304,18 +303,18 @@
     ).reshape(rows, pin)
 
     ring = [(i, (i + 1) % lon_size) for i in range(lon_size)]
-    picked_parts = [picked]
+    code_rows = -(-rows // pin)
+    code_tile = -(-code_rows // 16) * 16
+    code_part = jnp.pad(codes, (0, code_tile * pin - rows)).reshape(code_tile, pin)
+    picked_parts = [jnp.concatenate([picked, code_part.astype(jnp.bfloat16)], axis=0)]
     for _ in range(lon_size - 1):
         picked_parts.append(lax.ppermute(picked_parts[-1], "lon", ring))
-    picked_all = jnp.concatenate(picked_parts, axis=0)
+    picked_all = jnp.concatenate([part[:rows] for part in picked_parts], axis=0)
     all_rows = picked_all.shape[0]
-    all_codes = lax.all_gather(codes, ("lat", "lon"), axis=0, tiled=False).reshape(
-        2, lon_size, rows
-    )
-    order = (z - jnp.arange(lon_size, dtype=jnp.int32)) % lon_size
-    all_codes = all_codes[:, order].reshape(2, all_rows)
-    own_codes = all_codes[core]
-    other_codes = all_codes[1 - core]
+    own_codes = jnp.concatenate(
+        [part[rows : rows + code_rows].reshape(-1)[:rows] for part in picked_parts]
+    ).astype(jnp.int32)
+    other_codes = lax.ppermute(own_codes, "lat", swap_perm(2, 1))
 
     diagonal = []
     for b in range(batch_size):
@@ -404,6 +403,8 @@
     mixes = []
     for group in range(2):
         pieces, offsets = shared(local_shards[group], fetched[1 + group])
+        if group == 1:
+            pieces = after(pieces, fetched[3][:2])
         specs = [pl.BlockSpec((block, width), lambda i, _: (i, 0))]
         specs += [pl.BlockSpec((1, 1, block), lambda i, _: (i, 0, 0))]
         specs += [whole_block(a) for a in pieces]
@@ -431,6 +432,7 @@
         )
 
     pieces, offsets = shared(local_out, fetched[3])
+    pieces = after(pieces, (fetched[4][:2], fetched[5][:2]))
     (normed_own,) = call(
         functools.partial(out_kernel, len(pieces), len(mixes)),
         steps,
@@ -505,7 +507,7 @@
 def body(patches, kept_index, *weights):
     rows = patches.shape[1] * patches.shape[2] * kept_index.shape[3]
     sample_rows = rows * lax.axis_size("lat") * lax.axis_size("lon")
-    fits = sample_rows * HEADS * HD * 2 <= vmem_limit // 4
+    fits = patches.shape[3] <= 256 and sample_rows * HEADS * HD * 2 <= vmem_limit // 4
     if lax.axis_size("batch") == 4 and lax.axis_size("lat") == 2 and fits:
         return sample_body(patches, kept_index, *weights)
     return owner_body(patches, kept_index, *weights)

time: 280 us -> 254 us (0.907)
  blocking collectives: 25.2 us -> 0 us
  local copies, waits for them, and re-layouts: 24 us -> 28.5 us
  waiting for transfers between devices: 59.1 us -> 54.6 us
  starting transfers between devices: 35 us -> 31.6 us
    all_gather x1 -> x0, blocking collectives: 25.2 us -> none  [sample_body(): lax.all_gather(codes, ('lat', 'lon'), axis=0, tiled=False)]
    ppermute x7, waiting for transfers between devices: 29.3 us -> 20.7 us  [fetch(): along_x = lax.ppermute(part, 'batch', swap_perm(batch_size, 1))]
    ppermute x7, waiting for transfers between devices: 3.86 us -> 8.11 us  [fetch(): along_y = lax.ppermute(part, 'batch', swap_perm(batch_size, 2))]
    ppermute x7, waiting for transfers between devices: 10.6 us -> 7.02 us  [fetch(): across = lax.ppermute(forwarded, ('batch', 'lat'), diagonal)]
    ppermute x14, starting transfers between devices: 5.67 us -> 2.6 us  [other_core(): return lax.ppermute(value, 'lat', swap_perm(2, 1))]
    slice x0 -> x9, local copies, waits for them, and re-layouts: none -> 2.99 us  [the longest x3 2.19 us: sample_body(): picked_all = jnp.concatenate([part[:rows] for part in picked_parts], axis=0)]
    select_n x7, other arithmetic: 2.38 us -> 5.24 us  [fetch(): forwarded = jnp.where(core == 0, along_y, along_x)]
    unnamed x72 -> x67, local copies, waits for them, and re-layouts: 5.65 us -> 7.14 us
  transfers between devices with their start and end apart: 38 -> 39, of which waited for: 12 -> 14; matrix products, arithmetic and copies ran while one was open for 9% -> 13% of each run, Pallas kernels for 29% -> 24%
where the time goes in v2:
time: 254 us; the launch traced here: 253 us
  Pallas kernels  124 us (49%)
  waiting for transfers between devices  54.6 us (21%)
  starting transfers between devices  31.6 us (12%)
  local copies, waits for them, and re-layouts  28.5 us (11%)
  other arithmetic  14.4 us (6%)
    pallas_call x7, Pallas kernels, call(): pl.pallas_call(kernel, grid_spec=pltpu.PrefetchScalarGridSpec(num_scalar_...  57.3 us
    pallas_call x2, Pallas kernels, sample_body(): pl.pallas_call(functools.partial(window_kernel, len(pieces), kept_most, a...  43.3 us
    pallas_call x1, Pallas kernels, sample_body(): pl.pallas_call(group_kernel, grid=(2 * rows // query_block,), in_specs=[p...  23.3 us
    ppermute x7, waiting for transfers between devices, fetch(): along_x = lax.ppermute(part, 'batch', swap_perm(batch_size, 1))  20.7 us
    ppermute x3, waiting for transfers between devices, sample_body(): picked_parts.append(lax.ppermute(picked_parts[-1], 'lon', ring))  14.6 us
    ppermute x7, starting transfers between devices, fetch(): along_x = lax.ppermute(part, 'batch', swap_perm(batch_size, 1))  9.27 us
    ppermute x7, starting transfers between devices, fetch(): across = lax.ppermute(forwarded, ('batch', 'lat'), diagonal)  8.23 us
    ppermute x7, waiting for transfers between devices, fetch(): along_y = lax.ppermute(part, 'batch', swap_perm(batch_size, 2))  8.11 us
  transfers between devices with their start and end apart: 39, of which 14 were waited for; matrix products, arithmetic and copies ran while one was open for 13% of the time, Pallas kernels for 24%

profile of v2, /device:TPU:0, one launch (start us, length us, event | category | flops | bytes accessed | tf_op | source)
XLA Modules:
  0.0 253.4 jit_solution(3466597434622244121)
XLA Ops:
  0.0 1.7 constant_dynamic-slice_fusion.6
  1.7 2.9 %collective-permute-start.3 = (bf16[80,1280]{1,0:T(8,128)(2,1)}, bf16[80,1280]{1,0:T(8,128)(2,1)}, u32[]{:S(2)}, u32[]{:S(2)}) collective-permute-start(bf16[80,1280]{1,0:T(8,128)(2,1)} %constant_dynamic-slice_fusion.6), channel_id=1, source_target_pairs={{0,8},{8,0},{16,24},{24,16},{1,9},{9,1},{17,25},{25,17},{2,10},{10... | collective-permute-start | bytes 614408 | tf_op jit(solution)/shard_map/ppermute | solution.py:324
  4.7 1.5 collective-permute-start.5
  6.2 2.7 %fusion.6 = (bf16[320,640]{1,0:T(8,128)(2,1)S(1)}, bf16[320,640]{1,0:T(8,128)(2,1)S(1)}, bf16[320,640]{1,0:T(8,128)(2,1)}, bf16[320,640]{1,0:T(8,128)(2,1)}, bf1...) fusion(bf16[320,3840]{1,0:T(8,128)(2,1)} %param.11), kind=kLoop, calls=%fused_computation.52 | loop fusion | bytes 4915200 | tf_op jit(solution)/shard_map/slice | solution.py:355
  8.9 1.2 pad_maximum_fusion.2.refs_0_
  10.2 1.0 constant_dynamic-slice_fusion.5
  12.2 4.3 %gather_fusion = bf16[384,640]{1,0:T(8,128)(2,1)S(1)} fusion(bf16[6,128,640]{2,1,0:T(8,128)(2,1)S(1)} %bitcast.25, s32[384]{0:T(512)S(1)} %reshape.308), kind=kCustom, calls=%fused_computation | custom fusion | bytes 986112 | tf_op jit(solution)/shard_map/jit(take_along_axis)/gather | solution.py:301
  16.7 0.9 pad_maximum_fusion.4
  17.6 2.1 collective-permute-start
  19.8 1.6 copy-done.5
  21.4 1.0 constant_dynamic-slice_fusion
  22.4 0.9 constant_dynamic-slice_fusion.4
  23.3 0.8 constant_dynamic-slice_fusion.3
  24.1 1.6 collective-permute-start.15
  25.7 1.5 collective-permute-start.17
  27.9 1.0 broadcast_select_fusion.7
  29.0 1.1 collective-permute-start.21
  30.2 1.2 broadcast_select_fusion.1
  31.4 1.2 collective-permute-done
  32.6 1.5 collective-permute-start.7
  34.0 7.2 %collective-permute-done.15.refs_1_ = bf16[160,1920]{1,0:T(8,128)(2,1)S(1)} collective-permute-done((bf16[160,1920]{1,0:T(8,128)(2,1)}, bf16[160,1920]{1,0:T(8,128)(2,1)S(1)}, u32[]{:S(2)}, u32[]{:S(2)}) %collective-permute-start.15) | collective-permute-done | bytes 614432 | tf_op jit(solution)/shard_map/ppermute | solution.py:324
  41.2 1.5 collective-permute-start.13
  44.1 1.6 collective-permute-start.1
  46.4 1.1 slice.102
  47.5 3.2 %collective-permute-done.7.refs_5_ = bf16[80,1280]{1,0:T(8,128)(2,1)} collective-permute-done((bf16[80,1280]{1,0:T(8,128)(2,1)S(1)}, bf16[80,1280]{1,0:T(8,128)(2,1)}, u32[]{:S(2)}, u32[]{:S(2)}) %collective-permute-start.7) | collective-permute-done | bytes 204832 | tf_op jit(solution)/shard_map/ppermute | solution.py:327
  50.6 1.9 collective-permute-start.27
  53.1 1.8 broadcast_select_fusion.6
  54.9 0.8 collective-permute-start.25
  55.7 1.3 collective-permute-start.29
  57.0 3.6 %collective-permute-done.13.refs_5_ = bf16[160,1920]{1,0:T(8,128)(2,1)} collective-permute-done((bf16[160,1920]{1,0:T(8,128)(2,1)S(1)}, bf16[160,1920]{1,0:T(8,128)(2,1)}, u32[]{:S(2)}, u32[]{:S(2)}) %collective-permute-start.13) | collective-permute-done | bytes 614432 | tf_op jit(solution)/shard_map/ppermute | solution.py:327
  60.5 8.7 %collective-permute-done.27.refs_1_ = bf16[320,640]{1,0:T(8,128)(2,1)S(1)} collective-permute-done((bf16[320,640]{1,0:T(8,128)(2,1)S(1)}, bf16[320,640]{1,0:T(8,128)(2,1)S(1)}, u32[]{:S(2)}, u32[]{:S(2)}) %collective-permute-start.27) | collective-permute-done | bytes 409632 | tf_op jit(solution)/shard_map/ppermute | solution.py:324
  69.2 0.8 copy-done.11
  70.0 0.8 copy-done.13
  70.8 1.6 collective-permute-start.2
  72.5 13.4 %collective-permute-done.2 = bf16[400,640]{1,0:T(8,128)(2,1)S(1)} collective-permute-done((bf16[400,640]{1,0:T(8,128)(2,1)S(1)}, bf16[400,640]{1,0:T(8,128)(2,1)S(1)}, u32[]{:S(2)}, u32[]{:S(2)}) %collective-permute-start.2) | collective-permute-done | bytes 512032 | tf_op jit(solution)/shard_map/ppermute | solution.py:311
  86.8 1.1 slice.104
  88.4 1.2 collective-permute-start.19
  89.7 1.5 pad_maximum_fusion.picked_ref
  91.1 7.5 %collective-permute-done.30.refs_2_ = bf16[320,640]{1,0:T(8,128)(2,1)} collective-permute-done((bf16[320,640]{1,0:T(8,128)(2,1)}, bf16[320,640]{1,0:T(8,128)(2,1)}, u32[]{:S(2)}, u32[]{:S(2)}) %collective-permute-start.30) | collective-permute-done | bytes 409632 | tf_op jit(solution)/shard_map/ppermute | solution.py:325
  99.3 8.8 %embed.1 = (bf16[1536,1280]{1,0:T(8,128)(2,1)}, bf16[1536,1280]{1,0:T(8,128)(2,1)}) custom-call(s32[7]{0:T(128)} %stack.116.offset_ref, bf16[1536,640]{1,0:T(8,128)(2,1)} %pad_maximum_fusion.picked_ref, bf16[160,1280]{1,0:T(8,128)(2,1)} %refs_0_.1, bf16[80,1280]{1,0:T(8,128)(2,1)} %collective-permute-done.3.refs_1_, bf16[80,1280]{1,0:T(8,128)(2,1)} %copy-done.28, ...), custom_call_target="tpu_custom_call" | custom-call | flops 2516582400 | bytes 11468800 | tf_op jit(solution)/shard_map/embed/pallas_call | solution.py:146
  110.3 21.7 %windows.2.refs_0_ = bf16[1536,640]{1,0:T(8,128)(2,1)} custom-call(s32[7]{0:T(128)} %stack.51.offset_ref, bf16[1536,1280]{1,0:T(8,128)(2,1)} %get-tuple-element.27.normed_ref, s32[3,1,512]{2,1,0:T(1,128)} %fusion.code_ref, bf16[320,1920]{1,0:T(8,128)(2,1)} %copy-done.2, bf16[160,1920]{1,0:T(8,128)(2,1)} %collective-permute-done.9.refs_1_, ...), custom_call_target="tpu_custom_call" | custom-call | flops 7549747200 | bytes 16777216 | tf_op jit(solution)/shard_map/windows/pallas_call | solution.py:413
  132.0 0.8 copy-done.23
  133.0 0.8 copy-done.25
  133.9 21.7 %windows.3.refs_1_ = bf16[1536,640]{1,0:T(8,128)(2,1)} custom-call(s32[7]{0:T(128)} %stack.51.offset_ref, bf16[1536,1280]{1,0:T(8,128)(2,1)} %get-tuple-element.27.normed_ref, s32[3,1,512]{2,1,0:T(1,128)} %fusion.code_ref, bf16[320,1920]{1,0:T(8,128)(2,1)} %copy-done.3, bf16[160,1920]{1,0:T(8,128)(2,1)} %copy-done.6, bf16[160,1920]{1,0:T(8,128)(2,1)} %copy-done.23, ...), custom_call_target="tpu_custom_call" | custom-call | flops 7549747200 | bytes 16777216 | tf_op jit(solution)/shard_map/windows/pallas_call | solution.py:413
  155.5 13.6 %local_out.1.normed_ref = bf16[1536,1280]{1,0:T(8,128)(2,1)} custom-call(s32[7]{0:T(128)} %stack.51.offset_ref, bf16[1536,1280]{1,0:T(8,128)(2,1)} %get-tuple-element.26.embedded_ref, bf16[1536,640]{1,0:T(8,128)(2,1)} %windows.2.refs_0_, bf16[1536,640]{1,0:T(8,128)(2,1)} %windows.3.refs_1_, bf16[320,1280]{1,0:T(8,128)(2,1)} %refs_2_, ...), custom_call_target="tpu_custom_call" | custom-call | flops 5033164800 | bytes 15073280 | tf_op jit(solution)/shard_map/local_out/pallas_call | solution.py:146
  169.9 2.0 collective-permute-start.36
  172.6 1.1 broadcast_select_fusion.5
  173.8 2.2 collective-permute-done.33
  176.9 4.7 %collective-permute-done.35.refs_1_ = bf16[320,640]{1,0:T(8,128)(2,1)S(1)} collective-permute-done((bf16[320,640]{1,0:T(8,128)(2,1)S(1)}, bf16[320,640]{1,0:T(8,128)(2,1)S(1)}, u32[]{:S(2)}, u32[]{:S(2)}) %collective-permute-start.35) | collective-permute-done | bytes 409632 | tf_op jit(solution)/shard_map/ppermute | solution.py:324
  182.3 2.2 collective-permute-start.37
  184.4 0.8 broadcast_select_fusion.8.code_ref
  185.9 1.3 slice.109
  187.1 7.4 %keys.2.key_own_ref = bf16[1536,640]{1,0:T(8,128)(2,1)} custom-call(s32[4]{0:T(128)} %pad_add_fusion.1.offset_ref, bf16[1536,1280]{1,0:T(8,128)(2,1)} %local_out.1.normed_ref, bf16[320,640]{1,0:T(8,128)(2,1)} %copy-done.10, bf16[320,640]{1,0:T(8,128)(2,1)} %copy-done.11, bf16[320,640]{1,0:T(8,128)(2,1)} %copy-done.13, ...), custom_call_target="tpu_custom_call" | custom-call | flops 2516582400 | bytes 7536640 | tf_op jit(solution)/shard_map/keys/pallas_call | solution.py:146
  194.8 0.8 copy-done.27
  195.6 7.4 %values.2.value_own_ref = bf16[1536,640]{1,0:T(8,128)(2,1)} custom-call(s32[4]{0:T(128)} %pad_add_fusion.1.offset_ref, bf16[1536,1280]{1,0:T(8,128)(2,1)} %local_out.1.normed_ref, bf16[320,640]{1,0:T(8,128)(2,1)} %get-tuple-element.46.refs_0_, bf16[320,640]{1,0:T(8,128)(2,1)} %copy-done.15, bf16[320,640]{1,0:T(8,128)(2,1)} %copy-done.16, ...), custom_call_target="tpu_custom_call" | custom-call | flops 2516582400 | bytes 7536640 | tf_op jit(solution)/shard_map/values/pallas_call | solution.py:146
  203.0 7.4 %keys.3.key_other_ref = bf16[1536,640]{1,0:T(8,128)(2,1)} custom-call(s32[4]{0:T(128)} %pad_add_fusion.1.offset_ref, bf16[1536,1280]{1,0:T(8,128)(2,1)} %collective-permute-done.31.normed_ref, bf16[320,640]{1,0:T(8,128)(2,1)} %copy-done.10, bf16[320,640]{1,0:T(8,128)(2,1)} %copy-done.11, bf16[320,640]{1,0:T(8,128)(2,1)} %copy-done.13, ...), custom_call_target="tpu_custom_call" | custom-call | flops 2516582400 | bytes 7536640 | tf_op jit(solution)/shard_map/keys/pallas_call | solution.py:146
  210.3 7.3 %values.3.value_other_ref = bf16[1536,640]{1,0:T(8,128)(2,1)} custom-call(s32[4]{0:T(128)} %pad_add_fusion.1.offset_ref, bf16[1536,1280]{1,0:T(8,128)(2,1)} %collective-permute-done.31.normed_ref, bf16[320,640]{1,0:T(8,128)(2,1)} %get-tuple-element.46.refs_0_, bf16[320,640]{1,0:T(8,128)(2,1)} %copy-done.15, bf16[320,640]{1,0:T(8,128)(2,1)} %copy-done.16, ...), custom_call_target="tpu_custom_call" | custom-call | flops 2516582400 | bytes 7536640 | tf_op jit(solution)/shard_map/values/pallas_call | solution.py:146
  217.7 1.3 slice.110
  218.9 1.4 pad_maximum_fusion.1.normed_ref
  220.3 5.4 %queries.1.query_ref = bf16[768,640]{1,0:T(8,128)(2,1)} custom-call(s32[4]{0:T(128)} %pad_add_fusion.1.offset_ref, bf16[768,1280]{1,0:T(8,128)(2,1)} %pad_maximum_fusion.1.normed_ref, bf16[320,640]{1,0:T(8,128)(2,1)} %get-tuple-element.38.refs_0_, bf16[320,640]{1,0:T(8,128)(2,1)} %collective-permute-done.29.refs_1_, ...), custom_call_target="tpu_custom_call" | custom-call | flops 1258291200 | bytes 4587520 | tf_op jit(solution)/shard_map/queries/pallas_call | solution.py:146
  225.7 23.3 %groups.1 = bf16[768,640]{1,0:T(8,128)(2,1)} custom-call(bf16[768,640]{1,0:T(8,128)(2,1)} %queries.1.query_ref, s32[768,1]{1,0:T(8,128)} %broadcast_select_fusion.8.code_ref, s32[1,3072]{1,0:T(1,128)} %bitcast.28, bf16[1536,640]{1,0:T(8,128)(2,1)} %keys.2.key_own_ref, bf16[1536,640]{1,0:T(8,128)(2,1)} %keys.3.key_other_ref, ...), custom_call_target="tpu_custom_call" | custom-call | flops 6039797760 | bytes 16777216 | tf_op jit(solution)/shard_map/groups/pallas_call | solution.py:479
  249.0 1.3 fusion.7
  250.5 1.7 collective-permute-done.38
  252.2 1.2 maximum_select_fusion
  (147 shorter events, 13.7 us)
Async XLA Ops:
  0.0 12.2 %copy-start = (bf16[1,2,3,128,640]{4,3,2,1,0:T(8,128)(2,1)S(1)}, bf16[1,2,3,128,640]{4,3,2,1,0:T(8,128)(2,1)}, u32[]{:S(2)}) copy-start(bf16[1,2,3,128,640]{4,3,2,1,0:T(8,128)(2,1)} %param.7) | copy-start | bytes 2949124
  1.7 22.4 %collective-permute-start.3 = (bf16[80,1280]{1,0:T(8,128)(2,1)}, bf16[80,1280]{1,0:T(8,128)(2,1)}, u32[]{:S(2)}, u32[]{:S(2)}) collective-permute-start(bf16[80,1280]{1,0:T(8,128)(2,1)} %constant_dynamic-slice_fusion.6), channel_id=1, source_target_pairs={{0,8},{8,0},{16,24},{24,16},{1,9},{9,1},{17,25},{25,17},{2,10},{10... | collective-permute-start | bytes 614408 | tf_op jit(solution)/shard_map/ppermute | solution.py:324
  4.7 19.5 %collective-permute-start.5 = (bf16[80,1280]{1,0:T(8,128)(2,1)}, bf16[80,1280]{1,0:T(8,128)(2,1)}, u32[]{:S(2)}, u32[]{:S(2)}) collective-permute-start(bf16[80,1280]{1,0:T(8,128)(2,1)} %constant_dynamic-slice_fusion.6), channel_id=1, source_target_pairs={{0,16},{8,24},{16,0},{24,8},{1,17},{9,25},{17,1},{25,9},{2,18},{10... | collective-permute-start | bytes 614408 | tf_op jit(solution)/shard_map/ppermute | solution.py:325
  8.9 2.8 %copy-start.18 = (s32[1,2,3,64]{3,1,2,0:T(2,128)S(1)}, s32[1,2,3,64]{3,1,2,0:T(2,128)}, u32[]{:S(2)}) copy-start(s32[1,2,3,64]{3,1,2,0:T(2,128)} %param.8) | copy-start | bytes 4612
  8.9 2.8 %copy-start.31 = (s32[1,2,3]{2,1,0:T(2,128)S(1)}, s32[1,2,3]{2,1,0:T(2,128)}, u32[]{:S(2)}) copy-start(s32[1,2,3]{2,1,0:T(2,128)} %param.9) | copy-start | bytes 76
  10.2 6.4 %copy-start.2 = (bf16[320,1920]{1,0:T(8,128)(2,1)}, bf16[320,1920]{1,0:T(8,128)(2,1)S(1)}, u32[]{:S(2)}) copy-start(bf16[320,1920]{1,0:T(8,128)(2,1)S(1)} %pad_maximum_fusion.2.refs_0_) | copy-start | bytes 3686404
  11.1 16.2 %collective-permute-start.9 = (bf16[160,1920]{1,0:T(8,128)(2,1)}, bf16[160,1920]{1,0:T(8,128)(2,1)}, u32[]{:S(2)}, u32[]{:S(2)}) collective-permute-start(bf16[160,1920]{1,0:T(8,128)(2,1)} %constant_dynamic-slice_fusion.5), channel_id=1, source_target_pairs={{0,8},{8,0},{16,24},{24,16},{1,9},{9,1},{17,25},{25,17},{2,10},{10... | collective-permute-start | bytes 1843208 | tf_op jit(solution)/shard_map/ppermute | solution.py:324
  11.7 15.7 %collective-permute-start.11 = (bf16[160,1920]{1,0:T(8,128)(2,1)}, bf16[160,1920]{1,0:T(8,128)(2,1)}, u32[]{:S(2)}, u32[]{:S(2)}) collective-permute-start(bf16[160,1920]{1,0:T(8,128)(2,1)} %constant_dynamic-slice_fusion.5), channel_id=1, source_target_pairs={{0,16},{8,24},{16,0},{24,8},{1,17},{9,25},{17,1},{25,9},{2,18},{10... | collective-permute-start | bytes 1843208 | tf_op jit(solution)/shard_map/ppermute | solution.py:325
  16.5 3.1 %copy-start.4 = (bf16[320,640]{1,0:T(8,128)(2,1)S(1)}, bf16[320,640]{1,0:T(8,128)(2,1)}, u32[]{:S(2)}) copy-start(bf16[320,640]{1,0:T(8,128)(2,1)} %get-tuple-element.55) | copy-start | bytes 1228804
  17.6 15.0 %collective-permute-start = (bf16[400,640]{1,0:T(8,128)(2,1)}, bf16[400,640]{1,0:T(8,128)(2,1)}, u32[]{:S(2)}, u32[]{:S(2)}) collective-permute-start(bf16[400,640]{1,0:T(8,128)(2,1)} %pad_maximum_fusion.4), channel_id=1, source_target_pairs={{0,1},{1,2},{2,3},{3,0},{4,5},{5,6},{6,7},{7,4},{8,9},{9,10},{10,1... | collective-permute-start | bytes 1536008 | tf_op jit(solution)/shard_map/ppermute | solution.py:311
  19.7 1.7 copy-start.5
  21.4 2.8 %copy-start.3 = (bf16[320,1920]{1,0:T(8,128)(2,1)}, bf16[320,1920]{1,0:T(8,128)(2,1)S(1)}, u32[]{:S(2)}) copy-start(bf16[320,1920]{1,0:T(8,128)(2,1)S(1)} %pad_maximum_fusion.3.refs_0_) | copy-start | bytes 3686404
  21.4 2.0 copy-start.17
  22.4 30.1 %copy-start.10 = (bf16[320,640]{1,0:T(8,128)(2,1)}, bf16[320,640]{1,0:T(8,128)(2,1)S(1)}, u32[]{:S(2)}) copy-start(bf16[320,640]{1,0:T(8,128)(2,1)S(1)} %get-tuple-element.37.refs_0_) | copy-start | bytes 1228804
  24.1 17.1 %collective-permute-start.15 = (bf16[160,1920]{1,0:T(8,128)(2,1)}, bf16[160,1920]{1,0:T(8,128)(2,1)S(1)}, u32[]{:S(2)}, u32[]{:S(2)}) collective-permute-start(bf16[160,1920]{1,0:T(8,128)(2,1)} %constant_dynamic-slice_fusion.4), channel_id=1, source_target_pairs={{0,8},{8,0},{16,24},{24,16},{1,9},{9,1},{17,25},{25,17},{2,10},{10... | collective-permute-start | bytes 1843208 | tf_op jit(solution)/shard_map/ppermute | solution.py:324
  25.7 18.4 %collective-permute-start.17 = (bf16[160,1920]{1,0:T(8,128)(2,1)}, bf16[160,1920]{1,0:T(8,128)(2,1)S(1)}, u32[]{:S(2)}, u32[]{:S(2)}) collective-permute-start(bf16[160,1920]{1,0:T(8,128)(2,1)} %constant_dynamic-slice_fusion.4), channel_id=1, source_target_pairs={{0,16},{8,24},{16,0},{24,8},{1,17},{9,25},{17,1},{25,9},{2,18},{10... | collective-permute-start | bytes 1843208 | tf_op jit(solution)/shard_map/ppermute | solution.py:325
  27.4 1.7 collective-permute-start.4
  27.4 2.8 %collective-permute-start.6 = (bf16[80,1280]{1,0:T(8,128)(2,1)}, bf16[80,1280]{1,0:T(8,128)(2,1)S(1)}, u32[]{:S(2)}, u32[]{:S(2)}) collective-permute-start(bf16[80,1280]{1,0:T(8,128)(2,1)} %collective-permute-done.5.refs_3_), channel_id=1, source_target_pairs={{0,4},{4,0},{1,5},{5,1},{2,6},{6,2},{3,7},{7,3},{8,12},{12,8},{9,1... | collective-permute-start | bytes 614408 | tf_op jit(solution)/shard_map/ppermute | solution.py:331
  29.0 16.6 %copy-start.28 = (bf16[80,1280]{1,0:T(8,128)(2,1)}, bf16[80,1280]{1,0:T(8,128)(2,1)S(1)}, u32[]{:S(2)}) copy-start(bf16[80,1280]{1,0:T(8,128)(2,1)S(1)} %collective-permute-done.4.refs_2_) | copy-start | bytes 614404
  29.0 21.6 %collective-permute-start.21 = (bf16[160,1280]{1,0:T(8,128)(2,1)}, bf16[160,1280]{1,0:T(8,128)(2,1)}, u32[]{:S(2)}, u32[]{:S(2)}) collective-permute-start(bf16[160,1280]{1,0:T(8,128)(2,1)} %constant_dynamic-slice_fusion.3), channel_id=1, source_target_pairs={{0,8},{8,0},{16,24},{24,16},{1,9},{9,1},{17,25},{25,17},{2,10},{10... | collective-permute-start | bytes 1228808 | tf_op jit(solution)/shard_map/ppermute | solution.py:324
  30.2 15.5 %copy-start.29 = (bf16[80,1280]{1,0:T(8,128)(2,1)}, bf16[80,1280]{1,0:T(8,128)(2,1)S(1)}, u32[]{:S(2)}) copy-start(bf16[80,1280]{1,0:T(8,128)(2,1)S(1)} %collective-permute-done.6.refs_4_) | copy-start | bytes 614404
  30.2 22.3 %collective-permute-start.22 = (bf16[160,1280]{1,0:T(8,128)(2,1)}, bf16[160,1280]{1,0:T(8,128)(2,1)}, u32[]{:S(2)}, u32[]{:S(2)}) collective-permute-start(bf16[160,1280]{1,0:T(8,128)(2,1)} %constant_dynamic-slice_fusion.3), channel_id=1, source_target_pairs={{0,16},{8,24},{16,0},{24,8},{1,17},{9,25},{17,1},{25,9},{2,18},{10... | collective-permute-start | bytes 1228808 | tf_op jit(solution)/shard_map/ppermute | solution.py:325
  32.6 18.1 %collective-permute-start.7 = (bf16[80,1280]{1,0:T(8,128)(2,1)S(1)}, bf16[80,1280]{1,0:T(8,128)(2,1)}, u32[]{:S(2)}, u32[]{:S(2)}) collective-permute-start(bf16[80,1280]{1,0:T(8,128)(2,1)S(1)} %broadcast_select_fusion.7), channel_id=1, source_target_pairs={{0,8},{4,20},{8,0},{12,28},{16,24},{20,4},{24,16},{28,12},{1,9},{5... | collective-permute-start | bytes 614408 | tf_op jit(solution)/shard_map/ppermute | solution.py:327
  41.2 66.9 %copy-start.6 = (bf16[160,1920]{1,0:T(8,128)(2,1)}, bf16[160,1920]{1,0:T(8,128)(2,1)S(1)}, u32[]{:S(2)}) copy-start(bf16[160,1920]{1,0:T(8,128)(2,1)S(1)} %collective-permute-done.15.refs_1_) | copy-start | bytes 1843204
  41.2 19.3 %collective-permute-start.13 = (bf16[160,1920]{1,0:T(8,128)(2,1)S(1)}, bf16[160,1920]{1,0:T(8,128)(2,1)}, u32[]{:S(2)}, u32[]{:S(2)}) collective-permute-start(bf16[160,1920]{1,0:T(8,128)(2,1)S(1)} %broadcast_select_fusion.1), channel_id=1, source_target_pairs={{0,8},{4,20},{8,0},{12,28},{16,24},{20,4},{24,16},{28,12},{1,9},{5... | collective-permute-start | bytes 1843208 | tf_op jit(solution)/shard_map/ppermute | solution.py:327
  44.1 64.6 %copy-start.7 = (bf16[160,1920]{1,0:T(8,128)(2,1)}, bf16[160,1920]{1,0:T(8,128)(2,1)S(1)}, u32[]{:S(2)}) copy-start(bf16[160,1920]{1,0:T(8,128)(2,1)S(1)} %collective-permute-done.17.refs_3_) | copy-start | bytes 1843204
  44.1 11.6 %collective-permute-start.1 = (bf16[400,640]{1,0:T(8,128)(2,1)}, bf16[400,640]{1,0:T(8,128)(2,1)S(1)}, u32[]{:S(2)}, u32[]{:S(2)}) collective-permute-start(bf16[400,640]{1,0:T(8,128)(2,1)} %collective-permute-done), channel_id=1, source_target_pairs={{0,1},{1,2},{2,3},{3,0},{4,5},{5,6},{6,7},{7,4},{8,9},{9,10},{10,1... | collective-permute-start | bytes 1536008 | tf_op jit(solution)/shard_map/ppermute | solution.py:311
  50.6 4.3 %collective-permute-start.8 = (bf16[80,1280]{1,0:T(8,128)(2,1)}, bf16[80,1280]{1,0:T(8,128)(2,1)S(1)}, u32[]{:S(2)}, u32[]{:S(2)}) collective-permute-start(bf16[80,1280]{1,0:T(8,128)(2,1)} %collective-permute-done.7.refs_5_), channel_id=1, source_target_pairs={{0,4},{4,0},{1,5},{5,1},{2,6},{6,2},{3,7},{7,3},{8,12},{12,8},{9,1... | collective-permute-start | bytes 614408 | tf_op jit(solution)/shard_map/ppermute | solution.py:331
  50.6 18.6 %collective-permute-start.27 = (bf16[320,640]{1,0:T(8,128)(2,1)S(1)}, bf16[320,640]{1,0:T(8,128)(2,1)S(1)}, u32[]{:S(2)}, u32[]{:S(2)}) collective-permute-start(bf16[320,640]{1,0:T(8,128)(2,1)S(1)} %get-tuple-element.37.refs_0_), channel_id=1, source_target_pairs={{0,8},{8,0},{16,24},{24,16},{1,9},{9,1},{17,25},{25,17},{2,10},{10... | collective-permute-start | bytes 1228808 | tf_op jit(solution)/shard_map/ppermute | solution.py:324
  52.5 16.7 %collective-permute-start.28 = (bf16[320,640]{1,0:T(8,128)(2,1)S(1)}, bf16[320,640]{1,0:T(8,128)(2,1)S(1)}, u32[]{:S(2)}, u32[]{:S(2)}) collective-permute-start(bf16[320,640]{1,0:T(8,128)(2,1)S(1)} %get-tuple-element.37.refs_0_), channel_id=1, source_target_pairs={{0,16},{8,24},{16,0},{24,8},{1,17},{9,25},{17,1},{25,9},{2,18},{10... | collective-permute-start | bytes 1228808 | tf_op jit(solution)/shard_map/ppermute | solution.py:325
  54.9 17.5 %copy-start.30 = (bf16[80,1280]{1,0:T(8,128)(2,1)}, bf16[80,1280]{1,0:T(8,128)(2,1)S(1)}, u32[]{:S(2)}) copy-start(bf16[80,1280]{1,0:T(8,128)(2,1)S(1)} %collective-permute-done.8.refs_6_) | copy-start | bytes 614404
  54.9 33.5 %collective-permute-start.25 = (bf16[160,1280]{1,0:T(8,128)(2,1)}, bf16[160,1280]{1,0:T(8,128)(2,1)}, u32[]{:S(2)}, u32[]{:S(2)}) collective-permute-start(bf16[160,1280]{1,0:T(8,128)(2,1)} %broadcast_select_fusion.6), channel_id=1, source_target_pairs={{0,8},{4,20},{8,0},{12,28},{16,24},{20,4},{24,16},{28,12},{1,9},{5... | collective-permute-start | bytes 1228808 | tf_op jit(solution)/shard_map/ppermute | solution.py:327
  55.7 34.0 %collective-permute-start.29 = (bf16[320,640]{1,0:T(8,128)(2,1)}, bf16[320,640]{1,0:T(8,128)(2,1)}, u32[]{:S(2)}, u32[]{:S(2)}) collective-permute-start(bf16[320,640]{1,0:T(8,128)(2,1)} %get-tuple-element.38.refs_0_), channel_id=1, source_target_pairs={{0,8},{8,0},{16,24},{24,16},{1,9},{9,1},{17,25},{25,17},{2,10},{10... | collective-permute-start | bytes 1228808 | tf_op jit(solution)/shard_map/ppermute | solution.py:324
  60.5 27.3 %collective-permute-start.23 = (bf16[160,1280]{1,0:T(8,128)(2,1)}, bf16[160,1280]{1,0:T(8,128)(2,1)}, u32[]{:S(2)}, u32[]{:S(2)}) collective-permute-start(bf16[160,1280]{1,0:T(8,128)(2,1)} %collective-permute-done.21.refs_3_), channel_id=1, source_target_pairs={{0,4},{4,0},{1,5},{5,1},{2,6},{6,2},{3,7},{7,3},{8,12},{12,8},{9,1... | collective-permute-start | bytes 1228808 | tf_op jit(solution)/shard_map/ppermute | solution.py:331
  69.2 18.8 %collective-permute-start.24 = (bf16[160,1280]{1,0:T(8,128)(2,1)}, bf16[160,1280]{1,0:T(8,128)(2,1)}, u32[]{:S(2)}, u32[]{:S(2)}) collective-permute-start(bf16[160,1280]{1,0:T(8,128)(2,1)} %collective-permute-done.22.refs_5_), channel_id=1, source_target_pairs={{0,4},{4,0},{1,5},{5,1},{2,6},{6,2},{3,7},{7,3},{8,12},{12,8},{9,1... | collective-permute-start | bytes 1228808 | tf_op jit(solution)/shard_map/ppermute | solution.py:331
  70.8 15.2 %collective-permute-start.2 = (bf16[400,640]{1,0:T(8,128)(2,1)S(1)}, bf16[400,640]{1,0:T(8,128)(2,1)S(1)}, u32[]{:S(2)}, u32[]{:S(2)}) collective-permute-start(bf16[400,640]{1,0:T(8,128)(2,1)S(1)} %collective-permute-done.1), channel_id=1, source_target_pairs={{0,1},{1,2},{2,3},{3,0},{4,5},{5,6},{6,7},{7,4},{8,9},{9,10},{10,1... | collective-permute-start | bytes 1536008 | tf_op jit(solution)/shard_map/ppermute | solution.py:311
  85.9 12.7 %collective-permute-start.30 = (bf16[320,640]{1,0:T(8,128)(2,1)}, bf16[320,640]{1,0:T(8,128)(2,1)}, u32[]{:S(2)}, u32[]{:S(2)}) collective-permute-start(bf16[320,640]{1,0:T(8,128)(2,1)} %get-tuple-element.38.refs_0_), channel_id=1, source_target_pairs={{0,16},{8,24},{16,0},{24,8},{1,17},{9,25},{17,1},{25,9},{2,18},{10... | collective-permute-start | bytes 1228808 | tf_op jit(solution)/shard_map/ppermute | solution.py:325
  87.9 20.8 %collective-permute-start.10 = (bf16[160,1920]{1,0:T(8,128)(2,1)}, bf16[160,1920]{1,0:T(8,128)(2,1)S(1)}, u32[]{:S(2)}, u32[]{:S(2)}) collective-permute-start(bf16[160,1920]{1,0:T(8,128)(2,1)} %collective-permute-done.9.refs_1_), channel_id=1, source_target_pairs={{0,4},{4,0},{1,5},{5,1},{2,6},{6,2},{3,7},{7,3},{8,12},{12,8},{9,1... | collective-permute-start | bytes 1843208 | tf_op jit(solution)/shard_map/ppermute | solution.py:331
  87.9 21.3 %collective-permute-start.12 = (bf16[160,1920]{1,0:T(8,128)(2,1)}, bf16[160,1920]{1,0:T(8,128)(2,1)S(1)}, u32[]{:S(2)}, u32[]{:S(2)}) collective-permute-start(bf16[160,1920]{1,0:T(8,128)(2,1)} %collective-permute-done.11.refs_3_), channel_id=1, source_target_pairs={{0,4},{4,0},{1,5},{5,1},{2,6},{6,2},{3,7},{7,3},{8,12},{12,8},{9,1... | collective-permute-start | bytes 1843208 | tf_op jit(solution)/shard_map/ppermute | solution.py:331
  88.4 20.3 %collective-permute-start.19 = (bf16[160,1920]{1,0:T(8,128)(2,1)S(1)}, bf16[160,1920]{1,0:T(8,128)(2,1)S(1)}, u32[]{:S(2)}, u32[]{:S(2)}) collective-permute-start(bf16[160,1920]{1,0:T(8,128)(2,1)S(1)} %broadcast_select_fusion), channel_id=1, source_target_pairs={{0,8},{4,20},{8,0},{12,28},{16,24},{20,4},{24,16},{28,12},{1,9},{5... | collective-permute-start | bytes 1843208 | tf_op jit(solution)/shard_map/ppermute | solution.py:327
  89.7 19.6 %collective-permute-start.14 = (bf16[160,1920]{1,0:T(8,128)(2,1)}, bf16[160,1920]{1,0:T(8,128)(2,1)S(1)}, u32[]{:S(2)}, u32[]{:S(2)}) collective-permute-start(bf16[160,1920]{1,0:T(8,128)(2,1)} %collective-permute-done.13.refs_5_), channel_id=1, source_target_pairs={{0,4},{4,0},{1,5},{5,1},{2,6},{6,2},{3,7},{7,3},{8,12},{12,8},{9,1... | collective-permute-start | bytes 1843208 | tf_op jit(solution)/shard_map/ppermute | solution.py:331
  98.6 9.4 %collective-permute-start.26 = (bf16[160,1280]{1,0:T(8,128)(2,1)}, bf16[160,1280]{1,0:T(8,128)(2,1)S(1)}, u32[]{:S(2)}, u32[]{:S(2)}) collective-permute-start(bf16[160,1280]{1,0:T(8,128)(2,1)} %collective-permute-done.25.refs_7_), channel_id=1, source_target_pairs={{0,4},{4,0},{1,5},{5,1},{2,6},{6,2},{3,7},{7,3},{8,12},{12,8},{9,1... | collective-permute-start | bytes 1228808 | tf_op jit(solution)/shard_map/ppermute | solution.py:331
  108.1 23.9 %copy-start.26 = (bf16[160,1280]{1,0:T(8,128)(2,1)}, bf16[160,1280]{1,0:T(8,128)(2,1)S(1)}, u32[]{:S(2)}) copy-start(bf16[160,1280]{1,0:T(8,128)(2,1)S(1)} %collective-permute-done.26.refs_8_) | copy-start | bytes 1228804
  108.1 23.9 %collective-permute-start.16 = (bf16[160,1920]{1,0:T(8,128)(2,1)S(1)}, bf16[160,1920]{1,0:T(8,128)(2,1)S(1)}, u32[]{:S(2)}, u32[]{:S(2)}) collective-permute-start(bf16[160,1920]{1,0:T(8,128)(2,1)S(1)} %collective-permute-done.15.refs_1_), channel_id=1, source_target_pairs={{0,4},{4,0},{1,5},{5,1},{2,6},{6,2},{3,7},{7,3},{8,12},{12,8},{9,1... | collective-permute-start | bytes 1843208 | tf_op jit(solution)/shard_map/ppermute | solution.py:331
  108.7 23.3 %collective-permute-start.18 = (bf16[160,1920]{1,0:T(8,128)(2,1)S(1)}, bf16[160,1920]{1,0:T(8,128)(2,1)S(1)}, u32[]{:S(2)}, u32[]{:S(2)}) collective-permute-start(bf16[160,1920]{1,0:T(8,128)(2,1)S(1)} %collective-permute-done.17.refs_3_), channel_id=1, source_target_pairs={{0,4},{4,0},{1,5},{5,1},{2,6},{6,2},{3,7},{7,3},{8,12},{12,8},{9,1... | collective-permute-start | bytes 1843208 | tf_op jit(solution)/shard_map/ppermute | solution.py:331
  108.8 23.2 %copy-start.19 = (bf16[160,1920]{1,0:T(8,128)(2,1)}, bf16[160,1920]{1,0:T(8,128)(2,1)S(1)}, u32[]{:S(2)}) copy-start(bf16[160,1920]{1,0:T(8,128)(2,1)S(1)} %collective-permute-done.19.refs_5_) | copy-start | bytes 1843204
  108.8 23.2 %collective-permute-start.20 = (bf16[160,1920]{1,0:T(8,128)(2,1)S(1)}, bf16[160,1920]{1,0:T(8,128)(2,1)S(1)}, u32[]{:S(2)}, u32[]{:S(2)}) collective-permute-start(bf16[160,1920]{1,0:T(8,128)(2,1)S(1)} %collective-permute-done.19.refs_5_), channel_id=1, source_target_pairs={{0,4},{4,0},{1,5},{5,1},{2,6},{6,2},{3,7},{7,3},{8,12},{12,8},{9,1... | collective-permute-start | bytes 1843208 | tf_op jit(solution)/shard_map/ppermute | solution.py:331
  109.3 0.8 copy-start.21
  109.3 1.1 copy-start.22
  132.0 1.0 copy-start.24
  155.5 14.4 %copy-start.9 = (bf16[320,640]{1,0:T(8,128)(2,1)S(1)}, bf16[320,640]{1,0:T(8,128)(2,1)}, u32[]{:S(2)}) copy-start(bf16[320,640]{1,0:T(8,128)(2,1)} %get-tuple-element.46.refs_0_) | copy-start | bytes 1228804
  155.5 16.4 %copy-start.12 = (bf16[320,640]{1,0:T(8,128)(2,1)S(1)}, bf16[320,640]{1,0:T(8,128)(2,1)}, u32[]{:S(2)}) copy-start(bf16[320,640]{1,0:T(8,128)(2,1)} %copy-done.11) | copy-start | bytes 1228804
  155.5 16.4 %copy-start.14 = (bf16[320,640]{1,0:T(8,128)(2,1)S(1)}, bf16[320,640]{1,0:T(8,128)(2,1)}, u32[]{:S(2)}) copy-start(bf16[320,640]{1,0:T(8,128)(2,1)} %copy-done.13) | copy-start | bytes 1228804
  169.1 33.8 %collective-permute-start.31 = (bf16[1536,1280]{1,0:T(8,128)(2,1)}, bf16[1536,1280]{1,0:T(8,128)(2,1)}, u32[]{:S(2)}, u32[]{:S(2)}) collective-permute-start(bf16[1536,1280]{1,0:T(8,128)(2,1)} %local_out.1.normed_ref), channel_id=1, source_target_pairs={{0,4},{4,0},{1,5},{5,1},{2,6},{6,2},{3,7},{7,3},{8,12},{12,8},{9,1... | collective-permute-start | bytes 11796488 | tf_op jit(solution)/shard_map/ppermute | solution.py:331
  169.9 11.7 %collective-permute-start.35 = (bf16[320,640]{1,0:T(8,128)(2,1)S(1)}, bf16[320,640]{1,0:T(8,128)(2,1)S(1)}, u32[]{:S(2)}, u32[]{:S(2)}) collective-permute-start(bf16[320,640]{1,0:T(8,128)(2,1)S(1)} %copy-done.9), channel_id=1, source_target_pairs={{0,8},{8,0},{16,24},{24,16},{1,9},{9,1},{17,25},{25,17},{2,10},{10... | collective-permute-start | bytes 1228808 | tf_op jit(solution)/shard_map/ppermute | solution.py:324
  169.9 12.3 %collective-permute-start.36 = (bf16[320,640]{1,0:T(8,128)(2,1)S(1)}, bf16[320,640]{1,0:T(8,128)(2,1)S(1)}, u32[]{:S(2)}, u32[]{:S(2)}) collective-permute-start(bf16[320,640]{1,0:T(8,128)(2,1)S(1)} %copy-done.9), channel_id=1, source_target_pairs={{0,16},{8,24},{16,0},{24,8},{1,17},{9,25},{17,1},{25,9},{2,18},{10... | collective-permute-start | bytes 1228808 | tf_op jit(solution)/shard_map/ppermute | solution.py:325
  172.0 15.1 %collective-permute-start.34 = (bf16[320,640]{1,0:T(8,128)(2,1)S(1)}, bf16[320,640]{1,0:T(8,128)(2,1)}, u32[]{:S(2)}, u32[]{:S(2)}) collective-permute-start(bf16[320,640]{1,0:T(8,128)(2,1)S(1)} %broadcast_select_fusion.4), channel_id=1, source_target_pairs={{0,8},{4,20},{8,0},{12,28},{16,24},{20,4},{24,16},{28,12},{1,9},{5... | collective-permute-start | bytes 1228808 | tf_op jit(solution)/shard_map/ppermute | solution.py:327
  173.7 2.2 collective-permute-start.33
  175.9 44.4 %collective-permute-start.32 = (bf16[320,640]{1,0:T(8,128)(2,1)S(1)}, bf16[320,640]{1,0:T(8,128)(2,1)}, u32[]{:S(2)}, u32[]{:S(2)}) collective-permute-start(bf16[320,640]{1,0:T(8,128)(2,1)S(1)} %broadcast_select_fusion.5), channel_id=1, source_target_pairs={{0,8},{4,20},{8,0},{12,28},{16,24},{20,4},{24,16},{28,12},{1,9},{5... | collective-permute-start | bytes 1228808 | tf_op jit(solution)/shard_map/ppermute | solution.py:327
  181.6 5.5 %copy-start.15 = (bf16[320,640]{1,0:T(8,128)(2,1)}, bf16[320,640]{1,0:T(8,128)(2,1)S(1)}, u32[]{:S(2)}) copy-start(bf16[320,640]{1,0:T(8,128)(2,1)S(1)} %collective-permute-done.35.refs_1_) | copy-start | bytes 1228804
  182.2 4.9 %copy-start.16 = (bf16[320,640]{1,0:T(8,128)(2,1)}, bf16[320,640]{1,0:T(8,128)(2,1)S(1)}, u32[]{:S(2)}) copy-start(bf16[320,640]{1,0:T(8,128)(2,1)S(1)} %collective-permute-done.36.refs_2_) | copy-start | bytes 1228804
  182.3 12.5 %collective-permute-start.37 = (bf16[320,640]{1,0:T(8,128)(2,1)S(1)}, bf16[320,640]{1,0:T(8,128)(2,1)S(1)}, u32[]{:S(2)}, u32[]{:S(2)}) collective-permute-start(bf16[320,640]{1,0:T(8,128)(2,1)S(1)} %broadcast_select_fusion.3), channel_id=1, source_target_pairs={{0,8},{4,20},{8,0},{12,28},{16,24},{20,4},{24,16},{28,12},{1,9},{5... | collective-permute-start | bytes 1228808 | tf_op jit(solution)/shard_map/ppermute | solution.py:327
  225.7 27.7 %copy-start.1 = (bf16[1,2,3,128,640]{4,3,2,1,0:T(8,128)(2,1)S(1)}, bf16[1,2,3,128,640]{4,3,2,1,0:T(8,128)(2,1)}, u32[]{:S(2)}) copy-start(bf16[1,2,3,128,640]{4,3,2,1,0:T(8,128)(2,1)} %param.7) | copy-start | bytes 2949124
  250.3 1.9 collective-permute-start.38
  (7 other events, 5.6 us)

commit v3 on v0

--- a/solution.py
+++ b/solution.py
@@ -1,6 +1,10 @@
+import functools
+
 import jax
 import jax.numpy as jnp
 from jax import lax
+from jax.experimental import pallas as pl
+from jax.experimental.pallas import tpu as pltpu
 from jax.sharding import PartitionSpec as P
 
 HEADS = 8
@@ -9,6 +13,8 @@
 
 norm_eps = 1e-05
 mask_floor = -1e30
+vmem_limit = 56 * 1024 * 1024
+exp2_scale = HD ** (-0.5) * 1.4426950408889634
 
 
 def layer_norm(values):
@@ -51,7 +57,7 @@
     return attend(heads_split[:, :, 0], heads_split[:, :, 1], heads_split[:, :, 2], keep_mask)
 
 
-def body(patches, kept_index, kept_count, embed_weight, local_qkv, local_out, global_qkv):
+def owner_body(patches, kept_index, kept_count, embed_weight, local_qkv, local_out, global_qkv):
     lat_windows = patches.shape[1]
     lon_windows = patches.shape[2]
     windows = lat_windows * lon_windows
@@ -79,7 +85,6 @@
     back_sum = fold_product(local_mix, lax.all_gather(local_out, "batch", axis=0, tiled=True))
     hidden = (embedded.astype(jnp.float32) + back_sum).astype(jnp.bfloat16)
     normed_global = layer_norm(hidden.astype(jnp.float32)).astype(jnp.bfloat16)
-    whole_global = None
     whole_global = lax.all_gather(global_qkv, "batch", axis=0, tiled=True)
     sent_width = normed_global.shape[1]
     window_ids = lax.broadcasted_iota(jnp.int32, (windows, kept_most), 0)
@@ -93,9 +98,7 @@
         .at[index_rows, window_ids]
         .set(kept_mask.astype(jnp.bfloat16))
     )
-    lat_size = lax.axis_size("lat")
-    lon_size = lax.axis_size("lon")
-    owners = lat_size * lon_size
+    owners = lax.axis_size("lat") * lax.axis_size("lon")
     owned_count = window_tokens // owners
     blended = owner_work(
         lax.all_to_all(
@@ -122,6 +125,456 @@
     return result.reshape(1, lat_windows, lon_windows, kept_most, inner_width)
 
 
+MAIN = 128
+TAIL = HD - MAIN
+GROUP = MAIN // TAIL
+WIDE = GROUP * HD
+
+
+def whole_block(array):
+    zeros = (0,) * array.ndim
+    return pl.BlockSpec(array.shape, lambda *_: zeros)
+
+
+def assemble(offset_ref, piece_refs, weight_ref):
+    for at, piece in enumerate(piece_refs):
+        start = pl.multiple_of(offset_ref[at], 16)
+        weight_ref[pl.ds(start, piece.shape[0]), :] = piece[...]
+
+
+def reorder(source, start, target, at):
+    for head in range(GROUP):
+        first = start + head * HD
+        target[:, pl.ds(at + head * MAIN, MAIN)] = source[:, pl.ds(first, MAIN)]
+        target[:, pl.ds(at + GROUP * MAIN + head * TAIL, TAIL)] = source[:, pl.ds(first + MAIN, TAIL)]
+
+
+def prepare_local_kernel(core_ref, weight_ref, *refs):
+    groups = len(refs) // 2
+    inner = weight_ref.shape[1] // 3
+    for group in range(groups):
+        full, half = refs[group], refs[groups + group]
+        for which in range(3):
+            reorder(weight_ref, which * inner + group * WIDE, full, which * WIDE)
+        high = half.shape[0]
+        half[...] = full[pl.ds(pl.multiple_of(core_ref[0] * high, 16), high), :]
+
+
+def prepare_global_kernel(core_ref, query_ref, key_ref, value_ref, first_ref, second_ref):
+    reorder(key_ref, 0, first_ref, 0)
+    reorder(query_ref, 0, first_ref, WIDE)
+    reorder(value_ref, 0, second_ref, 0)
+
+
+def lane_head():
+    return lax.broadcasted_iota(jnp.int32, (1, MAIN), 1) // TAIL
+
+
+def head_tiles(ref, rows, at, head):
+    main = ref[rows, pl.ds(at + head * MAIN, MAIN)]
+    tail = ref[rows, pl.ds(at + GROUP * MAIN, MAIN)]
+    return main, tail
+
+
+def head_query(ref, rows, at, head):
+    main, tail = head_tiles(ref, rows, at, head)
+    return jnp.concatenate([main, jnp.where(lane_head() == head, tail, jnp.zeros_like(tail))], axis=1)
+
+
+def head_pair(ref, rows, at, head):
+    return jnp.concatenate(head_tiles(ref, rows, at, head), axis=1)
+
+
+def masked_scores(query, key, mask):
+    scores = lax.dot_general(
+        query, key, (((1,), (1,)), ((), ())), preferred_element_type=jnp.float32
+    )
+    return jnp.where(mask, scores, mask_floor)
+
+
+def mix_heads(proj_ref, code_ref, mix_ref, at_once, kept_most):
+    rows = proj_ref.shape[0]
+    own_window = lax.broadcasted_iota(jnp.int32, (at_once, 1), 0) // kept_most
+    for start in range(0, rows, at_once):
+        part = pl.ds(start, at_once)
+        mask = own_window == code_ref[0, :, part]
+        tails = None
+        for head in range(GROUP):
+            scores = masked_scores(
+                head_query(proj_ref, part, 0, head), head_pair(proj_ref, part, WIDE, head), mask
+            )
+            top = jnp.max(scores, axis=-1, keepdims=True)
+            weights = jnp.exp2((scores - top) * exp2_scale)
+            total = jnp.sum(weights, axis=-1, keepdims=True)
+            mixed = (
+                fold_product(
+                    weights.astype(jnp.bfloat16), head_pair(proj_ref, part, 2 * WIDE, head)
+                )
+                / total
+            )
+            mix_ref[part, pl.ds(head * MAIN, MAIN)] = mixed[:, :MAIN].astype(jnp.bfloat16)
+            tail = mixed[:, MAIN:]
+            tails = tail if tails is None else jnp.where(lane_head() == head, tail, tails)
+        mix_ref[part, pl.ds(GROUP * MAIN, MAIN)] = tails.astype(jnp.bfloat16)
+
+
+def embed_window_kernel(
+    at_once,
+    kept_most,
+    offset_ref,
+    picked_ref,
+    code_ref,
+    embed_ref,
+    *refs,
+):
+    *pieces, embedded_ref, normed_ref, mix_ref, weight_ref, proj_ref = refs
+
+    @pl.when(pl.program_id(0) == 0)
+    def _():
+        assemble(offset_ref, pieces, weight_ref)
+
+    embedded = fold_product(picked_ref[...], embed_ref[...]).astype(jnp.bfloat16)
+    embedded_ref[...] = embedded
+    normed = layer_norm(embedded.astype(jnp.float32)).astype(jnp.bfloat16)
+    normed_ref[...] = normed
+    proj_ref[...] = fold_product(normed, weight_ref[...]).astype(jnp.bfloat16)
+    mix_heads(proj_ref, code_ref, mix_ref, at_once, kept_most)
+
+
+def window_out_kernel(
+    at_once,
+    kept_most,
+    offset_ref,
+    embedded_ref,
+    normed_ref,
+    mix_ref,
+    code_ref,
+    out_ref,
+    *refs,
+):
+    *pieces, result_ref, weight_ref, proj_ref, own_mix_ref, row_ref = refs
+    inner = out_ref.shape[0]
+
+    @pl.when(pl.program_id(0) == 0)
+    def _():
+        assemble(offset_ref, pieces, weight_ref)
+        for start in range(0, inner, WIDE):
+            for head in range(GROUP):
+                first = start + head * HD
+                row_ref[pl.ds(start + head * MAIN, MAIN), :] = out_ref[pl.ds(first, MAIN), :]
+                row_ref[pl.ds(start + GROUP * MAIN + head * TAIL, TAIL), :] = out_ref[
+                    pl.ds(first + MAIN, TAIL), :
+                ]
+
+    proj_ref[...] = fold_product(normed_ref[...], weight_ref[...]).astype(jnp.bfloat16)
+    mix_heads(proj_ref, code_ref, own_mix_ref, at_once, kept_most)
+    hidden = embedded_ref[...].astype(jnp.float32)
+    hidden += fold_product(mix_ref[...], row_ref[pl.ds(0, WIDE), :])
+    hidden += fold_product(own_mix_ref[...], row_ref[pl.ds(WIDE, WIDE), :])
+    hidden = hidden.astype(jnp.bfloat16).astype(jnp.float32)
+    result_ref[...] = layer_norm(hidden).astype(jnp.bfloat16)
+
+
+def group_kernel(
+    steps,
+    rows,
+    key_chunk,
+    offset_ref,
+    own_ref,
+    other_ref,
+    code_ref,
+    key_code_ref,
+    *refs,
+):
+    *pieces, mixed_ref, first_ref, second_ref, key_ref, query_ref, value_ref = refs
+    step = pl.program_id(0)
+    block = own_ref.shape[0]
+    query_block = mixed_ref.shape[0]
+
+    @pl.when(step == 0)
+    def _():
+        assemble(offset_ref, pieces[:4], first_ref)
+        assemble(offset_ref, pieces[4:], second_ref)
+
+    def project(source_ref, at):
+        normed = source_ref[...]
+        part = pl.ds(pl.multiple_of(step * block, 16), block)
+        key_ref[part, :] = fold_product(normed, first_ref[:, pl.ds(0, WIDE)]).astype(jnp.bfloat16)
+        value_ref[part, :] = fold_product(normed, second_ref[...]).astype(jnp.bfloat16)
+
+        @pl.when(step == at * steps)
+        def _():
+            query_ref[pl.ds(at * rows, rows), :] = fold_product(
+                source_ref[pl.ds(0, rows), :], first_ref[:, pl.ds(WIDE, WIDE)]
+            ).astype(jnp.bfloat16)
+
+    @pl.when(step < steps)
+    def _():
+        project(own_ref, 0)
+
+    @pl.when((step >= steps) & (step < 2 * steps))
+    def _():
+        project(other_ref, 1)
+
+    @pl.when(step >= 2 * steps)
+    def _():
+        part = pl.ds(pl.multiple_of((step - 2 * steps) * query_block, 16), query_block)
+        codes = code_ref[...]
+        key_parts = [pl.ds(at, key_chunk) for at in range(0, key_ref.shape[0], key_chunk)]
+        for head in range(GROUP):
+            query = head_query(query_ref, part, 0, head)
+            scores = [
+                masked_scores(query, head_pair(key_ref, p, 0, head), codes == key_code_ref[:, p])
+                for p in key_parts
+            ]
+            top = functools.reduce(
+                jnp.maximum, [jnp.max(s, axis=-1, keepdims=True) for s in scores]
+            )
+            total = 0.0
+            mixed = 0.0
+            for p, s in zip(key_parts, scores):
+                weights = jnp.exp2((s - top) * exp2_scale)
+                total += jnp.sum(weights, axis=-1, keepdims=True)
+                mixed += fold_product(
+                    weights.astype(jnp.bfloat16), head_pair(value_ref, p, 0, head)
+                )
+            mixed = jnp.where(codes >= 0, mixed / total, 0.0).astype(jnp.bfloat16)
+            mixed_ref[:, pl.ds(head * HD, MAIN)] = mixed[:, :MAIN]
+            at = MAIN + head * TAIL
+            mixed_ref[:, pl.ds(head * HD + MAIN, TAIL)] = mixed[:, at : at + TAIL]
+
+
+def swap_perm(size, mask):
+    return [(i, i ^ mask) for i in range(size)]
+
+
+def after(value, earlier):
+    return lax.optimization_barrier((value, earlier))[0]
+
+
+def run(kernel, steps, scalars, specs, arrays, outs, out_specs, scratch, flops, name):
+    moved = sum(a.size * a.dtype.itemsize for a in arrays)
+    return pl.pallas_call(
+        kernel,
+        grid_spec=pltpu.PrefetchScalarGridSpec(
+            num_scalar_prefetch=1,
+            grid=(steps,),
+            in_specs=specs,
+            out_specs=out_specs,
+            scratch_shapes=[pltpu.VMEM(shape, jnp.bfloat16) for shape in scratch],
+        ),
+        out_shape=[jax.ShapeDtypeStruct(shape, jnp.bfloat16) for shape in outs],
+        compiler_params=pltpu.CompilerParams(vmem_limit_bytes=vmem_limit),
+        cost_estimate=pl.CostEstimate(flops=flops, bytes_accessed=moved, transcendentals=0),
+        name=name,
+    )(scalars, *arrays)
+
+
+def sample_body(patches, kept_index, kept_count, embed_weight, local_qkv, local_out, global_qkv):
+    lat_windows, lon_windows, window_tokens, pin = patches.shape[1:]
+    windows = lat_windows * lon_windows
+    kept_most = kept_index.shape[3]
+    rows = windows * kept_most
+    inner = HEADS * HD
+    width = embed_weight.shape[1]
+    lon_size = lax.axis_size("lon")
+    batch_size = lax.axis_size("batch")
+    core = lax.axis_index("lat")
+    chip = lax.axis_index("batch")
+    core_scalar = core.reshape(1).astype(jnp.int32)
+
+    def own_rows(shard):
+        part = shard.shape[0] // 2
+        return lax.dynamic_slice_in_dim(shard, core * part, part, axis=0)
+
+    whole_embed = lax.all_gather(own_rows(embed_weight), ("batch", "lat"), axis=0, tiled=True)
+    whole_out = lax.all_gather(own_rows(local_out), ("batch", "lat"), axis=0, tiled=True)
+
+    diagonal = []
+    for b in range(batch_size):
+        diagonal += [(2 * b, 2 * (b ^ 1)), (2 * b + 1, 2 * (b ^ 2) + 1)]
+
+    def sides(part):
+        along_x = lax.ppermute(part, "batch", swap_perm(batch_size, 1))
+        along_y = lax.ppermute(part, "batch", swap_perm(batch_size, 2))
+        return along_x, along_y
+
+    def across(along_x, along_y):
+        forwarded = jnp.where(core == 0, along_y, along_x)
+        return lax.ppermute(forwarded, ("batch", "lat"), diagonal)
+
+    def other_core(value):
+        return lax.ppermute(value, "lat", swap_perm(2, 1))
+
+    high = local_qkv.shape[0]
+    half = high // 2
+    *local_full, half_first, half_second = run(
+        prepare_local_kernel,
+        1,
+        core_scalar,
+        [whole_block(local_qkv)],
+        [local_qkv],
+        [(high, 3 * WIDE)] * 2 + [(half, 3 * WIDE)] * 2,
+        [pl.BlockSpec((h, 3 * WIDE), lambda *_: (0, 0)) for h in (high, high, half, half)],
+        [],
+        0,
+        "order_local",
+    )
+    local_sides = [sides(half_first), sides(half_second)]
+    global_first, global_second = run(
+        prepare_global_kernel,
+        1,
+        core_scalar,
+        [
+            pl.BlockSpec((high, WIDE), lambda i, c, which=which: (0, 2 * which + c[0]))
+            for which in range(3)
+        ],
+        [global_qkv] * 3,
+        [(high, 2 * WIDE), (high, WIDE)],
+        [pl.BlockSpec((high, w), lambda *_: (0, 0)) for w in (2 * WIDE, WIDE)],
+        [],
+        0,
+        "order_global",
+    )
+
+    index_rows = kept_index.reshape(windows, kept_most)
+    kept_mask = lax.broadcasted_iota(jnp.int32, (windows, kept_most), 1) < kept_count.reshape(
+        windows, 1
+    )
+    codes = jnp.where(kept_mask, index_rows, -1).reshape(rows)
+    picked = jnp.take_along_axis(
+        patches.reshape(windows, window_tokens, pin), index_rows[:, :, None], axis=1
+    ).reshape(rows, pin)
+
+    code_rows = -(-rows // pin)
+    code_tile = -(-code_rows // 16) * 16
+    code_part = jnp.pad(codes, (0, code_tile * pin - rows)).reshape(code_tile, pin)
+    sent = jnp.concatenate([picked, code_part.astype(jnp.bfloat16)], axis=0)
+    picked_parts = [sent]
+    for shift in range(1, lon_size):
+        picked_parts.append(
+            lax.ppermute(sent, "lon", [(i, (i + shift) % lon_size) for i in range(lon_size)])
+        )
+    picked_all = jnp.concatenate([part[:rows] for part in picked_parts], axis=0)
+    all_rows = picked_all.shape[0]
+    own_codes = jnp.concatenate(
+        [part[rows : rows + code_rows].reshape(-1)[:rows] for part in picked_parts]
+    ).astype(jnp.int32)
+    other_codes = other_core(own_codes)
+
+    local_across = [across(*s) for s in local_sides]
+    first_sides = sides(after(global_first, local_sides[0]))
+
+    def shared(shard, got):
+        pieces, offsets = [shard], [chip * high]
+        for which, value in zip((1, 2, 3), got):
+            pieces += [value, other_core(value)]
+            base = (chip ^ which) * high
+            offsets += [base + core * half, base + (1 - core) * half]
+        return pieces, jnp.stack(offsets).astype(jnp.int32)
+
+    block = all_rows // 3 if all_rows % (3 * 4 * kept_most) == 0 else all_rows
+    steps = all_rows // block
+    at_once = 2 * kept_most if block % (2 * kept_most) == 0 else kept_most
+    window_codes = jnp.where(
+        own_codes >= 0,
+        (jnp.arange(all_rows, dtype=jnp.int32) // kept_most) % (at_once // kept_most),
+        -1,
+    ).reshape(steps, 1, block)
+    code_spec = pl.BlockSpec((1, 1, block), lambda i, _: (i, 0, 0))
+    row_spec = lambda wide: pl.BlockSpec((block, wide), lambda i, _: (i, 0))
+
+    pieces, offsets = shared(local_full[0], [*local_sides[0], local_across[0]])
+    embedded, normed, first_mix = run(
+        functools.partial(embed_window_kernel, at_once, kept_most),
+        steps,
+        offsets,
+        [row_spec(pin), code_spec, whole_block(whole_embed), *map(whole_block, pieces)],
+        [picked_all, window_codes, whole_embed, *pieces],
+        [(all_rows, width), (all_rows, width), (all_rows, WIDE)],
+        [row_spec(width), row_spec(width), row_spec(WIDE)],
+        [(width, 3 * WIDE), (block, 3 * WIDE)],
+        2 * all_rows * (pin * width + width * 3 * WIDE),
+        "embed_windows",
+    )
+
+    pieces, offsets = shared(local_full[1], [*local_sides[1], local_across[1]])
+    pieces = after(pieces, first_sides)
+    first_across = across(*first_sides)
+    second_sides = sides(after(global_second, first_sides))
+    (normed_own,) = run(
+        functools.partial(window_out_kernel, at_once, kept_most),
+        steps,
+        offsets,
+        [
+            row_spec(width),
+            row_spec(width),
+            row_spec(WIDE),
+            code_spec,
+            whole_block(whole_out),
+            *map(whole_block, pieces),
+        ],
+        [embedded, normed, first_mix, window_codes, whole_out, *pieces],
+        [(all_rows, width)],
+        [row_spec(width)],
+        [(width, 3 * WIDE), (block, 3 * WIDE), (block, WIDE), (inner, width)],
+        2 * all_rows * (inner * width + width * 3 * WIDE),
+        "windows_out",
+    )
+    normed_other = other_core(normed_own)
+    second_across = across(*second_sides)
+
+    key_codes = jnp.concatenate([own_codes, other_codes]).reshape(1, 2 * all_rows)
+    query_codes = jnp.concatenate([own_codes[:rows], other_codes[:rows]]).reshape(2 * rows, 1)
+    query_codes = jnp.where(query_codes >= 0, query_codes, -2)
+    query_block = 256 if (2 * rows) % 256 == 0 else 2 * rows
+    query_steps = 2 * rows // query_block
+    pieces = [global_first, *first_sides, first_across, global_second, *second_sides, second_across]
+    offsets = jnp.stack([(chip ^ which) * high for which in range(4)]).astype(jnp.int32)
+    late = lambda i: jnp.clip(i - 2 * steps, 0, query_steps - 1)
+    (mixed,) = run(
+        functools.partial(group_kernel, steps, rows, block),
+        2 * steps + query_steps,
+        offsets,
+        [
+            pl.BlockSpec((block, width), lambda i, _: (jnp.minimum(i, steps - 1), 0)),
+            pl.BlockSpec((block, width), lambda i, _: (jnp.clip(i - steps, 0, steps - 1), 0)),
+            pl.BlockSpec((query_block, 1), lambda i, _: (late(i), 0)),
+            whole_block(key_codes),
+            *map(whole_block, pieces),
+        ],
+        [normed_own, normed_other, query_codes, key_codes, *pieces],
+        [(2 * rows, WIDE)],
+        [pl.BlockSpec((query_block, WIDE), lambda i, _: (late(i), 0))],
+        [
+            (width, 2 * WIDE),
+            (width, WIDE),
+            (2 * all_rows, WIDE),
+            (2 * rows, WIDE),
+            (2 * all_rows, WIDE),
+        ],
+        2 * WIDE * (2 * all_rows * 2 * width + 2 * rows * width + 4 * rows * 2 * all_rows),
+        "groups",
+    )
+
+    mine, theirs = mixed[:rows], other_core(mixed[rows:])
+    result = jnp.where(
+        core == 0,
+        jnp.concatenate([mine, theirs], axis=1),
+        jnp.concatenate([theirs, mine], axis=1),
+    )
+    return result.reshape(1, lat_windows, lon_windows, kept_most, inner)
+
+
+def body(patches, kept_index, *weights):
+    rows = patches.shape[1] * patches.shape[2] * kept_index.shape[3]
+    sample_rows = rows * lax.axis_size("lat") * lax.axis_size("lon")
+    fits = patches.shape[3] <= 256 and sample_rows * HEADS * HD * 2 <= vmem_limit // 4
+    if lax.axis_size("batch") == 4 and lax.axis_size("lat") == HEADS // GROUP == 2 and fits:
+        return sample_body(patches, kept_index, *weights)
+    return owner_body(patches, kept_index, *weights)
+
+
 def solution(mesh):
     return jax.shard_map(
         body,

time: 417 us -> 238 us (0.57)
  waiting for transfers between devices: 223 us -> 76.9 us
  local copies, waits for them, and re-layouts: 121 us -> 16.8 us
  Pallas kernels: 0 us -> 94.1 us
  matrix products: 35.5 us -> 0 us
  starting transfers between devices: 15.6 us -> 25.3 us
    all_gather x4 -> x2, waiting for transfers between devices: 130 us -> 0.02 us  [the longest x1 0.02 us: sample_body(): lax.all_gather(own_rows(embed_weight), ('batch', 'lat'), axis=0, tiled=True)]
    pallas_call x0 -> x5, Pallas kernels: none -> 94.1 us  [run(): pl.pallas_call(kernel, grid_spec=pltpu.PrefetchScalarGridSpec(num_scalar_...]
    all_to_all x3 -> x0, waiting for transfers between devices: 90.6 us -> none  [the longest x1 45.6 us: body(): lax.all_to_all(shaped, ('lat', 'lon'), split_axis=2, concat_axis=1, tiled...]
    ppermute x0 -> x24, waiting for transfers between devices: none -> 76.8 us  [the longest x4 28.3 us: across(): return lax.ppermute(forwarded, ('batch', 'lat'), diagonal)]
    scatter x2 -> x0, local copies, waits for them, and re-layouts: 46.3 us -> none  [the longest x1 27.9 us: body(): slot_rows = jnp.zeros((window_tokens, windows, sent_width), jnp.bfloat16)...]
    dot_general x8 -> x0, matrix products: 35.5 us -> none  [the longest x3 15.3 us: fold_product(): return jnp.dot(left_rows, shard_rows, preferred_element_type=jnp.float32)]
    another operation x6 -> x2, local copies, waits for them, and re-layouts: 30.4 us -> 0.75 us  [the longest x1 0.66 us: shared(): return (pieces, jnp.stack(offsets).astype(jnp.int32))]
    ppermute x0 -> x24, starting transfers between devices: none -> 25.3 us  [the longest x3 8.3 us: sample_body(): lax.ppermute(sent, 'lon', [(i, (i + shift) % lon_size) for i in range(lon...]
  transfers between devices with their start and end apart: 7 -> 26, of which waited for: 6 -> 11; matrix products, arithmetic and copies ran while one was open for 23% -> 9% of each run, Pallas kernels for 0% -> 14%
where the time goes in v3:
time: 238 us; the launch traced here: 237 us
  Pallas kernels  94.1 us (40%)
  waiting for transfers between devices  76.9 us (32%)
  starting transfers between devices  25.3 us (11%)
  local copies, waits for them, and re-layouts  16.8 us (7%)
  between operations  13.6 us (6%)
  other arithmetic  10.4 us (4%)
    pallas_call x5, Pallas kernels, run(): pl.pallas_call(kernel, grid_spec=pltpu.PrefetchScalarGridSpec(num_scalar_...  94.1 us
    ppermute x4, waiting for transfers between devices, across(): return lax.ppermute(forwarded, ('batch', 'lat'), diagonal)  28.3 us
    ppermute x4, waiting for transfers between devices, sides(): along_x = lax.ppermute(part, 'batch', swap_perm(batch_size, 1))  22 us
    ppermute x3, waiting for transfers between devices, sample_body(): lax.ppermute(sent, 'lon', [(i, (i + shift) % lon_size) for i in range(lon...  17 us
    ppermute x3, starting transfers between devices, sample_body(): lax.ppermute(sent, 'lon', [(i, (i + shift) % lon_size) for i in range(lon...  8.3 us
    ppermute x9, waiting for transfers between devices, other_core(): return lax.ppermute(value, 'lat', swap_perm(2, 1))  7.2 us
    ppermute x4, starting transfers between devices, sides(): along_x = lax.ppermute(part, 'batch', swap_perm(batch_size, 1))  5.3 us
  transfers between devices with their start and end apart: 26, of which 11 were waited for; matrix products, arithmetic and copies ran while one was open for 9% of the time, Pallas kernels for 14%

profile of v3, /device:TPU:0, one launch (start us, length us, event | category | flops | bytes accessed | tf_op | source)
XLA Modules:
  0.0 237.2 jit_solution(4381638778923651850)
XLA Ops:
  6.5 1.7 constant_dynamic-slice_fusion.1
  8.3 1.8 constant_dynamic-slice_fusion
  10.2 4.3 %order_local.1 = (bf16[320,1920]{1,0:T(8,128)(2,1)}, bf16[320,1920]{1,0:T(8,128)(2,1)}, bf16[160,1920]{1,0:T(8,128)(2,1)}, bf16[160,1920]{1,0:T(8,128)(2,1)}) custom-call(s32[1]{0:T(128)} %bitcast.12.core_ref, bf16[320,3840]{1,0:T(8,128)(2,1)} %weight_ref.1), custom_call_target="tpu_custom_call" | custom-call | bytes 2457600 | tf_op jit(solution)/shard_map/order_local/pallas_call | solution.py:357
  14.4 2.9 %collective-permute-start.3 = (bf16[160,1920]{1,0:T(8,128)(2,1)}, bf16[160,1920]{1,0:T(8,128)(2,1)S(1)}, u32[]{:S(2)}, u32[]{:S(2)}) collective-permute-start(bf16[160,1920]{1,0:T(8,128)(2,1)} %get-tuple-element.24), channel_id=1, source_target_pairs={{0,8},{8,0},{16,24},{24,16},{1,9},{9,1},{17,25},{25,17},{2,10},{10... | collective-permute-start | bytes 1843208 | tf_op jit(solution)/shard_map/ppermute | solution.py:398
  17.4 1.5 collective-permute-start.5
  18.9 0.5 collective-permute-start.9
  19.5 0.1 lt.45
  19.6 0.1 iota_compare_fusion
  19.6 0.1 lt.48
  19.7 0.1 broadcast_in_dim_reshape.5
  20.0 4.3 %gather_fusion = bf16[384,640]{1,0:T(8,128)(2,1)S(1)} fusion(bf16[6,128,640]{2,1,0:T(8,128)(2,1)S(1)} %bitcast.19, s32[384]{0:T(512)S(1)} %reshape.312), kind=kCustom, calls=%fused_computation | custom fusion | bytes 986112 | tf_op jit(solution)/shard_map/jit(take_along_axis)/gather | solution.py:445
  24.3 0.1 broadcast_select_fusion.3
  24.5 0.9 pad_maximum_fusion.1
  25.3 4.1 %collective-permute-start.2 = (bf16[400,640]{1,0:T(8,128)(2,1)}, bf16[400,640]{1,0:T(8,128)(2,1)}, u32[]{:S(2)}, u32[]{:S(2)}) collective-permute-start(bf16[400,640]{1,0:T(8,128)(2,1)} %pad_maximum_fusion.1), channel_id=1, source_target_pairs={{0,3},{1,0},{2,1},{3,2},{4,7},{5,4},{6,5},{7,6},{8,11},{9,8},{10,9... | collective-permute-start | bytes 1536008 | tf_op jit(solution)/shard_map/ppermute | solution.py:456
  29.4 2.8 %order_global.1 = (bf16[320,1280]{1,0:T(8,128)(2,1)}, bf16[320,640]{1,0:T(8,128)(2,1)}) custom-call(s32[1]{0:T(128)} %bitcast.12.core_ref, bf16[320,3840]{1,0:T(8,128)(2,1)} %value_ref.1, bf16[320,3840]{1,0:T(8,128)(2,1)} %value_ref.1, bf16[320,3840]{1,0:T(8,128)(2,1)} %value_ref.1), custom_call_target="tpu_custom_call" | custom-call | bytes 7372800 | tf_op jit(solution)/shard_map/order_global/pallas_call | solution.py:357
  32.3 3.7 %collective-permute-done.3.refs_1_ = bf16[160,1920]{1,0:T(8,128)(2,1)S(1)} collective-permute-done((bf16[160,1920]{1,0:T(8,128)(2,1)}, bf16[160,1920]{1,0:T(8,128)(2,1)S(1)}, u32[]{:S(2)}, u32[]{:S(2)}) %collective-permute-start.3) | collective-permute-done | bytes 614432 | tf_op jit(solution)/shard_map/ppermute | solution.py:398
  36.0 2.5 %collective-permute-start.1 = (bf16[400,640]{1,0:T(8,128)(2,1)}, bf16[400,640]{1,0:T(8,128)(2,1)}, u32[]{:S(2)}, u32[]{:S(2)}) collective-permute-start(bf16[400,640]{1,0:T(8,128)(2,1)} %pad_maximum_fusion.1), channel_id=1, source_target_pairs={{0,2},{1,3},{2,0},{3,1},{4,6},{5,7},{6,4},{7,5},{8,10},{9,11},{10,... | collective-permute-start | bytes 1536008 | tf_op jit(solution)/shard_map/ppermute | solution.py:456
  38.5 0.3 collective-permute-done.5.refs_3_
  38.8 1.7 collective-permute-start
  40.4 0.9 broadcast_select_fusion.2
  41.3 10.0 %collective-permute-done.9.refs_1_ = bf16[160,1920]{1,0:T(8,128)(2,1)} collective-permute-done((bf16[160,1920]{1,0:T(8,128)(2,1)}, bf16[160,1920]{1,0:T(8,128)(2,1)}, u32[]{:S(2)}, u32[]{:S(2)}) %collective-permute-start.9) | collective-permute-done | bytes 614432 | tf_op jit(solution)/shard_map/ppermute | solution.py:398
  51.3 1.7 collective-permute-start.7
  53.1 0.3 collective-permute-start.15
  53.3 2.0 broadcast_select_fusion.1
  55.4 17.0 %collective-permute-done.1 = bf16[400,640]{1,0:T(8,128)(2,1)} collective-permute-done((bf16[400,640]{1,0:T(8,128)(2,1)}, bf16[400,640]{1,0:T(8,128)(2,1)}, u32[]{:S(2)}, u32[]{:S(2)}) %collective-permute-start.1) | collective-permute-done | bytes 512032 | tf_op jit(solution)/shard_map/ppermute | solution.py:456
  72.4 1.5 collective-permute-start.13
  73.9 0.7 stack.56.offset_ref
  74.6 0.7 slice_reduce_fusion
  75.3 1.6 collective-permute-start.16
  76.9 0.7 slice_reduce_fusion.1
  77.6 0.7 slice_reduce_fusion.2
  78.4 0.5 collective-permute-start.6
  78.9 19.7 %collective-permute-done.13.refs_5_ = bf16[160,1920]{1,0:T(8,128)(2,1)} collective-permute-done((bf16[160,1920]{1,0:T(8,128)(2,1)}, bf16[160,1920]{1,0:T(8,128)(2,1)}, u32[]{:S(2)}, u32[]{:S(2)}) %collective-permute-start.13) | collective-permute-done | bytes 614432 | tf_op jit(solution)/shard_map/ppermute | solution.py:404
  98.6 0.5 collective-permute-start.14
  99.1 1.1 slice.72
  100.2 1.1 slice.71
  101.3 1.1 slice.70
  102.3 0.6 fusion.code_ref
  103.0 1.4 pad_maximum_fusion.picked_ref
  104.5 25.0 %embed_windows.1 = (bf16[1536,1280]{1,0:T(8,128)(2,1)}, bf16[1536,1280]{1,0:T(8,128)(2,1)}, bf16[1536,640]{1,0:T(8,128)(2,1)}) custom-call(s32[7]{0:T(128)} %stack.56.offset_ref, bf16[1536,640]{1,0:T(8,128)(2,1)} %pad_maximum_fusion.picked_ref, s32[3,1,512]{2,1,0:T(1,128)} %fusion.code_ref, bf16[640,1280]{1,0:T(8,128)(2,1)} %all-gather.3.cloned.1.call-done.embed_ref, ...), custom_call_target="tpu_custom_call" | custom-call | flops 10066329600 | bytes 8525824 | tf_op jit(solution)/shard_map/embed_windows/pallas_call | solution.py:357
  129.5 25.7 %windows_out.1.own_ref = bf16[1536,1280]{1,0:T(8,128)(2,1)} custom-call(s32[7]{0:T(128)} %stack.56.offset_ref, bf16[1536,1280]{1,0:T(8,128)(2,1)} %get-tuple-element.25.embedded_ref, bf16[1536,1280]{1,0:T(8,128)(2,1)} %get-tuple-element.26.normed_ref, bf16[1536,640]{1,0:T(8,128)(2,1)} %get-tuple-element.27.mix_ref, s32[3,1,512]{2,1,0:T(1,128)} %fusion.code_ref, ...), custom_call_target="tpu_custom_call" | custom-call | flops 12582912000 | bytes 18028544 | tf_op jit(solution)/shard_map/windows_out/pallas_call | solution.py:357
  155.2 1.6 collective-permute-start.17
  156.9 0.6 pad_add_fusion.1.offset_ref
  157.5 0.1 collective-permute-start.18
  157.6 5.7 %collective-permute-done.18 = s32[1536]{0:T(1024)S(1)} collective-permute-done((s32[1536]{0:T(1024)S(1)}, s32[1536]{0:T(1024)S(1)}, u32[]{:S(2)}, u32[]{:S(2)}) %collective-permute-start.18) | collective-permute-done | bytes 6176 | tf_op jit(solution)/shard_map/ppermute | solution.py:407
  163.3 1.5 collective-permute-start.20
  164.9 0.6 collective-permute-start.21
  165.4 1.0 broadcast_select_fusion
  166.4 0.3 collective-permute-start.19
  166.7 8.4 %collective-permute-done.20.refs_5_ = bf16[320,640]{1,0:T(8,128)(2,1)S(1)} collective-permute-done((bf16[320,640]{1,0:T(8,128)(2,1)S(1)}, bf16[320,640]{1,0:T(8,128)(2,1)S(1)}, u32[]{:S(2)}, u32[]{:S(2)}) %collective-permute-start.20) | collective-permute-done | bytes 409632 | tf_op jit(solution)/shard_map/ppermute | solution.py:398
  175.1 2.1 collective-permute-done.21.refs_6_
  177.2 0.6 collective-permute-start.22
  177.9 0.2 copy.23
  178.1 0.2 copy.22
  178.3 0.6 pad_add_fusion
  178.9 0.8 broadcast_select_fusion.5.code_ref
  179.7 4.3 %collective-permute-done.19.refs_3_ = bf16[320,1280]{1,0:T(8,128)(2,1)} collective-permute-done((bf16[320,1280]{1,0:T(8,128)(2,1)}, bf16[320,1280]{1,0:T(8,128)(2,1)}, u32[]{:S(2)}, u32[]{:S(2)}) %collective-permute-start.19) | collective-permute-done | bytes 819232 | tf_op jit(solution)/shard_map/ppermute | solution.py:404
  184.0 4.3 %collective-permute-done.22.refs_7_ = bf16[320,640]{1,0:T(8,128)(2,1)S(1)} collective-permute-done((bf16[320,640]{1,0:T(8,128)(2,1)S(1)}, bf16[320,640]{1,0:T(8,128)(2,1)S(1)}, u32[]{:S(2)}, u32[]{:S(2)}) %collective-permute-start.22) | collective-permute-done | bytes 409632 | tf_op jit(solution)/shard_map/ppermute | solution.py:404
  188.3 0.7 copy-done.9
  189.0 36.3 %groups.1 = bf16[768,640]{1,0:T(8,128)(2,1)} custom-call(s32[4]{0:T(128)} %pad_add_fusion.1.offset_ref, bf16[1536,1280]{1,0:T(8,128)(2,1)} %windows_out.1.own_ref, bf16[1536,1280]{1,0:T(8,128)(2,1)} %collective-permute-done.17.other_ref, s32[768,1]{1,0:T(8,128)} %broadcast_select_fusion.5.code_ref, s32[1,3072]{1,0:T(1,128)} %bitcast.22, ...), custom_call_target="tpu_custom_call" | custom-call | flops 17364418560 | bytes 12794880 | tf_op jit(solution)/shard_map/groups/pallas_call | solution.py:357
  225.3 1.3 fusion.6
  226.6 1.1 collective-permute-start.23
  227.7 1.5 collective-permute-done.23
  229.2 1.2 maximum_select_fusion
  (63 shorter events, 0.6 us)
Async XLA Ops:
  6.5 13.4 %copy-start = (bf16[1,2,3,128,640]{4,3,2,1,0:T(8,128)(2,1)S(1)}, bf16[1,2,3,128,640]{4,3,2,1,0:T(8,128)(2,1)}, u32[]{:S(2)}) copy-start(bf16[1,2,3,128,640]{4,3,2,1,0:T(8,128)(2,1)} %param.7) | copy-start | bytes 2949124
  6.5 97.9 %all-gather.3.cloned.1.call-start = ((), (), s32[]{:S(2)}) async-start(), calls=%async_computation | async-start | bytes 1843200 | tf_op jit(solution)/shard_map/all_gather | solution.py:390
  8.3 11.2 %copy-start.7 = (s32[1,2,3,64]{3,1,2,0:T(2,128)S(1)}, s32[1,2,3,64]{3,1,2,0:T(2,128)}, u32[]{:S(2)}) copy-start(s32[1,2,3,64]{3,1,2,0:T(2,128)} %param.8) | copy-start | bytes 4612
  8.3 11.2 %copy-start.10 = (s32[1,2,3]{2,1,0:T(2,128)S(1)}, s32[1,2,3]{2,1,0:T(2,128)}, u32[]{:S(2)}) copy-start(s32[1,2,3]{2,1,0:T(2,128)} %param.9) | copy-start | bytes 76
  8.3 121.2 %all-gather.5.cloned.1.call-start = ((), (), s32[]{:S(2)}) async-start(), calls=%async_computation.1 | async-start | bytes 3686400 | tf_op jit(solution)/shard_map/all_gather | solution.py:391
  14.4 21.5 %collective-permute-start.3 = (bf16[160,1920]{1,0:T(8,128)(2,1)}, bf16[160,1920]{1,0:T(8,128)(2,1)S(1)}, u32[]{:S(2)}, u32[]{:S(2)}) collective-permute-start(bf16[160,1920]{1,0:T(8,128)(2,1)} %get-tuple-element.24), channel_id=1, source_target_pairs={{0,8},{8,0},{16,24},{24,16},{1,9},{9,1},{17,25},{25,17},{2,10},{10... | collective-permute-start | bytes 1843208 | tf_op jit(solution)/shard_map/ppermute | solution.py:398
  17.4 21.4 %collective-permute-start.5 = (bf16[160,1920]{1,0:T(8,128)(2,1)}, bf16[160,1920]{1,0:T(8,128)(2,1)S(1)}, u32[]{:S(2)}, u32[]{:S(2)}) collective-permute-start(bf16[160,1920]{1,0:T(8,128)(2,1)} %get-tuple-element.24), channel_id=1, source_target_pairs={{0,16},{8,24},{16,0},{24,8},{1,17},{9,25},{17,1},{25,9},{2,18},{10... | collective-permute-start | bytes 1843208 | tf_op jit(solution)/shard_map/ppermute | solution.py:399
  18.9 32.4 %collective-permute-start.9 = (bf16[160,1920]{1,0:T(8,128)(2,1)}, bf16[160,1920]{1,0:T(8,128)(2,1)}, u32[]{:S(2)}, u32[]{:S(2)}) collective-permute-start(bf16[160,1920]{1,0:T(8,128)(2,1)} %get-tuple-element.29), channel_id=1, source_target_pairs={{0,8},{8,0},{16,24},{24,16},{1,9},{9,1},{17,25},{25,17},{2,10},{10... | collective-permute-start | bytes 1843208 | tf_op jit(solution)/shard_map/ppermute | solution.py:398
  19.4 33.6 %collective-permute-start.11 = (bf16[160,1920]{1,0:T(8,128)(2,1)}, bf16[160,1920]{1,0:T(8,128)(2,1)}, u32[]{:S(2)}, u32[]{:S(2)}) collective-permute-start(bf16[160,1920]{1,0:T(8,128)(2,1)} %get-tuple-element.29), channel_id=1, source_target_pairs={{0,16},{8,24},{16,0},{24,8},{1,17},{9,25},{17,1},{25,9},{2,18},{10... | collective-permute-start | bytes 1843208 | tf_op jit(solution)/shard_map/ppermute | solution.py:399
  25.3 30.0 %collective-permute-start.2 = (bf16[400,640]{1,0:T(8,128)(2,1)}, bf16[400,640]{1,0:T(8,128)(2,1)}, u32[]{:S(2)}, u32[]{:S(2)}) collective-permute-start(bf16[400,640]{1,0:T(8,128)(2,1)} %pad_maximum_fusion.1), channel_id=1, source_target_pairs={{0,3},{1,0},{2,1},{3,2},{4,7},{5,4},{6,5},{7,6},{8,11},{9,8},{10,9... | collective-permute-start | bytes 1536008 | tf_op jit(solution)/shard_map/ppermute | solution.py:456
  36.0 39.3 %copy-start.3 = (bf16[160,1920]{1,0:T(8,128)(2,1)}, bf16[160,1920]{1,0:T(8,128)(2,1)S(1)}, u32[]{:S(2)}) copy-start(bf16[160,1920]{1,0:T(8,128)(2,1)S(1)} %collective-permute-done.3.refs_1_) | copy-start | bytes 1843204
  36.0 36.4 %collective-permute-start.1 = (bf16[400,640]{1,0:T(8,128)(2,1)}, bf16[400,640]{1,0:T(8,128)(2,1)}, u32[]{:S(2)}, u32[]{:S(2)}) collective-permute-start(bf16[400,640]{1,0:T(8,128)(2,1)} %pad_maximum_fusion.1), channel_id=1, source_target_pairs={{0,2},{1,3},{2,0},{3,1},{4,6},{5,7},{6,4},{7,5},{8,10},{9,11},{10,... | collective-permute-start | bytes 1536008 | tf_op jit(solution)/shard_map/ppermute | solution.py:456
  38.7 36.5 %copy-start.4 = (bf16[160,1920]{1,0:T(8,128)(2,1)}, bf16[160,1920]{1,0:T(8,128)(2,1)S(1)}, u32[]{:S(2)}) copy-start(bf16[160,1920]{1,0:T(8,128)(2,1)S(1)} %collective-permute-done.5.refs_3_) | copy-start | bytes 1843204
  38.8 33.6 %collective-permute-start = (bf16[400,640]{1,0:T(8,128)(2,1)}, bf16[400,640]{1,0:T(8,128)(2,1)}, u32[]{:S(2)}, u32[]{:S(2)}) collective-permute-start(bf16[400,640]{1,0:T(8,128)(2,1)} %pad_maximum_fusion.1), channel_id=1, source_target_pairs={{0,1},{1,2},{2,3},{3,0},{4,5},{5,6},{6,7},{7,4},{8,9},{9,10},{10,1... | collective-permute-start | bytes 1536008 | tf_op jit(solution)/shard_map/ppermute | solution.py:456
  51.3 24.0 %collective-permute-start.7 = (bf16[160,1920]{1,0:T(8,128)(2,1)}, bf16[160,1920]{1,0:T(8,128)(2,1)}, u32[]{:S(2)}, u32[]{:S(2)}) collective-permute-start(bf16[160,1920]{1,0:T(8,128)(2,1)} %broadcast_select_fusion.2), channel_id=1, source_target_pairs={{0,8},{4,20},{8,0},{12,28},{16,24},{20,4},{24,16},{28,12},{1,9},{5... | collective-permute-start | bytes 1843208 | tf_op jit(solution)/shard_map/ppermute | solution.py:404
  53.1 45.5 %collective-permute-start.15 = (bf16[320,1280]{1,0:T(8,128)(2,1)}, bf16[320,1280]{1,0:T(8,128)(2,1)S(1)}, u32[]{:S(2)}, u32[]{:S(2)}) collective-permute-start(bf16[320,1280]{1,0:T(8,128)(2,1)} %get-tuple-element.31.refs_0_), channel_id=1, source_target_pairs={{0,8},{8,0},{16,24},{24,16},{1,9},{9,1},{17,25},{25,17},{2,10},{10... | collective-permute-start | bytes 2457608 | tf_op jit(solution)/shard_map/ppermute | solution.py:398
  55.4 22.9 %collective-permute-start.10 = (bf16[160,1920]{1,0:T(8,128)(2,1)}, bf16[160,1920]{1,0:T(8,128)(2,1)}, u32[]{:S(2)}, u32[]{:S(2)}) collective-permute-start(bf16[160,1920]{1,0:T(8,128)(2,1)} %collective-permute-done.9.refs_1_), channel_id=1, source_target_pairs={{0,4},{4,0},{1,5},{5,1},{2,6},{6,2},{3,7},{7,3},{8,12},{12,8},{9,1... | collective-permute-start | bytes 1843208 | tf_op jit(solution)/shard_map/ppermute | solution.py:407
  72.4 6.0 %collective-permute-start.12 = (bf16[160,1920]{1,0:T(8,128)(2,1)}, bf16[160,1920]{1,0:T(8,128)(2,1)}, u32[]{:S(2)}, u32[]{:S(2)}) collective-permute-start(bf16[160,1920]{1,0:T(8,128)(2,1)} %collective-permute-done.11.refs_3_), channel_id=1, source_target_pairs={{0,4},{4,0},{1,5},{5,1},{2,6},{6,2},{3,7},{7,3},{8,12},{12,8},{9,1... | collective-permute-start | bytes 1843208 | tf_op jit(solution)/shard_map/ppermute | solution.py:407
  72.4 26.2 %collective-permute-start.13 = (bf16[160,1920]{1,0:T(8,128)(2,1)}, bf16[160,1920]{1,0:T(8,128)(2,1)}, u32[]{:S(2)}, u32[]{:S(2)}) collective-permute-start(bf16[160,1920]{1,0:T(8,128)(2,1)} %broadcast_select_fusion.1), channel_id=1, source_target_pairs={{0,8},{4,20},{8,0},{12,28},{16,24},{20,4},{24,16},{28,12},{1,9},{5... | collective-permute-start | bytes 1843208 | tf_op jit(solution)/shard_map/ppermute | solution.py:404
  75.3 29.1 %collective-permute-start.16 = (bf16[320,1280]{1,0:T(8,128)(2,1)}, bf16[320,1280]{1,0:T(8,128)(2,1)S(1)}, u32[]{:S(2)}, u32[]{:S(2)}) collective-permute-start(bf16[320,1280]{1,0:T(8,128)(2,1)} %get-tuple-element.31.refs_0_), channel_id=1, source_target_pairs={{0,16},{8,24},{16,0},{24,8},{1,17},{9,25},{17,1},{25,9},{2,18},{10... | collective-permute-start | bytes 2457608 | tf_op jit(solution)/shard_map/ppermute | solution.py:399
  78.3 26.1 %collective-permute-start.4 = (bf16[160,1920]{1,0:T(8,128)(2,1)}, bf16[160,1920]{1,0:T(8,128)(2,1)}, u32[]{:S(2)}, u32[]{:S(2)}) collective-permute-start(bf16[160,1920]{1,0:T(8,128)(2,1)} %copy-done.3), channel_id=1, source_target_pairs={{0,4},{4,0},{1,5},{5,1},{2,6},{6,2},{3,7},{7,3},{8,12},{12,8},{9,1... | collective-permute-start | bytes 1843208 | tf_op jit(solution)/shard_map/ppermute | solution.py:407
  78.4 26.0 %collective-permute-start.6 = (bf16[160,1920]{1,0:T(8,128)(2,1)}, bf16[160,1920]{1,0:T(8,128)(2,1)}, u32[]{:S(2)}, u32[]{:S(2)}) collective-permute-start(bf16[160,1920]{1,0:T(8,128)(2,1)} %copy-done.4), channel_id=1, source_target_pairs={{0,4},{4,0},{1,5},{5,1},{2,6},{6,2},{3,7},{7,3},{8,12},{12,8},{9,1... | collective-permute-start | bytes 1843208 | tf_op jit(solution)/shard_map/ppermute | solution.py:407
  98.6 5.9 %collective-permute-start.8 = (bf16[160,1920]{1,0:T(8,128)(2,1)}, bf16[160,1920]{1,0:T(8,128)(2,1)}, u32[]{:S(2)}, u32[]{:S(2)}) collective-permute-start(bf16[160,1920]{1,0:T(8,128)(2,1)} %collective-permute-done.7.refs_5_), channel_id=1, source_target_pairs={{0,4},{4,0},{1,5},{5,1},{2,6},{6,2},{3,7},{7,3},{8,12},{12,8},{9,1... | collective-permute-start | bytes 1843208 | tf_op jit(solution)/shard_map/ppermute | solution.py:407
  98.6 66.8 %copy-start.1 = (bf16[320,1280]{1,0:T(8,128)(2,1)}, bf16[320,1280]{1,0:T(8,128)(2,1)S(1)}, u32[]{:S(2)}) copy-start(bf16[320,1280]{1,0:T(8,128)(2,1)S(1)} %collective-permute-done.15.refs_1_) | copy-start | bytes 2457604
  98.6 5.8 %collective-permute-start.14 = (bf16[160,1920]{1,0:T(8,128)(2,1)}, bf16[160,1920]{1,0:T(8,128)(2,1)}, u32[]{:S(2)}, u32[]{:S(2)}) collective-permute-start(bf16[160,1920]{1,0:T(8,128)(2,1)} %collective-permute-done.13.refs_5_), channel_id=1, source_target_pairs={{0,4},{4,0},{1,5},{5,1},{2,6},{6,2},{3,7},{7,3},{8,12},{12,8},{9,1... | collective-permute-start | bytes 1843208 | tf_op jit(solution)/shard_map/ppermute | solution.py:407
  104.4 61.0 %copy-start.2 = (bf16[320,1280]{1,0:T(8,128)(2,1)}, bf16[320,1280]{1,0:T(8,128)(2,1)S(1)}, u32[]{:S(2)}) copy-start(bf16[320,1280]{1,0:T(8,128)(2,1)S(1)} %collective-permute-done.16.refs_2_) | copy-start | bytes 2457604
  129.5 33.8 %copy-start.8 = (bf16[320,640]{1,0:T(8,128)(2,1)S(1)}, bf16[320,640]{1,0:T(8,128)(2,1)}, u32[]{:S(2)}) copy-start(bf16[320,640]{1,0:T(8,128)(2,1)} %get-tuple-element.40.refs_4_) | copy-start | bytes 1228804
  155.2 33.1 %collective-permute-start.17 = (bf16[1536,1280]{1,0:T(8,128)(2,1)}, bf16[1536,1280]{1,0:T(8,128)(2,1)}, u32[]{:S(2)}, u32[]{:S(2)}) collective-permute-start(bf16[1536,1280]{1,0:T(8,128)(2,1)} %windows_out.1.own_ref), channel_id=1, source_target_pairs={{0,4},{4,0},{1,5},{5,1},{2,6},{6,2},{3,7},{7,3},{8,12},{12,8},{9,1... | collective-permute-start | bytes 11796488 | tf_op jit(solution)/shard_map/ppermute | solution.py:407
  157.5 5.8 %collective-permute-start.18 = (s32[1536]{0:T(1024)S(1)}, s32[1536]{0:T(1024)S(1)}, u32[]{:S(2)}, u32[]{:S(2)}) collective-permute-start(s32[1536]{0:T(1024)S(1)} %maximum_convert_fusion), channel_id=1, source_target_pairs={{0,4},{4,0},{1,5},{5,1},{2,6},{6,2},{3,7},{7,3},{8,12},{12,8},{9,1... | collective-permute-start | bytes 18440 | tf_op jit(solution)/shard_map/ppermute | solution.py:407
  163.3 11.8 %collective-permute-start.20 = (bf16[320,640]{1,0:T(8,128)(2,1)S(1)}, bf16[320,640]{1,0:T(8,128)(2,1)S(1)}, u32[]{:S(2)}, u32[]{:S(2)}) collective-permute-start(bf16[320,640]{1,0:T(8,128)(2,1)S(1)} %copy-done.8), channel_id=1, source_target_pairs={{0,8},{8,0},{16,24},{24,16},{1,9},{9,1},{17,25},{25,17},{2,10},{10... | collective-permute-start | bytes 1228808 | tf_op jit(solution)/shard_map/ppermute | solution.py:398
  164.9 12.3 %collective-permute-start.21 = (bf16[320,640]{1,0:T(8,128)(2,1)S(1)}, bf16[320,640]{1,0:T(8,128)(2,1)S(1)}, u32[]{:S(2)}, u32[]{:S(2)}) collective-permute-start(bf16[320,640]{1,0:T(8,128)(2,1)S(1)} %copy-done.8), channel_id=1, source_target_pairs={{0,16},{8,24},{16,0},{24,8},{1,17},{9,25},{17,1},{25,9},{2,18},{10... | collective-permute-start | bytes 1228808 | tf_op jit(solution)/shard_map/ppermute | solution.py:399
  166.4 17.6 %collective-permute-start.19 = (bf16[320,1280]{1,0:T(8,128)(2,1)}, bf16[320,1280]{1,0:T(8,128)(2,1)}, u32[]{:S(2)}, u32[]{:S(2)}) collective-permute-start(bf16[320,1280]{1,0:T(8,128)(2,1)} %broadcast_select_fusion), channel_id=1, source_target_pairs={{0,8},{4,20},{8,0},{12,28},{16,24},{20,4},{24,16},{28,12},{1,9},{5... | collective-permute-start | bytes 2457608 | tf_op jit(solution)/shard_map/ppermute | solution.py:404
  175.1 13.2 %copy-start.5 = (bf16[320,640]{1,0:T(8,128)(2,1)}, bf16[320,640]{1,0:T(8,128)(2,1)S(1)}, u32[]{:S(2)}) copy-start(bf16[320,640]{1,0:T(8,128)(2,1)S(1)} %collective-permute-done.20.refs_5_) | copy-start | bytes 1228804
  177.2 11.1 %copy-start.6 = (bf16[320,640]{1,0:T(8,128)(2,1)}, bf16[320,640]{1,0:T(8,128)(2,1)S(1)}, u32[]{:S(2)}) copy-start(bf16[320,640]{1,0:T(8,128)(2,1)S(1)} %collective-permute-done.21.refs_6_) | copy-start | bytes 1228804
  177.2 11.0 %collective-permute-start.22 = (bf16[320,640]{1,0:T(8,128)(2,1)S(1)}, bf16[320,640]{1,0:T(8,128)(2,1)S(1)}, u32[]{:S(2)}, u32[]{:S(2)}) collective-permute-start(bf16[320,640]{1,0:T(8,128)(2,1)S(1)} %broadcast_select_fusion.4), channel_id=1, source_target_pairs={{0,8},{4,20},{8,0},{12,28},{16,24},{20,4},{24,16},{28,12},{1,9},{5... | collective-permute-start | bytes 1228808 | tf_op jit(solution)/shard_map/ppermute | solution.py:404
  188.3 0.8 copy-start.9
  226.6 2.6 %collective-permute-start.23 = (bf16[384,640]{1,0:T(8,128)(2,1)S(1)}, bf16[384,640]{1,0:T(8,128)(2,1)S(1)}, u32[]{:S(2)}, u32[]{:S(2)}) collective-permute-start(bf16[384,640]{1,0:T(8,128)(2,1)S(1)} %get-tuple-element.42), channel_id=1, source_target_pairs={{0,4},{4,0},{1,5},{5,1},{2,6},{6,2},{3,7},{7,3},{8,12},{12,8},{9,1... | collective-permute-start | bytes 1474568 | tf_op jit(solution)/shard_map/ppermute | solution.py:407
Sparse Core Ops, SparseCore 0:
  9.2 35.4 all-gather.2
  46.6 42.8 all-gather.4

commit v4 on v3

--- a/solution.py
+++ b/solution.py
@@ -136,10 +136,12 @@
     return pl.BlockSpec(array.shape, lambda *_: zeros)
 
 
-def assemble(offset_ref, piece_refs, weight_ref):
-    for at, piece in enumerate(piece_refs):
-        start = pl.multiple_of(offset_ref[at], 16)
-        weight_ref[pl.ds(start, piece.shape[0]), :] = piece[...]
+def parts_of(pieces, high):
+    return [piece.at[pl.ds(at, high)] for piece in pieces for at in range(0, piece.shape[0], high)]
+
+
+def first_row(offset_ref, at, unit):
+    return pl.multiple_of(offset_ref[at], unit)
 
 
 def reorder(source, start, target, at):
@@ -149,15 +151,57 @@
         target[:, pl.ds(at + GROUP * MAIN + head * TAIL, TAIL)] = source[:, pl.ds(first + MAIN, TAIL)]
 
 
-def prepare_local_kernel(core_ref, weight_ref, *refs):
-    groups = len(refs) // 2
+def pick_kernel(count_ref, patch_ref, index_ref, sent_ref):
+    windows, window_tokens, _ = patch_ref.shape
+    kept_most = index_ref.shape[1]
+    rows = windows * kept_most
+    offsets = lax.broadcasted_iota(jnp.int32, (window_tokens, kept_most), 0)
+    places = lax.broadcasted_iota(jnp.int32, (1, kept_most), 1)
+    sent_ref[0, pl.ds(rows, sent_ref.shape[1] - rows), :] = jnp.zeros(
+        (sent_ref.shape[1] - rows, sent_ref.shape[2]), jnp.bfloat16
+    )
+    codes = []
+    for window in range(windows):
+        index = index_ref[pl.ds(window, 1), :]
+        chosen = (offsets == index).astype(jnp.float32).astype(jnp.bfloat16)
+        picked = lax.dot_general(
+            chosen, patch_ref[window], (((0,), (0,)), ((), ())), preferred_element_type=jnp.float32
+        )
+        sent_ref[0, pl.ds(window * kept_most, kept_most), :] = picked.astype(jnp.bfloat16)
+        codes.append(jnp.where(places < count_ref[window], index, -1))
+    codes = jnp.concatenate(codes, axis=0).astype(jnp.float32).astype(jnp.bfloat16)
+    sent_ref[0, pl.ds(rows, windows), pl.ds(0, kept_most)] = codes
+    for copy in range(1, sent_ref.shape[0]):
+        sent_ref[copy] = sent_ref[0]
+
+
+def pack_columns(group, weight_ref, full_ref):
     inner = weight_ref.shape[1] // 3
-    for group in range(groups):
-        full, half = refs[group], refs[groups + group]
-        for which in range(3):
-            reorder(weight_ref, which * inner + group * WIDE, full, which * WIDE)
-        high = half.shape[0]
-        half[...] = full[pl.ds(pl.multiple_of(core_ref[0] * high, 16), high), :]
+    for which in range(3):
+        reorder(weight_ref, which * inner + group * WIDE, full_ref, which * WIDE)
+
+
+def own_half(core_ref, full_ref, half_ref):
+    half = half_ref.shape[0]
+    half_ref[...] = full_ref[pl.ds(pl.multiple_of(core_ref[0] * half, 16), half), :]
+
+
+def pack_first_kernel(core_ref, weight_ref, embed_ref, full_ref, half_ref):
+    pack_columns(0, weight_ref, full_ref)
+    quarter = half_ref.shape[0] // 2
+    wide = embed_ref.shape[1] // 2
+    for at in range(4):
+        core, side = at // 2, at % 2
+        full_ref[pl.ds(at * quarter, quarter), pl.ds(3 * WIDE, wide)] = embed_ref[
+            pl.ds(core * quarter, quarter), pl.ds(side * wide, wide)
+        ]
+    own_half(core_ref, full_ref, half_ref)
+
+
+def pack_second_kernel(core_ref, weight_ref, out_ref, full_ref, half_ref):
+    pack_columns(1, weight_ref, full_ref)
+    full_ref[:, pl.ds(3 * WIDE, out_ref.shape[1])] = out_ref[...]
+    own_half(core_ref, full_ref, half_ref)
 
 
 def prepare_global_kernel(core_ref, query_ref, key_ref, value_ref, first_ref, second_ref):
@@ -224,14 +268,23 @@
     offset_ref,
     picked_ref,
     code_ref,
-    embed_ref,
     *refs,
 ):
-    *pieces, embedded_ref, normed_ref, mix_ref, weight_ref, proj_ref = refs
+    *pieces, embedded_ref, normed_ref, mix_ref, weight_ref, embed_ref, proj_ref = refs
 
     @pl.when(pl.program_id(0) == 0)
     def _():
-        assemble(offset_ref, pieces, weight_ref)
+        high = pieces[0].shape[0] // 2
+        quarter = high // 2
+        wide = embed_ref.shape[1] // 2
+        for at, part in enumerate(parts_of(pieces, high)):
+            start = first_row(offset_ref, 3 * at, 32)
+            weight_ref[pl.ds(start, high), :] = part[:, pl.ds(0, 3 * WIDE)]
+            start = pl.multiple_of(start // 2, 16)
+            for side in range(2):
+                embed_ref[pl.ds(start, quarter), pl.ds(side * wide, wide)] = part[
+                    pl.ds(side * quarter, quarter), pl.ds(3 * WIDE, wide)
+                ]
 
     embedded = fold_product(picked_ref[...], embed_ref[...]).astype(jnp.bfloat16)
     embedded_ref[...] = embedded
@@ -249,22 +302,21 @@
     normed_ref,
     mix_ref,
     code_ref,
-    out_ref,
     *refs,
 ):
     *pieces, result_ref, weight_ref, proj_ref, own_mix_ref, row_ref = refs
-    inner = out_ref.shape[0]
 
     @pl.when(pl.program_id(0) == 0)
     def _():
-        assemble(offset_ref, pieces, weight_ref)
-        for start in range(0, inner, WIDE):
-            for head in range(GROUP):
-                first = start + head * HD
-                row_ref[pl.ds(start + head * MAIN, MAIN), :] = out_ref[pl.ds(first, MAIN), :]
-                row_ref[pl.ds(start + GROUP * MAIN + head * TAIL, TAIL), :] = out_ref[
-                    pl.ds(first + MAIN, TAIL), :
-                ]
+        wide = row_ref.shape[1]
+        for at, part in enumerate(parts_of(pieces, HD)):
+            weight_ref[pl.ds(first_row(offset_ref, 3 * at, 32), HD), :] = part[:, pl.ds(0, 3 * WIDE)]
+            row_ref[pl.ds(first_row(offset_ref, 3 * at + 1, 32), MAIN), :] = part[
+                pl.ds(0, MAIN), pl.ds(3 * WIDE, wide)
+            ]
+            row_ref[pl.ds(first_row(offset_ref, 3 * at + 2, 32), TAIL), :] = part[
+                pl.ds(MAIN, TAIL), pl.ds(3 * WIDE, wide)
+            ]
 
     proj_ref[...] = fold_product(normed_ref[...], weight_ref[...]).astype(jnp.bfloat16)
     mix_heads(proj_ref, code_ref, own_mix_ref, at_once, kept_most)
@@ -277,7 +329,6 @@
 
 def group_kernel(
     steps,
-    rows,
     key_chunk,
     offset_ref,
     own_ref,
@@ -293,8 +344,9 @@
 
     @pl.when(step == 0)
     def _():
-        assemble(offset_ref, pieces[:4], first_ref)
-        assemble(offset_ref, pieces[4:], second_ref)
+        for target, parts in ((first_ref, pieces[:4]), (second_ref, pieces[4:])):
+            for at, part in enumerate(parts):
+                target[pl.ds(first_row(offset_ref, at, 32), part.shape[0]), :] = part[...]
 
     def project(source_ref, at):
         normed = source_ref[...]
@@ -302,10 +354,10 @@
         key_ref[part, :] = fold_product(normed, first_ref[:, pl.ds(0, WIDE)]).astype(jnp.bfloat16)
         value_ref[part, :] = fold_product(normed, second_ref[...]).astype(jnp.bfloat16)
 
-        @pl.when(step == at * steps)
+        @pl.when(step == at * steps + offset_ref[4])
         def _():
-            query_ref[pl.ds(at * rows, rows), :] = fold_product(
-                source_ref[pl.ds(0, rows), :], first_ref[:, pl.ds(WIDE, WIDE)]
+            query_ref[pl.ds(at * block, block), :] = fold_product(
+                normed, first_ref[:, pl.ds(WIDE, WIDE)]
             ).astype(jnp.bfloat16)
 
     @pl.when(step < steps)
@@ -381,14 +433,11 @@
     batch_size = lax.axis_size("batch")
     core = lax.axis_index("lat")
     chip = lax.axis_index("batch")
+    place = lax.axis_index("lon")
     core_scalar = core.reshape(1).astype(jnp.int32)
 
-    def own_rows(shard):
-        part = shard.shape[0] // 2
-        return lax.dynamic_slice_in_dim(shard, core * part, part, axis=0)
-
-    whole_embed = lax.all_gather(own_rows(embed_weight), ("batch", "lat"), axis=0, tiled=True)
-    whole_out = lax.all_gather(own_rows(local_out), ("batch", "lat"), axis=0, tiled=True)
+    def other_core(value):
+        return lax.ppermute(value, "lat", swap_perm(2, 1))
 
     diagonal = []
     for b in range(batch_size):
@@ -403,28 +452,58 @@
         forwarded = jnp.where(core == 0, along_y, along_x)
         return lax.ppermute(forwarded, ("batch", "lat"), diagonal)
 
-    def other_core(value):
-        return lax.ppermute(value, "lat", swap_perm(2, 1))
-
     high = local_qkv.shape[0]
     half = high // 2
-    *local_full, half_first, half_second = run(
-        prepare_local_kernel,
+    first_wide = 3 * WIDE + width // 2
+    second_wide = 3 * WIDE + width
+
+    def pack(kernel, scalar, other, wide, name):
+        shapes = [(high, wide), (half, wide)]
+        return run(
+            kernel,
+            1,
+            scalar,
+            [whole_block(local_qkv), whole_block(other)],
+            [local_qkv, other],
+            shapes,
+            [pl.BlockSpec(shape, lambda *_: (0, 0)) for shape in shapes],
+            [],
+            0,
+            name,
+        )
+
+    local_first, half_first = pack(
+        pack_first_kernel, core_scalar, embed_weight, first_wide, "pack_first"
+    )
+
+    code_tile = -(-windows // 16) * 16
+    sent_shape = (lon_size, rows + code_tile, pin)
+    patch_rows = patches.reshape(windows, window_tokens, pin)
+    index_rows = kept_index.reshape(windows, kept_most)
+    (sent,) = run(
+        pick_kernel,
         1,
-        core_scalar,
-        [whole_block(local_qkv)],
-        [local_qkv],
-        [(high, 3 * WIDE)] * 2 + [(half, 3 * WIDE)] * 2,
-        [pl.BlockSpec((h, 3 * WIDE), lambda *_: (0, 0)) for h in (high, high, half, half)],
+        after(kept_count.reshape(windows), half_first),
+        [whole_block(patch_rows), whole_block(index_rows)],
+        [patch_rows, index_rows],
+        [sent_shape],
+        [pl.BlockSpec(sent_shape, lambda *_: (0, 0, 0))],
         [],
         0,
-        "order_local",
-    )
-    local_sides = [sides(half_first), sides(half_second)]
+        "pick",
+    )
+    got = lax.all_to_all(sent, "lon", 0, 0, tiled=True)
+    all_rows = lon_size * rows
+    own_codes = got[:, rows : rows + windows, :kept_most].reshape(-1).astype(jnp.int32)
+    other_codes = other_core(own_codes)
+
+    local_second, half_second = pack(
+        pack_second_kernel, after(core_scalar, sent), local_out, second_wide, "pack_second"
+    )
     global_first, global_second = run(
         prepare_global_kernel,
         1,
-        core_scalar,
+        after(core_scalar, half_second),
         [
             pl.BlockSpec((high, WIDE), lambda i, c, which=which: (0, 2 * which + c[0]))
             for which in range(3)
@@ -436,45 +515,29 @@
         0,
         "order_global",
     )
-
-    index_rows = kept_index.reshape(windows, kept_most)
-    kept_mask = lax.broadcasted_iota(jnp.int32, (windows, kept_most), 1) < kept_count.reshape(
-        windows, 1
-    )
-    codes = jnp.where(kept_mask, index_rows, -1).reshape(rows)
-    picked = jnp.take_along_axis(
-        patches.reshape(windows, window_tokens, pin), index_rows[:, :, None], axis=1
-    ).reshape(rows, pin)
-
-    code_rows = -(-rows // pin)
-    code_tile = -(-code_rows // 16) * 16
-    code_part = jnp.pad(codes, (0, code_tile * pin - rows)).reshape(code_tile, pin)
-    sent = jnp.concatenate([picked, code_part.astype(jnp.bfloat16)], axis=0)
-    picked_parts = [sent]
-    for shift in range(1, lon_size):
-        picked_parts.append(
-            lax.ppermute(sent, "lon", [(i, (i + shift) % lon_size) for i in range(lon_size)])
-        )
-    picked_all = jnp.concatenate([part[:rows] for part in picked_parts], axis=0)
-    all_rows = picked_all.shape[0]
-    own_codes = jnp.concatenate(
-        [part[rows : rows + code_rows].reshape(-1)[:rows] for part in picked_parts]
-    ).astype(jnp.int32)
-    other_codes = other_core(own_codes)
-
-    local_across = [across(*s) for s in local_sides]
-    first_sides = sides(after(global_first, local_sides[0]))
-
-    def shared(shard, got):
-        pieces, offsets = [shard], [chip * high]
-        for which, value in zip((1, 2, 3), got):
-            pieces += [value, other_core(value)]
-            base = (chip ^ which) * high
-            offsets += [base + core * half, base + (1 - core) * half]
-        return pieces, jnp.stack(offsets).astype(jnp.int32)
-
-    block = all_rows // 3 if all_rows % (3 * 4 * kept_most) == 0 else all_rows
-    steps = all_rows // block
+    sides_first = sides(half_first)
+    half_second, _ = after((half_second, global_first), sides_first)
+    sides_second = sides(half_second)
+    across_first = across(*sides_first)
+    global_sides = sides(after(global_first, sides_second))
+    across_second = across(*sides_second)
+
+    def shared(shard, got, earlier):
+        joined = jnp.concatenate(got[:2], axis=0)
+        pieces = [shard, joined, other_core(joined), got[2], other_core(after(got[2], earlier))]
+        bases = [(chip ^ which) * high for which in (1, 2, 3)]
+        firsts = [chip * high, chip * high + half]
+        for group in (bases[:2], bases[2:]):
+            firsts += [base + core * half for base in group]
+            firsts += [base + (1 - core) * half for base in group]
+        firsts = jnp.stack(firsts).astype(jnp.int32)
+        head = firsts // HD
+        group_start = head // GROUP * WIDE
+        main = group_start + head % GROUP * MAIN
+        tail = group_start + GROUP * MAIN + head % GROUP * TAIL
+        return pieces, jnp.stack([firsts, main, tail], axis=1).reshape(-1)
+
+    block, steps = rows, lon_size
     at_once = 2 * kept_most if block % (2 * kept_most) == 0 else kept_most
     window_codes = jnp.where(
         own_codes >= 0,
@@ -483,59 +546,61 @@
     ).reshape(steps, 1, block)
     code_spec = pl.BlockSpec((1, 1, block), lambda i, _: (i, 0, 0))
     row_spec = lambda wide: pl.BlockSpec((block, wide), lambda i, _: (i, 0))
-
-    pieces, offsets = shared(local_full[0], [*local_sides[0], local_across[0]])
+    at_home = lambda a: lax.dynamic_slice_in_dim(a, place * rows, rows, axis=0)
+    key_codes = jnp.concatenate([own_codes, other_codes]).reshape(1, 2 * all_rows)
+    query_codes = jnp.concatenate([at_home(own_codes), at_home(other_codes)]).reshape(2 * rows, 1)
+    query_codes = jnp.where(query_codes >= 0, query_codes, -2)
+    global_starts = [(chip ^ which) * high for which in range(4)]
+    global_offsets = jnp.stack([*global_starts, place]).astype(jnp.int32)
+
+    pieces, offsets = shared(local_first, [*sides_first, across_first], core_scalar)
+    window_codes, _ = after((window_codes, 0), (key_codes, query_codes, global_offsets))
     embedded, normed, first_mix = run(
         functools.partial(embed_window_kernel, at_once, kept_most),
         steps,
         offsets,
-        [row_spec(pin), code_spec, whole_block(whole_embed), *map(whole_block, pieces)],
-        [picked_all, window_codes, whole_embed, *pieces],
+        [
+            pl.BlockSpec((None, rows, pin), lambda i, _: (i, 0, 0)),
+            code_spec,
+            *map(whole_block, pieces),
+        ],
+        [got, window_codes, *pieces],
         [(all_rows, width), (all_rows, width), (all_rows, WIDE)],
         [row_spec(width), row_spec(width), row_spec(WIDE)],
-        [(width, 3 * WIDE), (block, 3 * WIDE)],
+        [(width, 3 * WIDE), (pin, width), (block, 3 * WIDE)],
         2 * all_rows * (pin * width + width * 3 * WIDE),
         "embed_windows",
     )
 
-    pieces, offsets = shared(local_full[1], [*local_sides[1], local_across[1]])
-    pieces = after(pieces, first_sides)
-    first_across = across(*first_sides)
-    second_sides = sides(after(global_second, first_sides))
+    pieces, offsets = shared(local_second, [*sides_second, across_second], first_mix)
+    global_sides, _ = after((global_sides, 0), first_mix)
+    global_across = across(*global_sides)
+    value_sides = sides(after(global_second, global_sides))
     (normed_own,) = run(
         functools.partial(window_out_kernel, at_once, kept_most),
         steps,
         offsets,
-        [
-            row_spec(width),
-            row_spec(width),
-            row_spec(WIDE),
-            code_spec,
-            whole_block(whole_out),
-            *map(whole_block, pieces),
-        ],
-        [embedded, normed, first_mix, window_codes, whole_out, *pieces],
+        [row_spec(width), row_spec(width), row_spec(WIDE), code_spec, *map(whole_block, pieces)],
+        [embedded, normed, first_mix, window_codes, *pieces],
         [(all_rows, width)],
         [row_spec(width)],
         [(width, 3 * WIDE), (block, 3 * WIDE), (block, WIDE), (inner, width)],
         2 * all_rows * (inner * width + width * 3 * WIDE),
         "windows_out",
     )
+    normed_own = after(normed_own, (global_across, value_sides))
     normed_other = other_core(normed_own)
-    second_across = across(*second_sides)
-
-    key_codes = jnp.concatenate([own_codes, other_codes]).reshape(1, 2 * all_rows)
-    query_codes = jnp.concatenate([own_codes[:rows], other_codes[:rows]]).reshape(2 * rows, 1)
-    query_codes = jnp.where(query_codes >= 0, query_codes, -2)
+    value_across = across(*value_sides)
+
     query_block = 256 if (2 * rows) % 256 == 0 else 2 * rows
     query_steps = 2 * rows // query_block
-    pieces = [global_first, *first_sides, first_across, global_second, *second_sides, second_across]
-    offsets = jnp.stack([(chip ^ which) * high for which in range(4)]).astype(jnp.int32)
+    pieces = [global_first, *global_sides, global_across, global_second, *value_sides, value_across]
+    key_chunk = 512 if (2 * all_rows) % 512 == 0 else block
     late = lambda i: jnp.clip(i - 2 * steps, 0, query_steps - 1)
     (mixed,) = run(
-        functools.partial(group_kernel, steps, rows, block),
+        functools.partial(group_kernel, steps, key_chunk),
         2 * steps + query_steps,
-        offsets,
+        global_offsets,
         [
             pl.BlockSpec((block, width), lambda i, _: (jnp.minimum(i, steps - 1), 0)),
             pl.BlockSpec((block, width), lambda i, _: (jnp.clip(i - steps, 0, steps - 1), 0)),
@@ -566,13 +631,16 @@
     return result.reshape(1, lat_windows, lon_windows, kept_most, inner)
 
 
-def body(patches, kept_index, *weights):
-    rows = patches.shape[1] * patches.shape[2] * kept_index.shape[3]
+def body(patches, kept_index, kept_count, embed_weight, local_qkv, local_out, global_qkv):
+    args = (patches, kept_index, kept_count, embed_weight, local_qkv, local_out, global_qkv)
+    windows = patches.shape[1] * patches.shape[2]
+    rows = windows * kept_index.shape[3]
     sample_rows = rows * lax.axis_size("lat") * lax.axis_size("lon")
-    fits = patches.shape[3] <= 256 and sample_rows * HEADS * HD * 2 <= vmem_limit // 4
-    if lax.axis_size("batch") == 4 and lax.axis_size("lat") == HEADS // GROUP == 2 and fits:
-        return sample_body(patches, kept_index, *weights)
-    return owner_body(patches, kept_index, *weights)
+    fits = patches.shape[3] <= 256 and windows <= 16 and sample_rows * HEADS * HD * 2 <= vmem_limit // 4
+    shards = embed_weight.shape[0] * 2 == local_qkv.shape[0] == local_out.shape[0] == 2 * HD
+    if lax.axis_size("batch") == 4 and lax.axis_size("lat") == HEADS // GROUP == 2 and fits and shards:
+        return sample_body(*args)
+    return owner_body(*args)
 
 
 def solution(mesh):

time: 238 us -> 180 us (0.76)
  waiting for transfers between devices: 76.9 us -> 37.4 us
  between operations: 13.6 us -> 0.21 us
  Pallas kernels: 94.1 us -> 102 us
  local copies, waits for them, and re-layouts: 16.8 us -> 10.5 us
  starting transfers between devices: 25.3 us -> 20.1 us
    ppermute x4, waiting for transfers between devices: 22 us -> 1.58 us  [sides(): along_x = lax.ppermute(part, 'batch', swap_perm(batch_size, 1))]
    ppermute x3 -> x0, waiting for transfers between devices: 17 us -> none  [sample_body(): lax.ppermute(sent, 'lon', [(i, (i + shift) % lon_size) for i in range(lon...]
    pallas_call x5 -> x7, Pallas kernels: 94.1 us -> 102 us  [run(): pl.pallas_call(kernel, grid_spec=pltpu.PrefetchScalarGridSpec(num_scalar_...]
    ppermute x3 -> x0, starting transfers between devices: 8.3 us -> none  [sample_body(): lax.ppermute(sent, 'lon', [(i, (i + shift) % lon_size) for i in range(lon...]
    slice x9 -> x0, local copies, waits for them, and re-layouts: 5.37 us -> none  [the longest x3 3.22 us: sample_body(): picked_all = jnp.concatenate([part[:rows] for part in picked_parts], axis=0)]
    all_to_all x0 -> x1, starting transfers between devices: none -> 4.87 us  [sample_body(): got = lax.all_to_all(sent, 'lon', 0, 0, tiled=True)]
    gather x2 -> x0, local copies, waits for them, and re-layouts: 4.39 us -> none  [sample_body(): jnp.take_along_axis(patches.reshape(windows, window_tokens, pin), index_r...]
    ppermute x9 -> x7, waiting for transfers between devices: 7.2 us -> 2.95 us  [other_core(): return lax.ppermute(value, 'lat', swap_perm(2, 1))]
  transfers between devices with their start and end apart: 26 -> 20, of which waited for: 11 -> 7; matrix products, arithmetic and copies ran while one was open for 9% -> 7% of each run, Pallas kernels for 14% -> 35%
where the time goes in v4:
time: 180 us; the launch traced here: 179 us
  Pallas kernels  102 us (57%)
  waiting for transfers between devices  37.4 us (21%)
  starting transfers between devices  20.1 us (11%)
  local copies, waits for them, and re-layouts  10.5 us (6%)
  other arithmetic  8.53 us (5%)
    pallas_call x7, Pallas kernels, run(): pl.pallas_call(kernel, grid_spec=pltpu.PrefetchScalarGridSpec(num_scalar_...  102 us
    ppermute x4, waiting for transfers between devices, across(): return lax.ppermute(forwarded, ('batch', 'lat'), diagonal)  31.8 us
    ppermute x4, starting transfers between devices, sides(): along_x = lax.ppermute(part, 'batch', swap_perm(batch_size, 1))  5.29 us
    ppermute x4, starting transfers between devices, sides(): along_y = lax.ppermute(part, 'batch', swap_perm(batch_size, 2))  5.29 us
    all_to_all x1, starting transfers between devices, sample_body(): got = lax.all_to_all(sent, 'lon', 0, 0, tiled=True)  4.87 us
    ppermute x4, starting transfers between devices, across(): return lax.ppermute(forwarded, ('batch', 'lat'), diagonal)  3.96 us
    select_n x4, other arithmetic, across(): forwarded = jnp.where(core == 0, along_y, along_x)  3.87 us
    unnamed x22, local copies, waits for them, and re-layouts  3.62 us
  transfers between devices with their start and end apart: 20, of which 7 were waited for; matrix products, arithmetic and copies ran while one was open for 7% of the time, Pallas kernels for 35%

profile of v4, /device:TPU:0, one launch (start us, length us, event | category | flops | bytes accessed | tf_op | source)
XLA Modules:
  0.0 179.1 jit_solution(8733864111278493855)
XLA Ops:
  0.0 3.8 %pack_first.1 = (bf16[320,2560]{1,0:T(8,128)(2,1)}, bf16[160,2560]{1,0:T(8,128)(2,1)}) custom-call(s32[1]{0:T(128)} %bitcast.21.core_ref, bf16[320,3840]{1,0:T(8,128)(2,1)} %weight_ref.3, bf16[160,1280]{1,0:T(8,128)(2,1)} %embed_ref.1), custom_call_target="tpu_custom_call" | custom-call | bytes 2867200 | tf_op jit(solution)/shard_map/pack_first/pallas_call | solution.py:409
  3.8 3.0 %collective-permute-start.2 = (bf16[160,2560]{1,0:T(8,128)(2,1)}, bf16[160,2560]{1,0:T(8,128)(2,1)S(1)}, u32[]{:S(2)}, u32[]{:S(2)}) collective-permute-start(bf16[160,2560]{1,0:T(8,128)(2,1)} %get-tuple-element.26), channel_id=1, source_target_pairs={{0,16},{8,24},{16,0},{24,8},{1,17},{9,25},{17,1},{25,9},{2,18},{10... | collective-permute-start | bytes 2457608 | tf_op jit(solution)/shard_map/ppermute | solution.py:448
  6.8 1.5 collective-permute-start.1
  8.3 0.6 reshape.825.count_ref
  8.9 0.6 reshape.828.index_ref
  9.5 3.5 %pick.1 = bf16[4,400,640]{2,1,0:T(8,128)(2,1)} custom-call(s32[6]{0:T(128)} %reshape.825.count_ref, bf16[6,128,640]{2,1,0:T(8,128)(2,1)} %bitcast.27, s32[6,64]{1,0:T(8,128)} %reshape.828.index_ref), custom_call_target="tpu_custom_call" | custom-call | bytes 984576 | tf_op jit(solution)/shard_map/pick/pallas_call | solution.py:409
  13.0 4.9 %all-to-all-start = ((bf16[4,400,640]{2,1,0:T(8,128)(2,1)}), bf16[4,400,640]{2,1,0:T(8,128)(2,1)}, u32[]{:S(2)}, u32[]{:S(2)}) async-start(bf16[4,400,640]{2,1,0:T(8,128)(2,1)} %pick.1), calls=%async_computation | async-start | bytes 4096000 | tf_op jit(solution)/shard_map/all_to_all | solution.py:495
  17.9 4.2 %pack_second.1 = (bf16[320,3200]{1,0:T(8,128)(2,1)}, bf16[160,3200]{1,0:T(8,128)(2,1)}) custom-call(s32[1]{0:T(128)} %bitcast.21.core_ref, bf16[320,3840]{1,0:T(8,128)(2,1)} %weight_ref.3, bf16[320,1280]{1,0:T(8,128)(2,1)} %out_ref.1), custom_call_target="tpu_custom_call" | custom-call | bytes 3276800 | tf_op jit(solution)/shard_map/pack_second/pallas_call | solution.py:409
  22.1 2.8 %order_global.1 = (bf16[320,1280]{1,0:T(8,128)(2,1)}, bf16[320,640]{1,0:T(8,128)(2,1)}) custom-call(s32[1]{0:T(128)} %bitcast.21.core_ref, bf16[320,3840]{1,0:T(8,128)(2,1)} %value_ref.1, bf16[320,3840]{1,0:T(8,128)(2,1)} %value_ref.1, bf16[320,3840]{1,0:T(8,128)(2,1)} %value_ref.1), custom_call_target="tpu_custom_call" | custom-call | bytes 7372800 | tf_op jit(solution)/shard_map/order_global/pallas_call | solution.py:409
  24.9 0.1 stack.105
  25.0 0.1 stack.95
  25.1 0.1 collective-permute-done.2
  25.2 1.6 collective-permute-done.1
  26.8 0.3 collective-permute-start.7
  27.1 1.7 collective-permute-start.6
  28.8 2.5 %broadcast_select_fusion.2 = (bf16[160,2560]{1,0:T(8,128)(2,1)}, bf16[320,2560]{1,0:T(8,128)(2,1)}) fusion(bf16[160,2560]{1,0:T(8,128)(2,1)S(1)} %collective-permute-done.2, bf16[160,2560]{1,0:T(8,128)(2,1)} %collective-permute-done.1, pred[]{:T(512)S(6)} %eq.14), kind=kLoop, calls=%fused_computation.3 | loop fusion | flops 409599 | bytes 3276801 | tf_op jit(solution)/shard_map/jit(_where)/select_n | solution.py:452
  31.4 0.3 collective-permute-start.4
  31.7 0.1 copy.21
  31.8 0.6 reshape.824.offset_ref
  32.4 0.7 stack.87.offset_ref
  33.1 1.0 constant_dynamic-update-slice_fusion.2.refs_1_
  34.1 25.3 %collective-permute-done.4.refs_3_ = bf16[160,2560]{1,0:T(8,128)(2,1)} collective-permute-done((bf16[160,2560]{1,0:T(8,128)(2,1)}, bf16[160,2560]{1,0:T(8,128)(2,1)}, u32[]{:S(2)}, u32[]{:S(2)}) %collective-permute-start.4) | collective-permute-done | bytes 819232 | tf_op jit(solution)/shard_map/ppermute | solution.py:453
  59.4 0.0 collective-permute-start.5
  59.4 0.0 collective-permute-done.7
  59.4 0.0 collective-permute-done.6
  59.4 1.2 broadcast_select_fusion
  60.6 1.1 constant_dynamic-update-slice_fusion.4.refs_1_
  61.7 0.5 collective-permute-start.8
  62.2 1.5 collective-permute-start.9
  63.7 0.9 all-to-all-done.picked_ref
  64.6 0.7 broadcast_compare_fusion
  65.3 0.1 ge.38
  65.4 0.7 slice_convert_fusion
  66.1 0.6 fusion.code_ref
  66.7 0.1 reshape.830
  66.8 0.0 collective-permute-start
  66.8 0.1 dynamic_slice.6
  66.9 1.1 collective-permute-done
  68.0 0.5 collective-permute-start.11
  68.5 0.1 dynamic_slice.7
  68.6 0.2 copy.25
  68.8 0.2 copy.24
  69.0 0.8 broadcast_select_fusion.4.code_ref
  69.9 0.6 pad_add_fusion
  70.5 0.0 collective-permute-done.3.refs_2_
  70.5 0.5 collective-permute-start.12
  71.0 25.8 %embed_windows.1 = (bf16[1536,1280]{1,0:T(8,128)(2,1)}, bf16[1536,1280]{1,0:T(8,128)(2,1)}, bf16[1536,640]{1,0:T(8,128)(2,1)}) custom-call(s32[24]{0:T(128)} %reshape.824.offset_ref, bf16[4,400,640]{2,1,0:T(8,128)(2,1)} %all-to-all-done.picked_ref, s32[4,1,384]{2,1,0:T(1,128)} %fusion.code_ref, bf16[320,2560]{1,0:T(8,128)(2,1)} %get-tuple-element.29.refs_0_, ...), custom_call_target="tpu_custom_call" | custom-call | flops 10066329600 | bytes 8607744 | tf_op jit(solution)/shard_map/embed_windows/pallas_call | solution.py:409
  96.8 0.1 collective-permute-start.10
  96.9 1.6 collective-permute-start.14
  98.4 1.5 collective-permute-start.15
  100.0 0.1 broadcast_select_fusion.1
  100.1 0.6 collective-permute-start.13
  100.7 1.0 copy-done.6
  101.6 25.7 %windows_out.1.own_ref = bf16[1536,1280]{1,0:T(8,128)(2,1)} custom-call(s32[24]{0:T(128)} %reshape.824.offset_ref, bf16[1536,1280]{1,0:T(8,128)(2,1)} %get-tuple-element.31.embedded_ref, bf16[1536,1280]{1,0:T(8,128)(2,1)} %get-tuple-element.32.normed_ref, bf16[1536,640]{1,0:T(8,128)(2,1)} %get-tuple-element.33.mix_ref, s32[4,1,384]{2,1,0:T(1,128)} %fusion.code_ref, ...), custom_call_target="tpu_custom_call" | custom-call | flops 12582912000 | bytes 18028544 | tf_op jit(solution)/shard_map/windows_out/pallas_call | solution.py:409
  127.3 0.1 collective-permute-start.16
  127.5 1.6 collective-permute-start.17
  129.0 6.5 %collective-permute-done.17.refs_7_ = bf16[320,640]{1,0:T(8,128)(2,1)S(1)} collective-permute-done((bf16[320,640]{1,0:T(8,128)(2,1)S(1)}, bf16[320,640]{1,0:T(8,128)(2,1)S(1)}, u32[]{:S(2)}, u32[]{:S(2)}) %collective-permute-start.17) | collective-permute-done | bytes 409632 | tf_op jit(solution)/shard_map/ppermute | solution.py:453
  135.5 0.7 copy-done.8
  136.2 1.9 %copy-done.5 = bf16[1536,1280]{1,0:T(8,128)(2,1)} copy-done((bf16[1536,1280]{1,0:T(8,128)(2,1)}, bf16[1536,1280]{1,0:T(8,128)(2,1)S(1)}, u32[]{:S(2)}) %copy-start.5) | copy-done | bytes 3932184
  138.1 36.6 %groups.1 = bf16[768,640]{1,0:T(8,128)(2,1)} custom-call(s32[5]{0:T(128)} %stack.87.offset_ref, bf16[1536,1280]{1,0:T(8,128)(2,1)} %windows_out.1.own_ref, bf16[1536,1280]{1,0:T(8,128)(2,1)} %copy-done.5, s32[768,1]{1,0:T(8,128)} %broadcast_select_fusion.4.code_ref, s32[1,3072]{1,0:T(1,128)} %bitcast.29, bf16[320,1280]{1,0:T(8,128)(2,1)} %get-tuple-element.41.refs_0_, ...), custom_call_target="tpu_custom_call" | custom-call | flops 17364418560 | bytes 12794880 | tf_op jit(solution)/shard_map/groups/pallas_call | solution.py:409
  174.8 1.3 fusion.4
  176.0 0.1 collective-permute-start.18
  176.1 1.9 %collective-permute-done.18 = bf16[384,640]{1,0:T(8,128)(2,1)S(1)} collective-permute-done((bf16[384,640]{1,0:T(8,128)(2,1)S(1)}, bf16[384,640]{1,0:T(8,128)(2,1)S(1)}, u32[]{:S(2)}, u32[]{:S(2)}) %collective-permute-start.18) | collective-permute-done | bytes 491552 | tf_op jit(solution)/shard_map/ppermute | solution.py:440
  178.0 1.2 maximum_select_fusion
  (36 shorter events, 0.2 us)
Async XLA Ops:
  0.0 8.3 %copy-start.9 = (s32[1,2,3]{2,1,0:T(2,128)S(1)}, s32[1,2,3]{2,1,0:T(2,128)}, u32[]{:S(2)}) copy-start(s32[1,2,3]{2,1,0:T(2,128)} %param.9) | copy-start | bytes 76
  0.0 8.9 %copy-start.4 = (s32[1,2,3,64]{3,1,2,0:T(2,128)S(1)}, s32[1,2,3,64]{3,1,2,0:T(2,128)}, u32[]{:S(2)}) copy-start(s32[1,2,3,64]{3,1,2,0:T(2,128)} %param.8) | copy-start | bytes 4612
  3.8 21.4 %collective-permute-start.2 = (bf16[160,2560]{1,0:T(8,128)(2,1)}, bf16[160,2560]{1,0:T(8,128)(2,1)S(1)}, u32[]{:S(2)}, u32[]{:S(2)}) collective-permute-start(bf16[160,2560]{1,0:T(8,128)(2,1)} %get-tuple-element.26), channel_id=1, source_target_pairs={{0,16},{8,24},{16,0},{24,8},{1,17},{9,25},{17,1},{25,9},{2,18},{10... | collective-permute-start | bytes 2457608 | tf_op jit(solution)/shard_map/ppermute | solution.py:448
  6.8 20.0 %collective-permute-start.1 = (bf16[160,2560]{1,0:T(8,128)(2,1)}, bf16[160,2560]{1,0:T(8,128)(2,1)}, u32[]{:S(2)}, u32[]{:S(2)}) collective-permute-start(bf16[160,2560]{1,0:T(8,128)(2,1)} %get-tuple-element.26), channel_id=1, source_target_pairs={{0,8},{8,0},{16,24},{24,16},{1,9},{9,1},{17,25},{25,17},{2,10},{10... | collective-permute-start | bytes 2457608 | tf_op jit(solution)/shard_map/ppermute | solution.py:447
  13.0 51.6 %all-to-all-start = ((bf16[4,400,640]{2,1,0:T(8,128)(2,1)}), bf16[4,400,640]{2,1,0:T(8,128)(2,1)}, u32[]{:S(2)}, u32[]{:S(2)}) async-start(bf16[4,400,640]{2,1,0:T(8,128)(2,1)} %pick.1), calls=%async_computation | async-start | bytes 4096000 | tf_op jit(solution)/shard_map/all_to_all | solution.py:495
  26.8 32.6 %collective-permute-start.7 = (bf16[160,3200]{1,0:T(8,128)(2,1)}, bf16[160,3200]{1,0:T(8,128)(2,1)S(1)}, u32[]{:S(2)}, u32[]{:S(2)}) collective-permute-start(bf16[160,3200]{1,0:T(8,128)(2,1)} %get-tuple-element.39), channel_id=1, source_target_pairs={{0,16},{8,24},{16,0},{24,8},{1,17},{9,25},{17,1},{25,9},{2,18},{10... | collective-permute-start | bytes 3072008 | tf_op jit(solution)/shard_map/ppermute | solution.py:448
  27.1 32.3 %collective-permute-start.6 = (bf16[160,3200]{1,0:T(8,128)(2,1)}, bf16[160,3200]{1,0:T(8,128)(2,1)S(1)}, u32[]{:S(2)}, u32[]{:S(2)}) collective-permute-start(bf16[160,3200]{1,0:T(8,128)(2,1)} %get-tuple-element.39), channel_id=1, source_target_pairs={{0,8},{8,0},{16,24},{24,16},{1,9},{9,1},{17,25},{25,17},{2,10},{10... | collective-permute-start | bytes 3072008 | tf_op jit(solution)/shard_map/ppermute | solution.py:447
  31.4 28.1 %collective-permute-start.4 = (bf16[160,2560]{1,0:T(8,128)(2,1)}, bf16[160,2560]{1,0:T(8,128)(2,1)}, u32[]{:S(2)}, u32[]{:S(2)}) collective-permute-start(bf16[160,2560]{1,0:T(8,128)(2,1)} %get-tuple-element.54), channel_id=1, source_target_pairs={{0,8},{4,20},{8,0},{12,28},{16,24},{20,4},{24,16},{28,12},{1,9},{5... | collective-permute-start | bytes 2457608 | tf_op jit(solution)/shard_map/ppermute | solution.py:453
  34.1 36.3 %collective-permute-start.3 = (bf16[320,2560]{1,0:T(8,128)(2,1)}, bf16[320,2560]{1,0:T(8,128)(2,1)}, u32[]{:S(2)}, u32[]{:S(2)}) collective-permute-start(bf16[320,2560]{1,0:T(8,128)(2,1)} %constant_dynamic-update-slice_fusion.2.refs_1_), channel_id=1, source_target_pairs={{0,4},{4,0},{1,5},{5,1},{2,6},{6,2},{3,7},{7,3},{8,12},{12,8},{9,1... | collective-permute-start | bytes 4915208 | tf_op jit(solution)/shard_map/ppermute | solution.py:440
  59.4 11.5 %collective-permute-start.5 = (bf16[160,2560]{1,0:T(8,128)(2,1)}, bf16[160,2560]{1,0:T(8,128)(2,1)}, u32[]{:S(2)}, u32[]{:S(2)}) collective-permute-start(bf16[160,2560]{1,0:T(8,128)(2,1)} %collective-permute-done.4.refs_3_), channel_id=1, source_target_pairs={{0,4},{4,0},{1,5},{5,1},{2,6},{6,2},{3,7},{7,3},{8,12},{12,8},{9,1... | collective-permute-start | bytes 2457608 | tf_op jit(solution)/shard_map/ppermute | solution.py:440
  61.7 39.0 %collective-permute-start.8 = (bf16[320,3200]{1,0:T(8,128)(2,1)}, bf16[320,3200]{1,0:T(8,128)(2,1)}, u32[]{:S(2)}, u32[]{:S(2)}) collective-permute-start(bf16[320,3200]{1,0:T(8,128)(2,1)} %constant_dynamic-update-slice_fusion.4.refs_1_), channel_id=1, source_target_pairs={{0,4},{4,0},{1,5},{5,1},{2,6},{6,2},{3,7},{7,3},{8,12},{12,8},{9,1... | collective-permute-start | bytes 6144008 | tf_op jit(solution)/shard_map/ppermute | solution.py:440
  62.2 34.6 %collective-permute-start.9 = (bf16[160,3200]{1,0:T(8,128)(2,1)S(1)}, bf16[160,3200]{1,0:T(8,128)(2,1)}, u32[]{:S(2)}, u32[]{:S(2)}) collective-permute-start(bf16[160,3200]{1,0:T(8,128)(2,1)S(1)} %get-tuple-element.50), channel_id=1, source_target_pairs={{0,8},{4,20},{8,0},{12,28},{16,24},{20,4},{24,16},{28,12},{1,9},{5... | collective-permute-start | bytes 3072008 | tf_op jit(solution)/shard_map/ppermute | solution.py:453
  66.8 1.2 collective-permute-start
  68.0 28.9 %collective-permute-start.11 = (bf16[320,1280]{1,0:T(8,128)(2,1)}, bf16[320,1280]{1,0:T(8,128)(2,1)S(1)}, u32[]{:S(2)}, u32[]{:S(2)}) collective-permute-start(bf16[320,1280]{1,0:T(8,128)(2,1)} %get-tuple-element.41.refs_0_), channel_id=1, source_target_pairs={{0,8},{8,0},{16,24},{24,16},{1,9},{9,1},{17,25},{25,17},{2,10},{10... | collective-permute-start | bytes 2457608 | tf_op jit(solution)/shard_map/ppermute | solution.py:447
  70.5 26.4 %collective-permute-start.12 = (bf16[320,1280]{1,0:T(8,128)(2,1)}, bf16[320,1280]{1,0:T(8,128)(2,1)S(1)}, u32[]{:S(2)}, u32[]{:S(2)}) collective-permute-start(bf16[320,1280]{1,0:T(8,128)(2,1)} %get-tuple-element.41.refs_0_), channel_id=1, source_target_pairs={{0,16},{8,24},{16,0},{24,8},{1,17},{9,25},{17,1},{25,9},{2,18},{10... | collective-permute-start | bytes 2457608 | tf_op jit(solution)/shard_map/ppermute | solution.py:448
  71.0 25.9 %copy-start.7 = (bf16[320,640]{1,0:T(8,128)(2,1)S(1)}, bf16[320,640]{1,0:T(8,128)(2,1)}, u32[]{:S(2)}) copy-start(bf16[320,640]{1,0:T(8,128)(2,1)} %get-tuple-element.45.refs_4_) | copy-start | bytes 1228804
  96.8 3.9 %collective-permute-start.10 = (bf16[160,3200]{1,0:T(8,128)(2,1)}, bf16[160,3200]{1,0:T(8,128)(2,1)S(1)}, u32[]{:S(2)}, u32[]{:S(2)}) collective-permute-start(bf16[160,3200]{1,0:T(8,128)(2,1)} %collective-permute-done.9.refs_3_), channel_id=1, source_target_pairs={{0,4},{4,0},{1,5},{5,1},{2,6},{6,2},{3,7},{7,3},{8,12},{12,8},{9,1... | collective-permute-start | bytes 3072008 | tf_op jit(solution)/shard_map/ppermute | solution.py:440
  96.8 30.4 %copy-start = (bf16[320,1280]{1,0:T(8,128)(2,1)}, bf16[320,1280]{1,0:T(8,128)(2,1)S(1)}, u32[]{:S(2)}) copy-start(bf16[320,1280]{1,0:T(8,128)(2,1)S(1)} %collective-permute-done.11.refs_1_) | copy-start | bytes 2457604
  96.9 30.4 %copy-start.1 = (bf16[320,1280]{1,0:T(8,128)(2,1)}, bf16[320,1280]{1,0:T(8,128)(2,1)S(1)}, u32[]{:S(2)}) copy-start(bf16[320,1280]{1,0:T(8,128)(2,1)S(1)} %collective-permute-done.12.refs_2_) | copy-start | bytes 2457604
  96.9 30.4 %collective-permute-start.14 = (bf16[320,640]{1,0:T(8,128)(2,1)S(1)}, bf16[320,640]{1,0:T(8,128)(2,1)S(1)}, u32[]{:S(2)}, u32[]{:S(2)}) collective-permute-start(bf16[320,640]{1,0:T(8,128)(2,1)S(1)} %copy-done.7), channel_id=1, source_target_pairs={{0,8},{8,0},{16,24},{24,16},{1,9},{9,1},{17,25},{25,17},{2,10},{10... | collective-permute-start | bytes 1228808 | tf_op jit(solution)/shard_map/ppermute | solution.py:447
  98.4 28.9 %collective-permute-start.15 = (bf16[320,640]{1,0:T(8,128)(2,1)S(1)}, bf16[320,640]{1,0:T(8,128)(2,1)S(1)}, u32[]{:S(2)}, u32[]{:S(2)}) collective-permute-start(bf16[320,640]{1,0:T(8,128)(2,1)S(1)} %copy-done.7), channel_id=1, source_target_pairs={{0,16},{8,24},{16,0},{24,8},{1,17},{9,25},{17,1},{25,9},{2,18},{10... | collective-permute-start | bytes 1228808 | tf_op jit(solution)/shard_map/ppermute | solution.py:448
  100.1 27.3 %collective-permute-start.13 = (bf16[320,1280]{1,0:T(8,128)(2,1)S(1)}, bf16[320,1280]{1,0:T(8,128)(2,1)}, u32[]{:S(2)}, u32[]{:S(2)}) collective-permute-start(bf16[320,1280]{1,0:T(8,128)(2,1)S(1)} %broadcast_select_fusion.1), channel_id=1, source_target_pairs={{0,8},{4,20},{8,0},{12,28},{16,24},{20,4},{24,16},{28,12},{1,9},{5... | collective-permute-start | bytes 2457608 | tf_op jit(solution)/shard_map/ppermute | solution.py:453
  100.7 1.0 copy-start.6
  127.3 8.2 %copy-start.2 = (bf16[320,640]{1,0:T(8,128)(2,1)}, bf16[320,640]{1,0:T(8,128)(2,1)S(1)}, u32[]{:S(2)}) copy-start(bf16[320,640]{1,0:T(8,128)(2,1)S(1)} %collective-permute-done.14.refs_5_) | copy-start | bytes 1228804
  127.3 8.2 %copy-start.3 = (bf16[320,640]{1,0:T(8,128)(2,1)}, bf16[320,640]{1,0:T(8,128)(2,1)S(1)}, u32[]{:S(2)}) copy-start(bf16[320,640]{1,0:T(8,128)(2,1)S(1)} %collective-permute-done.15.refs_6_) | copy-start | bytes 1228804
  127.3 8.2 %collective-permute-start.16 = (bf16[1536,1280]{1,0:T(8,128)(2,1)}, bf16[1536,1280]{1,0:T(8,128)(2,1)S(1)}, u32[]{:S(2)}, u32[]{:S(2)}) collective-permute-start(bf16[1536,1280]{1,0:T(8,128)(2,1)} %windows_out.1.own_ref), channel_id=1, source_target_pairs={{0,4},{4,0},{1,5},{5,1},{2,6},{6,2},{3,7},{7,3},{8,12},{12,8},{9,1... | collective-permute-start | bytes 11796488 | tf_op jit(solution)/shard_map/ppermute | solution.py:440
  127.5 8.0 %collective-permute-start.17 = (bf16[320,640]{1,0:T(8,128)(2,1)S(1)}, bf16[320,640]{1,0:T(8,128)(2,1)S(1)}, u32[]{:S(2)}, u32[]{:S(2)}) collective-permute-start(bf16[320,640]{1,0:T(8,128)(2,1)S(1)} %broadcast_select_fusion.3), channel_id=1, source_target_pairs={{0,8},{4,20},{8,0},{12,28},{16,24},{20,4},{24,16},{28,12},{1,9},{5... | collective-permute-start | bytes 1228808 | tf_op jit(solution)/shard_map/ppermute | solution.py:453
  135.5 0.7 copy-start.8
  136.2 1.9 %copy-start.5 = (bf16[1536,1280]{1,0:T(8,128)(2,1)}, bf16[1536,1280]{1,0:T(8,128)(2,1)S(1)}, u32[]{:S(2)}) copy-start(bf16[1536,1280]{1,0:T(8,128)(2,1)S(1)} %collective-permute-done.16.other_ref) | copy-start | bytes 11796484
  176.0 1.9 %collective-permute-start.18 = (bf16[384,640]{1,0:T(8,128)(2,1)S(1)}, bf16[384,640]{1,0:T(8,128)(2,1)S(1)}, u32[]{:S(2)}, u32[]{:S(2)}) collective-permute-start(bf16[384,640]{1,0:T(8,128)(2,1)S(1)} %get-tuple-element.53), channel_id=1, source_target_pairs={{0,4},{4,0},{1,5},{5,1},{2,6},{6,2},{3,7},{7,3},{8,12},{12,8},{9,1... | collective-permute-start | bytes 1474568 | tf_op jit(solution)/shard_map/ppermute | solution.py:440

commit v5 on v4

--- a/solution.py
+++ b/solution.py
@@ -151,28 +151,32 @@
         target[:, pl.ds(at + GROUP * MAIN + head * TAIL, TAIL)] = source[:, pl.ds(first + MAIN, TAIL)]
 
 
-def pick_kernel(count_ref, patch_ref, index_ref, sent_ref):
-    windows, window_tokens, _ = patch_ref.shape
-    kept_most = index_ref.shape[1]
-    rows = windows * kept_most
+def pick_kernel(_, patch_ref, code_ref, partner_ref, *sent_refs):
+    window_tokens = patch_ref.shape[1]
+    windows, kept_most = code_ref.shape
+    count = windows // len(sent_refs)
+    rows = count * kept_most
     offsets = lax.broadcasted_iota(jnp.int32, (window_tokens, kept_most), 0)
-    places = lax.broadcasted_iota(jnp.int32, (1, kept_most), 1)
-    sent_ref[0, pl.ds(rows, sent_ref.shape[1] - rows), :] = jnp.zeros(
-        (sent_ref.shape[1] - rows, sent_ref.shape[2]), jnp.bfloat16
-    )
-    codes = []
-    for window in range(windows):
-        index = index_ref[pl.ds(window, 1), :]
-        chosen = (offsets == index).astype(jnp.float32).astype(jnp.bfloat16)
-        picked = lax.dot_general(
-            chosen, patch_ref[window], (((0,), (0,)), ((), ())), preferred_element_type=jnp.float32
+    for which, sent_ref in enumerate(sent_refs):
+        tile = sent_ref.shape[1] - rows
+        sent_ref[0, pl.ds(rows, tile), :] = jnp.zeros((tile, sent_ref.shape[2]), jnp.bfloat16)
+        for at in range(count):
+            window = which * count + at
+            chosen = (offsets == code_ref[pl.ds(window, 1), :]).astype(jnp.float32)
+            picked = lax.dot_general(
+                chosen.astype(jnp.bfloat16),
+                patch_ref[window],
+                (((0,), (0,)), ((), ())),
+                preferred_element_type=jnp.float32,
+            )
+            sent_ref[0, pl.ds(at * kept_most, kept_most), :] = picked.astype(jnp.bfloat16)
+        part = pl.ds(which * count, count)
+        codes = jnp.concatenate([code_ref[part, :], partner_ref[part, :]], axis=0)
+        sent_ref[0, pl.ds(rows, 2 * count), pl.ds(0, kept_most)] = codes.astype(jnp.float32).astype(
+            jnp.bfloat16
         )
-        sent_ref[0, pl.ds(window * kept_most, kept_most), :] = picked.astype(jnp.bfloat16)
-        codes.append(jnp.where(places < count_ref[window], index, -1))
-    codes = jnp.concatenate(codes, axis=0).astype(jnp.float32).astype(jnp.bfloat16)
-    sent_ref[0, pl.ds(rows, windows), pl.ds(0, kept_most)] = codes
-    for copy in range(1, sent_ref.shape[0]):
-        sent_ref[copy] = sent_ref[0]
+        for copy in range(1, sent_ref.shape[0]):
+            sent_ref[copy] = sent_ref[0]
 
 
 def pack_columns(group, weight_ref, full_ref):
@@ -236,12 +240,21 @@
     return jnp.where(mask, scores, mask_floor)
 
 
-def mix_heads(proj_ref, code_ref, mix_ref, at_once, kept_most):
+def code_row(tile, at, kept_most):
+    return tile[at : at + 1, :kept_most]
+
+
+def mix_heads(proj_ref, code_ref, mix_ref, count, kept_most, at_once):
     rows = proj_ref.shape[0]
     own_window = lax.broadcasted_iota(jnp.int32, (at_once, 1), 0) // kept_most
+    key_window = lax.broadcasted_iota(jnp.int32, (1, at_once), 1) // kept_most
+    tiles = [code_ref[at].astype(jnp.float32) for at in range(code_ref.shape[0])]
+    codes = [code_row(tile, at, kept_most) for tile in tiles for at in range(count)]
     for start in range(0, rows, at_once):
         part = pl.ds(start, at_once)
-        mask = own_window == code_ref[0, :, part]
+        first = start // kept_most
+        key_codes = jnp.concatenate(codes[first : first + at_once // kept_most], axis=1)
+        mask = own_window == jnp.where(key_codes >= 0, key_window, -1)
         tails = None
         for head in range(GROUP):
             scores = masked_scores(
@@ -263,8 +276,7 @@
 
 
 def embed_window_kernel(
-    at_once,
-    kept_most,
+    mix,
     offset_ref,
     picked_ref,
     code_ref,
@@ -286,17 +298,17 @@
                     pl.ds(side * quarter, quarter), pl.ds(3 * WIDE, wide)
                 ]
 
-    embedded = fold_product(picked_ref[...], embed_ref[...]).astype(jnp.bfloat16)
+    picked = picked_ref[...].reshape(proj_ref.shape[0], picked_ref.shape[2])
+    embedded = fold_product(picked, embed_ref[...]).astype(jnp.bfloat16)
     embedded_ref[...] = embedded
     normed = layer_norm(embedded.astype(jnp.float32)).astype(jnp.bfloat16)
     normed_ref[...] = normed
     proj_ref[...] = fold_product(normed, weight_ref[...]).astype(jnp.bfloat16)
-    mix_heads(proj_ref, code_ref, mix_ref, at_once, kept_most)
+    mix(proj_ref, code_ref, mix_ref)
 
 
 def window_out_kernel(
-    at_once,
-    kept_most,
+    mix,
     offset_ref,
     embedded_ref,
     normed_ref,
@@ -319,7 +331,7 @@
             ]
 
     proj_ref[...] = fold_product(normed_ref[...], weight_ref[...]).astype(jnp.bfloat16)
-    mix_heads(proj_ref, code_ref, own_mix_ref, at_once, kept_most)
+    mix(proj_ref, code_ref, own_mix_ref)
     hidden = embedded_ref[...].astype(jnp.float32)
     hidden += fold_product(mix_ref[...], row_ref[pl.ds(0, WIDE), :])
     hidden += fold_product(own_mix_ref[...], row_ref[pl.ds(WIDE, WIDE), :])
@@ -327,50 +339,52 @@
     result_ref[...] = layer_norm(hidden).astype(jnp.bfloat16)
 
 
-def group_kernel(
-    steps,
-    key_chunk,
-    offset_ref,
-    own_ref,
-    other_ref,
-    code_ref,
-    key_code_ref,
-    *refs,
-):
-    *pieces, mixed_ref, first_ref, second_ref, key_ref, query_ref, value_ref = refs
+def group_kernel(steps, parts, count, kept_most, key_chunk, offset_ref, *refs):
+    many = 2 * parts
+    normed_refs, refs = refs[:many], refs[many:]
+    tile_refs, refs = refs[:parts], refs[parts:]
+    code_ref, *pieces, mixed_ref, first_ref, second_ref, key_ref, query_ref, value_ref, key_code_ref = refs
     step = pl.program_id(0)
-    block = own_ref.shape[0]
+    block = normed_refs[0].shape[0]
     query_block = mixed_ref.shape[0]
+    part_rows = count * kept_most
+    shared = block // part_rows
 
     @pl.when(step == 0)
     def _():
-        for target, parts in ((first_ref, pieces[:4]), (second_ref, pieces[4:])):
-            for at, part in enumerate(parts):
-                target[pl.ds(first_row(offset_ref, at, 32), part.shape[0]), :] = part[...]
-
-    def project(source_ref, at):
-        normed = source_ref[...]
-        part = pl.ds(pl.multiple_of(step * block, 16), block)
-        key_ref[part, :] = fold_product(normed, first_ref[:, pl.ds(0, WIDE)]).astype(jnp.bfloat16)
-        value_ref[part, :] = fold_product(normed, second_ref[...]).astype(jnp.bfloat16)
-
-        @pl.when(step == at * steps + offset_ref[4])
+        for target, arrays in ((first_ref, pieces[:4]), (second_ref, pieces[4:])):
+            for at, array in enumerate(arrays):
+                target[pl.ds(first_row(offset_ref, at, 32), array.shape[0]), :] = array[...]
+        at = 0
+        for core in range(2):
+            for tile_ref in tile_refs:
+                for device in range(tile_ref.shape[0]):
+                    tile = tile_ref[device].astype(jnp.float32)
+                    for window in range(count):
+                        key_code_ref[:, pl.ds(at, kept_most)] = code_row(
+                            tile, core * count + window, kept_most
+                        )
+                        at += kept_most
+
+    for which, normed_ref in enumerate(normed_refs):
+
+        @pl.when((step >= which * steps) & (step < (which + 1) * steps))
         def _():
-            query_ref[pl.ds(at * block, block), :] = fold_product(
-                normed, first_ref[:, pl.ds(WIDE, WIDE)]
+            normed = normed_ref[...]
+            part = pl.ds(pl.multiple_of(step * block, 16), block)
+            key_ref[part, :] = fold_product(normed, first_ref[:, pl.ds(0, WIDE)]).astype(jnp.bfloat16)
+            value_ref[part, :] = fold_product(normed, second_ref[...]).astype(jnp.bfloat16)
+
+        @pl.when(step == which * steps + offset_ref[4] // shared)
+        def _():
+            start = pl.multiple_of(offset_ref[4] % shared * part_rows, 16)
+            query_ref[pl.ds(which * part_rows, part_rows), :] = fold_product(
+                normed_ref[pl.ds(start, part_rows), :], first_ref[:, pl.ds(WIDE, WIDE)]
             ).astype(jnp.bfloat16)
 
-    @pl.when(step < steps)
+    @pl.when(step >= many * steps)
     def _():
-        project(own_ref, 0)
-
-    @pl.when((step >= steps) & (step < 2 * steps))
-    def _():
-        project(other_ref, 1)
-
-    @pl.when(step >= 2 * steps)
-    def _():
-        part = pl.ds(pl.multiple_of((step - 2 * steps) * query_block, 16), query_block)
+        part = pl.ds(pl.multiple_of((step - many * steps) * query_block, 16), query_block)
         codes = code_ref[...]
         key_parts = [pl.ds(at, key_chunk) for at in range(0, key_ref.shape[0], key_chunk)]
         for head in range(GROUP):
@@ -413,7 +427,10 @@
             grid=(steps,),
             in_specs=specs,
             out_specs=out_specs,
-            scratch_shapes=[pltpu.VMEM(shape, jnp.bfloat16) for shape in scratch],
+            scratch_shapes=[
+                pltpu.VMEM(shape, jnp.bfloat16) if isinstance(shape, tuple) else shape
+                for shape in scratch
+            ],
         ),
         out_shape=[jax.ShapeDtypeStruct(shape, jnp.bfloat16) for shape in outs],
         compiler_params=pltpu.CompilerParams(vmem_limit_bytes=vmem_limit),
@@ -476,26 +493,38 @@
         pack_first_kernel, core_scalar, embed_weight, first_wide, "pack_first"
     )
 
-    code_tile = -(-windows // 16) * 16
-    sent_shape = (lon_size, rows + code_tile, pin)
+    parts = 1
+    count = windows // parts
+    part_rows = count * kept_most
+    code_tile = -(-2 * count // 16) * 16
+    sent_shape = (lon_size, part_rows + code_tile, pin)
     patch_rows = patches.reshape(windows, window_tokens, pin)
-    index_rows = kept_index.reshape(windows, kept_most)
-    (sent,) = run(
+    kept_mask = lax.broadcasted_iota(jnp.int32, (windows, kept_most), 1) < kept_count.reshape(
+        windows, 1
+    )
+    codes = jnp.where(kept_mask, kept_index.reshape(windows, kept_most), -1)
+    partner_codes = other_core(codes)
+    query_codes = jnp.concatenate([codes, partner_codes], axis=0).astype(jnp.float32)
+    query_codes = query_codes.reshape(2 * rows, 1)
+    global_starts = [(chip ^ which) * high for which in range(4)]
+    global_offsets = jnp.stack([*global_starts, place]).astype(jnp.int32)
+    sent = run(
         pick_kernel,
         1,
-        after(kept_count.reshape(windows), half_first),
-        [whole_block(patch_rows), whole_block(index_rows)],
-        [patch_rows, index_rows],
-        [sent_shape],
-        [pl.BlockSpec(sent_shape, lambda *_: (0, 0, 0))],
+        after(core_scalar, half_first),
+        [whole_block(patch_rows), whole_block(codes), whole_block(partner_codes)],
+        [patch_rows, codes, partner_codes],
+        [sent_shape] * parts,
+        [pl.BlockSpec(sent_shape, lambda *_: (0, 0, 0))] * parts,
         [],
         0,
         "pick",
     )
-    got = lax.all_to_all(sent, "lon", 0, 0, tiled=True)
-    all_rows = lon_size * rows
-    own_codes = got[:, rows : rows + windows, :kept_most].reshape(-1).astype(jnp.int32)
-    other_codes = other_core(own_codes)
+    query_codes, global_offsets = after((query_codes, global_offsets), sent)
+    got = []
+    for value in sent:
+        value = after(value, got[-1]) if got else value
+        got.append(lax.all_to_all(value, "lon", 0, 0, tiled=True))
 
     local_second, half_second = pack(
         pack_second_kernel, after(core_scalar, sent), local_out, second_wide, "pack_second"
@@ -516,8 +545,8 @@
         "order_global",
     )
     sides_first = sides(half_first)
-    half_second, _ = after((half_second, global_first), sides_first)
-    sides_second = sides(half_second)
+    sides_first = after(sides_first, (sent, global_first))
+    sides_second = sides(after(half_second, sides_first))
     across_first = across(*sides_first)
     global_sides = sides(after(global_first, sides_second))
     across_second = across(*sides_second)
@@ -537,78 +566,90 @@
         tail = group_start + GROUP * MAIN + head % GROUP * TAIL
         return pieces, jnp.stack([firsts, main, tail], axis=1).reshape(-1)
 
-    block, steps = rows, lon_size
+    shared_by = 2 if lon_size % 2 == 0 else 1
+    block = shared_by * part_rows
+    steps = lon_size // shared_by
+    many_rows = lon_size * part_rows
     at_once = 2 * kept_most if block % (2 * kept_most) == 0 else kept_most
-    window_codes = jnp.where(
-        own_codes >= 0,
-        (jnp.arange(all_rows, dtype=jnp.int32) // kept_most) % (at_once // kept_most),
-        -1,
-    ).reshape(steps, 1, block)
-    code_spec = pl.BlockSpec((1, 1, block), lambda i, _: (i, 0, 0))
+    mix = functools.partial(mix_heads, count=count, kept_most=kept_most, at_once=at_once)
     row_spec = lambda wide: pl.BlockSpec((block, wide), lambda i, _: (i, 0))
-    at_home = lambda a: lax.dynamic_slice_in_dim(a, place * rows, rows, axis=0)
-    key_codes = jnp.concatenate([own_codes, other_codes]).reshape(1, 2 * all_rows)
-    query_codes = jnp.concatenate([at_home(own_codes), at_home(other_codes)]).reshape(2 * rows, 1)
-    query_codes = jnp.where(query_codes >= 0, query_codes, -2)
-    global_starts = [(chip ^ which) * high for which in range(4)]
-    global_offsets = jnp.stack([*global_starts, place]).astype(jnp.int32)
+    tile_spec = pl.BlockSpec((shared_by, code_tile, MAIN), lambda i, _: (i, part_rows // code_tile, 0))
 
     pieces, offsets = shared(local_first, [*sides_first, across_first], core_scalar)
-    window_codes, _ = after((window_codes, 0), (key_codes, query_codes, global_offsets))
-    embedded, normed, first_mix = run(
-        functools.partial(embed_window_kernel, at_once, kept_most),
-        steps,
-        offsets,
+    embedded, normed, mixes = [], [], []
+    for which in range(parts):
+        if which == parts - 1:
+            pieces = after(pieces, (sides_second, mixes))
+        result = run(
+            functools.partial(embed_window_kernel, mix),
+            steps,
+            offsets,
+            [
+                pl.BlockSpec((shared_by, part_rows, pin), lambda i, _: (i, 0, 0)),
+                tile_spec,
+                *map(whole_block, pieces),
+            ],
+            [got[which], got[which], *pieces],
+            [(many_rows, width), (many_rows, width), (many_rows, WIDE)],
+            [row_spec(width), row_spec(width), row_spec(WIDE)],
+            [(width, 3 * WIDE), (pin, width), (block, 3 * WIDE)],
+            2 * many_rows * (pin * width + width * 3 * WIDE),
+            "embed_windows",
+        )
+        for values, value in zip((embedded, normed, mixes), result):
+            values.append(value)
+
+    pieces, offsets = shared(local_second, [*sides_second, across_second], mixes[0])
+    own, partner = [], []
+    for which in range(parts):
+        if which == parts - 1:
+            pieces = after(pieces, (global_sides, own))
+            global_sides, _ = after((global_sides, 0), own or mixes)
+            global_across = across(*global_sides)
+            value_sides = sides(after(global_second, global_sides))
+        (result,) = run(
+            functools.partial(window_out_kernel, mix),
+            steps,
+            offsets,
+            [row_spec(width), row_spec(width), row_spec(WIDE), tile_spec, *map(whole_block, pieces)],
+            [embedded[which], normed[which], mixes[which], got[which], *pieces],
+            [(many_rows, width)],
+            [row_spec(width)],
+            [(width, 3 * WIDE), (block, 3 * WIDE), (block, WIDE), (inner, width)],
+            2 * many_rows * (inner * width + width * 3 * WIDE),
+            "windows_out",
+        )
+        own.append(result)
+        if which == parts - 1:
+            result = after(result, (global_across, value_sides))
+        partner.append(other_core(result))
+    value_across = across(*value_sides)
+
+    all_rows = lon_size * rows
+    query_block = 256 if (2 * rows) % 256 == 0 else 2 * rows
+    query_steps = 2 * rows // query_block
+    project_steps = 2 * parts * steps
+    pieces = [global_first, *global_sides, global_across, global_second, *value_sides, value_across]
+    key_chunk = 512 if (2 * all_rows) % 512 == 0 else block
+    late = lambda i: jnp.clip(i - project_steps, 0, query_steps - 1)
+    normed_specs = [
+        pl.BlockSpec((block, width), lambda i, _, at=at: (jnp.clip(i - at * steps, 0, steps - 1), 0))
+        for at in range(2 * parts)
+    ]
+    whole_tile = pl.BlockSpec(
+        (lon_size, code_tile, MAIN), lambda *_: (0, part_rows // code_tile, 0)
+    )
+    (mixed,) = run(
+        functools.partial(group_kernel, steps, parts, count, kept_most, key_chunk),
+        project_steps + query_steps,
+        global_offsets,
         [
-            pl.BlockSpec((None, rows, pin), lambda i, _: (i, 0, 0)),
-            code_spec,
+            *normed_specs,
+            *[whole_tile] * parts,
+            pl.BlockSpec((query_block, 1), lambda i, _: (late(i), 0)),
             *map(whole_block, pieces),
         ],
-        [got, window_codes, *pieces],
-        [(all_rows, width), (all_rows, width), (all_rows, WIDE)],
-        [row_spec(width), row_spec(width), row_spec(WIDE)],
-        [(width, 3 * WIDE), (pin, width), (block, 3 * WIDE)],
-        2 * all_rows * (pin * width + width * 3 * WIDE),
-        "embed_windows",
-    )
-
-    pieces, offsets = shared(local_second, [*sides_second, across_second], first_mix)
-    global_sides, _ = after((global_sides, 0), first_mix)
-    global_across = across(*global_sides)
-    value_sides = sides(after(global_second, global_sides))
-    (normed_own,) = run(
-        functools.partial(window_out_kernel, at_once, kept_most),
-        steps,
-        offsets,
-        [row_spec(width), row_spec(width), row_spec(WIDE), code_spec, *map(whole_block, pieces)],
-        [embedded, normed, first_mix, window_codes, *pieces],
-        [(all_rows, width)],
-        [row_spec(width)],
-        [(width, 3 * WIDE), (block, 3 * WIDE), (block, WIDE), (inner, width)],
-        2 * all_rows * (inner * width + width * 3 * WIDE),
-        "windows_out",
-    )
-    normed_own = after(normed_own, (global_across, value_sides))
-    normed_other = other_core(normed_own)
-    value_across = across(*value_sides)
-
-    query_block = 256 if (2 * rows) % 256 == 0 else 2 * rows
-    query_steps = 2 * rows // query_block
-    pieces = [global_first, *global_sides, global_across, global_second, *value_sides, value_across]
-    key_chunk = 512 if (2 * all_rows) % 512 == 0 else block
-    late = lambda i: jnp.clip(i - 2 * steps, 0, query_steps - 1)
-    (mixed,) = run(
-        functools.partial(group_kernel, steps, key_chunk),
-        2 * steps + query_steps,
-        global_offsets,
-        [
-            pl.BlockSpec((block, width), lambda i, _: (jnp.minimum(i, steps - 1), 0)),
-            pl.BlockSpec((block, width), lambda i, _: (jnp.clip(i - steps, 0, steps - 1), 0)),
-            pl.BlockSpec((query_block, 1), lambda i, _: (late(i), 0)),
-            whole_block(key_codes),
-            *map(whole_block, pieces),
-        ],
-        [normed_own, normed_other, query_codes, key_codes, *pieces],
+        [*own, *partner, *got, query_codes, *pieces],
         [(2 * rows, WIDE)],
         [pl.BlockSpec((query_block, WIDE), lambda i, _: (late(i), 0))],
         [
@@ -617,6 +658,7 @@
             (2 * all_rows, WIDE),
             (2 * rows, WIDE),
             (2 * all_rows, WIDE),
+            pltpu.VMEM((1, 2 * all_rows), jnp.float32),
         ],
         2 * WIDE * (2 * all_rows * 2 * width + 2 * rows * width + 4 * rows * 2 * all_rows),
         "groups",
@@ -636,7 +678,7 @@
     windows = patches.shape[1] * patches.shape[2]
     rows = windows * kept_index.shape[3]
     sample_rows = rows * lax.axis_size("lat") * lax.axis_size("lon")
-    fits = patches.shape[3] <= 256 and windows <= 16 and sample_rows * HEADS * HD * 2 <= vmem_limit // 4
+    fits = patches.shape[3] <= 256 and windows % 2 == 0 and windows * kept_index.shape[3] % 32 == 0 and sample_rows * HEADS * HD * 2 <= vmem_limit // 4
     shards = embed_weight.shape[0] * 2 == local_qkv.shape[0] == local_out.shape[0] == 2 * HD
     if lax.axis_size("batch") == 4 and lax.axis_size("lat") == HEADS // GROUP == 2 and fits and shards:
         return sample_body(*args)

time: 180 us -> 177 us (0.983)
  other arithmetic: 8.53 us -> 5.58 us
  local copies, waits for them, and re-layouts: 10.5 us -> 8.2 us
    unnamed x22 -> x31, local copies, waits for them, and re-layouts: 3.62 us -> 2.35 us
  transfers between devices with their start and end apart: 20 -> 20, of which waited for: 7 -> 7; matrix products, arithmetic and copies ran while one was open for 7% -> 5% of each run, Pallas kernels for 35% -> 34%
where the time goes in v5:
time: 177 us
  Pallas kernels  102 us (58%)
  waiting for transfers between devices  39 us (22%)
  starting transfers between devices  21.9 us (12%)
  local copies, waits for them, and re-layouts  8.2 us (5%)
  other arithmetic  5.58 us (3%)
    pallas_call x7, Pallas kernels, run(): pl.pallas_call(kernel, grid_spec=pltpu.PrefetchScalarGridSpec(num_scalar_...  102 us
    ppermute x4, waiting for transfers between devices, across(): return lax.ppermute(forwarded, ('batch', 'lat'), diagonal)  31.2 us
    ppermute x4, starting transfers between devices, sides(): along_x = lax.ppermute(part, 'batch', swap_perm(batch_size, 1))  6.2 us
    ppermute x4, starting transfers between devices, sides(): along_y = lax.ppermute(part, 'batch', swap_perm(batch_size, 2))  5.75 us
    all_to_all x1, starting transfers between devices, sample_body(): got.append(lax.all_to_all(value, 'lon', 0, 0, tiled=True))  4.87 us
    select_n x4, other arithmetic, across(): forwarded = jnp.where(core == 0, along_y, along_x)  4.28 us
    ppermute x4, starting transfers between devices, across(): return lax.ppermute(forwarded, ('batch', 'lat'), diagonal)  4 us
  transfers between devices with their start and end apart: 20, of which 7 were waited for; matrix products, arithmetic and copies ran while one was open for 5% of the time, Pallas kernels for 34%

profile of v5, /device:TPU:0, one launch (start us, length us, event | category | flops | bytes accessed | tf_op | source)
XLA Modules:
  0.0 176.9 jit_solution(2356934680711768527)
XLA Ops:
  0.0 3.8 %pack_first.1 = (bf16[320,2560]{1,0:T(8,128)(2,1)}, bf16[160,2560]{1,0:T(8,128)(2,1)}) custom-call(s32[1]{0:T(128)} %bitcast.5.core_ref._, bf16[320,3840]{1,0:T(8,128)(2,1)} %weight_ref.3, bf16[160,1280]{1,0:T(8,128)(2,1)} %embed_ref.1), custom_call_target="tpu_custom_call" | custom-call | bytes 2867200 | tf_op jit(solution)/shard_map/pack_first/pallas_call | solution.py:423
  3.8 2.9 %collective-permute-start.1 = (bf16[160,2560]{1,0:T(8,128)(2,1)}, bf16[160,2560]{1,0:T(8,128)(2,1)S(1)}, u32[]{:S(2)}, u32[]{:S(2)}) collective-permute-start(bf16[160,2560]{1,0:T(8,128)(2,1)} %get-tuple-element.39), channel_id=1, source_target_pairs={{0,8},{8,0},{16,24},{24,16},{1,9},{9,1},{17,25},{25,17},{2,10},{10... | collective-permute-start | bytes 2457608 | tf_op jit(solution)/shard_map/ppermute | solution.py:464
  6.8 1.5 collective-permute-start.2
  8.3 0.1 lt.22
  8.4 0.1 fusion.code_ref
  8.5 0.0 collective-permute-start
  8.5 1.2 collective-permute-done.partner_ref
  9.6 0.6 copy-done.7
  10.2 3.0 %pick.1 = bf16[4,400,640]{2,1,0:T(8,128)(2,1)} custom-call(s32[1]{0:T(128)} %bitcast.5.core_ref._, bf16[6,128,640]{2,1,0:T(8,128)(2,1)} %bitcast.26, s32[6,64]{1,0:T(8,128)} %copy-done.5, s32[6,64]{1,0:T(8,128)} %copy-done.7), custom_call_target="tpu_custom_call" | custom-call | bytes 986112 | tf_op jit(solution)/shard_map/pick/pallas_call | solution.py:423
  13.2 4.9 %all-to-all-start = ((bf16[4,400,640]{2,1,0:T(8,128)(2,1)}), bf16[4,400,640]{2,1,0:T(8,128)(2,1)}, u32[]{:S(2)}, u32[]{:S(2)}) async-start(bf16[4,400,640]{2,1,0:T(8,128)(2,1)} %pick.1), calls=%async_computation | async-start | bytes 4096000 | tf_op jit(solution)/shard_map/all_to_all | solution.py:527
  18.1 4.2 %pack_second.1 = (bf16[320,3200]{1,0:T(8,128)(2,1)}, bf16[160,3200]{1,0:T(8,128)(2,1)}) custom-call(s32[1]{0:T(128)} %bitcast.5.core_ref._, bf16[320,3840]{1,0:T(8,128)(2,1)} %weight_ref.3, bf16[320,1280]{1,0:T(8,128)(2,1)} %out_ref.1), custom_call_target="tpu_custom_call" | custom-call | bytes 3276800 | tf_op jit(solution)/shard_map/pack_second/pallas_call | solution.py:423
  22.3 2.8 %order_global.1 = (bf16[320,1280]{1,0:T(8,128)(2,1)}, bf16[320,640]{1,0:T(8,128)(2,1)}) custom-call(s32[1]{0:T(128)} %bitcast.5.core_ref._, bf16[320,3840]{1,0:T(8,128)(2,1)} %value_ref.1, bf16[320,3840]{1,0:T(8,128)(2,1)} %value_ref.1, bf16[320,3840]{1,0:T(8,128)(2,1)} %value_ref.1), custom_call_target="tpu_custom_call" | custom-call | bytes 7372800 | tf_op jit(solution)/shard_map/order_global/pallas_call | solution.py:423
  25.1 0.1 collective-permute-done.1
  25.2 1.5 collective-permute-done.2
  26.7 1.2 collective-permute-start.6
  27.9 1.5 collective-permute-start.7
  29.4 2.5 %broadcast_select_fusion.2 = (bf16[160,2560]{1,0:T(8,128)(2,1)}, bf16[320,2560]{1,0:T(8,128)(2,1)}) fusion(bf16[160,2560]{1,0:T(8,128)(2,1)S(1)} %collective-permute-done.2, bf16[160,2560]{1,0:T(8,128)(2,1)} %copy-done, pred[]{:T(512)S(6)} %eq.12), kind=kLoop, calls=%fused_computation.3 | loop fusion | flops 409599 | bytes 3276801 | tf_op jit(solution)/shard_map/jit(_where)/select_n | solution.py:469
  31.9 0.8 collective-permute-start.4
  32.8 0.1 stack.105
  32.9 1.0 constant_dynamic-update-slice_fusion.refs_1_
  33.9 0.0 collective-permute-start.3
  33.9 0.1 stack.95
  34.0 25.6 %collective-permute-done.4.refs_3_ = bf16[160,2560]{1,0:T(8,128)(2,1)} collective-permute-done((bf16[160,2560]{1,0:T(8,128)(2,1)}, bf16[160,2560]{1,0:T(8,128)(2,1)}, u32[]{:S(2)}, u32[]{:S(2)}) %collective-permute-start.4) | collective-permute-done | bytes 819232 | tf_op jit(solution)/shard_map/ppermute | solution.py:470
  59.5 0.9 collective-permute-start.5
  60.4 0.0 collective-permute-done.6
  60.4 0.0 collective-permute-done.7
  60.4 1.6 broadcast_select_fusion
  62.0 1.0 constant_dynamic-update-slice_fusion.2.refs_1_
  63.0 0.0 collective-permute-start.8
  63.1 1.0 collective-permute-start.9
  64.1 0.1 copy.11
  64.1 0.6 reshape.656.offset_ref
  64.7 1.0 collective-permute-start.11
  65.8 0.0 collective-permute-done.3.refs_2_
  65.8 1.5 collective-permute-start.12
  67.3 0.0 collective-permute-done.5.refs_4_
  67.3 0.0 all-to-all-done.picked_ref.code_ref.refs_2_
  67.3 24.8 %embed_windows.1 = (bf16[1536,1280]{1,0:T(8,128)(2,1)}, bf16[1536,1280]{1,0:T(8,128)(2,1)}, bf16[1536,640]{1,0:T(8,128)(2,1)}) custom-call(s32[24]{0:T(128)} %reshape.656.offset_ref, bf16[4,400,640]{2,1,0:T(8,128)(2,1)} %all-to-all-done.picked_ref.code_ref.refs_2_, bf16[4,400,640]{2,1,0:T(8,128)(2,1)} %all-to-all-done.picked_ref.code_ref.refs_2_, ...), custom_call_target="tpu_custom_call" | custom-call | flops 10066329600 | bytes 10649600 | tf_op jit(solution)/shard_map/embed_windows/pallas_call | solution.py:423
  92.1 0.0 collective-permute-done.9.refs_3_
  92.1 0.1 collective-permute-start.10
  92.2 3.2 %collective-permute-done.11.refs_5_ = bf16[320,1280]{1,0:T(8,128)(2,1)S(1)} collective-permute-done((bf16[320,1280]{1,0:T(8,128)(2,1)S(1)}, bf16[320,1280]{1,0:T(8,128)(2,1)S(1)}, u32[]{:S(2)}, u32[]{:S(2)}) %collective-permute-start.11) | collective-permute-done | bytes 819232 | tf_op jit(solution)/shard_map/ppermute | solution.py:464
  95.4 0.0 collective-permute-done.12.refs_6_
  95.4 1.1 collective-permute-start.14
  96.4 1.2 collective-permute-start.15
  97.6 0.1 broadcast_select_fusion.1
  97.7 1.4 collective-permute-start.13
  99.1 0.0 collective-permute-done.8.refs_2_
  99.1 0.0 collective-permute-done.10.refs_4_
  99.1 1.0 copy-done.10
  100.1 25.9 %windows_out.1.refs_0_ = bf16[1536,1280]{1,0:T(8,128)(2,1)} custom-call(s32[24]{0:T(128)} %reshape.656.offset_ref, bf16[1536,1280]{1,0:T(8,128)(2,1)} %get-tuple-element.56.embedded_ref, bf16[1536,1280]{1,0:T(8,128)(2,1)} %get-tuple-element.57.normed_ref, bf16[1536,640]{1,0:T(8,128)(2,1)} %get-tuple-element.58.mix_ref, ...), custom_call_target="tpu_custom_call" | custom-call | flops 12582912000 | bytes 20070400 | tf_op jit(solution)/shard_map/windows_out/pallas_call | solution.py:423
  126.0 0.0 collective-permute-done.14.refs_9_
  126.0 0.0 collective-permute-done.15.refs_10_
  126.1 0.1 collective-permute-start.16
  126.2 0.7 collective-permute-start.17
  126.9 0.6 stack.87.offset_ref
  127.6 0.1 convert_element_type.14
  127.6 0.9 copy.12.refs_3_
  128.6 5.6 %collective-permute-done.17.refs_11_ = bf16[320,640]{1,0:T(8,128)(2,1)S(1)} collective-permute-done((bf16[320,640]{1,0:T(8,128)(2,1)S(1)}, bf16[320,640]{1,0:T(8,128)(2,1)S(1)}, u32[]{:S(2)}, u32[]{:S(2)}) %collective-permute-start.17) | collective-permute-done | bytes 409632 | tf_op jit(solution)/shard_map/ppermute | solution.py:470
  134.2 0.7 copy-done.13
  135.0 37.6 %groups.1 = bf16[768,640]{1,0:T(8,128)(2,1)} custom-call(s32[5]{0:T(128)} %stack.87.offset_ref, bf16[1536,1280]{1,0:T(8,128)(2,1)} %windows_out.1.refs_0_, bf16[1536,1280]{1,0:T(8,128)(2,1)} %collective-permute-done.16.refs_1_, bf16[4,400,640]{2,1,0:T(8,128)(2,1)} %all-to-all-done.picked_ref.code_ref.refs_2_, f32[768,1]{1,0:T(8,128)} %copy.12.refs_3_, ...), custom_call_target="tpu_custom_call" | custom-call | flops 17364418560 | bytes 14830592 | tf_op jit(solution)/shard_map/groups/pallas_call | solution.py:423
  172.6 1.3 fusion.3
  173.8 0.1 collective-permute-start.18
  173.9 1.9 %collective-permute-done.18 = bf16[384,640]{1,0:T(8,128)(2,1)S(1)} collective-permute-done((bf16[384,640]{1,0:T(8,128)(2,1)S(1)}, bf16[384,640]{1,0:T(8,128)(2,1)S(1)}, u32[]{:S(2)}, u32[]{:S(2)}) %collective-permute-start.18) | collective-permute-done | bytes 491552 | tf_op jit(solution)/shard_map/ppermute | solution.py:457
  175.8 1.2 maximum_select_fusion
  (36 shorter events, 0.2 us)
Async XLA Ops:
  0.0 8.3 %copy-start.9 = (s32[1,2,3,64]{3,1,2,0:T(2,128)S(1)}, s32[1,2,3,64]{3,1,2,0:T(2,128)}, u32[]{:S(2)}) copy-start(s32[1,2,3,64]{3,1,2,0:T(2,128)} %param.8) | copy-start | bytes 4612
  0.0 8.3 %copy-start.14 = (s32[1,2,3]{2,1,0:T(2,128)S(1)}, s32[1,2,3]{2,1,0:T(2,128)}, u32[]{:S(2)}) copy-start(s32[1,2,3]{2,1,0:T(2,128)} %param.9) | copy-start | bytes 76
  3.8 21.4 %collective-permute-start.1 = (bf16[160,2560]{1,0:T(8,128)(2,1)}, bf16[160,2560]{1,0:T(8,128)(2,1)S(1)}, u32[]{:S(2)}, u32[]{:S(2)}) collective-permute-start(bf16[160,2560]{1,0:T(8,128)(2,1)} %get-tuple-element.39), channel_id=1, source_target_pairs={{0,8},{8,0},{16,24},{24,16},{1,9},{9,1},{17,25},{25,17},{2,10},{10... | collective-permute-start | bytes 2457608 | tf_op jit(solution)/shard_map/ppermute | solution.py:464
  6.8 19.9 %collective-permute-start.2 = (bf16[160,2560]{1,0:T(8,128)(2,1)}, bf16[160,2560]{1,0:T(8,128)(2,1)S(1)}, u32[]{:S(2)}, u32[]{:S(2)}) collective-permute-start(bf16[160,2560]{1,0:T(8,128)(2,1)} %get-tuple-element.39), channel_id=1, source_target_pairs={{0,16},{8,24},{16,0},{24,8},{1,17},{9,25},{17,1},{25,9},{2,18},{10... | collective-permute-start | bytes 2457608 | tf_op jit(solution)/shard_map/ppermute | solution.py:465
  8.5 1.2 copy-start.5
  8.5 1.2 collective-permute-start
  9.6 0.6 copy-start.7
  13.2 54.1 %all-to-all-start = ((bf16[4,400,640]{2,1,0:T(8,128)(2,1)}), bf16[4,400,640]{2,1,0:T(8,128)(2,1)}, u32[]{:S(2)}, u32[]{:S(2)}) async-start(bf16[4,400,640]{2,1,0:T(8,128)(2,1)} %pick.1), calls=%async_computation | async-start | bytes 4096000 | tf_op jit(solution)/shard_map/all_to_all | solution.py:527
  25.2 1.5 copy-start
  26.7 33.7 %collective-permute-start.6 = (bf16[160,3200]{1,0:T(8,128)(2,1)}, bf16[160,3200]{1,0:T(8,128)(2,1)S(1)}, u32[]{:S(2)}, u32[]{:S(2)}) collective-permute-start(bf16[160,3200]{1,0:T(8,128)(2,1)} %get-tuple-element.50), channel_id=1, source_target_pairs={{0,8},{8,0},{16,24},{24,16},{1,9},{9,1},{17,25},{25,17},{2,10},{10... | collective-permute-start | bytes 3072008 | tf_op jit(solution)/shard_map/ppermute | solution.py:464
  27.9 32.5 %collective-permute-start.7 = (bf16[160,3200]{1,0:T(8,128)(2,1)}, bf16[160,3200]{1,0:T(8,128)(2,1)S(1)}, u32[]{:S(2)}, u32[]{:S(2)}) collective-permute-start(bf16[160,3200]{1,0:T(8,128)(2,1)} %get-tuple-element.50), channel_id=1, source_target_pairs={{0,16},{8,24},{16,0},{24,8},{1,17},{9,25},{17,1},{25,9},{2,18},{10... | collective-permute-start | bytes 3072008 | tf_op jit(solution)/shard_map/ppermute | solution.py:465
  31.9 27.6 %collective-permute-start.4 = (bf16[160,2560]{1,0:T(8,128)(2,1)}, bf16[160,2560]{1,0:T(8,128)(2,1)}, u32[]{:S(2)}, u32[]{:S(2)}) collective-permute-start(bf16[160,2560]{1,0:T(8,128)(2,1)} %get-tuple-element.80), channel_id=1, source_target_pairs={{0,8},{4,20},{8,0},{12,28},{16,24},{20,4},{24,16},{28,12},{1,9},{5... | collective-permute-start | bytes 2457608 | tf_op jit(solution)/shard_map/ppermute | solution.py:470
  33.9 31.9 %collective-permute-start.3 = (bf16[320,2560]{1,0:T(8,128)(2,1)}, bf16[320,2560]{1,0:T(8,128)(2,1)}, u32[]{:S(2)}, u32[]{:S(2)}) collective-permute-start(bf16[320,2560]{1,0:T(8,128)(2,1)} %constant_dynamic-update-slice_fusion.refs_1_), channel_id=1, source_target_pairs={{0,4},{4,0},{1,5},{5,1},{2,6},{6,2},{3,7},{7,3},{8,12},{12,8},{9,1... | collective-permute-start | bytes 4915208 | tf_op jit(solution)/shard_map/ppermute | solution.py:457
  59.5 7.8 %collective-permute-start.5 = (bf16[160,2560]{1,0:T(8,128)(2,1)}, bf16[160,2560]{1,0:T(8,128)(2,1)}, u32[]{:S(2)}, u32[]{:S(2)}) collective-permute-start(bf16[160,2560]{1,0:T(8,128)(2,1)} %collective-permute-done.4.refs_3_), channel_id=1, source_target_pairs={{0,4},{4,0},{1,5},{5,1},{2,6},{6,2},{3,7},{7,3},{8,12},{12,8},{9,1... | collective-permute-start | bytes 2457608 | tf_op jit(solution)/shard_map/ppermute | solution.py:457
  62.0 2.7 %copy-start.11 = (bf16[320,1280]{1,0:T(8,128)(2,1)S(1)}, bf16[320,1280]{1,0:T(8,128)(2,1)}, u32[]{:S(2)}) copy-start(bf16[320,1280]{1,0:T(8,128)(2,1)} %get-tuple-element.61.refs_4_) | copy-start | bytes 2457604
  63.0 36.1 %collective-permute-start.8 = (bf16[320,3200]{1,0:T(8,128)(2,1)}, bf16[320,3200]{1,0:T(8,128)(2,1)}, u32[]{:S(2)}, u32[]{:S(2)}) collective-permute-start(bf16[320,3200]{1,0:T(8,128)(2,1)} %constant_dynamic-update-slice_fusion.2.refs_1_), channel_id=1, source_target_pairs={{0,4},{4,0},{1,5},{5,1},{2,6},{6,2},{3,7},{7,3},{8,12},{12,8},{9,1... | collective-permute-start | bytes 6144008 | tf_op jit(solution)/shard_map/ppermute | solution.py:457
  63.1 29.0 %collective-permute-start.9 = (bf16[160,3200]{1,0:T(8,128)(2,1)}, bf16[160,3200]{1,0:T(8,128)(2,1)}, u32[]{:S(2)}, u32[]{:S(2)}) collective-permute-start(bf16[160,3200]{1,0:T(8,128)(2,1)} %get-tuple-element.76), channel_id=1, source_target_pairs={{0,8},{4,20},{8,0},{12,28},{16,24},{20,4},{24,16},{28,12},{1,9},{5... | collective-permute-start | bytes 3072008 | tf_op jit(solution)/shard_map/ppermute | solution.py:470
  64.7 30.6 %collective-permute-start.11 = (bf16[320,1280]{1,0:T(8,128)(2,1)S(1)}, bf16[320,1280]{1,0:T(8,128)(2,1)S(1)}, u32[]{:S(2)}, u32[]{:S(2)}) collective-permute-start(bf16[320,1280]{1,0:T(8,128)(2,1)S(1)} %copy-done.11), channel_id=1, source_target_pairs={{0,8},{8,0},{16,24},{24,16},{1,9},{9,1},{17,25},{25,17},{2,10},{10... | collective-permute-start | bytes 2457608 | tf_op jit(solution)/shard_map/ppermute | solution.py:464
  65.8 29.6 %collective-permute-start.12 = (bf16[320,1280]{1,0:T(8,128)(2,1)S(1)}, bf16[320,1280]{1,0:T(8,128)(2,1)S(1)}, u32[]{:S(2)}, u32[]{:S(2)}) collective-permute-start(bf16[320,1280]{1,0:T(8,128)(2,1)S(1)} %copy-done.11), channel_id=1, source_target_pairs={{0,16},{8,24},{16,0},{24,8},{1,17},{9,25},{17,1},{25,9},{2,18},{10... | collective-permute-start | bytes 2457608 | tf_op jit(solution)/shard_map/ppermute | solution.py:465
  92.1 7.1 %collective-permute-start.10 = (bf16[160,3200]{1,0:T(8,128)(2,1)}, bf16[160,3200]{1,0:T(8,128)(2,1)S(1)}, u32[]{:S(2)}, u32[]{:S(2)}) collective-permute-start(bf16[160,3200]{1,0:T(8,128)(2,1)} %collective-permute-done.9.refs_3_), channel_id=1, source_target_pairs={{0,4},{4,0},{1,5},{5,1},{2,6},{6,2},{3,7},{7,3},{8,12},{12,8},{9,1... | collective-permute-start | bytes 3072008 | tf_op jit(solution)/shard_map/ppermute | solution.py:457
  95.4 30.6 %copy-start.1 = (bf16[320,1280]{1,0:T(8,128)(2,1)}, bf16[320,1280]{1,0:T(8,128)(2,1)S(1)}, u32[]{:S(2)}) copy-start(bf16[320,1280]{1,0:T(8,128)(2,1)S(1)} %collective-permute-done.11.refs_5_) | copy-start | bytes 2457604
  95.4 30.6 %copy-start.2 = (bf16[320,1280]{1,0:T(8,128)(2,1)}, bf16[320,1280]{1,0:T(8,128)(2,1)S(1)}, u32[]{:S(2)}) copy-start(bf16[320,1280]{1,0:T(8,128)(2,1)S(1)} %collective-permute-done.12.refs_6_) | copy-start | bytes 2457604
  95.4 30.6 %collective-permute-start.14 = (bf16[320,640]{1,0:T(8,128)(2,1)}, bf16[320,640]{1,0:T(8,128)(2,1)S(1)}, u32[]{:S(2)}, u32[]{:S(2)}) collective-permute-start(bf16[320,640]{1,0:T(8,128)(2,1)} %get-tuple-element.70.refs_8_), channel_id=1, source_target_pairs={{0,8},{8,0},{16,24},{24,16},{1,9},{9,1},{17,25},{25,17},{2,10},{10... | collective-permute-start | bytes 1228808 | tf_op jit(solution)/shard_map/ppermute | solution.py:464
  96.4 29.6 %collective-permute-start.15 = (bf16[320,640]{1,0:T(8,128)(2,1)}, bf16[320,640]{1,0:T(8,128)(2,1)S(1)}, u32[]{:S(2)}, u32[]{:S(2)}) collective-permute-start(bf16[320,640]{1,0:T(8,128)(2,1)} %get-tuple-element.70.refs_8_), channel_id=1, source_target_pairs={{0,16},{8,24},{16,0},{24,8},{1,17},{9,25},{17,1},{25,9},{2,18},{10... | collective-permute-start | bytes 1228808 | tf_op jit(solution)/shard_map/ppermute | solution.py:465
  97.7 28.3 %collective-permute-start.13 = (bf16[320,1280]{1,0:T(8,128)(2,1)S(1)}, bf16[320,1280]{1,0:T(8,128)(2,1)S(1)}, u32[]{:S(2)}, u32[]{:S(2)}) collective-permute-start(bf16[320,1280]{1,0:T(8,128)(2,1)S(1)} %broadcast_select_fusion.1), channel_id=1, source_target_pairs={{0,8},{4,20},{8,0},{12,28},{16,24},{20,4},{24,16},{28,12},{1,9},{5... | collective-permute-start | bytes 2457608 | tf_op jit(solution)/shard_map/ppermute | solution.py:470
  99.1 1.0 copy-start.10
  100.1 27.4 %copy-start.6 = (s32[6,64]{1,0:T(8,128)S(1)}, s32[6,64]{1,0:T(8,128)}, u32[]{:S(2)}) copy-start(s32[6,64]{1,0:T(8,128)} %copy-done.5) | copy-start | bytes 4612
  100.1 27.4 %copy-start.8 = (s32[6,64]{1,0:T(8,128)S(1)}, s32[6,64]{1,0:T(8,128)}, u32[]{:S(2)}) copy-start(s32[6,64]{1,0:T(8,128)} %copy-done.7) | copy-start | bytes 4612
  126.0 8.2 %copy-start.3 = (bf16[320,640]{1,0:T(8,128)(2,1)}, bf16[320,640]{1,0:T(8,128)(2,1)S(1)}, u32[]{:S(2)}) copy-start(bf16[320,640]{1,0:T(8,128)(2,1)S(1)} %collective-permute-done.14.refs_9_) | copy-start | bytes 1228804
  126.0 8.2 %copy-start.4 = (bf16[320,640]{1,0:T(8,128)(2,1)}, bf16[320,640]{1,0:T(8,128)(2,1)S(1)}, u32[]{:S(2)}) copy-start(bf16[320,640]{1,0:T(8,128)(2,1)S(1)} %collective-permute-done.15.refs_10_) | copy-start | bytes 1228804
  126.1 8.2 %copy-start.12 = (bf16[320,1280]{1,0:T(8,128)(2,1)}, bf16[320,1280]{1,0:T(8,128)(2,1)S(1)}, u32[]{:S(2)}) copy-start(bf16[320,1280]{1,0:T(8,128)(2,1)S(1)} %collective-permute-done.13.refs_7_) | copy-start | bytes 2457604
  126.1 8.2 %collective-permute-start.16 = (bf16[1536,1280]{1,0:T(8,128)(2,1)}, bf16[1536,1280]{1,0:T(8,128)(2,1)}, u32[]{:S(2)}, u32[]{:S(2)}) collective-permute-start(bf16[1536,1280]{1,0:T(8,128)(2,1)} %windows_out.1.refs_0_), channel_id=1, source_target_pairs={{0,4},{4,0},{1,5},{5,1},{2,6},{6,2},{3,7},{7,3},{8,12},{12,8},{9,1... | collective-permute-start | bytes 11796488 | tf_op jit(solution)/shard_map/ppermute | solution.py:457
  126.2 8.0 %collective-permute-start.17 = (bf16[320,640]{1,0:T(8,128)(2,1)S(1)}, bf16[320,640]{1,0:T(8,128)(2,1)S(1)}, u32[]{:S(2)}, u32[]{:S(2)}) collective-permute-start(bf16[320,640]{1,0:T(8,128)(2,1)S(1)} %broadcast_select_fusion.3), channel_id=1, source_target_pairs={{0,8},{4,20},{8,0},{12,28},{16,24},{20,4},{24,16},{28,12},{1,9},{5... | collective-permute-start | bytes 1228808 | tf_op jit(solution)/shard_map/ppermute | solution.py:470
  134.2 0.8 copy-start.13
  173.8 1.9 %collective-permute-start.18 = (bf16[384,640]{1,0:T(8,128)(2,1)S(1)}, bf16[384,640]{1,0:T(8,128)(2,1)S(1)}, u32[]{:S(2)}, u32[]{:S(2)}) collective-permute-start(bf16[384,640]{1,0:T(8,128)(2,1)S(1)} %get-tuple-element.79), channel_id=1, source_target_pairs={{0,4},{4,0},{1,5},{5,1},{2,6},{6,2},{3,7},{7,3},{8,12},{12,8},{9,1... | collective-permute-start | bytes 1474568 | tf_op jit(solution)/shard_map/ppermute | solution.py:457

commit v6 on v5

--- a/solution.py
+++ b/solution.py
@@ -13,7 +13,7 @@
 
 norm_eps = 1e-05
 mask_floor = -1e30
-vmem_limit = 56 * 1024 * 1024
+vmem_limit = 60 * 1024 * 1024
 exp2_scale = HD ** (-0.5) * 1.4426950408889634
 
 
@@ -133,7 +133,7 @@
 
 def whole_block(array):
     zeros = (0,) * array.ndim
-    return pl.BlockSpec(array.shape, lambda *_: zeros)
+    return pl.BlockSpec(array.shape, lambda *_: zeros, pipeline_mode=pl.Buffered(1))
 
 
 def parts_of(pieces, high):
@@ -179,10 +179,9 @@
             sent_ref[copy] = sent_ref[0]
 
 
-def pack_columns(group, weight_ref, full_ref):
-    inner = weight_ref.shape[1] // 3
-    for which in range(3):
-        reorder(weight_ref, which * inner + group * WIDE, full_ref, which * WIDE)
+def pack_columns(column_refs, full_ref):
+    for which, column_ref in enumerate(column_refs):
+        reorder(column_ref, 0, full_ref, which * WIDE)
 
 
 def own_half(core_ref, full_ref, half_ref):
@@ -190,8 +189,8 @@
     half_ref[...] = full_ref[pl.ds(pl.multiple_of(core_ref[0] * half, 16), half), :]
 
 
-def pack_first_kernel(core_ref, weight_ref, embed_ref, full_ref, half_ref):
-    pack_columns(0, weight_ref, full_ref)
+def pack_first_kernel(core_ref, query_ref, key_ref, value_ref, embed_ref, full_ref, half_ref):
+    pack_columns((query_ref, key_ref, value_ref), full_ref)
     quarter = half_ref.shape[0] // 2
     wide = embed_ref.shape[1] // 2
     for at in range(4):
@@ -202,8 +201,8 @@
     own_half(core_ref, full_ref, half_ref)
 
 
-def pack_second_kernel(core_ref, weight_ref, out_ref, full_ref, half_ref):
-    pack_columns(1, weight_ref, full_ref)
+def pack_second_kernel(core_ref, query_ref, key_ref, value_ref, out_ref, full_ref, half_ref):
+    pack_columns((query_ref, key_ref, value_ref), full_ref)
     full_ref[:, pl.ds(3 * WIDE, out_ref.shape[1])] = out_ref[...]
     own_half(core_ref, full_ref, half_ref)
 
@@ -469,19 +468,29 @@
         forwarded = jnp.where(core == 0, along_y, along_x)
         return lax.ppermute(forwarded, ("batch", "lat"), diagonal)
 
+    def across_of(joined):
+        forwarded = lax.dynamic_slice_in_dim(joined, (1 - core) * half, half, axis=0)
+        return lax.ppermute(forwarded, ("batch", "lat"), diagonal)
+
     high = local_qkv.shape[0]
     half = high // 2
     first_wide = 3 * WIDE + width // 2
     second_wide = 3 * WIDE + width
 
-    def pack(kernel, scalar, other, wide, name):
+    def pack(kernel, group, scalar, other, wide, name):
         shapes = [(high, wide), (half, wide)]
         return run(
             kernel,
             1,
             scalar,
-            [whole_block(local_qkv), whole_block(other)],
-            [local_qkv, other],
+            [
+                *[
+                    pl.BlockSpec((high, WIDE), lambda i, c, at=2 * which + group: (0, at))
+                    for which in range(3)
+                ],
+                whole_block(other),
+            ],
+            [local_qkv] * 3 + [other],
             shapes,
             [pl.BlockSpec(shape, lambda *_: (0, 0)) for shape in shapes],
             [],
@@ -490,7 +499,7 @@
         )
 
     local_first, half_first = pack(
-        pack_first_kernel, core_scalar, embed_weight, first_wide, "pack_first"
+        pack_first_kernel, 0, core_scalar, embed_weight, first_wide, "pack_first"
     )
 
     parts = 1
@@ -527,7 +536,7 @@
         got.append(lax.all_to_all(value, "lon", 0, 0, tiled=True))
 
     local_second, half_second = pack(
-        pack_second_kernel, after(core_scalar, sent), local_out, second_wide, "pack_second"
+        pack_second_kernel, 1, after(core_scalar, sent), local_out, second_wide, "pack_second"
     )
     global_first, global_second = run(
         prepare_global_kernel,
@@ -547,13 +556,15 @@
     sides_first = sides(half_first)
     sides_first = after(sides_first, (sent, global_first))
     sides_second = sides(after(half_second, sides_first))
-    across_first = across(*sides_first)
+    joined_first = lax.optimization_barrier(jnp.concatenate(sides_first, axis=0))
+    across_first = across_of(joined_first)
     global_sides = sides(after(global_first, sides_second))
-    across_second = across(*sides_second)
-
-    def shared(shard, got, earlier):
-        joined = jnp.concatenate(got[:2], axis=0)
-        pieces = [shard, joined, other_core(joined), got[2], other_core(after(got[2], earlier))]
+    joined_second = lax.optimization_barrier(jnp.concatenate(sides_second, axis=0))
+    across_second = across_of(joined_second)
+
+    def shared(shard, joined, diagonal_part, earlier):
+        pieces = [shard, joined, other_core(joined), diagonal_part]
+        pieces.append(other_core(after(diagonal_part, earlier)))
         bases = [(chip ^ which) * high for which in (1, 2, 3)]
         firsts = [chip * high, chip * high + half]
         for group in (bases[:2], bases[2:]):
@@ -566,7 +577,7 @@
         tail = group_start + GROUP * MAIN + head % GROUP * TAIL
         return pieces, jnp.stack([firsts, main, tail], axis=1).reshape(-1)
 
-    shared_by = 2 if lon_size % 2 == 0 else 1
+    shared_by = 1
     block = shared_by * part_rows
     steps = lon_size // shared_by
     many_rows = lon_size * part_rows
@@ -575,11 +586,11 @@
     row_spec = lambda wide: pl.BlockSpec((block, wide), lambda i, _: (i, 0))
     tile_spec = pl.BlockSpec((shared_by, code_tile, MAIN), lambda i, _: (i, part_rows // code_tile, 0))
 
-    pieces, offsets = shared(local_first, [*sides_first, across_first], core_scalar)
+    pieces, offsets = shared(local_first, joined_first, across_first, core_scalar)
     embedded, normed, mixes = [], [], []
     for which in range(parts):
         if which == parts - 1:
-            pieces = after(pieces, (sides_second, mixes))
+            pieces = after(pieces, (joined_second, mixes))
         result = run(
             functools.partial(embed_window_kernel, mix),
             steps,
@@ -599,7 +610,7 @@
         for values, value in zip((embedded, normed, mixes), result):
             values.append(value)
 
-    pieces, offsets = shared(local_second, [*sides_second, across_second], mixes[0])
+    pieces, offsets = shared(local_second, joined_second, across_second, mixes[0])
     own, partner = [], []
     for which in range(parts):
         if which == parts - 1:

time: 177 us -> 176 us (level)
  waiting for transfers between devices: 39 us -> 41.4 us
  starting transfers between devices: 21.9 us -> 19.7 us
    ppermute x0 -> x2, waiting for transfers between devices: none -> 27.3 us  [across_of(): return lax.ppermute(forwarded, ('batch', 'lat'), diagonal)]
    ppermute x4 -> x2, waiting for transfers between devices: 31.2 us -> 5.62 us  [across(): return lax.ppermute(forwarded, ('batch', 'lat'), diagonal)]
    select_n x4 -> x2, other arithmetic: 4.28 us -> 1.29 us  [across(): forwarded = jnp.where(core == 0, along_y, along_x)]
    concatenate x0 -> x2, other arithmetic: none -> 2.67 us  [the longest x1 1.36 us: sample_body(): jnp.concatenate(sides_second, axis=0)]
    ppermute x0 -> x2, starting transfers between devices: none -> 2.22 us  [across_of(): return lax.ppermute(forwarded, ('batch', 'lat'), diagonal)]
    concatenate x2 -> x0, local copies, waits for them, and re-layouts: 1.99 us -> none  [shared(): joined = jnp.concatenate(got[:2], axis=0)]
    ppermute x4 -> x2, starting transfers between devices: 4 us -> 2.15 us  [across(): return lax.ppermute(forwarded, ('batch', 'lat'), diagonal)]
  transfers between devices with their start and end apart: 20 -> 20, of which waited for: 7 -> 7; matrix products, arithmetic and copies ran while one was open for 5% -> 5% of each run, Pallas kernels for 34% -> 35%
where the time goes in v6:
time: 176 us; the launch traced here: 175 us
  Pallas kernels  102 us (58%)
  waiting for transfers between devices  41.4 us (24%)
  starting transfers between devices  19.7 us (11%)
  local copies, waits for them, and re-layouts  6.51 us (4%)
  other arithmetic  5.26 us (3%)
    pallas_call x7, Pallas kernels, run(): pl.pallas_call(kernel, grid_spec=pltpu.PrefetchScalarGridSpec(num_scalar_...  102 us
    ppermute x2, waiting for transfers between devices, across_of(): return lax.ppermute(forwarded, ('batch', 'lat'), diagonal)  27.3 us
    ppermute x2, waiting for transfers between devices, across(): return lax.ppermute(forwarded, ('batch', 'lat'), diagonal)  5.62 us
    ppermute x4, starting transfers between devices, sides(): along_x = lax.ppermute(part, 'batch', swap_perm(batch_size, 1))  5.5 us
    all_to_all x1, starting transfers between devices, sample_body(): got.append(lax.all_to_all(value, 'lon', 0, 0, tiled=True))  4.87 us
    ppermute x4, starting transfers between devices, sides(): along_y = lax.ppermute(part, 'batch', swap_perm(batch_size, 2))  4.11 us
    ppermute x4, waiting for transfers between devices, sides(): along_x = lax.ppermute(part, 'batch', swap_perm(batch_size, 1))  4.03 us
  transfers between devices with their start and end apart: 20, of which 7 were waited for; matrix products, arithmetic and copies ran while one was open for 5% of the time, Pallas kernels for 35%

profile of v6, /device:TPU:0, one launch (start us, length us, event | category | flops | bytes accessed | tf_op | source)
XLA Modules:
  0.0 175.1 jit_solution(6125543416242344456)
XLA Ops:
  0.0 3.5 %pack_first.1 = (bf16[320,2560]{1,0:T(8,128)(2,1)}, bf16[160,2560]{1,0:T(8,128)(2,1)}) custom-call(s32[1]{0:T(128)} %bitcast.5.core_ref._, bf16[320,3840]{1,0:T(8,128)(2,1)} %value_ref.4, bf16[320,3840]{1,0:T(8,128)(2,1)} %value_ref.4, bf16[320,3840]{1,0:T(8,128)(2,1)} %value_ref.4, bf16[160,1280]{1,0:T(8,128)(2,1)} %embed_ref.1), custom_call_target="tpu_custom_call" | custom-call | bytes 7782400 | tf_op jit(solution)/shard_map/pack_first/pallas_call | solution.py:422
  3.5 2.9 %collective-permute-start.1 = (bf16[160,2560]{1,0:T(8,128)(2,1)}, bf16[160,2560]{1,0:T(8,128)(2,1)S(1)}, u32[]{:S(2)}, u32[]{:S(2)}) collective-permute-start(bf16[160,2560]{1,0:T(8,128)(2,1)} %get-tuple-element.39), channel_id=1, source_target_pairs={{0,8},{8,0},{16,24},{24,16},{1,9},{9,1},{17,25},{25,17},{2,10},{10... | collective-permute-start | bytes 2457608 | tf_op jit(solution)/shard_map/ppermute | solution.py:463
  6.4 1.5 collective-permute-start.2
  7.9 0.1 lt.26
  8.0 0.1 fusion.code_ref
  8.1 0.0 collective-permute-start
  8.1 1.2 collective-permute-done.partner_ref
  9.3 0.6 copy-done.5
  9.9 2.9 %pick.1 = bf16[4,400,640]{2,1,0:T(8,128)(2,1)} custom-call(s32[1]{0:T(128)} %bitcast.5.core_ref._, bf16[6,128,640]{2,1,0:T(8,128)(2,1)} %bitcast.26, s32[6,64]{1,0:T(8,128)} %copy-done.3, s32[6,64]{1,0:T(8,128)} %copy-done.5), custom_call_target="tpu_custom_call" | custom-call | bytes 986112 | tf_op jit(solution)/shard_map/pick/pallas_call | solution.py:422
  12.7 4.9 %all-to-all-start = ((bf16[4,400,640]{2,1,0:T(8,128)(2,1)}), bf16[4,400,640]{2,1,0:T(8,128)(2,1)}, u32[]{:S(2)}, u32[]{:S(2)}) async-start(bf16[4,400,640]{2,1,0:T(8,128)(2,1)} %pick.1), calls=%async_computation | async-start | bytes 4096000 | tf_op jit(solution)/shard_map/all_to_all | solution.py:536
  17.6 3.9 %pack_second.1 = (bf16[320,3200]{1,0:T(8,128)(2,1)}, bf16[160,3200]{1,0:T(8,128)(2,1)}) custom-call(s32[1]{0:T(128)} %bitcast.5.core_ref._, bf16[320,3840]{1,0:T(8,128)(2,1)} %value_ref.4, bf16[320,3840]{1,0:T(8,128)(2,1)} %value_ref.4, bf16[320,3840]{1,0:T(8,128)(2,1)} %value_ref.4, bf16[320,1280]{1,0:T(8,128)(2,1)} %out_ref.1), custom_call_target="tpu_custom_call" | custom-call | bytes 8192000 | tf_op jit(solution)/shard_map/pack_second/pallas_call | solution.py:422
  21.5 2.8 %order_global.1 = (bf16[320,1280]{1,0:T(8,128)(2,1)}, bf16[320,640]{1,0:T(8,128)(2,1)}) custom-call(s32[1]{0:T(128)} %bitcast.5.core_ref._, bf16[320,3840]{1,0:T(8,128)(2,1)} %value_ref.5, bf16[320,3840]{1,0:T(8,128)(2,1)} %value_ref.5, bf16[320,3840]{1,0:T(8,128)(2,1)} %value_ref.5), custom_call_target="tpu_custom_call" | custom-call | bytes 7372800 | tf_op jit(solution)/shard_map/order_global/pallas_call | solution.py:422
  24.4 0.5 collective-permute-done.1
  24.9 1.5 collective-permute-done.2
  26.3 1.5 collective-permute-start.7
  27.8 0.5 collective-permute-start.6
  28.4 1.3 pad_maximum_fusion.1.refs_1_
  29.7 1.2 constant_dynamic-slice_fusion.1
  30.9 1.6 collective-permute-start.4
  32.4 0.0 collective-permute-start.3
  32.5 0.1 stack.105
  32.6 0.1 stack.95
  32.7 27.3 %collective-permute-done.4.refs_3_ = bf16[160,2560]{1,0:T(8,128)(2,1)} collective-permute-done((bf16[160,2560]{1,0:T(8,128)(2,1)S(1)}, bf16[160,2560]{1,0:T(8,128)(2,1)}, u32[]{:S(2)}, u32[]{:S(2)}) %collective-permute-start.4) | collective-permute-done | bytes 819232 | tf_op jit(solution)/shard_map/ppermute | solution.py:473
  59.9 0.0 collective-permute-start.5
  59.9 0.0 collective-permute-done.7
  60.0 0.0 collective-permute-done.6
  60.0 1.4 pad_maximum_fusion.refs_1_
  61.3 0.6 collective-permute-start.8
  61.9 0.1 constant_dynamic-slice_fusion
  62.0 0.7 collective-permute-start.9
  62.7 0.1 copy.11
  62.7 0.6 reshape.656.offset_ref
  63.3 1.4 collective-permute-start.11
  64.8 0.0 collective-permute-done.3.refs_2_
  64.8 0.5 collective-permute-start.12
  65.3 0.0 collective-permute-done.5.refs_4_
  65.3 0.0 all-to-all-done.picked_ref.code_ref.refs_2_
  65.3 25.3 %embed_windows.1 = (bf16[1536,1280]{1,0:T(8,128)(2,1)}, bf16[1536,1280]{1,0:T(8,128)(2,1)}, bf16[1536,640]{1,0:T(8,128)(2,1)}) custom-call(s32[24]{0:T(128)} %reshape.656.offset_ref, bf16[4,400,640]{2,1,0:T(8,128)(2,1)} %all-to-all-done.picked_ref.code_ref.refs_2_, bf16[4,400,640]{2,1,0:T(8,128)(2,1)} %all-to-all-done.picked_ref.code_ref.refs_2_, ...), custom_call_target="tpu_custom_call" | custom-call | flops 10066329600 | bytes 10649600 | tf_op jit(solution)/shard_map/embed_windows/pallas_call | solution.py:422
  90.6 0.0 collective-permute-done.9.refs_3_
  90.6 0.1 collective-permute-start.10
  90.7 3.5 %collective-permute-done.11.refs_5_ = bf16[320,1280]{1,0:T(8,128)(2,1)} collective-permute-done((bf16[320,1280]{1,0:T(8,128)(2,1)}, bf16[320,1280]{1,0:T(8,128)(2,1)}, u32[]{:S(2)}, u32[]{:S(2)}) %collective-permute-start.11) | collective-permute-done | bytes 819232 | tf_op jit(solution)/shard_map/ppermute | solution.py:463
  94.2 0.0 collective-permute-done.12.refs_6_
  94.2 0.6 collective-permute-start.14
  94.8 0.6 collective-permute-start.15
  95.4 1.2 broadcast_select_fusion
  96.6 1.4 collective-permute-start.13
  98.1 0.0 collective-permute-done.8.refs_2_
  98.1 0.0 collective-permute-done.10.refs_4_
  98.1 25.5 %windows_out.1.refs_0_ = bf16[1536,1280]{1,0:T(8,128)(2,1)} custom-call(s32[24]{0:T(128)} %reshape.656.offset_ref, bf16[1536,1280]{1,0:T(8,128)(2,1)} %get-tuple-element.56.embedded_ref, bf16[1536,1280]{1,0:T(8,128)(2,1)} %get-tuple-element.57.normed_ref, bf16[1536,640]{1,0:T(8,128)(2,1)} %get-tuple-element.58.mix_ref, ...), custom_call_target="tpu_custom_call" | custom-call | flops 12582912000 | bytes 20070400 | tf_op jit(solution)/shard_map/windows_out/pallas_call | solution.py:422
  123.6 0.0 collective-permute-done.14.refs_9_
  123.7 0.1 collective-permute-start.16
  123.8 0.1 broadcast_select_fusion.1
  123.8 0.7 collective-permute-start.17
  124.5 0.6 stack.87.offset_ref
  125.2 0.1 convert_element_type.14
  125.3 0.9 copy.12.refs_3_
  126.2 5.6 %collective-permute-done.17.refs_11_ = bf16[320,640]{1,0:T(8,128)(2,1)S(1)} collective-permute-done((bf16[320,640]{1,0:T(8,128)(2,1)S(1)}, bf16[320,640]{1,0:T(8,128)(2,1)S(1)}, u32[]{:S(2)}, u32[]{:S(2)}) %collective-permute-start.17) | collective-permute-done | bytes 409632 | tf_op jit(solution)/shard_map/ppermute | solution.py:469
  131.8 0.0 collective-permute-done.16.refs_1_
  131.9 0.7 copy-done.8
  132.6 38.1 %groups.1 = bf16[768,640]{1,0:T(8,128)(2,1)} custom-call(s32[5]{0:T(128)} %stack.87.offset_ref, bf16[1536,1280]{1,0:T(8,128)(2,1)} %windows_out.1.refs_0_, bf16[1536,1280]{1,0:T(8,128)(2,1)} %collective-permute-done.16.refs_1_, bf16[4,400,640]{2,1,0:T(8,128)(2,1)} %all-to-all-done.picked_ref.code_ref.refs_2_, f32[768,1]{1,0:T(8,128)} %copy.12.refs_3_, ...), custom_call_target="tpu_custom_call" | custom-call | flops 17364418560 | bytes 14830592 | tf_op jit(solution)/shard_map/groups/pallas_call | solution.py:422
  170.7 1.3 fusion.3
  172.0 0.1 collective-permute-start.18
  172.0 1.9 %collective-permute-done.18 = bf16[384,640]{1,0:T(8,128)(2,1)S(1)} collective-permute-done((bf16[384,640]{1,0:T(8,128)(2,1)S(1)}, bf16[384,640]{1,0:T(8,128)(2,1)S(1)}, u32[]{:S(2)}, u32[]{:S(2)}) %collective-permute-start.18) | collective-permute-done | bytes 491552 | tf_op jit(solution)/shard_map/ppermute | solution.py:456
  173.9 1.2 maximum_select_fusion
  (26 shorter events, 0.1 us)
Async XLA Ops:
  0.0 7.9 %copy-start.7 = (s32[1,2,3,64]{3,1,2,0:T(2,128)S(1)}, s32[1,2,3,64]{3,1,2,0:T(2,128)}, u32[]{:S(2)}) copy-start(s32[1,2,3,64]{3,1,2,0:T(2,128)} %param.8) | copy-start | bytes 4612
  0.0 7.9 %copy-start.9 = (s32[1,2,3]{2,1,0:T(2,128)S(1)}, s32[1,2,3]{2,1,0:T(2,128)}, u32[]{:S(2)}) copy-start(s32[1,2,3]{2,1,0:T(2,128)} %param.9) | copy-start | bytes 76
  3.5 21.4 %collective-permute-start.1 = (bf16[160,2560]{1,0:T(8,128)(2,1)}, bf16[160,2560]{1,0:T(8,128)(2,1)S(1)}, u32[]{:S(2)}, u32[]{:S(2)}) collective-permute-start(bf16[160,2560]{1,0:T(8,128)(2,1)} %get-tuple-element.39), channel_id=1, source_target_pairs={{0,8},{8,0},{16,24},{24,16},{1,9},{9,1},{17,25},{25,17},{2,10},{10... | collective-permute-start | bytes 2457608 | tf_op jit(solution)/shard_map/ppermute | solution.py:463
  6.4 19.9 %collective-permute-start.2 = (bf16[160,2560]{1,0:T(8,128)(2,1)}, bf16[160,2560]{1,0:T(8,128)(2,1)S(1)}, u32[]{:S(2)}, u32[]{:S(2)}) collective-permute-start(bf16[160,2560]{1,0:T(8,128)(2,1)} %get-tuple-element.39), channel_id=1, source_target_pairs={{0,16},{8,24},{16,0},{24,8},{1,17},{9,25},{17,1},{25,9},{2,18},{10... | collective-permute-start | bytes 2457608 | tf_op jit(solution)/shard_map/ppermute | solution.py:464
  8.1 1.2 copy-start.3
  8.1 1.2 collective-permute-start
  9.3 0.6 copy-start.5
  12.7 52.5 %all-to-all-start = ((bf16[4,400,640]{2,1,0:T(8,128)(2,1)}), bf16[4,400,640]{2,1,0:T(8,128)(2,1)}, u32[]{:S(2)}, u32[]{:S(2)}) async-start(bf16[4,400,640]{2,1,0:T(8,128)(2,1)} %pick.1), calls=%async_computation | async-start | bytes 4096000 | tf_op jit(solution)/shard_map/all_to_all | solution.py:536
  26.3 33.6 %collective-permute-start.7 = (bf16[160,3200]{1,0:T(8,128)(2,1)}, bf16[160,3200]{1,0:T(8,128)(2,1)S(1)}, u32[]{:S(2)}, u32[]{:S(2)}) collective-permute-start(bf16[160,3200]{1,0:T(8,128)(2,1)} %get-tuple-element.50), channel_id=1, source_target_pairs={{0,16},{8,24},{16,0},{24,8},{1,17},{9,25},{17,1},{25,9},{2,18},{10... | collective-permute-start | bytes 3072008 | tf_op jit(solution)/shard_map/ppermute | solution.py:464
  27.8 32.1 %collective-permute-start.6 = (bf16[160,3200]{1,0:T(8,128)(2,1)}, bf16[160,3200]{1,0:T(8,128)(2,1)}, u32[]{:S(2)}, u32[]{:S(2)}) collective-permute-start(bf16[160,3200]{1,0:T(8,128)(2,1)} %get-tuple-element.50), channel_id=1, source_target_pairs={{0,8},{8,0},{16,24},{24,16},{1,9},{9,1},{17,25},{25,17},{2,10},{10... | collective-permute-start | bytes 3072008 | tf_op jit(solution)/shard_map/ppermute | solution.py:463
  30.9 29.1 %collective-permute-start.4 = (bf16[160,2560]{1,0:T(8,128)(2,1)S(1)}, bf16[160,2560]{1,0:T(8,128)(2,1)}, u32[]{:S(2)}, u32[]{:S(2)}) collective-permute-start(bf16[160,2560]{1,0:T(8,128)(2,1)S(1)} %constant_dynamic-slice_fusion.1), channel_id=1, source_target_pairs={{0,8},{4,20},{8,0},{12,28},{16,24},{20,4},{24,16},{28,12},{1,9},{5... | collective-permute-start | bytes 2457608 | tf_op jit(solution)/shard_map/ppermute | solution.py:473
  32.4 32.3 %collective-permute-start.3 = (bf16[320,2560]{1,0:T(8,128)(2,1)}, bf16[320,2560]{1,0:T(8,128)(2,1)}, u32[]{:S(2)}, u32[]{:S(2)}) collective-permute-start(bf16[320,2560]{1,0:T(8,128)(2,1)} %pad_maximum_fusion.1.refs_1_), channel_id=1, source_target_pairs={{0,4},{4,0},{1,5},{5,1},{2,6},{6,2},{3,7},{7,3},{8,12},{12,8},{9,1... | collective-permute-start | bytes 4915208 | tf_op jit(solution)/shard_map/ppermute | solution.py:456
  59.9 5.3 %collective-permute-start.5 = (bf16[160,2560]{1,0:T(8,128)(2,1)}, bf16[160,2560]{1,0:T(8,128)(2,1)}, u32[]{:S(2)}, u32[]{:S(2)}) collective-permute-start(bf16[160,2560]{1,0:T(8,128)(2,1)} %collective-permute-done.4.refs_3_), channel_id=1, source_target_pairs={{0,4},{4,0},{1,5},{5,1},{2,6},{6,2},{3,7},{7,3},{8,12},{12,8},{9,1... | collective-permute-start | bytes 2457608 | tf_op jit(solution)/shard_map/ppermute | solution.py:456
  61.3 29.3 %copy-start = (bf16[320,3200]{1,0:T(8,128)(2,1)}, bf16[320,3200]{1,0:T(8,128)(2,1)S(1)}, u32[]{:S(2)}) copy-start(bf16[320,3200]{1,0:T(8,128)(2,1)S(1)} %pad_maximum_fusion.refs_1_) | copy-start | bytes 6144004
  61.3 36.7 %collective-permute-start.8 = (bf16[320,3200]{1,0:T(8,128)(2,1)S(1)}, bf16[320,3200]{1,0:T(8,128)(2,1)}, u32[]{:S(2)}, u32[]{:S(2)}) collective-permute-start(bf16[320,3200]{1,0:T(8,128)(2,1)S(1)} %pad_maximum_fusion.refs_1_), channel_id=1, source_target_pairs={{0,4},{4,0},{1,5},{5,1},{2,6},{6,2},{3,7},{7,3},{8,12},{12,8},{9,1... | collective-permute-start | bytes 6144008 | tf_op jit(solution)/shard_map/ppermute | solution.py:456
  62.0 28.6 %collective-permute-start.9 = (bf16[160,3200]{1,0:T(8,128)(2,1)S(1)}, bf16[160,3200]{1,0:T(8,128)(2,1)}, u32[]{:S(2)}, u32[]{:S(2)}) collective-permute-start(bf16[160,3200]{1,0:T(8,128)(2,1)S(1)} %constant_dynamic-slice_fusion), channel_id=1, source_target_pairs={{0,8},{4,20},{8,0},{12,28},{16,24},{20,4},{24,16},{28,12},{1,9},{5... | collective-permute-start | bytes 3072008 | tf_op jit(solution)/shard_map/ppermute | solution.py:473
  63.3 30.9 %collective-permute-start.11 = (bf16[320,1280]{1,0:T(8,128)(2,1)}, bf16[320,1280]{1,0:T(8,128)(2,1)}, u32[]{:S(2)}, u32[]{:S(2)}) collective-permute-start(bf16[320,1280]{1,0:T(8,128)(2,1)} %get-tuple-element.61.refs_4_), channel_id=1, source_target_pairs={{0,8},{8,0},{16,24},{24,16},{1,9},{9,1},{17,25},{25,17},{2,10},{10... | collective-permute-start | bytes 2457608 | tf_op jit(solution)/shard_map/ppermute | solution.py:463
  64.8 29.5 %collective-permute-start.12 = (bf16[320,1280]{1,0:T(8,128)(2,1)}, bf16[320,1280]{1,0:T(8,128)(2,1)}, u32[]{:S(2)}, u32[]{:S(2)}) collective-permute-start(bf16[320,1280]{1,0:T(8,128)(2,1)} %get-tuple-element.61.refs_4_), channel_id=1, source_target_pairs={{0,16},{8,24},{16,0},{24,8},{1,17},{9,25},{17,1},{25,9},{2,18},{10... | collective-permute-start | bytes 2457608 | tf_op jit(solution)/shard_map/ppermute | solution.py:464
  90.6 7.5 %collective-permute-start.10 = (bf16[160,3200]{1,0:T(8,128)(2,1)}, bf16[160,3200]{1,0:T(8,128)(2,1)}, u32[]{:S(2)}, u32[]{:S(2)}) collective-permute-start(bf16[160,3200]{1,0:T(8,128)(2,1)} %collective-permute-done.9.refs_3_), channel_id=1, source_target_pairs={{0,4},{4,0},{1,5},{5,1},{2,6},{6,2},{3,7},{7,3},{8,12},{12,8},{9,1... | collective-permute-start | bytes 3072008 | tf_op jit(solution)/shard_map/ppermute | solution.py:456
  94.2 29.4 %collective-permute-start.14 = (bf16[320,640]{1,0:T(8,128)(2,1)}, bf16[320,640]{1,0:T(8,128)(2,1)S(1)}, u32[]{:S(2)}, u32[]{:S(2)}) collective-permute-start(bf16[320,640]{1,0:T(8,128)(2,1)} %get-tuple-element.70.refs_8_), channel_id=1, source_target_pairs={{0,8},{8,0},{16,24},{24,16},{1,9},{9,1},{17,25},{25,17},{2,10},{10... | collective-permute-start | bytes 1228808 | tf_op jit(solution)/shard_map/ppermute | solution.py:463
  94.8 28.8 %collective-permute-start.15 = (bf16[320,640]{1,0:T(8,128)(2,1)}, bf16[320,640]{1,0:T(8,128)(2,1)S(1)}, u32[]{:S(2)}, u32[]{:S(2)}) collective-permute-start(bf16[320,640]{1,0:T(8,128)(2,1)} %get-tuple-element.70.refs_8_), channel_id=1, source_target_pairs={{0,16},{8,24},{16,0},{24,8},{1,17},{9,25},{17,1},{25,9},{2,18},{10... | collective-permute-start | bytes 1228808 | tf_op jit(solution)/shard_map/ppermute | solution.py:464
  96.6 27.0 %collective-permute-start.13 = (bf16[320,1280]{1,0:T(8,128)(2,1)S(1)}, bf16[320,1280]{1,0:T(8,128)(2,1)}, u32[]{:S(2)}, u32[]{:S(2)}) collective-permute-start(bf16[320,1280]{1,0:T(8,128)(2,1)S(1)} %broadcast_select_fusion), channel_id=1, source_target_pairs={{0,8},{4,20},{8,0},{12,28},{16,24},{20,4},{24,16},{28,12},{1,9},{5... | collective-permute-start | bytes 2457608 | tf_op jit(solution)/shard_map/ppermute | solution.py:469
  98.1 27.1 %copy-start.4 = (s32[6,64]{1,0:T(8,128)S(1)}, s32[6,64]{1,0:T(8,128)}, u32[]{:S(2)}) copy-start(s32[6,64]{1,0:T(8,128)} %copy-done.3) | copy-start | bytes 4612
  98.1 27.1 %copy-start.6 = (s32[6,64]{1,0:T(8,128)S(1)}, s32[6,64]{1,0:T(8,128)}, u32[]{:S(2)}) copy-start(s32[6,64]{1,0:T(8,128)} %copy-done.5) | copy-start | bytes 4612
  123.6 8.2 %copy-start.1 = (bf16[320,640]{1,0:T(8,128)(2,1)}, bf16[320,640]{1,0:T(8,128)(2,1)S(1)}, u32[]{:S(2)}) copy-start(bf16[320,640]{1,0:T(8,128)(2,1)S(1)} %collective-permute-done.14.refs_9_) | copy-start | bytes 1228804
  123.7 8.2 %copy-start.2 = (bf16[320,640]{1,0:T(8,128)(2,1)}, bf16[320,640]{1,0:T(8,128)(2,1)S(1)}, u32[]{:S(2)}) copy-start(bf16[320,640]{1,0:T(8,128)(2,1)S(1)} %collective-permute-done.15.refs_10_) | copy-start | bytes 1228804
  123.7 8.2 %collective-permute-start.16 = (bf16[1536,1280]{1,0:T(8,128)(2,1)}, bf16[1536,1280]{1,0:T(8,128)(2,1)}, u32[]{:S(2)}, u32[]{:S(2)}) collective-permute-start(bf16[1536,1280]{1,0:T(8,128)(2,1)} %windows_out.1.refs_0_), channel_id=1, source_target_pairs={{0,4},{4,0},{1,5},{5,1},{2,6},{6,2},{3,7},{7,3},{8,12},{12,8},{9,1... | collective-permute-start | bytes 11796488 | tf_op jit(solution)/shard_map/ppermute | solution.py:456
  123.8 8.0 %collective-permute-start.17 = (bf16[320,640]{1,0:T(8,128)(2,1)S(1)}, bf16[320,640]{1,0:T(8,128)(2,1)S(1)}, u32[]{:S(2)}, u32[]{:S(2)}) collective-permute-start(bf16[320,640]{1,0:T(8,128)(2,1)S(1)} %broadcast_select_fusion.1), channel_id=1, source_target_pairs={{0,8},{4,20},{8,0},{12,28},{16,24},{20,4},{24,16},{28,12},{1,9},{5... | collective-permute-start | bytes 1228808 | tf_op jit(solution)/shard_map/ppermute | solution.py:469
  131.8 0.8 copy-start.8
  172.0 1.9 %collective-permute-start.18 = (bf16[384,640]{1,0:T(8,128)(2,1)S(1)}, bf16[384,640]{1,0:T(8,128)(2,1)S(1)}, u32[]{:S(2)}, u32[]{:S(2)}) collective-permute-start(bf16[384,640]{1,0:T(8,128)(2,1)S(1)} %get-tuple-element.77), channel_id=1, source_target_pairs={{0,4},{4,0},{1,5},{5,1},{2,6},{6,2},{3,7},{7,3},{8,12},{12,8},{9,1... | collective-permute-start | bytes 1474568 | tf_op jit(solution)/shard_map/ppermute | solution.py:456

commit v7 on v6

--- a/solution.py
+++ b/solution.py
@@ -433,7 +433,7 @@
         ),
         out_shape=[jax.ShapeDtypeStruct(shape, jnp.bfloat16) for shape in outs],
         compiler_params=pltpu.CompilerParams(vmem_limit_bytes=vmem_limit),
-        cost_estimate=pl.CostEstimate(flops=flops, bytes_accessed=moved, transcendentals=0),
+        cost_estimate=pl.CostEstimate(flops=flops, bytes_accessed=moved if flops else 0, transcendentals=0),
         name=name,
     )(scalars, *arrays)
 
@@ -604,7 +604,7 @@
             [(many_rows, width), (many_rows, width), (many_rows, WIDE)],
             [row_spec(width), row_spec(width), row_spec(WIDE)],
             [(width, 3 * WIDE), (pin, width), (block, 3 * WIDE)],
-            2 * many_rows * (pin * width + width * 3 * WIDE),
+            0,
             "embed_windows",
         )
         for values, value in zip((embedded, normed, mixes), result):

time: 176 us -> 174 us (0.989)
  waiting for transfers between devices: 41.4 us -> 33.5 us
  local copies, waits for them, and re-layouts: 6.51 us -> 10.1 us
  other arithmetic: 5.26 us -> 7.91 us
    ppermute x2, waiting for transfers between devices: 27.3 us -> 2.66 us  [across_of(): return lax.ppermute(forwarded, ('batch', 'lat'), diagonal)]
    ppermute x4, waiting for transfers between devices: 1.47 us -> 19.9 us  [sides(): along_y = lax.ppermute(part, 'batch', swap_perm(batch_size, 2))]
    ppermute x4, waiting for transfers between devices: 4.03 us -> 0.55 us  [sides(): along_x = lax.ppermute(part, 'batch', swap_perm(batch_size, 1))]
    unnamed x21 -> x27, local copies, waits for them, and re-layouts: 1.35 us -> 3.7 us
    all_to_all x1, waiting for transfers between devices: 0.01 us -> 2.18 us  [sample_body(): got.append(lax.all_to_all(value, 'lon', 0, 0, tiled=True))]
  transfers between devices with their start and end apart: 20 -> 20, of which waited for: 7 -> 8; matrix products, arithmetic and copies ran while one was open for 5% -> 7% of each run, Pallas kernels for 35% -> 35%
where the time goes in v7:
time: 174 us
  Pallas kernels  102 us (59%)
  waiting for transfers between devices  33.5 us (19%)
  starting transfers between devices  20.1 us (12%)
  local copies, waits for them, and re-layouts  10.1 us (6%)
  other arithmetic  7.91 us (5%)
    pallas_call x7, Pallas kernels, run(): pl.pallas_call(kernel, grid_spec=pltpu.PrefetchScalarGridSpec(num_scalar_...  102 us
    ppermute x4, waiting for transfers between devices, sides(): along_y = lax.ppermute(part, 'batch', swap_perm(batch_size, 2))  19.9 us
    ppermute x4, starting transfers between devices, sides(): along_x = lax.ppermute(part, 'batch', swap_perm(batch_size, 1))  6.13 us
    ppermute x2, waiting for transfers between devices, across(): return lax.ppermute(forwarded, ('batch', 'lat'), diagonal)  5.2 us
    all_to_all x1, starting transfers between devices, sample_body(): got.append(lax.all_to_all(value, 'lon', 0, 0, tiled=True))  4.87 us
    ppermute x4, starting transfers between devices, sides(): along_y = lax.ppermute(part, 'batch', swap_perm(batch_size, 2))  4.06 us
    unnamed x27, local copies, waits for them, and re-layouts  3.7 us
  transfers between devices with their start and end apart: 20, of which 8 were waited for; matrix products, arithmetic and copies ran while one was open for 7% of the time, Pallas kernels for 35%

profile of v7, /device:TPU:0, one launch (start us, length us, event | category | flops | bytes accessed | tf_op | source)
XLA Modules:
  0.0 173.9 jit_solution(9324299096839669988)
XLA Ops:
  0.0 3.5 %pack_first.1 = (bf16[320,2560]{1,0:T(8,128)(2,1)}, bf16[160,2560]{1,0:T(8,128)(2,1)}) custom-call(s32[1]{0:T(128)} %bitcast.5.core_ref._, bf16[320,3840]{1,0:T(8,128)(2,1)} %value_ref.4, bf16[320,3840]{1,0:T(8,128)(2,1)} %value_ref.4, bf16[320,3840]{1,0:T(8,128)(2,1)} %value_ref.4, bf16[160,1280]{1,0:T(8,128)(2,1)} %embed_ref.1), custom_call_target="tpu_custom_call" | custom-call | tf_op jit(solution)/shard_map/pack_first/pallas_call | solution.py:422
  3.5 2.9 %collective-permute-start.1 = (bf16[160,2560]{1,0:T(8,128)(2,1)}, bf16[160,2560]{1,0:T(8,128)(2,1)S(1)}, u32[]{:S(2)}, u32[]{:S(2)}) collective-permute-start(bf16[160,2560]{1,0:T(8,128)(2,1)} %get-tuple-element.39), channel_id=1, source_target_pairs={{0,8},{8,0},{16,24},{24,16},{1,9},{9,1},{17,25},{25,17},{2,10},{10... | collective-permute-start | bytes 2457608 | tf_op jit(solution)/shard_map/ppermute | solution.py:463
  6.4 1.5 collective-permute-start.2
  7.9 0.1 lt.26
  8.0 0.1 fusion.code_ref
  8.1 0.0 collective-permute-start
  8.1 1.2 collective-permute-done.partner_ref
  9.3 0.6 copy-done.6
  9.9 2.9 %pick.1 = bf16[4,400,640]{2,1,0:T(8,128)(2,1)} custom-call(s32[1]{0:T(128)} %bitcast.5.core_ref._, bf16[6,128,640]{2,1,0:T(8,128)(2,1)} %bitcast.26, s32[6,64]{1,0:T(8,128)} %copy-done.4, s32[6,64]{1,0:T(8,128)} %copy-done.6), custom_call_target="tpu_custom_call" | custom-call | tf_op jit(solution)/shard_map/pick/pallas_call | solution.py:422
  12.8 4.9 %all-to-all-start = ((bf16[4,400,640]{2,1,0:T(8,128)(2,1)}), bf16[4,400,640]{2,1,0:T(8,128)(2,1)S(1)}, u32[]{:S(2)}, u32[]{:S(2)}) async-start(bf16[4,400,640]{2,1,0:T(8,128)(2,1)} %pick.1), calls=%async_computation | async-start | bytes 4096000 | tf_op jit(solution)/shard_map/all_to_all | solution.py:536
  17.7 3.8 %pack_second.1 = (bf16[320,3200]{1,0:T(8,128)(2,1)}, bf16[160,3200]{1,0:T(8,128)(2,1)}) custom-call(s32[1]{0:T(128)} %bitcast.5.core_ref._, bf16[320,3840]{1,0:T(8,128)(2,1)} %value_ref.4, bf16[320,3840]{1,0:T(8,128)(2,1)} %value_ref.4, bf16[320,3840]{1,0:T(8,128)(2,1)} %value_ref.4, bf16[320,1280]{1,0:T(8,128)(2,1)} %out_ref.1), custom_call_target="tpu_custom_call" | custom-call | tf_op jit(solution)/shard_map/pack_second/pallas_call | solution.py:422
  21.5 2.8 %order_global.1 = (bf16[320,1280]{1,0:T(8,128)(2,1)}, bf16[320,640]{1,0:T(8,128)(2,1)}) custom-call(s32[1]{0:T(128)} %bitcast.5.core_ref._, bf16[320,3840]{1,0:T(8,128)(2,1)} %value_ref.5, bf16[320,3840]{1,0:T(8,128)(2,1)} %value_ref.5, bf16[320,3840]{1,0:T(8,128)(2,1)} %value_ref.5), custom_call_target="tpu_custom_call" | custom-call | tf_op jit(solution)/shard_map/order_global/pallas_call | solution.py:422
  24.3 0.5 collective-permute-done.1
  24.9 1.6 collective-permute-done.2
  26.4 1.5 collective-permute-start.7
  28.0 1.1 collective-permute-start.6
  29.0 2.7 %pad_maximum_fusion.1.refs_1_ = bf16[320,2560]{1,0:T(8,128)(2,1)} fusion(bf16[160,2560]{1,0:T(8,128)(2,1)} %collective-permute-done.2, bf16[160,2560]{1,0:T(8,128)(2,1)} %copy-done.1), kind=kLoop, calls=%fused_computation.1 | loop fusion | flops 3276800 | bytes 3276800 | tf_op jit(solution)/shard_map/concatenate | solution.py:559
  31.7 0.0 collective-permute-start.3
  31.7 1.2 constant_dynamic-slice_fusion.1
  32.9 1.0 collective-permute-start.4
  33.9 18.3 %collective-permute-done.7 = bf16[160,3200]{1,0:T(8,128)(2,1)S(1)} collective-permute-done((bf16[160,3200]{1,0:T(8,128)(2,1)}, bf16[160,3200]{1,0:T(8,128)(2,1)S(1)}, u32[]{:S(2)}, u32[]{:S(2)}) %collective-permute-start.7) | collective-permute-done | bytes 1024032 | tf_op jit(solution)/shard_map/ppermute | solution.py:464
  52.2 0.0 collective-permute-done.6
  52.2 2.6 %pad_maximum_fusion.refs_1_ = bf16[320,3200]{1,0:T(8,128)(2,1)} fusion(bf16[160,3200]{1,0:T(8,128)(2,1)S(1)} %collective-permute-done.7, bf16[160,3200]{1,0:T(8,128)(2,1)} %collective-permute-done.6), kind=kLoop, calls=%fused_computation | loop fusion | flops 4096000 | bytes 4096000 | tf_op jit(solution)/shard_map/concatenate | solution.py:562
  54.9 1.3 constant_dynamic-slice_fusion
  56.2 1.2 collective-permute-start.9
  57.3 0.0 collective-permute-start.8
  57.3 2.7 %collective-permute-done.4.refs_3_ = bf16[160,2560]{1,0:T(8,128)(2,1)} collective-permute-done((bf16[160,2560]{1,0:T(8,128)(2,1)S(1)}, bf16[160,2560]{1,0:T(8,128)(2,1)}, u32[]{:S(2)}, u32[]{:S(2)}) %collective-permute-start.4) | collective-permute-done | bytes 819232 | tf_op jit(solution)/shard_map/ppermute | solution.py:473
  60.0 0.0 collective-permute-start.5
  60.0 0.1 stack.105
  60.1 1.5 collective-permute-start.11
  61.6 0.0 collective-permute-done.3.refs_2_
  61.6 0.5 collective-permute-start.12
  62.1 0.1 stack.95
  62.2 0.1 copy.11
  62.3 0.7 reshape.656.offset_ref
  63.0 0.0 collective-permute-done.5.refs_4_
  63.0 2.2 %all-to-all-done.picked_ref.code_ref.refs_2_ = bf16[4,400,640]{2,1,0:T(8,128)(2,1)S(1)} async-done(((bf16[4,400,640]{2,1,0:T(8,128)(2,1)}), bf16[4,400,640]{2,1,0:T(8,128)(2,1)S(1)}, u32[]{:S(2)}, u32[]{:S(2)}) %all-to-all-start) | async-done | bytes 2048032 | tf_op jit(solution)/shard_map/all_to_all | solution.py:536
  65.2 1.4 copy-done
  66.5 25.3 %embed_windows.1 = (bf16[1536,1280]{1,0:T(8,128)(2,1)}, bf16[1536,1280]{1,0:T(8,128)(2,1)}, bf16[1536,640]{1,0:T(8,128)(2,1)}) custom-call(s32[24]{0:T(128)} %reshape.656.offset_ref, bf16[4,400,640]{2,1,0:T(8,128)(2,1)} %copy-done, bf16[4,400,640]{2,1,0:T(8,128)(2,1)} %copy-done, bf16[320,2560]{1,0:T(8,128)(2,1)} %get-tuple-element.51.refs_0_, ...), custom_call_target="tpu_custom_call" | custom-call | tf_op jit(solution)/shard_map/embed_windows/pallas_call | solution.py:422
  91.8 0.1 collective-permute-start.10
  91.9 0.0 collective-permute-done.11.refs_5_
  91.9 0.6 collective-permute-start.14
  92.5 0.5 collective-permute-start.15
  93.0 1.2 broadcast_select_fusion
  94.2 1.6 collective-permute-start.13
  95.8 0.0 collective-permute-done.8.refs_2_
  95.8 0.0 collective-permute-done.10.refs_4_
  95.8 1.0 copy-done.9
  96.8 25.6 %windows_out.1.refs_0_ = bf16[1536,1280]{1,0:T(8,128)(2,1)} custom-call(s32[24]{0:T(128)} %reshape.656.offset_ref, bf16[1536,1280]{1,0:T(8,128)(2,1)} %get-tuple-element.56.embedded_ref, bf16[1536,1280]{1,0:T(8,128)(2,1)} %get-tuple-element.57.normed_ref, bf16[1536,640]{1,0:T(8,128)(2,1)} %get-tuple-element.58.mix_ref, bf16[4,400,640]{2,1,0:T(8,128)(2,1)} %copy-done, ...), custom_call_target="tpu_custom_call" | custom-call | flops 12582912000 | bytes 20070400 | tf_op jit(solution)/shard_map/windows_out/pallas_call | solution.py:422
  122.4 0.0 collective-permute-done.14.refs_9_
  122.4 0.0 collective-permute-done.13.refs_7_
  122.5 0.1 collective-permute-start.16
  122.6 1.1 collective-permute-start.17
  123.7 0.6 stack.87.offset_ref
  124.4 0.1 convert_element_type.14
  124.5 1.0 copy.12.refs_3_
  125.4 5.2 %collective-permute-done.17.refs_11_ = bf16[320,640]{1,0:T(8,128)(2,1)S(1)} collective-permute-done((bf16[320,640]{1,0:T(8,128)(2,1)S(1)}, bf16[320,640]{1,0:T(8,128)(2,1)S(1)}, u32[]{:S(2)}, u32[]{:S(2)}) %collective-permute-start.17) | collective-permute-done | bytes 409632 | tf_op jit(solution)/shard_map/ppermute | solution.py:469
  130.6 0.0 collective-permute-done.16.refs_1_
  130.6 0.7 copy-done.11
  131.4 38.1 %groups.1 = bf16[768,640]{1,0:T(8,128)(2,1)} custom-call(s32[5]{0:T(128)} %stack.87.offset_ref, bf16[1536,1280]{1,0:T(8,128)(2,1)} %windows_out.1.refs_0_, bf16[1536,1280]{1,0:T(8,128)(2,1)} %collective-permute-done.16.refs_1_, bf16[4,400,640]{2,1,0:T(8,128)(2,1)} %copy-done, f32[768,1]{1,0:T(8,128)} %copy.12.refs_3_, ...), custom_call_target="tpu_custom_call" | custom-call | flops 17364418560 | bytes 14830592 | tf_op jit(solution)/shard_map/groups/pallas_call | solution.py:422
  169.5 1.3 fusion.3
  170.8 0.1 collective-permute-start.18
  170.8 1.9 %collective-permute-done.18 = bf16[384,640]{1,0:T(8,128)(2,1)S(1)} collective-permute-done((bf16[384,640]{1,0:T(8,128)(2,1)S(1)}, bf16[384,640]{1,0:T(8,128)(2,1)S(1)}, u32[]{:S(2)}, u32[]{:S(2)}) %collective-permute-start.18) | collective-permute-done | bytes 491552 | tf_op jit(solution)/shard_map/ppermute | solution.py:456
  172.7 1.2 maximum_select_fusion
  (32 shorter events, 0.2 us)
Async XLA Ops:
  0.0 7.9 %copy-start.8 = (s32[1,2,3,64]{3,1,2,0:T(2,128)S(1)}, s32[1,2,3,64]{3,1,2,0:T(2,128)}, u32[]{:S(2)}) copy-start(s32[1,2,3,64]{3,1,2,0:T(2,128)} %param.8) | copy-start | bytes 4612
  0.0 7.9 %copy-start.12 = (s32[1,2,3]{2,1,0:T(2,128)S(1)}, s32[1,2,3]{2,1,0:T(2,128)}, u32[]{:S(2)}) copy-start(s32[1,2,3]{2,1,0:T(2,128)} %param.9) | copy-start | bytes 76
  3.5 21.4 %collective-permute-start.1 = (bf16[160,2560]{1,0:T(8,128)(2,1)}, bf16[160,2560]{1,0:T(8,128)(2,1)S(1)}, u32[]{:S(2)}, u32[]{:S(2)}) collective-permute-start(bf16[160,2560]{1,0:T(8,128)(2,1)} %get-tuple-element.39), channel_id=1, source_target_pairs={{0,8},{8,0},{16,24},{24,16},{1,9},{9,1},{17,25},{25,17},{2,10},{10... | collective-permute-start | bytes 2457608 | tf_op jit(solution)/shard_map/ppermute | solution.py:463
  6.4 20.0 %collective-permute-start.2 = (bf16[160,2560]{1,0:T(8,128)(2,1)}, bf16[160,2560]{1,0:T(8,128)(2,1)}, u32[]{:S(2)}, u32[]{:S(2)}) collective-permute-start(bf16[160,2560]{1,0:T(8,128)(2,1)} %get-tuple-element.39), channel_id=1, source_target_pairs={{0,16},{8,24},{16,0},{24,8},{1,17},{9,25},{17,1},{25,9},{2,18},{10... | collective-permute-start | bytes 2457608 | tf_op jit(solution)/shard_map/ppermute | solution.py:464
  8.1 1.2 copy-start.4
  8.1 1.2 collective-permute-start
  9.3 0.6 copy-start.6
  12.8 52.3 %all-to-all-start = ((bf16[4,400,640]{2,1,0:T(8,128)(2,1)}), bf16[4,400,640]{2,1,0:T(8,128)(2,1)S(1)}, u32[]{:S(2)}, u32[]{:S(2)}) async-start(bf16[4,400,640]{2,1,0:T(8,128)(2,1)} %pick.1), calls=%async_computation | async-start | bytes 4096000 | tf_op jit(solution)/shard_map/all_to_all | solution.py:536
  24.9 1.6 copy-start.1
  26.4 25.8 %collective-permute-start.7 = (bf16[160,3200]{1,0:T(8,128)(2,1)}, bf16[160,3200]{1,0:T(8,128)(2,1)S(1)}, u32[]{:S(2)}, u32[]{:S(2)}) collective-permute-start(bf16[160,3200]{1,0:T(8,128)(2,1)} %get-tuple-element.50), channel_id=1, source_target_pairs={{0,16},{8,24},{16,0},{24,8},{1,17},{9,25},{17,1},{25,9},{2,18},{10... | collective-permute-start | bytes 3072008 | tf_op jit(solution)/shard_map/ppermute | solution.py:464
  28.0 24.3 %collective-permute-start.6 = (bf16[160,3200]{1,0:T(8,128)(2,1)}, bf16[160,3200]{1,0:T(8,128)(2,1)}, u32[]{:S(2)}, u32[]{:S(2)}) collective-permute-start(bf16[160,3200]{1,0:T(8,128)(2,1)} %get-tuple-element.50), channel_id=1, source_target_pairs={{0,8},{8,0},{16,24},{24,16},{1,9},{9,1},{17,25},{25,17},{2,10},{10... | collective-permute-start | bytes 3072008 | tf_op jit(solution)/shard_map/ppermute | solution.py:463
  31.7 29.9 %collective-permute-start.3 = (bf16[320,2560]{1,0:T(8,128)(2,1)}, bf16[320,2560]{1,0:T(8,128)(2,1)}, u32[]{:S(2)}, u32[]{:S(2)}) collective-permute-start(bf16[320,2560]{1,0:T(8,128)(2,1)} %pad_maximum_fusion.1.refs_1_), channel_id=1, source_target_pairs={{0,4},{4,0},{1,5},{5,1},{2,6},{6,2},{3,7},{7,3},{8,12},{12,8},{9,1... | collective-permute-start | bytes 4915208 | tf_op jit(solution)/shard_map/ppermute | solution.py:456
  32.9 27.0 %collective-permute-start.4 = (bf16[160,2560]{1,0:T(8,128)(2,1)S(1)}, bf16[160,2560]{1,0:T(8,128)(2,1)}, u32[]{:S(2)}, u32[]{:S(2)}) collective-permute-start(bf16[160,2560]{1,0:T(8,128)(2,1)S(1)} %constant_dynamic-slice_fusion.1), channel_id=1, source_target_pairs={{0,8},{4,20},{8,0},{12,28},{16,24},{20,4},{24,16},{28,12},{1,9},{5... | collective-permute-start | bytes 2457608 | tf_op jit(solution)/shard_map/ppermute | solution.py:473
  56.2 35.6 %collective-permute-start.9 = (bf16[160,3200]{1,0:T(8,128)(2,1)S(1)}, bf16[160,3200]{1,0:T(8,128)(2,1)}, u32[]{:S(2)}, u32[]{:S(2)}) collective-permute-start(bf16[160,3200]{1,0:T(8,128)(2,1)S(1)} %constant_dynamic-slice_fusion), channel_id=1, source_target_pairs={{0,8},{4,20},{8,0},{12,28},{16,24},{20,4},{24,16},{28,12},{1,9},{5... | collective-permute-start | bytes 3072008 | tf_op jit(solution)/shard_map/ppermute | solution.py:473
  57.3 38.5 %collective-permute-start.8 = (bf16[320,3200]{1,0:T(8,128)(2,1)}, bf16[320,3200]{1,0:T(8,128)(2,1)}, u32[]{:S(2)}, u32[]{:S(2)}) collective-permute-start(bf16[320,3200]{1,0:T(8,128)(2,1)} %pad_maximum_fusion.refs_1_), channel_id=1, source_target_pairs={{0,4},{4,0},{1,5},{5,1},{2,6},{6,2},{3,7},{7,3},{8,12},{12,8},{9,1... | collective-permute-start | bytes 6144008 | tf_op jit(solution)/shard_map/ppermute | solution.py:456
  60.0 3.0 %collective-permute-start.5 = (bf16[160,2560]{1,0:T(8,128)(2,1)}, bf16[160,2560]{1,0:T(8,128)(2,1)}, u32[]{:S(2)}, u32[]{:S(2)}) collective-permute-start(bf16[160,2560]{1,0:T(8,128)(2,1)} %collective-permute-done.4.refs_3_), channel_id=1, source_target_pairs={{0,4},{4,0},{1,5},{5,1},{2,6},{6,2},{3,7},{7,3},{8,12},{12,8},{9,1... | collective-permute-start | bytes 2457608 | tf_op jit(solution)/shard_map/ppermute | solution.py:456
  60.1 31.8 %collective-permute-start.11 = (bf16[320,1280]{1,0:T(8,128)(2,1)}, bf16[320,1280]{1,0:T(8,128)(2,1)}, u32[]{:S(2)}, u32[]{:S(2)}) collective-permute-start(bf16[320,1280]{1,0:T(8,128)(2,1)} %get-tuple-element.61.refs_4_), channel_id=1, source_target_pairs={{0,8},{8,0},{16,24},{24,16},{1,9},{9,1},{17,25},{25,17},{2,10},{10... | collective-permute-start | bytes 2457608 | tf_op jit(solution)/shard_map/ppermute | solution.py:463
  61.6 30.3 %collective-permute-start.12 = (bf16[320,1280]{1,0:T(8,128)(2,1)}, bf16[320,1280]{1,0:T(8,128)(2,1)}, u32[]{:S(2)}, u32[]{:S(2)}) collective-permute-start(bf16[320,1280]{1,0:T(8,128)(2,1)} %get-tuple-element.61.refs_4_), channel_id=1, source_target_pairs={{0,16},{8,24},{16,0},{24,8},{1,17},{9,25},{17,1},{25,9},{2,18},{10... | collective-permute-start | bytes 2457608 | tf_op jit(solution)/shard_map/ppermute | solution.py:464
  65.1 1.4 copy-start
  91.8 4.0 %collective-permute-start.10 = (bf16[160,3200]{1,0:T(8,128)(2,1)}, bf16[160,3200]{1,0:T(8,128)(2,1)S(1)}, u32[]{:S(2)}, u32[]{:S(2)}) collective-permute-start(bf16[160,3200]{1,0:T(8,128)(2,1)} %collective-permute-done.9.refs_3_), channel_id=1, source_target_pairs={{0,4},{4,0},{1,5},{5,1},{2,6},{6,2},{3,7},{7,3},{8,12},{12,8},{9,1... | collective-permute-start | bytes 3072008 | tf_op jit(solution)/shard_map/ppermute | solution.py:456
  91.9 30.5 %collective-permute-start.14 = (bf16[320,640]{1,0:T(8,128)(2,1)}, bf16[320,640]{1,0:T(8,128)(2,1)S(1)}, u32[]{:S(2)}, u32[]{:S(2)}) collective-permute-start(bf16[320,640]{1,0:T(8,128)(2,1)} %get-tuple-element.70.refs_8_), channel_id=1, source_target_pairs={{0,8},{8,0},{16,24},{24,16},{1,9},{9,1},{17,25},{25,17},{2,10},{10... | collective-permute-start | bytes 1228808 | tf_op jit(solution)/shard_map/ppermute | solution.py:463
  92.5 29.9 %collective-permute-start.15 = (bf16[320,640]{1,0:T(8,128)(2,1)}, bf16[320,640]{1,0:T(8,128)(2,1)S(1)}, u32[]{:S(2)}, u32[]{:S(2)}) collective-permute-start(bf16[320,640]{1,0:T(8,128)(2,1)} %get-tuple-element.70.refs_8_), channel_id=1, source_target_pairs={{0,16},{8,24},{16,0},{24,8},{1,17},{9,25},{17,1},{25,9},{2,18},{10... | collective-permute-start | bytes 1228808 | tf_op jit(solution)/shard_map/ppermute | solution.py:464
  94.2 28.2 %collective-permute-start.13 = (bf16[320,1280]{1,0:T(8,128)(2,1)S(1)}, bf16[320,1280]{1,0:T(8,128)(2,1)S(1)}, u32[]{:S(2)}, u32[]{:S(2)}) collective-permute-start(bf16[320,1280]{1,0:T(8,128)(2,1)S(1)} %broadcast_select_fusion), channel_id=1, source_target_pairs={{0,8},{4,20},{8,0},{12,28},{16,24},{20,4},{24,16},{28,12},{1,9},{5... | collective-permute-start | bytes 2457608 | tf_op jit(solution)/shard_map/ppermute | solution.py:469
  95.8 1.0 copy-start.9
  96.8 27.6 %copy-start.5 = (s32[6,64]{1,0:T(8,128)S(1)}, s32[6,64]{1,0:T(8,128)}, u32[]{:S(2)}) copy-start(s32[6,64]{1,0:T(8,128)} %copy-done.4) | copy-start | bytes 4612
  96.8 27.6 %copy-start.7 = (s32[6,64]{1,0:T(8,128)S(1)}, s32[6,64]{1,0:T(8,128)}, u32[]{:S(2)}) copy-start(s32[6,64]{1,0:T(8,128)} %copy-done.6) | copy-start | bytes 4612
  122.4 8.2 %copy-start.2 = (bf16[320,640]{1,0:T(8,128)(2,1)}, bf16[320,640]{1,0:T(8,128)(2,1)S(1)}, u32[]{:S(2)}) copy-start(bf16[320,640]{1,0:T(8,128)(2,1)S(1)} %collective-permute-done.14.refs_9_) | copy-start | bytes 1228804
  122.4 8.2 %copy-start.3 = (bf16[320,640]{1,0:T(8,128)(2,1)}, bf16[320,640]{1,0:T(8,128)(2,1)S(1)}, u32[]{:S(2)}) copy-start(bf16[320,640]{1,0:T(8,128)(2,1)S(1)} %collective-permute-done.15.refs_10_) | copy-start | bytes 1228804
  122.4 8.2 %copy-start.10 = (bf16[320,1280]{1,0:T(8,128)(2,1)}, bf16[320,1280]{1,0:T(8,128)(2,1)S(1)}, u32[]{:S(2)}) copy-start(bf16[320,1280]{1,0:T(8,128)(2,1)S(1)} %collective-permute-done.13.refs_7_) | copy-start | bytes 2457604
  122.5 8.2 %collective-permute-start.16 = (bf16[1536,1280]{1,0:T(8,128)(2,1)}, bf16[1536,1280]{1,0:T(8,128)(2,1)}, u32[]{:S(2)}, u32[]{:S(2)}) collective-permute-start(bf16[1536,1280]{1,0:T(8,128)(2,1)} %windows_out.1.refs_0_), channel_id=1, source_target_pairs={{0,4},{4,0},{1,5},{5,1},{2,6},{6,2},{3,7},{7,3},{8,12},{12,8},{9,1... | collective-permute-start | bytes 11796488 | tf_op jit(solution)/shard_map/ppermute | solution.py:456
  122.6 8.0 %collective-permute-start.17 = (bf16[320,640]{1,0:T(8,128)(2,1)S(1)}, bf16[320,640]{1,0:T(8,128)(2,1)S(1)}, u32[]{:S(2)}, u32[]{:S(2)}) collective-permute-start(bf16[320,640]{1,0:T(8,128)(2,1)S(1)} %broadcast_select_fusion.1), channel_id=1, source_target_pairs={{0,8},{4,20},{8,0},{12,28},{16,24},{20,4},{24,16},{28,12},{1,9},{5... | collective-permute-start | bytes 1228808 | tf_op jit(solution)/shard_map/ppermute | solution.py:469
  130.6 0.8 copy-start.11
  170.8 1.9 %collective-permute-start.18 = (bf16[384,640]{1,0:T(8,128)(2,1)S(1)}, bf16[384,640]{1,0:T(8,128)(2,1)S(1)}, u32[]{:S(2)}, u32[]{:S(2)}) collective-permute-start(bf16[384,640]{1,0:T(8,128)(2,1)S(1)} %get-tuple-element.77), channel_id=1, source_target_pairs={{0,4},{4,0},{1,5},{5,1},{2,6},{6,2},{3,7},{7,3},{8,12},{12,8},{9,1... | collective-permute-start | bytes 1474568 | tf_op jit(solution)/shard_map/ppermute | solution.py:456

commit v8 on v7

--- a/solution.py
+++ b/solution.py
@@ -151,7 +151,7 @@
         target[:, pl.ds(at + GROUP * MAIN + head * TAIL, TAIL)] = source[:, pl.ds(first + MAIN, TAIL)]
 
 
-def pick_kernel(_, patch_ref, code_ref, partner_ref, *sent_refs):
+def pick_kernel(_, patch_ref, code_ref, *sent_refs):
     window_tokens = patch_ref.shape[1]
     windows, kept_most = code_ref.shape
     count = windows // len(sent_refs)
@@ -171,10 +171,8 @@
             )
             sent_ref[0, pl.ds(at * kept_most, kept_most), :] = picked.astype(jnp.bfloat16)
         part = pl.ds(which * count, count)
-        codes = jnp.concatenate([code_ref[part, :], partner_ref[part, :]], axis=0)
-        sent_ref[0, pl.ds(rows, 2 * count), pl.ds(0, kept_most)] = codes.astype(jnp.float32).astype(
-            jnp.bfloat16
-        )
+        codes = code_ref[part, :].astype(jnp.float32).astype(jnp.bfloat16)
+        sent_ref[0, pl.ds(rows, count), pl.ds(0, kept_most)] = codes
         for copy in range(1, sent_ref.shape[0]):
             sent_ref[copy] = sent_ref[0]
 
@@ -341,7 +339,7 @@
 def group_kernel(steps, parts, count, kept_most, key_chunk, offset_ref, *refs):
     many = 2 * parts
     normed_refs, refs = refs[:many], refs[many:]
-    tile_refs, refs = refs[:parts], refs[parts:]
+    tile_refs, refs = refs[:many], refs[many:]
     code_ref, *pieces, mixed_ref, first_ref, second_ref, key_ref, query_ref, value_ref, key_code_ref = refs
     step = pl.program_id(0)
     block = normed_refs[0].shape[0]
@@ -355,15 +353,12 @@
             for at, array in enumerate(arrays):
                 target[pl.ds(first_row(offset_ref, at, 32), array.shape[0]), :] = array[...]
         at = 0
-        for core in range(2):
-            for tile_ref in tile_refs:
-                for device in range(tile_ref.shape[0]):
-                    tile = tile_ref[device].astype(jnp.float32)
-                    for window in range(count):
-                        key_code_ref[:, pl.ds(at, kept_most)] = code_row(
-                            tile, core * count + window, kept_most
-                        )
-                        at += kept_most
+        for tile_ref in tile_refs:
+            for device in range(tile_ref.shape[0]):
+                tile = tile_ref[device].astype(jnp.float32)
+                for window in range(count):
+                    key_code_ref[:, pl.ds(at, kept_most)] = code_row(tile, window, kept_most)
+                    at += kept_most
 
     for which, normed_ref in enumerate(normed_refs):
 
@@ -505,7 +500,7 @@
     parts = 1
     count = windows // parts
     part_rows = count * kept_most
-    code_tile = -(-2 * count // 16) * 16
+    code_tile = -(-count // 16) * 16
     sent_shape = (lon_size, part_rows + code_tile, pin)
     patch_rows = patches.reshape(windows, window_tokens, pin)
     kept_mask = lax.broadcasted_iota(jnp.int32, (windows, kept_most), 1) < kept_count.reshape(
@@ -521,8 +516,8 @@
         pick_kernel,
         1,
         after(core_scalar, half_first),
-        [whole_block(patch_rows), whole_block(codes), whole_block(partner_codes)],
-        [patch_rows, codes, partner_codes],
+        [whole_block(patch_rows), whole_block(codes)],
+        [patch_rows, codes],
         [sent_shape] * parts,
         [pl.BlockSpec(sent_shape, lambda *_: (0, 0, 0))] * parts,
         [],
@@ -635,6 +630,9 @@
             result = after(result, (global_across, value_sides))
         partner.append(other_core(result))
     value_across = across(*value_sides)
+    partner_tiles = [
+        other_core(after(value, own)[:, part_rows : part_rows + code_tile, :MAIN]) for value in got
+    ]
 
     all_rows = lon_size * rows
     query_block = 256 if (2 * rows) % 256 == 0 else 2 * rows
@@ -657,10 +655,11 @@
         [
             *normed_specs,
             *[whole_tile] * parts,
+            *map(whole_block, partner_tiles),
             pl.BlockSpec((query_block, 1), lambda i, _: (late(i), 0)),
             *map(whole_block, pieces),
         ],
-        [*own, *partner, *got, query_codes, *pieces],
+        [*own, *partner, *got, *partner_tiles, query_codes, *pieces],
         [(2 * rows, WIDE)],
         [pl.BlockSpec((query_block, WIDE), lambda i, _: (late(i), 0))],
         [

time: 174 us -> 173 us (level)
  waiting for transfers between devices: 33.5 us -> 30.3 us
    ppermute x2, waiting for transfers between devices: 5.2 us -> 0.25 us  [across(): return lax.ppermute(forwarded, ('batch', 'lat'), diagonal)]
    ppermute x7 -> x8, waiting for transfers between devices: 3.03 us -> 5.72 us  [other_core(): return lax.ppermute(value, 'lat', swap_perm(2, 1))]
    all_to_all x1, waiting for transfers between devices: 2.18 us -> 0.12 us  [sample_body(): got.append(lax.all_to_all(value, 'lon', 0, 0, tiled=True))]
    unnamed x27 -> x23, local copies, waits for them, and re-layouts: 3.7 us -> 3.11 us
  transfers between devices with their start and end apart: 20 -> 21, of which waited for: 8 -> 8; matrix products, arithmetic and copies ran while one was open for 7% -> 8% of each run, Pallas kernels for 35% -> 35%
where the time goes in v8:
time: 173 us
  Pallas kernels  102 us (59%)
  waiting for transfers between devices  30.3 us (18%)
  starting transfers between devices  21.4 us (12%)
  local copies, waits for them, and re-layouts  10.3 us (6%)
  other arithmetic  8.51 us (5%)
    pallas_call x7, Pallas kernels, run(): pl.pallas_call(kernel, grid_spec=pltpu.PrefetchScalarGridSpec(num_scalar_...  102 us
    ppermute x4, waiting for transfers between devices, sides(): along_y = lax.ppermute(part, 'batch', swap_perm(batch_size, 2))  19.9 us
    ppermute x4, starting transfers between devices, sides(): along_x = lax.ppermute(part, 'batch', swap_perm(batch_size, 1))  6.68 us
    ppermute x8, waiting for transfers between devices, other_core(): return lax.ppermute(value, 'lat', swap_perm(2, 1))  5.72 us
    all_to_all x1, starting transfers between devices, sample_body(): got.append(lax.all_to_all(value, 'lon', 0, 0, tiled=True))  4.87 us
    ppermute x4, starting transfers between devices, sides(): along_y = lax.ppermute(part, 'batch', swap_perm(batch_size, 2))  4.8 us
  transfers between devices with their start and end apart: 21, of which 8 were waited for; matrix products, arithmetic and copies ran while one was open for 8% of the time, Pallas kernels for 35%

profile of v8, /device:TPU:0, one launch (start us, length us, event | category | flops | bytes accessed | tf_op | source)
XLA Modules:
  0.0 172.6 jit_solution(3064889973811045762)
XLA Ops:
  0.0 3.5 %pack_first.1 = (bf16[320,2560]{1,0:T(8,128)(2,1)}, bf16[160,2560]{1,0:T(8,128)(2,1)}) custom-call(s32[1]{0:T(128)} %bitcast.5.core_ref._, bf16[320,3840]{1,0:T(8,128)(2,1)} %value_ref.4, bf16[320,3840]{1,0:T(8,128)(2,1)} %value_ref.4, bf16[320,3840]{1,0:T(8,128)(2,1)} %value_ref.4, bf16[160,1280]{1,0:T(8,128)(2,1)} %embed_ref.1), custom_call_target="tpu_custom_call" | custom-call | tf_op jit(solution)/shard_map/pack_first/pallas_call | solution.py:417
  3.5 2.9 %collective-permute-start.1 = (bf16[160,2560]{1,0:T(8,128)(2,1)}, bf16[160,2560]{1,0:T(8,128)(2,1)S(1)}, u32[]{:S(2)}, u32[]{:S(2)}) collective-permute-start(bf16[160,2560]{1,0:T(8,128)(2,1)} %get-tuple-element.40), channel_id=1, source_target_pairs={{0,8},{8,0},{16,24},{24,16},{1,9},{9,1},{17,25},{25,17},{2,10},{10... | collective-permute-start | bytes 2457608 | tf_op jit(solution)/shard_map/ppermute | solution.py:458
  6.4 1.5 collective-permute-start.2
  7.9 0.1 lt.26
  8.0 0.7 fusion.code_ref
  8.7 2.9 %pick.1 = bf16[4,400,640]{2,1,0:T(8,128)(2,1)} custom-call(s32[1]{0:T(128)} %bitcast.5.core_ref._, bf16[6,128,640]{2,1,0:T(8,128)(2,1)} %bitcast.26, s32[6,64]{1,0:T(8,128)} %fusion.code_ref), custom_call_target="tpu_custom_call" | custom-call | tf_op jit(solution)/shard_map/pick/pallas_call | solution.py:417
  11.6 4.9 %all-to-all-start = ((bf16[4,400,640]{2,1,0:T(8,128)(2,1)}), bf16[4,400,640]{2,1,0:T(8,128)(2,1)S(1)}, u32[]{:S(2)}, u32[]{:S(2)}) async-start(bf16[4,400,640]{2,1,0:T(8,128)(2,1)} %pick.1), calls=%async_computation | async-start | bytes 4096000 | tf_op jit(solution)/shard_map/all_to_all | solution.py:531
  16.5 3.8 %pack_second.1 = (bf16[320,3200]{1,0:T(8,128)(2,1)}, bf16[160,3200]{1,0:T(8,128)(2,1)}) custom-call(s32[1]{0:T(128)} %bitcast.5.core_ref._, bf16[320,3840]{1,0:T(8,128)(2,1)} %value_ref.4, bf16[320,3840]{1,0:T(8,128)(2,1)} %value_ref.4, bf16[320,3840]{1,0:T(8,128)(2,1)} %value_ref.4, bf16[320,1280]{1,0:T(8,128)(2,1)} %out_ref.1), custom_call_target="tpu_custom_call" | custom-call | tf_op jit(solution)/shard_map/pack_second/pallas_call | solution.py:417
  20.3 2.8 %order_global.1 = (bf16[320,1280]{1,0:T(8,128)(2,1)}, bf16[320,640]{1,0:T(8,128)(2,1)}) custom-call(s32[1]{0:T(128)} %bitcast.5.core_ref._, bf16[320,3840]{1,0:T(8,128)(2,1)} %value_ref.5, bf16[320,3840]{1,0:T(8,128)(2,1)} %value_ref.5, bf16[320,3840]{1,0:T(8,128)(2,1)} %value_ref.5), custom_call_target="tpu_custom_call" | custom-call | tf_op jit(solution)/shard_map/order_global/pallas_call | solution.py:417
  23.2 1.7 collective-permute-done.1
  24.9 1.6 collective-permute-done.2
  26.4 1.5 collective-permute-start.7
  28.0 1.1 collective-permute-start.6
  29.0 2.7 %pad_maximum_fusion.1.refs_1_ = bf16[320,2560]{1,0:T(8,128)(2,1)} fusion(bf16[160,2560]{1,0:T(8,128)(2,1)} %collective-permute-done.2, bf16[160,2560]{1,0:T(8,128)(2,1)} %copy-done.1), kind=kLoop, calls=%fused_computation.1 | loop fusion | flops 3276800 | bytes 3276800 | tf_op jit(solution)/shard_map/concatenate | solution.py:554
  31.7 0.0 collective-permute-start.3
  31.7 1.2 constant_dynamic-slice_fusion.1
  32.9 1.0 collective-permute-start.4
  33.9 18.3 %collective-permute-done.7 = bf16[160,3200]{1,0:T(8,128)(2,1)S(1)} collective-permute-done((bf16[160,3200]{1,0:T(8,128)(2,1)}, bf16[160,3200]{1,0:T(8,128)(2,1)S(1)}, u32[]{:S(2)}, u32[]{:S(2)}) %collective-permute-start.7) | collective-permute-done | bytes 1024032 | tf_op jit(solution)/shard_map/ppermute | solution.py:459
  52.2 2.7 %pad_maximum_fusion.refs_1_ = bf16[320,3200]{1,0:T(8,128)(2,1)} fusion(bf16[160,3200]{1,0:T(8,128)(2,1)S(1)} %collective-permute-done.7, bf16[160,3200]{1,0:T(8,128)(2,1)} %collective-permute-done.6), kind=kLoop, calls=%fused_computation | loop fusion | flops 4096000 | bytes 4096000 | tf_op jit(solution)/shard_map/concatenate | solution.py:557
  54.9 1.3 constant_dynamic-slice_fusion
  56.2 1.1 collective-permute-start.9
  57.3 2.6 %collective-permute-done.4.refs_3_ = bf16[160,2560]{1,0:T(8,128)(2,1)} collective-permute-done((bf16[160,2560]{1,0:T(8,128)(2,1)S(1)}, bf16[160,2560]{1,0:T(8,128)(2,1)}, u32[]{:S(2)}, u32[]{:S(2)}) %collective-permute-start.4) | collective-permute-done | bytes 819232 | tf_op jit(solution)/shard_map/ppermute | solution.py:468
  60.0 0.0 collective-permute-start.5
  60.0 0.1 stack.105
  60.1 1.5 collective-permute-start.11
  61.6 0.0 collective-permute-done.3.refs_2_
  61.6 0.5 collective-permute-start.12
  62.1 0.1 stack.95
  62.2 0.1 copy.11
  62.3 0.7 reshape.656.offset_ref
  63.0 0.0 collective-permute-done.5.refs_4_
  63.0 0.1 all-to-all-done.picked_ref.code_ref.refs_2_
  63.1 1.4 copy-done
  64.5 25.3 %embed_windows.1 = (bf16[1536,1280]{1,0:T(8,128)(2,1)}, bf16[1536,1280]{1,0:T(8,128)(2,1)}, bf16[1536,640]{1,0:T(8,128)(2,1)}) custom-call(s32[24]{0:T(128)} %reshape.656.offset_ref, bf16[4,400,640]{2,1,0:T(8,128)(2,1)} %copy-done, bf16[4,400,640]{2,1,0:T(8,128)(2,1)} %copy-done, bf16[320,2560]{1,0:T(8,128)(2,1)} %get-tuple-element.52.refs_0_, ...), custom_call_target="tpu_custom_call" | custom-call | tf_op jit(solution)/shard_map/embed_windows/pallas_call | solution.py:417
  89.7 0.0 collective-permute-done.9.refs_3_
  89.7 0.1 collective-permute-start.10
  89.8 0.0 collective-permute-done.12.refs_7_
  89.8 1.2 collective-permute-start.14
  91.0 1.3 collective-permute-start.15
  92.3 1.2 broadcast_select_fusion
  93.5 1.2 collective-permute-start.13
  94.7 0.0 collective-permute-done.8.refs_2_
  94.7 0.0 collective-permute-done.10.refs_4_
  94.7 1.0 copy-done.6
  95.7 25.6 %windows_out.1.refs_0_ = bf16[1536,1280]{1,0:T(8,128)(2,1)} custom-call(s32[24]{0:T(128)} %reshape.656.offset_ref, bf16[1536,1280]{1,0:T(8,128)(2,1)} %get-tuple-element.57.embedded_ref, bf16[1536,1280]{1,0:T(8,128)(2,1)} %get-tuple-element.58.normed_ref, bf16[1536,640]{1,0:T(8,128)(2,1)} %get-tuple-element.59.mix_ref, bf16[4,400,640]{2,1,0:T(8,128)(2,1)} %copy-done, ...), custom_call_target="tpu_custom_call" | custom-call | flops 12582912000 | bytes 20070400 | tf_op jit(solution)/shard_map/windows_out/pallas_call | solution.py:417
  121.3 0.0 collective-permute-done.14.refs_10_
  121.3 0.1 collective-permute-start.16
  121.4 1.0 collective-permute-start.18
  122.5 0.6 stack.87.offset_ref
  123.1 0.7 slice.9
  123.8 0.5 collective-permute-start.17
  124.3 3.9 %collective-permute-done = s32[6,64]{1,0:T(8,128)S(1)} collective-permute-done((s32[6,64]{1,0:T(8,128)S(1)}, s32[6,64]{1,0:T(8,128)S(1)}, u32[]{:S(2)}, u32[]{:S(2)}) %collective-permute-start) | collective-permute-done | bytes 1568 | tf_op jit(solution)/shard_map/ppermute | solution.py:451
  128.2 0.1 convert_element_type.14
  128.3 1.0 copy.12.refs_4_
  129.2 0.2 collective-permute-done.18.refs_12_
  129.5 0.0 collective-permute-done.17.refs_3_
  129.5 0.0 collective-permute-done.16.refs_1_
  129.5 0.7 copy-done.8
  130.2 0.0 copy-done.9
  130.2 38.0 %groups.1 = bf16[768,640]{1,0:T(8,128)(2,1)} custom-call(s32[5]{0:T(128)} %stack.87.offset_ref, bf16[1536,1280]{1,0:T(8,128)(2,1)} %windows_out.1.refs_0_, bf16[1536,1280]{1,0:T(8,128)(2,1)} %collective-permute-done.16.refs_1_, bf16[4,400,640]{2,1,0:T(8,128)(2,1)} %copy-done, bf16[4,16,128]{2,1,0:T(8,128)(2,1)} %copy-done.9, f32[768,1]{1,0:T(8,128)} %copy.12.refs_4_, ...), custom_call_target="tpu_custom_call" | custom-call | flops 17364418560 | bytes 14846976 | tf_op jit(solution)/shard_map/groups/pallas_call | solution.py:417
  168.2 1.3 fusion.3
  169.5 0.1 collective-permute-start.19
  169.6 1.9 %collective-permute-done.19 = bf16[384,640]{1,0:T(8,128)(2,1)S(1)} collective-permute-done((bf16[384,640]{1,0:T(8,128)(2,1)S(1)}, bf16[384,640]{1,0:T(8,128)(2,1)S(1)}, u32[]{:S(2)}, u32[]{:S(2)}) %collective-permute-start.19) | collective-permute-done | bytes 491552 | tf_op jit(solution)/shard_map/ppermute | solution.py:451
  171.4 1.2 maximum_select_fusion
  (31 shorter events, 0.2 us)
Async XLA Ops:
  0.0 7.9 %copy-start.5 = (s32[1,2,3,64]{3,1,2,0:T(2,128)S(1)}, s32[1,2,3,64]{3,1,2,0:T(2,128)}, u32[]{:S(2)}) copy-start(s32[1,2,3,64]{3,1,2,0:T(2,128)} %param.8) | copy-start | bytes 4612
  0.0 7.9 %copy-start.10 = (s32[1,2,3]{2,1,0:T(2,128)S(1)}, s32[1,2,3]{2,1,0:T(2,128)}, u32[]{:S(2)}) copy-start(s32[1,2,3]{2,1,0:T(2,128)} %param.9) | copy-start | bytes 76
  3.5 21.4 %collective-permute-start.1 = (bf16[160,2560]{1,0:T(8,128)(2,1)}, bf16[160,2560]{1,0:T(8,128)(2,1)S(1)}, u32[]{:S(2)}, u32[]{:S(2)}) collective-permute-start(bf16[160,2560]{1,0:T(8,128)(2,1)} %get-tuple-element.40), channel_id=1, source_target_pairs={{0,8},{8,0},{16,24},{24,16},{1,9},{9,1},{17,25},{25,17},{2,10},{10... | collective-permute-start | bytes 2457608 | tf_op jit(solution)/shard_map/ppermute | solution.py:458
  6.4 20.0 %collective-permute-start.2 = (bf16[160,2560]{1,0:T(8,128)(2,1)}, bf16[160,2560]{1,0:T(8,128)(2,1)}, u32[]{:S(2)}, u32[]{:S(2)}) collective-permute-start(bf16[160,2560]{1,0:T(8,128)(2,1)} %get-tuple-element.40), channel_id=1, source_target_pairs={{0,16},{8,24},{16,0},{24,8},{1,17},{9,25},{17,1},{25,9},{2,18},{10... | collective-permute-start | bytes 2457608 | tf_op jit(solution)/shard_map/ppermute | solution.py:459
  11.6 51.5 %all-to-all-start = ((bf16[4,400,640]{2,1,0:T(8,128)(2,1)}), bf16[4,400,640]{2,1,0:T(8,128)(2,1)S(1)}, u32[]{:S(2)}, u32[]{:S(2)}) async-start(bf16[4,400,640]{2,1,0:T(8,128)(2,1)} %pick.1), calls=%async_computation | async-start | bytes 4096000 | tf_op jit(solution)/shard_map/all_to_all | solution.py:531
  24.9 1.6 copy-start.1
  26.4 25.8 %collective-permute-start.7 = (bf16[160,3200]{1,0:T(8,128)(2,1)}, bf16[160,3200]{1,0:T(8,128)(2,1)S(1)}, u32[]{:S(2)}, u32[]{:S(2)}) collective-permute-start(bf16[160,3200]{1,0:T(8,128)(2,1)} %get-tuple-element.51), channel_id=1, source_target_pairs={{0,16},{8,24},{16,0},{24,8},{1,17},{9,25},{17,1},{25,9},{2,18},{10... | collective-permute-start | bytes 3072008 | tf_op jit(solution)/shard_map/ppermute | solution.py:459
  28.0 24.3 %collective-permute-start.6 = (bf16[160,3200]{1,0:T(8,128)(2,1)}, bf16[160,3200]{1,0:T(8,128)(2,1)}, u32[]{:S(2)}, u32[]{:S(2)}) collective-permute-start(bf16[160,3200]{1,0:T(8,128)(2,1)} %get-tuple-element.51), channel_id=1, source_target_pairs={{0,8},{8,0},{16,24},{24,16},{1,9},{9,1},{17,25},{25,17},{2,10},{10... | collective-permute-start | bytes 3072008 | tf_op jit(solution)/shard_map/ppermute | solution.py:458
  31.7 29.9 %collective-permute-start.3 = (bf16[320,2560]{1,0:T(8,128)(2,1)}, bf16[320,2560]{1,0:T(8,128)(2,1)}, u32[]{:S(2)}, u32[]{:S(2)}) collective-permute-start(bf16[320,2560]{1,0:T(8,128)(2,1)} %pad_maximum_fusion.1.refs_1_), channel_id=1, source_target_pairs={{0,4},{4,0},{1,5},{5,1},{2,6},{6,2},{3,7},{7,3},{8,12},{12,8},{9,1... | collective-permute-start | bytes 4915208 | tf_op jit(solution)/shard_map/ppermute | solution.py:451
  32.9 27.1 %collective-permute-start.4 = (bf16[160,2560]{1,0:T(8,128)(2,1)S(1)}, bf16[160,2560]{1,0:T(8,128)(2,1)}, u32[]{:S(2)}, u32[]{:S(2)}) collective-permute-start(bf16[160,2560]{1,0:T(8,128)(2,1)S(1)} %constant_dynamic-slice_fusion.1), channel_id=1, source_target_pairs={{0,8},{4,20},{8,0},{12,28},{16,24},{20,4},{24,16},{28,12},{1,9},{5... | collective-permute-start | bytes 2457608 | tf_op jit(solution)/shard_map/ppermute | solution.py:468
  56.2 33.6 %collective-permute-start.9 = (bf16[160,3200]{1,0:T(8,128)(2,1)S(1)}, bf16[160,3200]{1,0:T(8,128)(2,1)}, u32[]{:S(2)}, u32[]{:S(2)}) collective-permute-start(bf16[160,3200]{1,0:T(8,128)(2,1)S(1)} %constant_dynamic-slice_fusion), channel_id=1, source_target_pairs={{0,8},{4,20},{8,0},{12,28},{16,24},{20,4},{24,16},{28,12},{1,9},{5... | collective-permute-start | bytes 3072008 | tf_op jit(solution)/shard_map/ppermute | solution.py:468
  57.3 37.3 %collective-permute-start.8 = (bf16[320,3200]{1,0:T(8,128)(2,1)}, bf16[320,3200]{1,0:T(8,128)(2,1)}, u32[]{:S(2)}, u32[]{:S(2)}) collective-permute-start(bf16[320,3200]{1,0:T(8,128)(2,1)} %pad_maximum_fusion.refs_1_), channel_id=1, source_target_pairs={{0,4},{4,0},{1,5},{5,1},{2,6},{6,2},{3,7},{7,3},{8,12},{12,8},{9,1... | collective-permute-start | bytes 6144008 | tf_op jit(solution)/shard_map/ppermute | solution.py:451
  60.0 3.0 %collective-permute-start.5 = (bf16[160,2560]{1,0:T(8,128)(2,1)}, bf16[160,2560]{1,0:T(8,128)(2,1)}, u32[]{:S(2)}, u32[]{:S(2)}) collective-permute-start(bf16[160,2560]{1,0:T(8,128)(2,1)} %collective-permute-done.4.refs_3_), channel_id=1, source_target_pairs={{0,4},{4,0},{1,5},{5,1},{2,6},{6,2},{3,7},{7,3},{8,12},{12,8},{9,1... | collective-permute-start | bytes 2457608 | tf_op jit(solution)/shard_map/ppermute | solution.py:451
  60.1 29.8 %collective-permute-start.11 = (bf16[320,1280]{1,0:T(8,128)(2,1)}, bf16[320,1280]{1,0:T(8,128)(2,1)}, u32[]{:S(2)}, u32[]{:S(2)}) collective-permute-start(bf16[320,1280]{1,0:T(8,128)(2,1)} %get-tuple-element.62.refs_5_), channel_id=1, source_target_pairs={{0,8},{8,0},{16,24},{24,16},{1,9},{9,1},{17,25},{25,17},{2,10},{10... | collective-permute-start | bytes 2457608 | tf_op jit(solution)/shard_map/ppermute | solution.py:458
  61.6 28.3 %collective-permute-start.12 = (bf16[320,1280]{1,0:T(8,128)(2,1)}, bf16[320,1280]{1,0:T(8,128)(2,1)}, u32[]{:S(2)}, u32[]{:S(2)}) collective-permute-start(bf16[320,1280]{1,0:T(8,128)(2,1)} %get-tuple-element.62.refs_5_), channel_id=1, source_target_pairs={{0,16},{8,24},{16,0},{24,8},{1,17},{9,25},{17,1},{25,9},{2,18},{10... | collective-permute-start | bytes 2457608 | tf_op jit(solution)/shard_map/ppermute | solution.py:459
  63.1 1.4 copy-start
  89.7 4.9 %collective-permute-start.10 = (bf16[160,3200]{1,0:T(8,128)(2,1)}, bf16[160,3200]{1,0:T(8,128)(2,1)S(1)}, u32[]{:S(2)}, u32[]{:S(2)}) collective-permute-start(bf16[160,3200]{1,0:T(8,128)(2,1)} %collective-permute-done.9.refs_3_), channel_id=1, source_target_pairs={{0,4},{4,0},{1,5},{5,1},{2,6},{6,2},{3,7},{7,3},{8,12},{12,8},{9,1... | collective-permute-start | bytes 3072008 | tf_op jit(solution)/shard_map/ppermute | solution.py:451
  89.8 31.4 %collective-permute-start.14 = (bf16[320,640]{1,0:T(8,128)(2,1)}, bf16[320,640]{1,0:T(8,128)(2,1)S(1)}, u32[]{:S(2)}, u32[]{:S(2)}) collective-permute-start(bf16[320,640]{1,0:T(8,128)(2,1)} %get-tuple-element.71.refs_9_), channel_id=1, source_target_pairs={{0,8},{8,0},{16,24},{24,16},{1,9},{9,1},{17,25},{25,17},{2,10},{10... | collective-permute-start | bytes 1228808 | tf_op jit(solution)/shard_map/ppermute | solution.py:458
  91.0 30.3 %collective-permute-start.15 = (bf16[320,640]{1,0:T(8,128)(2,1)}, bf16[320,640]{1,0:T(8,128)(2,1)S(1)}, u32[]{:S(2)}, u32[]{:S(2)}) collective-permute-start(bf16[320,640]{1,0:T(8,128)(2,1)} %get-tuple-element.71.refs_9_), channel_id=1, source_target_pairs={{0,16},{8,24},{16,0},{24,8},{1,17},{9,25},{17,1},{25,9},{2,18},{10... | collective-permute-start | bytes 1228808 | tf_op jit(solution)/shard_map/ppermute | solution.py:459
  93.5 27.8 %collective-permute-start.13 = (bf16[320,1280]{1,0:T(8,128)(2,1)S(1)}, bf16[320,1280]{1,0:T(8,128)(2,1)S(1)}, u32[]{:S(2)}, u32[]{:S(2)}) collective-permute-start(bf16[320,1280]{1,0:T(8,128)(2,1)S(1)} %broadcast_select_fusion), channel_id=1, source_target_pairs={{0,8},{4,20},{8,0},{12,28},{16,24},{20,4},{24,16},{28,12},{1,9},{5... | collective-permute-start | bytes 2457608 | tf_op jit(solution)/shard_map/ppermute | solution.py:464
  94.7 1.0 copy-start.6
  95.6 26.8 %copy-start.4 = (s32[6,64]{1,0:T(8,128)S(1)}, s32[6,64]{1,0:T(8,128)}, u32[]{:S(2)}) copy-start(s32[6,64]{1,0:T(8,128)} %fusion.code_ref) | copy-start | bytes 4612
  121.3 8.2 %copy-start.2 = (bf16[320,640]{1,0:T(8,128)(2,1)}, bf16[320,640]{1,0:T(8,128)(2,1)S(1)}, u32[]{:S(2)}) copy-start(bf16[320,640]{1,0:T(8,128)(2,1)S(1)} %collective-permute-done.14.refs_10_) | copy-start | bytes 1228804
  121.3 8.2 %copy-start.3 = (bf16[320,640]{1,0:T(8,128)(2,1)}, bf16[320,640]{1,0:T(8,128)(2,1)S(1)}, u32[]{:S(2)}) copy-start(bf16[320,640]{1,0:T(8,128)(2,1)S(1)} %collective-permute-done.15.refs_11_) | copy-start | bytes 1228804
  121.3 8.2 %copy-start.7 = (bf16[320,1280]{1,0:T(8,128)(2,1)}, bf16[320,1280]{1,0:T(8,128)(2,1)S(1)}, u32[]{:S(2)}) copy-start(bf16[320,1280]{1,0:T(8,128)(2,1)S(1)} %collective-permute-done.13.refs_8_) | copy-start | bytes 2457604
  121.3 8.2 %collective-permute-start.16 = (bf16[1536,1280]{1,0:T(8,128)(2,1)}, bf16[1536,1280]{1,0:T(8,128)(2,1)}, u32[]{:S(2)}, u32[]{:S(2)}) collective-permute-start(bf16[1536,1280]{1,0:T(8,128)(2,1)} %windows_out.1.refs_0_), channel_id=1, source_target_pairs={{0,4},{4,0},{1,5},{5,1},{2,6},{6,2},{3,7},{7,3},{8,12},{12,8},{9,1... | collective-permute-start | bytes 11796488 | tf_op jit(solution)/shard_map/ppermute | solution.py:451
  121.4 8.0 %collective-permute-start.18 = (bf16[320,640]{1,0:T(8,128)(2,1)S(1)}, bf16[320,640]{1,0:T(8,128)(2,1)S(1)}, u32[]{:S(2)}, u32[]{:S(2)}) collective-permute-start(bf16[320,640]{1,0:T(8,128)(2,1)S(1)} %broadcast_select_fusion.1), channel_id=1, source_target_pairs={{0,8},{4,20},{8,0},{12,28},{16,24},{20,4},{24,16},{28,12},{1,9},{5... | collective-permute-start | bytes 1228808 | tf_op jit(solution)/shard_map/ppermute | solution.py:464
  122.4 5.7 %collective-permute-start = (s32[6,64]{1,0:T(8,128)S(1)}, s32[6,64]{1,0:T(8,128)S(1)}, u32[]{:S(2)}, u32[]{:S(2)}) collective-permute-start(s32[6,64]{1,0:T(8,128)S(1)} %copy-done.4), channel_id=1, source_target_pairs={{0,4},{4,0},{1,5},{5,1},{2,6},{6,2},{3,7},{7,3},{8,12},{12,8},{9,1... | collective-permute-start | bytes 4616 | tf_op jit(solution)/shard_map/ppermute | solution.py:451
  123.8 5.7 %collective-permute-start.17 = (bf16[4,16,128]{2,1,0:T(8,128)(2,1)S(1)}, bf16[4,16,128]{2,1,0:T(8,128)(2,1)S(1)}, u32[]{:S(2)}, u32[]{:S(2)}) collective-permute-start(bf16[4,16,128]{2,1,0:T(8,128)(2,1)S(1)} %slice.9), channel_id=1, source_target_pairs={{0,4},{4,0},{1,5},{5,1},{2,6},{6,2},{3,7},{7,3},{8,12},{12,8},{9,1... | collective-permute-start | bytes 49160 | tf_op jit(solution)/shard_map/ppermute | solution.py:451
  129.5 0.8 copy-start.8
  129.5 0.8 copy-start.9
  169.5 1.9 %collective-permute-start.19 = (bf16[384,640]{1,0:T(8,128)(2,1)S(1)}, bf16[384,640]{1,0:T(8,128)(2,1)S(1)}, u32[]{:S(2)}, u32[]{:S(2)}) collective-permute-start(bf16[384,640]{1,0:T(8,128)(2,1)S(1)} %get-tuple-element.79), channel_id=1, source_target_pairs={{0,4},{4,0},{1,5},{5,1},{2,6},{6,2},{3,7},{7,3},{8,12},{12,8},{9,1... | collective-permute-start | bytes 1474568 | tf_op jit(solution)/shard_map/ppermute | solution.py:451

commit v9 on v8

--- a/solution.py
+++ b/solution.py
@@ -572,7 +572,7 @@
         tail = group_start + GROUP * MAIN + head % GROUP * TAIL
         return pieces, jnp.stack([firsts, main, tail], axis=1).reshape(-1)
 
-    shared_by = 1
+    shared_by = 2 if lon_size % 2 == 0 else 1
     block = shared_by * part_rows
     steps = lon_size // shared_by
     many_rows = lon_size * part_rows

time: 173 us -> 173 us (level)
  no operation moved by 1% of the time
where the time goes in v9:
time: 173 us; the launch traced here: 172 us
  Pallas kernels  101 us (58%)
  waiting for transfers between devices  30.3 us (18%)
  starting transfers between devices  21.4 us (12%)
  local copies, waits for them, and re-layouts  10.3 us (6%)
  other arithmetic  8.51 us (5%)
    pallas_call x7, Pallas kernels, run(): pl.pallas_call(kernel, grid_spec=pltpu.PrefetchScalarGridSpec(num_scalar_...  101 us
    ppermute x4, waiting for transfers between devices, sides(): along_y = lax.ppermute(part, 'batch', swap_perm(batch_size, 2))  19.9 us
    ppermute x4, starting transfers between devices, sides(): along_x = lax.ppermute(part, 'batch', swap_perm(batch_size, 1))  6.68 us
    ppermute x8, waiting for transfers between devices, other_core(): return lax.ppermute(value, 'lat', swap_perm(2, 1))  5.71 us
    all_to_all x1, starting transfers between devices, sample_body(): got.append(lax.all_to_all(value, 'lon', 0, 0, tiled=True))  4.87 us
    ppermute x4, starting transfers between devices, sides(): along_y = lax.ppermute(part, 'batch', swap_perm(batch_size, 2))  4.81 us
  transfers between devices with their start and end apart: 21, of which 8 were waited for; matrix products, arithmetic and copies ran while one was open for 8% of the time, Pallas kernels for 35%

profile of v9, /device:TPU:0, one launch (start us, length us, event | category | flops | bytes accessed | tf_op | source)
XLA Modules:
  0.0 172.0 jit_solution(15137657425669795406)
XLA Ops:
  0.0 3.5 %pack_first.1 = (bf16[320,2560]{1,0:T(8,128)(2,1)}, bf16[160,2560]{1,0:T(8,128)(2,1)}) custom-call(s32[1]{0:T(128)} %bitcast.5.core_ref._, bf16[320,3840]{1,0:T(8,128)(2,1)} %value_ref.4, bf16[320,3840]{1,0:T(8,128)(2,1)} %value_ref.4, bf16[320,3840]{1,0:T(8,128)(2,1)} %value_ref.4, bf16[160,1280]{1,0:T(8,128)(2,1)} %embed_ref.1), custom_call_target="tpu_custom_call" | custom-call | tf_op jit(solution)/shard_map/pack_first/pallas_call | solution.py:417
  3.5 2.9 %collective-permute-start.1 = (bf16[160,2560]{1,0:T(8,128)(2,1)}, bf16[160,2560]{1,0:T(8,128)(2,1)S(1)}, u32[]{:S(2)}, u32[]{:S(2)}) collective-permute-start(bf16[160,2560]{1,0:T(8,128)(2,1)} %get-tuple-element.40), channel_id=1, source_target_pairs={{0,8},{8,0},{16,24},{24,16},{1,9},{9,1},{17,25},{25,17},{2,10},{10... | collective-permute-start | bytes 2457608 | tf_op jit(solution)/shard_map/ppermute | solution.py:458
  6.4 1.5 collective-permute-start.2
  7.9 0.1 lt.26
  8.0 0.7 fusion.code_ref
  8.7 2.9 %pick.1 = bf16[4,400,640]{2,1,0:T(8,128)(2,1)} custom-call(s32[1]{0:T(128)} %bitcast.5.core_ref._, bf16[6,128,640]{2,1,0:T(8,128)(2,1)} %bitcast.26, s32[6,64]{1,0:T(8,128)} %fusion.code_ref), custom_call_target="tpu_custom_call" | custom-call | tf_op jit(solution)/shard_map/pick/pallas_call | solution.py:417
  11.6 4.9 %all-to-all-start = ((bf16[4,400,640]{2,1,0:T(8,128)(2,1)}), bf16[4,400,640]{2,1,0:T(8,128)(2,1)S(1)}, u32[]{:S(2)}, u32[]{:S(2)}) async-start(bf16[4,400,640]{2,1,0:T(8,128)(2,1)} %pick.1), calls=%async_computation | async-start | bytes 4096000 | tf_op jit(solution)/shard_map/all_to_all | solution.py:531
  16.5 3.8 %pack_second.1 = (bf16[320,3200]{1,0:T(8,128)(2,1)}, bf16[160,3200]{1,0:T(8,128)(2,1)}) custom-call(s32[1]{0:T(128)} %bitcast.5.core_ref._, bf16[320,3840]{1,0:T(8,128)(2,1)} %value_ref.4, bf16[320,3840]{1,0:T(8,128)(2,1)} %value_ref.4, bf16[320,3840]{1,0:T(8,128)(2,1)} %value_ref.4, bf16[320,1280]{1,0:T(8,128)(2,1)} %out_ref.1), custom_call_target="tpu_custom_call" | custom-call | tf_op jit(solution)/shard_map/pack_second/pallas_call | solution.py:417
  20.3 2.8 %order_global.1 = (bf16[320,1280]{1,0:T(8,128)(2,1)}, bf16[320,640]{1,0:T(8,128)(2,1)}) custom-call(s32[1]{0:T(128)} %bitcast.5.core_ref._, bf16[320,3840]{1,0:T(8,128)(2,1)} %value_ref.5, bf16[320,3840]{1,0:T(8,128)(2,1)} %value_ref.5, bf16[320,3840]{1,0:T(8,128)(2,1)} %value_ref.5), custom_call_target="tpu_custom_call" | custom-call | tf_op jit(solution)/shard_map/order_global/pallas_call | solution.py:417
  23.2 1.7 collective-permute-done.1
  24.9 1.6 collective-permute-done.2
  26.4 1.5 collective-permute-start.7
  28.0 1.1 collective-permute-start.6
  29.0 2.7 %pad_maximum_fusion.1.refs_1_ = bf16[320,2560]{1,0:T(8,128)(2,1)} fusion(bf16[160,2560]{1,0:T(8,128)(2,1)} %collective-permute-done.2, bf16[160,2560]{1,0:T(8,128)(2,1)} %copy-done.1), kind=kLoop, calls=%fused_computation.1 | loop fusion | flops 3276800 | bytes 3276800 | tf_op jit(solution)/shard_map/concatenate | solution.py:554
  31.7 0.0 collective-permute-start.3
  31.7 1.2 constant_dynamic-slice_fusion.1
  32.9 1.0 collective-permute-start.4
  33.9 18.3 %collective-permute-done.7 = bf16[160,3200]{1,0:T(8,128)(2,1)S(1)} collective-permute-done((bf16[160,3200]{1,0:T(8,128)(2,1)}, bf16[160,3200]{1,0:T(8,128)(2,1)S(1)}, u32[]{:S(2)}, u32[]{:S(2)}) %collective-permute-start.7) | collective-permute-done | bytes 1024032 | tf_op jit(solution)/shard_map/ppermute | solution.py:459
  52.2 0.0 collective-permute-done.6
  52.2 2.7 %pad_maximum_fusion.refs_1_ = bf16[320,3200]{1,0:T(8,128)(2,1)} fusion(bf16[160,3200]{1,0:T(8,128)(2,1)S(1)} %collective-permute-done.7, bf16[160,3200]{1,0:T(8,128)(2,1)} %collective-permute-done.6), kind=kLoop, calls=%fused_computation | loop fusion | flops 4096000 | bytes 4096000 | tf_op jit(solution)/shard_map/concatenate | solution.py:557
  54.9 1.3 constant_dynamic-slice_fusion
  56.2 1.1 collective-permute-start.9
  57.3 0.0 collective-permute-start.8
  57.3 2.6 %collective-permute-done.4.refs_3_ = bf16[160,2560]{1,0:T(8,128)(2,1)} collective-permute-done((bf16[160,2560]{1,0:T(8,128)(2,1)S(1)}, bf16[160,2560]{1,0:T(8,128)(2,1)}, u32[]{:S(2)}, u32[]{:S(2)}) %collective-permute-start.4) | collective-permute-done | bytes 819232 | tf_op jit(solution)/shard_map/ppermute | solution.py:468
  60.0 0.1 stack.105
  60.1 1.5 collective-permute-start.11
  61.6 0.5 collective-permute-start.12
  62.1 0.1 stack.95
  62.2 0.1 copy.11
  62.3 0.7 reshape.656.offset_ref
  63.0 0.1 all-to-all-done.picked_ref.code_ref.refs_2_
  63.1 1.4 copy-done
  64.5 24.7 %embed_windows.1 = (bf16[1536,1280]{1,0:T(8,128)(2,1)}, bf16[1536,1280]{1,0:T(8,128)(2,1)}, bf16[1536,640]{1,0:T(8,128)(2,1)}) custom-call(s32[24]{0:T(128)} %reshape.656.offset_ref, bf16[4,400,640]{2,1,0:T(8,128)(2,1)} %copy-done, bf16[4,400,640]{2,1,0:T(8,128)(2,1)} %copy-done, bf16[320,2560]{1,0:T(8,128)(2,1)} %get-tuple-element.52.refs_0_, ...), custom_call_target="tpu_custom_call" | custom-call | tf_op jit(solution)/shard_map/embed_windows/pallas_call | solution.py:417
  89.2 0.0 collective-permute-done.9.refs_3_
  89.2 0.1 collective-permute-start.10
  89.3 0.0 collective-permute-done.12.refs_7_
  89.3 1.2 collective-permute-start.14
  90.4 1.3 collective-permute-start.15
  91.7 1.2 broadcast_select_fusion
  93.0 1.1 collective-permute-start.13
  94.1 0.0 collective-permute-done.8.refs_2_
  94.1 0.0 collective-permute-done.10.refs_4_
  94.1 1.0 copy-done.6
  95.1 25.9 %windows_out.1.refs_0_ = bf16[1536,1280]{1,0:T(8,128)(2,1)} custom-call(s32[24]{0:T(128)} %reshape.656.offset_ref, bf16[1536,1280]{1,0:T(8,128)(2,1)} %get-tuple-element.57.embedded_ref, bf16[1536,1280]{1,0:T(8,128)(2,1)} %get-tuple-element.58.normed_ref, bf16[1536,640]{1,0:T(8,128)(2,1)} %get-tuple-element.59.mix_ref, bf16[4,400,640]{2,1,0:T(8,128)(2,1)} %copy-done, ...), custom_call_target="tpu_custom_call" | custom-call | flops 12582912000 | bytes 20070400 | tf_op jit(solution)/shard_map/windows_out/pallas_call | solution.py:417
  121.0 0.0 collective-permute-done.14.refs_10_
  121.0 0.0 collective-permute-done.13.refs_8_
  121.1 0.1 collective-permute-start.16
  121.2 1.0 collective-permute-start.18
  122.2 0.6 stack.87.offset_ref
  122.8 0.7 slice.9
  123.6 0.5 collective-permute-start.17
  124.1 3.8 %collective-permute-done = s32[6,64]{1,0:T(8,128)S(1)} collective-permute-done((s32[6,64]{1,0:T(8,128)S(1)}, s32[6,64]{1,0:T(8,128)S(1)}, u32[]{:S(2)}, u32[]{:S(2)}) %collective-permute-start) | collective-permute-done | bytes 1568 | tf_op jit(solution)/shard_map/ppermute | solution.py:451
  127.9 0.1 convert_element_type.14
  128.0 1.0 copy.12.refs_4_
  129.0 0.2 collective-permute-done.18.refs_12_
  129.2 0.0 collective-permute-done.17.refs_3_
  129.2 0.0 collective-permute-done.16.refs_1_
  129.3 0.7 copy-done.8
  130.0 0.0 copy-done.9
  130.0 37.6 %groups.1 = bf16[768,640]{1,0:T(8,128)(2,1)} custom-call(s32[5]{0:T(128)} %stack.87.offset_ref, bf16[1536,1280]{1,0:T(8,128)(2,1)} %windows_out.1.refs_0_, bf16[1536,1280]{1,0:T(8,128)(2,1)} %collective-permute-done.16.refs_1_, bf16[4,400,640]{2,1,0:T(8,128)(2,1)} %copy-done, bf16[4,16,128]{2,1,0:T(8,128)(2,1)} %copy-done.9, f32[768,1]{1,0:T(8,128)} %copy.12.refs_4_, ...), custom_call_target="tpu_custom_call" | custom-call | flops 17364418560 | bytes 14846976 | tf_op jit(solution)/shard_map/groups/pallas_call | solution.py:417
  167.6 1.3 fusion.3
  168.9 0.1 collective-permute-start.19
  168.9 1.9 %collective-permute-done.19 = bf16[384,640]{1,0:T(8,128)(2,1)S(1)} collective-permute-done((bf16[384,640]{1,0:T(8,128)(2,1)S(1)}, bf16[384,640]{1,0:T(8,128)(2,1)S(1)}, u32[]{:S(2)}, u32[]{:S(2)}) %collective-permute-start.19) | collective-permute-done | bytes 491552 | tf_op jit(solution)/shard_map/ppermute | solution.py:451
  170.8 1.2 maximum_select_fusion
  (31 shorter events, 0.2 us)
Async XLA Ops:
  0.0 7.9 %copy-start.5 = (s32[1,2,3,64]{3,1,2,0:T(2,128)S(1)}, s32[1,2,3,64]{3,1,2,0:T(2,128)}, u32[]{:S(2)}) copy-start(s32[1,2,3,64]{3,1,2,0:T(2,128)} %param.8) | copy-start | bytes 4612
  0.0 7.9 %copy-start.10 = (s32[1,2,3]{2,1,0:T(2,128)S(1)}, s32[1,2,3]{2,1,0:T(2,128)}, u32[]{:S(2)}) copy-start(s32[1,2,3]{2,1,0:T(2,128)} %param.9) | copy-start | bytes 76
  3.5 21.4 %collective-permute-start.1 = (bf16[160,2560]{1,0:T(8,128)(2,1)}, bf16[160,2560]{1,0:T(8,128)(2,1)S(1)}, u32[]{:S(2)}, u32[]{:S(2)}) collective-permute-start(bf16[160,2560]{1,0:T(8,128)(2,1)} %get-tuple-element.40), channel_id=1, source_target_pairs={{0,8},{8,0},{16,24},{24,16},{1,9},{9,1},{17,25},{25,17},{2,10},{10... | collective-permute-start | bytes 2457608 | tf_op jit(solution)/shard_map/ppermute | solution.py:458
  6.4 20.0 %collective-permute-start.2 = (bf16[160,2560]{1,0:T(8,128)(2,1)}, bf16[160,2560]{1,0:T(8,128)(2,1)}, u32[]{:S(2)}, u32[]{:S(2)}) collective-permute-start(bf16[160,2560]{1,0:T(8,128)(2,1)} %get-tuple-element.40), channel_id=1, source_target_pairs={{0,16},{8,24},{16,0},{24,8},{1,17},{9,25},{17,1},{25,9},{2,18},{10... | collective-permute-start | bytes 2457608 | tf_op jit(solution)/shard_map/ppermute | solution.py:459
  11.6 51.5 %all-to-all-start = ((bf16[4,400,640]{2,1,0:T(8,128)(2,1)}), bf16[4,400,640]{2,1,0:T(8,128)(2,1)S(1)}, u32[]{:S(2)}, u32[]{:S(2)}) async-start(bf16[4,400,640]{2,1,0:T(8,128)(2,1)} %pick.1), calls=%async_computation | async-start | bytes 4096000 | tf_op jit(solution)/shard_map/all_to_all | solution.py:531
  24.9 1.6 copy-start.1
  26.4 25.8 %collective-permute-start.7 = (bf16[160,3200]{1,0:T(8,128)(2,1)}, bf16[160,3200]{1,0:T(8,128)(2,1)S(1)}, u32[]{:S(2)}, u32[]{:S(2)}) collective-permute-start(bf16[160,3200]{1,0:T(8,128)(2,1)} %get-tuple-element.51), channel_id=1, source_target_pairs={{0,16},{8,24},{16,0},{24,8},{1,17},{9,25},{17,1},{25,9},{2,18},{10... | collective-permute-start | bytes 3072008 | tf_op jit(solution)/shard_map/ppermute | solution.py:459
  28.0 24.3 %collective-permute-start.6 = (bf16[160,3200]{1,0:T(8,128)(2,1)}, bf16[160,3200]{1,0:T(8,128)(2,1)}, u32[]{:S(2)}, u32[]{:S(2)}) collective-permute-start(bf16[160,3200]{1,0:T(8,128)(2,1)} %get-tuple-element.51), channel_id=1, source_target_pairs={{0,8},{8,0},{16,24},{24,16},{1,9},{9,1},{17,25},{25,17},{2,10},{10... | collective-permute-start | bytes 3072008 | tf_op jit(solution)/shard_map/ppermute | solution.py:458
  31.7 29.9 %collective-permute-start.3 = (bf16[320,2560]{1,0:T(8,128)(2,1)}, bf16[320,2560]{1,0:T(8,128)(2,1)}, u32[]{:S(2)}, u32[]{:S(2)}) collective-permute-start(bf16[320,2560]{1,0:T(8,128)(2,1)} %pad_maximum_fusion.1.refs_1_), channel_id=1, source_target_pairs={{0,4},{4,0},{1,5},{5,1},{2,6},{6,2},{3,7},{7,3},{8,12},{12,8},{9,1... | collective-permute-start | bytes 4915208 | tf_op jit(solution)/shard_map/ppermute | solution.py:451
  32.9 27.1 %collective-permute-start.4 = (bf16[160,2560]{1,0:T(8,128)(2,1)S(1)}, bf16[160,2560]{1,0:T(8,128)(2,1)}, u32[]{:S(2)}, u32[]{:S(2)}) collective-permute-start(bf16[160,2560]{1,0:T(8,128)(2,1)S(1)} %constant_dynamic-slice_fusion.1), channel_id=1, source_target_pairs={{0,8},{4,20},{8,0},{12,28},{16,24},{20,4},{24,16},{28,12},{1,9},{5... | collective-permute-start | bytes 2457608 | tf_op jit(solution)/shard_map/ppermute | solution.py:468
  56.2 33.0 %collective-permute-start.9 = (bf16[160,3200]{1,0:T(8,128)(2,1)S(1)}, bf16[160,3200]{1,0:T(8,128)(2,1)}, u32[]{:S(2)}, u32[]{:S(2)}) collective-permute-start(bf16[160,3200]{1,0:T(8,128)(2,1)S(1)} %constant_dynamic-slice_fusion), channel_id=1, source_target_pairs={{0,8},{4,20},{8,0},{12,28},{16,24},{20,4},{24,16},{28,12},{1,9},{5... | collective-permute-start | bytes 3072008 | tf_op jit(solution)/shard_map/ppermute | solution.py:468
  57.3 36.8 %collective-permute-start.8 = (bf16[320,3200]{1,0:T(8,128)(2,1)}, bf16[320,3200]{1,0:T(8,128)(2,1)}, u32[]{:S(2)}, u32[]{:S(2)}) collective-permute-start(bf16[320,3200]{1,0:T(8,128)(2,1)} %pad_maximum_fusion.refs_1_), channel_id=1, source_target_pairs={{0,4},{4,0},{1,5},{5,1},{2,6},{6,2},{3,7},{7,3},{8,12},{12,8},{9,1... | collective-permute-start | bytes 6144008 | tf_op jit(solution)/shard_map/ppermute | solution.py:451
  60.0 3.0 %collective-permute-start.5 = (bf16[160,2560]{1,0:T(8,128)(2,1)}, bf16[160,2560]{1,0:T(8,128)(2,1)}, u32[]{:S(2)}, u32[]{:S(2)}) collective-permute-start(bf16[160,2560]{1,0:T(8,128)(2,1)} %collective-permute-done.4.refs_3_), channel_id=1, source_target_pairs={{0,4},{4,0},{1,5},{5,1},{2,6},{6,2},{3,7},{7,3},{8,12},{12,8},{9,1... | collective-permute-start | bytes 2457608 | tf_op jit(solution)/shard_map/ppermute | solution.py:451
  60.1 29.2 %collective-permute-start.11 = (bf16[320,1280]{1,0:T(8,128)(2,1)}, bf16[320,1280]{1,0:T(8,128)(2,1)}, u32[]{:S(2)}, u32[]{:S(2)}) collective-permute-start(bf16[320,1280]{1,0:T(8,128)(2,1)} %get-tuple-element.62.refs_5_), channel_id=1, source_target_pairs={{0,8},{8,0},{16,24},{24,16},{1,9},{9,1},{17,25},{25,17},{2,10},{10... | collective-permute-start | bytes 2457608 | tf_op jit(solution)/shard_map/ppermute | solution.py:458
  61.6 27.7 %collective-permute-start.12 = (bf16[320,1280]{1,0:T(8,128)(2,1)}, bf16[320,1280]{1,0:T(8,128)(2,1)}, u32[]{:S(2)}, u32[]{:S(2)}) collective-permute-start(bf16[320,1280]{1,0:T(8,128)(2,1)} %get-tuple-element.62.refs_5_), channel_id=1, source_target_pairs={{0,16},{8,24},{16,0},{24,8},{1,17},{9,25},{17,1},{25,9},{2,18},{10... | collective-permute-start | bytes 2457608 | tf_op jit(solution)/shard_map/ppermute | solution.py:459
  63.1 1.4 copy-start
  89.2 4.9 %collective-permute-start.10 = (bf16[160,3200]{1,0:T(8,128)(2,1)}, bf16[160,3200]{1,0:T(8,128)(2,1)S(1)}, u32[]{:S(2)}, u32[]{:S(2)}) collective-permute-start(bf16[160,3200]{1,0:T(8,128)(2,1)} %collective-permute-done.9.refs_3_), channel_id=1, source_target_pairs={{0,4},{4,0},{1,5},{5,1},{2,6},{6,2},{3,7},{7,3},{8,12},{12,8},{9,1... | collective-permute-start | bytes 3072008 | tf_op jit(solution)/shard_map/ppermute | solution.py:451
  89.3 31.7 %collective-permute-start.14 = (bf16[320,640]{1,0:T(8,128)(2,1)}, bf16[320,640]{1,0:T(8,128)(2,1)S(1)}, u32[]{:S(2)}, u32[]{:S(2)}) collective-permute-start(bf16[320,640]{1,0:T(8,128)(2,1)} %get-tuple-element.71.refs_9_), channel_id=1, source_target_pairs={{0,8},{8,0},{16,24},{24,16},{1,9},{9,1},{17,25},{25,17},{2,10},{10... | collective-permute-start | bytes 1228808 | tf_op jit(solution)/shard_map/ppermute | solution.py:458
  90.4 30.6 %collective-permute-start.15 = (bf16[320,640]{1,0:T(8,128)(2,1)}, bf16[320,640]{1,0:T(8,128)(2,1)S(1)}, u32[]{:S(2)}, u32[]{:S(2)}) collective-permute-start(bf16[320,640]{1,0:T(8,128)(2,1)} %get-tuple-element.71.refs_9_), channel_id=1, source_target_pairs={{0,16},{8,24},{16,0},{24,8},{1,17},{9,25},{17,1},{25,9},{2,18},{10... | collective-permute-start | bytes 1228808 | tf_op jit(solution)/shard_map/ppermute | solution.py:459
  93.0 28.1 %collective-permute-start.13 = (bf16[320,1280]{1,0:T(8,128)(2,1)S(1)}, bf16[320,1280]{1,0:T(8,128)(2,1)S(1)}, u32[]{:S(2)}, u32[]{:S(2)}) collective-permute-start(bf16[320,1280]{1,0:T(8,128)(2,1)S(1)} %broadcast_select_fusion), channel_id=1, source_target_pairs={{0,8},{4,20},{8,0},{12,28},{16,24},{20,4},{24,16},{28,12},{1,9},{5... | collective-permute-start | bytes 2457608 | tf_op jit(solution)/shard_map/ppermute | solution.py:464
  94.1 1.0 copy-start.6
  95.1 27.1 %copy-start.4 = (s32[6,64]{1,0:T(8,128)S(1)}, s32[6,64]{1,0:T(8,128)}, u32[]{:S(2)}) copy-start(s32[6,64]{1,0:T(8,128)} %fusion.code_ref) | copy-start | bytes 4612
  121.0 8.2 %copy-start.2 = (bf16[320,640]{1,0:T(8,128)(2,1)}, bf16[320,640]{1,0:T(8,128)(2,1)S(1)}, u32[]{:S(2)}) copy-start(bf16[320,640]{1,0:T(8,128)(2,1)S(1)} %collective-permute-done.14.refs_10_) | copy-start | bytes 1228804
  121.0 8.2 %copy-start.3 = (bf16[320,640]{1,0:T(8,128)(2,1)}, bf16[320,640]{1,0:T(8,128)(2,1)S(1)}, u32[]{:S(2)}) copy-start(bf16[320,640]{1,0:T(8,128)(2,1)S(1)} %collective-permute-done.15.refs_11_) | copy-start | bytes 1228804
  121.1 8.2 %copy-start.7 = (bf16[320,1280]{1,0:T(8,128)(2,1)}, bf16[320,1280]{1,0:T(8,128)(2,1)S(1)}, u32[]{:S(2)}) copy-start(bf16[320,1280]{1,0:T(8,128)(2,1)S(1)} %collective-permute-done.13.refs_8_) | copy-start | bytes 2457604
  121.1 8.2 %collective-permute-start.16 = (bf16[1536,1280]{1,0:T(8,128)(2,1)}, bf16[1536,1280]{1,0:T(8,128)(2,1)}, u32[]{:S(2)}, u32[]{:S(2)}) collective-permute-start(bf16[1536,1280]{1,0:T(8,128)(2,1)} %windows_out.1.refs_0_), channel_id=1, source_target_pairs={{0,4},{4,0},{1,5},{5,1},{2,6},{6,2},{3,7},{7,3},{8,12},{12,8},{9,1... | collective-permute-start | bytes 11796488 | tf_op jit(solution)/shard_map/ppermute | solution.py:451
  121.2 8.0 %collective-permute-start.18 = (bf16[320,640]{1,0:T(8,128)(2,1)S(1)}, bf16[320,640]{1,0:T(8,128)(2,1)S(1)}, u32[]{:S(2)}, u32[]{:S(2)}) collective-permute-start(bf16[320,640]{1,0:T(8,128)(2,1)S(1)} %broadcast_select_fusion.1), channel_id=1, source_target_pairs={{0,8},{4,20},{8,0},{12,28},{16,24},{20,4},{24,16},{28,12},{1,9},{5... | collective-permute-start | bytes 1228808 | tf_op jit(solution)/shard_map/ppermute | solution.py:464
  122.2 5.7 %collective-permute-start = (s32[6,64]{1,0:T(8,128)S(1)}, s32[6,64]{1,0:T(8,128)S(1)}, u32[]{:S(2)}, u32[]{:S(2)}) collective-permute-start(s32[6,64]{1,0:T(8,128)S(1)} %copy-done.4), channel_id=1, source_target_pairs={{0,4},{4,0},{1,5},{5,1},{2,6},{6,2},{3,7},{7,3},{8,12},{12,8},{9,1... | collective-permute-start | bytes 4616 | tf_op jit(solution)/shard_map/ppermute | solution.py:451
  123.6 5.7 %collective-permute-start.17 = (bf16[4,16,128]{2,1,0:T(8,128)(2,1)S(1)}, bf16[4,16,128]{2,1,0:T(8,128)(2,1)S(1)}, u32[]{:S(2)}, u32[]{:S(2)}) collective-permute-start(bf16[4,16,128]{2,1,0:T(8,128)(2,1)S(1)} %slice.9), channel_id=1, source_target_pairs={{0,4},{4,0},{1,5},{5,1},{2,6},{6,2},{3,7},{7,3},{8,12},{12,8},{9,1... | collective-permute-start | bytes 49160 | tf_op jit(solution)/shard_map/ppermute | solution.py:451
  129.2 0.8 copy-start.8
  129.2 0.8 copy-start.9
  168.9 1.9 %collective-permute-start.19 = (bf16[384,640]{1,0:T(8,128)(2,1)S(1)}, bf16[384,640]{1,0:T(8,128)(2,1)S(1)}, u32[]{:S(2)}, u32[]{:S(2)}) collective-permute-start(bf16[384,640]{1,0:T(8,128)(2,1)S(1)} %get-tuple-element.79), channel_id=1, source_target_pairs={{0,4},{4,0},{1,5},{5,1},{2,6},{6,2},{3,7},{7,3},{8,12},{12,8},{9,1... | collective-permute-start | bytes 1474568 | tf_op jit(solution)/shard_map/ppermute | solution.py:451
